TPU v7x, 32 devices: a whole 2x2x4 slice. The times are simulated.
32 devices in a mesh: dp: 16 (over z, y, core), fsdp: 2 (over x).
Axes of the slice: x: 2, y: 2, z: 4, core: 2. Of those that a mesh axis runs over, the one named last changes fastest.
Arguments:
- coarse_clips: bfloat16 [128, 8, 8, 1024], P(('dp', 'fsdp')), may hold values from -6 to 6
- medium_clips: bfloat16 [128, 12, 12, 1024], P(('dp', 'fsdp')), may hold values from -6 to 6
- fine_clips: bfloat16 [128, 14, 14, 1024], P(('dp', 'fsdp')), may hold values from -6 to 6
- clip_counts: int32 [32, 3], P(('dp', 'fsdp')), may hold values from 0 to 1, as said below
- frame_counts: int32 [32, 3], P(('dp', 'fsdp')), may hold values from 2 to 4, as said below
- reduce_one: float32 [1024, 512], P(('dp', 'fsdp')), may hold values from -0.1875 to 0.1875
- spatial_one: float32 [4608, 512], P(('dp', 'fsdp')), may hold values from -0.09375 to 0.09375
- expand_one: float32 [512, 2048], P(('dp', 'fsdp')), may hold values from -0.25 to 0.25
- shortcut_one: float32 [1024, 2048], P(('dp', 'fsdp')), may hold values from -0.1875 to 0.1875
- reduce_two: float32 [2048, 512], P(('dp', 'fsdp')), may hold values from -0.125 to 0.125
- excite_down: float32 [512, 32], P(('dp', 'fsdp')), may hold values from -0.25 to 0.25
- excite_up: float32 [32, 512], P(None, ('dp', 'fsdp')), may hold values from -4 to 4
- temporal_mix: float32 [27, 16384], P(None, ('dp', 'fsdp')), may hold values from -0.1875 to 0.1875
- expand_two: float32 [512, 2048], P(('dp', 'fsdp')), may hold values from -0.25 to 0.25
- norm_params: float32 [2, 8192], P(None, ('dp', 'fsdp')), may hold values from -1 to 1.5, as said below
- motion_kernel: float32 [9, 32], replicated, may hold values from -1.5 to 1.5
- coarse_cot: bfloat16 [128, 4, 4, 2048], P(('dp', 'fsdp')), may hold values from -6 to 6
- medium_cot: bfloat16 [128, 6, 6, 2048], P(('dp', 'fsdp')), may hold values from -6 to 6
- fine_cot: bfloat16 [128, 7, 7, 2048], P(('dp', 'fsdp')), may hold values from -6 to 6
Outputs:
- coarse_out: bfloat16 [128, 4, 4, 2048], P(('dp', 'fsdp'))
- medium_out: bfloat16 [128, 6, 6, 2048], P(('dp', 'fsdp'))
- fine_out: bfloat16 [128, 7, 7, 2048], P(('dp', 'fsdp'))
- coarse_input_grad: bfloat16 [128, 8, 8, 1024], P(('dp', 'fsdp'))
- medium_input_grad: bfloat16 [128, 12, 12, 1024], P(('dp', 'fsdp'))
- fine_input_grad: bfloat16 [128, 14, 14, 1024], P(('dp', 'fsdp'))
- reduce_one_grad: float32 [1024, 512], P(('dp', 'fsdp'))
- spatial_one_grad: float32 [4608, 512], P(('dp', 'fsdp'))
- expand_one_grad: float32 [512, 2048], P(('dp', 'fsdp'))
- shortcut_one_grad: float32 [1024, 2048], P(('dp', 'fsdp'))
- reduce_two_grad: float32 [2048, 512], P(('dp', 'fsdp'))
- excite_down_grad: float32 [512, 32], P(('dp', 'fsdp'))
- excite_up_grad: float32 [32, 512], P(None, ('dp', 'fsdp'))
- temporal_mix_grad: float32 [27, 16384], P(None, ('dp', 'fsdp'))
- expand_two_grad: float32 [512, 2048], P(('dp', 'fsdp'))
- norm_params_grad: float32 [2, 8192], P(None, ('dp', 'fsdp'))
- motion_kernel_grad: float32 [9, 32], replicated
Inputs may be any that keep to these rules, and one draw needn't show every extreme that they name: `clip_counts`: in every group some device has 1 live clips. `frame_counts`: in every group some slot has 4 live frames. `norm_params`: row 0 gains, row 1 biases.
All inputs are finite; a program needn't handle non-finite values.
Results may differ from a plain program's by a relative error of at most 0.017.
The roundings to bfloat16 on the way count: a program that leaves them out, or rounds other values in their place, can miss the bound.
Values may be sent and summed in bfloat16 or wider, within the bound.
No kernel may reach another device: no remote copies, remote signals or barrier semaphores. Data moves between devices by JAX's collectives and lax.ppermute only.
A program may use at most 320 MiB of HBM per device.

v0:
```python
from functools import reduce

import jax
import jax.numpy as jnp
from jax import lax
from jax.sharding import PartitionSpec as P

MID = 512
C_OUT = 2048
FRAMES = 4
CLIPS = 1
GROUP = 128
SHIFT = 16


epsilon = 1e-05
highest = lax.Precision.HIGHEST


def sigmoid_linear(values):
    return values * jax.nn.sigmoid(values)


def pointwise(inputs_low, weight_low):
    return jnp.einsum("bhwc,cd->bhwd", inputs_low, weight_low, preferred_element_type=jnp.float32)


def pointwise_input_grad(grad_low, weight_low):
    return jnp.einsum("bhwd,cd->bhwc", grad_low, weight_low, preferred_element_type=jnp.float32)


def pointwise_weight_grad(inputs_low, grad_low):
    return jnp.einsum("bhwc,bhwd->cd", inputs_low, grad_low, preferred_element_type=jnp.float32)


def tap_window(padded, tap_id, stride, rows_out, cols_out):
    row_start, col_start = divmod(tap_id, 3)
    return padded[
        :,
        row_start : row_start + stride * (rows_out - 1) + 1 : stride,
        col_start : col_start + stride * (cols_out - 1) + 1 : stride,
        :,
    ]


def conv_spatial(inputs_low, kernel_low, stride):
    padded = jnp.pad(inputs_low, ((0, 0), (1, 1), (1, 1), (0, 0)))
    rows_out = inputs_low.shape[1] // stride
    cols_out = inputs_low.shape[2] // stride
    terms = [
        jnp.einsum(
            "bhwc,cd->bhwd",
            tap_window(padded, tap_id, stride, rows_out, cols_out),
            kernel_low[tap_id],
            preferred_element_type=jnp.float32,
        )
        for tap_id in range(9)
    ]
    return reduce(jnp.add, terms)


def conv_input_grad(grad_low, kernel_low, stride, rows_in, cols_in):
    rows_out = grad_low.shape[1]
    cols_out = grad_low.shape[2]
    span_rows = stride * (rows_out - 1) + 1
    span_cols = stride * (cols_out - 1) + 1
    summed = jnp.zeros(
        (grad_low.shape[0], rows_in + 2, cols_in + 2, kernel_low.shape[1]), jnp.float32
    )
    for tap_id in range(9):
        row_start, col_start = divmod(tap_id, 3)
        placed = jnp.einsum(
            "bhwd,cd->bhwc", grad_low, kernel_low[tap_id], preferred_element_type=jnp.float32
        )
        placed = lax.pad(
            placed,
            jnp.float32(0.0),
            (
                (0, 0, 0),
                (row_start, rows_in + 2 - span_rows - row_start, stride - 1),
                (col_start, cols_in + 2 - span_cols - col_start, stride - 1),
                (0, 0, 0),
            ),
        )
        summed = summed + placed
    return summed[:, 1:-1, 1:-1, :]


def conv_weight_grad(inputs_low, grad_low, stride):
    padded = jnp.pad(inputs_low, ((0, 0), (1, 1), (1, 1), (0, 0)))
    rows_out = grad_low.shape[1]
    cols_out = grad_low.shape[2]
    return jnp.stack(
        [
            jnp.einsum(
                "bhwc,bhwd->cd",
                tap_window(padded, tap_id, stride, rows_out, cols_out),
                grad_low,
                preferred_element_type=jnp.float32,
            )
            for tap_id in range(9)
        ]
    )


def local_sums(values, masks):
    sum_first = jnp.zeros((values[0].shape[-1],), jnp.float32)
    sum_second = jnp.zeros((values[0].shape[-1],), jnp.float32)
    for tensor, live_mask in zip(values, masks):
        sum_first = sum_first + jnp.sum(tensor * live_mask, axis=(0, 1, 2))
        sum_second = sum_second + jnp.sum(tensor * tensor * live_mask, axis=(0, 1, 2))
    return (sum_first, sum_second)


def global_sums(values, masks):
    sum_first, sum_second = local_sums(values, masks)
    return lax.psum((sum_first, sum_second), ("dp", "fsdp"))


def norm_apply(tensor, sum_first, sum_second, total_count, gain_row, biases):
    center = sum_first / total_count
    spread = sum_second / total_count - center * center
    return (tensor - center) * lax.rsqrt(spread + epsilon) * gain_row + biases


def act_forward(values, sums, gain_row, biases, total_count, masks):
    return [
        live_mask
        * sigmoid_linear(norm_apply(tensor, sums[0], sums[1], total_count, gain_row, biases))
        for tensor, live_mask in zip(values, masks)
    ]


def combine_back(values, masks, local_grads, global_first, global_second):
    return [
        grad_one + live_mask * (global_first + 2.0 * tensor * global_second)
        for tensor, live_mask, grad_one in zip(values, masks, local_grads)
    ]


def act_back_local(values, sums, gain_row, biases, total_count, masks, grads):

    def piece(vals, sum_a, sum_b, gain_vals, bias_vals):
        return act_forward(vals, (sum_a, sum_b), gain_vals, bias_vals, total_count, masks)

    unused, pull_back = jax.vjp(piece, values, sums[0], sums[1], gain_row, biases)
    return pull_back(grads)


def finish_back(values, masks, local_grads, grad_first, grad_second):
    global_first, global_second = lax.psum((grad_first, grad_second), ("dp", "fsdp"))
    return combine_back(values, masks, local_grads, global_first, global_second)


def act_back(values, sums, gain_row, biases, total_count, masks, grads):
    grad_vals, grad_first, grad_second, grad_gain, grad_bias = act_back_local(
        values, sums, gain_row, biases, total_count, masks, grads
    )
    return (finish_back(values, masks, grad_vals, grad_first, grad_second), grad_gain, grad_bias)


def shift_frames(values, frames, channels_moved):
    layout = values.shape
    blocks = values.reshape((-1, frames) + layout[1:])
    earlier = jnp.pad(blocks[:, :-1], ((0, 0), (1, 0), (0, 0), (0, 0), (0, 0)))
    later_frames = jnp.pad(blocks[:, 1:], ((0, 0), (0, 1), (0, 0), (0, 0), (0, 0)))
    joined = jnp.concatenate(
        [
            earlier[..., :channels_moved],
            later_frames[..., channels_moved : 2 * channels_moved],
            blocks[..., 2 * channels_moved :],
        ],
        axis=-1,
    )
    return joined.reshape(layout)


def shift_frames_back(grads, frames, channels_moved):
    layout = grads.shape
    blocks = grads.reshape((-1, frames) + layout[1:])
    earlier = jnp.pad(blocks[:, :-1], ((0, 0), (1, 0), (0, 0), (0, 0), (0, 0)))
    later_frames = jnp.pad(blocks[:, 1:], ((0, 0), (0, 1), (0, 0), (0, 0), (0, 0)))
    joined = jnp.concatenate(
        [
            later_frames[..., :channels_moved],
            earlier[..., channels_moved : 2 * channels_moved],
            blocks[..., 2 * channels_moved :],
        ],
        axis=-1,
    )
    return joined.reshape(layout)


def next_frame(values, frames):
    layout = values.shape
    blocks = values.reshape((-1, frames) + layout[1:])
    later_frames = jnp.pad(blocks[:, 1:], ((0, 0), (0, 1), (0, 0), (0, 0), (0, 0)))
    return later_frames.reshape(layout)


def depthwise(values, kernel):
    padded = jnp.pad(values, ((0, 0), (1, 1), (1, 1), (0, 0)))
    rows_out = values.shape[1]
    cols_out = values.shape[2]
    summed = jnp.zeros(values.shape, jnp.float32)
    for tap_id in range(9):
        row_start, col_start = divmod(tap_id, 3)
        summed = (
            summed
            + padded[:, row_start : row_start + rows_out, col_start : col_start + cols_out, :]
            * kernel[tap_id]
        )
    return summed


def excite(features, squeezed, up_weight, kernel, next_masks, frames):
    gated_all = []
    for feature_one, squeezed_one, next_mask in zip(features, squeezed, next_masks):
        motion = next_mask * (depthwise(next_frame(squeezed_one, frames), kernel) - squeezed_one)
        pooled = jnp.mean(motion, axis=(1, 2))
        logits = jnp.dot(pooled, up_weight, precision=highest)
        gated_all.append(feature_one * (0.5 + jax.nn.sigmoid(logits))[:, None, None, :])
    return gated_all


def on_device(
    coarse_clips,
    medium_clips,
    fine_clips,
    clip_counts,
    frame_counts,
    reduce_one,
    spatial_one,
    expand_one,
    shortcut_one,
    reduce_two,
    excite_down,
    excite_up,
    temporal_mix,
    expand_two,
    norm_params,
    motion_kernel,
    coarse_cot,
    medium_cot,
    fine_cot,
):
    frames = FRAMES
    clips = [coarse_clips, medium_clips, fine_clips]
    cotangents = [tensor.astype(jnp.float32) for tensor in (coarse_cot, medium_cot, fine_cot)]
    slot_ids = jnp.arange(CLIPS, dtype=jnp.int32)
    frame_ids = jnp.arange(FRAMES, dtype=jnp.int32)
    masks = []
    next_masks = []
    local_in = jnp.zeros((), jnp.float32)
    local_out = jnp.zeros((), jnp.float32)
    for group_id in range(3):
        clip_alive = slot_ids < clip_counts[0, group_id]
        frame_alive = frame_ids[None, :] < frame_counts[:, group_id][:, None]
        alive_now = (clip_alive[:, None] & frame_alive).astype(jnp.float32)
        later_alive = jnp.pad(alive_now[:, 1:], ((0, 0), (0, 1)))
        masks.append(alive_now.reshape(-1, 1, 1, 1))
        next_masks.append(later_alive.reshape(-1, 1, 1, 1))
        side_in = clips[group_id].shape[1]
        local_in = local_in + jnp.sum(alive_now) * (side_in * side_in)
        local_out = local_out + jnp.sum(alive_now) * (side_in // 2 * (side_in // 2))
    inputs = [tensor * live_mask.astype(jnp.bfloat16) for tensor, live_mask in zip(clips, masks)]
    bounds = [
        0,
        MID,
        2 * MID,
        2 * MID + C_OUT,
        2 * MID + 2 * C_OUT,
        3 * MID + 2 * C_OUT,
        4 * MID + 2 * C_OUT,
        4 * MID + 3 * C_OUT,
    ]
    reduce1_low, spatial1_low, expand1_low, short1_low, norm_low = (
        lax.all_gather(reduce_one.astype(jnp.bfloat16), ("dp", "fsdp"), axis=0, tiled=True),
        lax.all_gather(spatial_one.astype(jnp.bfloat16), ("dp", "fsdp"), axis=0, tiled=True),
        lax.all_gather(expand_one.astype(jnp.bfloat16), ("dp", "fsdp"), axis=0, tiled=True),
        lax.all_gather(shortcut_one.astype(jnp.bfloat16), ("dp", "fsdp"), axis=0, tiled=True),
        lax.all_gather(norm_params.astype(jnp.bfloat16), ("dp", "fsdp"), axis=1, tiled=True),
    )
    norm_full = norm_low.astype(jnp.float32)
    gain_segs = [norm_full[0, bounds[seg_id] : bounds[seg_id + 1]] for seg_id in range(7)]
    bias_segs = [norm_full[1, bounds[seg_id] : bounds[seg_id + 1]] for seg_id in range(7)]
    spatial_kernel = spatial1_low.reshape(9, MID, MID)
    conv_first = [pointwise(tensor, reduce1_low) for tensor in inputs]
    first_a, first_b = local_sums(conv_first, masks)
    sum_one, square_one, count_in, count_out = lax.psum(
        (first_a, first_b, local_in, local_out), ("dp", "fsdp")
    )
    sums_first = (sum_one, square_one)
    hidden_one = [
        tensor.astype(jnp.bfloat16)
        for tensor in act_forward(
            conv_first, sums_first, gain_segs[0], bias_segs[0], count_in, masks
        )
    ]
    conv_second = [conv_spatial(tensor, spatial_kernel, 2) for tensor in hidden_one]
    sums_second = global_sums(conv_second, masks)
    hidden_two = [
        tensor.astype(jnp.bfloat16)
        for tensor in act_forward(
            conv_second, sums_second, gain_segs[1], bias_segs[1], count_out, masks
        )
    ]
    conv_third = [pointwise(tensor, expand1_low) for tensor in hidden_two]
    strided = [tensor[:, ::2, ::2, :] for tensor in inputs]
    conv_skip = [pointwise(tensor, short1_low) for tensor in strided]
    third_a, third_b = local_sums(conv_third, masks)
    skip_a, skip_b = local_sums(conv_skip, masks)
    joint_third_a, joint_third_b, joint_skip_a, joint_skip_b = lax.psum(
        (third_a, third_b, skip_a, skip_b), ("dp", "fsdp")
    )

    def joint_piece(
        third_vals,
        skip_vals,
        sum_third,
        square_third,
        sum_skip,
        square_skip,
        gain_third,
        bias_third,
        gain_skip,
        bias_skip,
    ):
        return [
            live_mask
            * sigmoid_linear(
                norm_apply(third, sum_third, square_third, count_out, gain_third, bias_third)
                + norm_apply(skipped, sum_skip, square_skip, count_out, gain_skip, bias_skip)
            )
            for third, skipped, live_mask in zip(third_vals, skip_vals, masks)
        ]

    block_one = joint_piece(
        conv_third,
        conv_skip,
        joint_third_a,
        joint_third_b,
        joint_skip_a,
        joint_skip_b,
        gain_segs[2],
        bias_segs[2],
        gain_segs[3],
        bias_segs[3],
    )
    reduce2_low, down_low, up_low, mix_low, expand2_low = (
        lax.all_gather(reduce_two.astype(jnp.bfloat16), ("dp", "fsdp"), axis=0, tiled=True),
        lax.all_gather(excite_down.astype(jnp.bfloat16), ("dp", "fsdp"), axis=0, tiled=True),
        lax.all_gather(excite_up.astype(jnp.bfloat16), ("dp", "fsdp"), axis=1, tiled=True),
        lax.all_gather(temporal_mix.astype(jnp.bfloat16), ("dp", "fsdp"), axis=1, tiled=True),
        lax.all_gather(expand_two.astype(jnp.bfloat16), ("dp", "fsdp"), axis=0, tiled=True),
    )
    up_weight = up_low.astype(jnp.float32)
    mix_kernel = mix_low.reshape(3, 9, GROUP, GROUP)
    entry_low = [tensor.astype(jnp.bfloat16) for tensor in block_one]
    conv_entry = [pointwise(tensor, reduce2_low) for tensor in entry_low]
    sums_entry = global_sums(conv_entry, masks)
    features = act_forward(conv_entry, sums_entry, gain_segs[4], bias_segs[4], count_out, masks)
    features_low = [tensor.astype(jnp.bfloat16) for tensor in features]
    squeezed = [pointwise(tensor, down_low) for tensor in features_low]
    gated_all = excite(features, squeezed, up_weight, motion_kernel, next_masks, frames)
    mixed_all = []
    saved_inputs = []
    for gated_one, live_mask in zip(gated_all, masks):
        pieces = jnp.split(gated_one, 4, axis=-1)
        outputs = [pieces[0]]
        kept_low = []
        for branch_id in range(1, 4):
            shifted = shift_frames(pieces[branch_id] + outputs[-1], frames, SHIFT).astype(
                jnp.bfloat16
            )
            kept_low.append(shifted)
            outputs.append(live_mask * conv_spatial(shifted, mix_kernel[branch_id - 1], 1))
        saved_inputs.append(kept_low)
        mixed_all.append(jnp.concatenate(outputs, axis=-1))
    sums_mixed = global_sums(mixed_all, masks)
    activated_low = [
        tensor.astype(jnp.bfloat16)
        for tensor in act_forward(
            mixed_all, sums_mixed, gain_segs[5], bias_segs[5], count_out, masks
        )
    ]
    conv_last = [pointwise(tensor, expand2_low) for tensor in activated_low]
    sums_last = global_sums(conv_last, masks)

    def final_piece(last_vals, sum_last, square_last, gain_last, bias_last, skip_vals):
        return [
            live_mask
            * sigmoid_linear(
                norm_apply(tensor, sum_last, square_last, count_out, gain_last, bias_last) + skipped
            )
            for tensor, skipped, live_mask in zip(last_vals, skip_vals, masks)
        ]

    results, pull_final = jax.vjp(
        final_piece, conv_last, sums_last[0], sums_last[1], gain_segs[6], bias_segs[6], block_one
    )
    grad_last, grad_last_a, grad_last_b, grad_gain6, grad_bias6, grad_block = pull_final(cotangents)
    grad_last = finish_back(conv_last, masks, grad_last, grad_last_a, grad_last_b)
    reduce2_low, down_low, up_low, mix_low, expand2_low = (
        lax.all_gather(reduce_two.astype(jnp.bfloat16), ("dp", "fsdp"), axis=0, tiled=True),
        lax.all_gather(excite_down.astype(jnp.bfloat16), ("dp", "fsdp"), axis=0, tiled=True),
        lax.all_gather(excite_up.astype(jnp.bfloat16), ("dp", "fsdp"), axis=1, tiled=True),
        lax.all_gather(temporal_mix.astype(jnp.bfloat16), ("dp", "fsdp"), axis=1, tiled=True),
        lax.all_gather(expand_two.astype(jnp.bfloat16), ("dp", "fsdp"), axis=0, tiled=True),
    )
    up_weight = up_low.astype(jnp.float32)
    mix_kernel = mix_low.reshape(3, 9, GROUP, GROUP)
    grad_last_low = [tensor.astype(jnp.bfloat16) for tensor in grad_last]
    grad_expand2 = reduce(
        jnp.add,
        [
            pointwise_weight_grad(act_low, grad_low)
            for act_low, grad_low in zip(activated_low, grad_last_low)
        ],
    )
    grad_activated = [pointwise_input_grad(grad_low, expand2_low) for grad_low in grad_last_low]
    grad_mixed, grad_gain5, grad_bias5 = act_back(
        mixed_all, sums_mixed, gain_segs[5], bias_segs[5], count_out, masks, grad_activated
    )
    grad_mix = [jnp.zeros((9, GROUP, GROUP), jnp.float32) for branch_id in range(3)]
    grad_gated = []
    for group_id in range(3):
        live_mask = masks[group_id]
        rows_here = grad_mixed[group_id].shape[1]
        cols_here = grad_mixed[group_id].shape[2]
        grad_pieces = jnp.split(grad_mixed[group_id], 4, axis=-1)
        carried = jnp.zeros(grad_pieces[0].shape, jnp.float32)
        grad_groups = [None, None, None, None]
        for branch_id in (3, 2, 1):
            grad_conv_low = (live_mask * (grad_pieces[branch_id] + carried)).astype(jnp.bfloat16)
            grad_mix[branch_id - 1] = grad_mix[branch_id - 1] + conv_weight_grad(
                saved_inputs[group_id][branch_id - 1], grad_conv_low, 1
            )
            grad_shifted = conv_input_grad(
                grad_conv_low, mix_kernel[branch_id - 1], 1, rows_here, cols_here
            )
            carried = shift_frames_back(grad_shifted, frames, SHIFT)
            grad_groups[branch_id] = carried
        grad_groups[0] = grad_pieces[0] + carried
        grad_gated.append(jnp.concatenate(grad_groups, axis=-1))

    def excite_piece(feature_vals, squeezed_vals, up_vals, kernel_vals):
        return excite(feature_vals, squeezed_vals, up_vals, kernel_vals, next_masks, frames)

    gated_again, pull_excite = jax.vjp(excite_piece, features, squeezed, up_weight, motion_kernel)
    grad_features, grad_squeezed, grad_up, grad_kernel_local = pull_excite(grad_gated)
    grad_squeezed_low = [tensor.astype(jnp.bfloat16) for tensor in grad_squeezed]
    grad_down = reduce(
        jnp.add,
        [
            pointwise_weight_grad(feat_low, grad_low)
            for feat_low, grad_low in zip(features_low, grad_squeezed_low)
        ],
    )
    grad_features = [
        direct + pointwise_input_grad(grad_low, down_low)
        for direct, grad_low in zip(grad_features, grad_squeezed_low)
    ]
    grad_entry, grad_entry_a, grad_entry_b, grad_gain4, grad_bias4 = act_back_local(
        conv_entry, sums_entry, gain_segs[4], bias_segs[4], count_out, masks, grad_features
    )
    global_entry_a, global_entry_b, kernel_grad = lax.psum(
        (grad_entry_a, grad_entry_b, grad_kernel_local), ("dp", "fsdp")
    )
    grad_entry = combine_back(conv_entry, masks, grad_entry, global_entry_a, global_entry_b)
    grad_entry_low = [tensor.astype(jnp.bfloat16) for tensor in grad_entry]
    grad_reduce2 = reduce(
        jnp.add,
        [
            pointwise_weight_grad(ent_low, grad_low)
            for ent_low, grad_low in zip(entry_low, grad_entry_low)
        ],
    )
    grad_block = [
        direct + pointwise_input_grad(grad_low, reduce2_low)
        for direct, grad_low in zip(grad_block, grad_entry_low)
    ]
    grad_mix_all = jnp.stack(grad_mix).reshape(27, GROUP * GROUP)
    second_grads = (
        lax.psum_scatter(grad_reduce2, ("dp", "fsdp"), scatter_dimension=0, tiled=True),
        lax.psum_scatter(grad_down, ("dp", "fsdp"), scatter_dimension=0, tiled=True),
        lax.psum_scatter(grad_up, ("dp", "fsdp"), scatter_dimension=1, tiled=True),
        lax.psum_scatter(grad_mix_all, ("dp", "fsdp"), scatter_dimension=1, tiled=True),
        lax.psum_scatter(grad_expand2, ("dp", "fsdp"), scatter_dimension=0, tiled=True),
    )
    reduce1_low, spatial1_low, expand1_low, short1_low = (
        lax.all_gather(reduce_one.astype(jnp.bfloat16), ("dp", "fsdp"), axis=0, tiled=True),
        lax.all_gather(spatial_one.astype(jnp.bfloat16), ("dp", "fsdp"), axis=0, tiled=True),
        lax.all_gather(expand_one.astype(jnp.bfloat16), ("dp", "fsdp"), axis=0, tiled=True),
        lax.all_gather(shortcut_one.astype(jnp.bfloat16), ("dp", "fsdp"), axis=0, tiled=True),
    )
    spatial_kernel = spatial1_low.reshape(9, MID, MID)
    unused_block, pull_joint = jax.vjp(
        joint_piece,
        conv_third,
        conv_skip,
        joint_third_a,
        joint_third_b,
        joint_skip_a,
        joint_skip_b,
        gain_segs[2],
        bias_segs[2],
        gain_segs[3],
        bias_segs[3],
    )
    (
        grad_third,
        grad_skip,
        grad_ta,
        grad_tb,
        grad_sa,
        grad_sb,
        grad_gain2,
        grad_bias2,
        grad_gain3,
        grad_bias3,
    ) = pull_joint(grad_block)
    global_ta, global_tb, global_sa, global_sb = lax.psum(
        (grad_ta, grad_tb, grad_sa, grad_sb), ("dp", "fsdp")
    )
    grad_third = combine_back(conv_third, masks, grad_third, global_ta, global_tb)
    grad_skip = combine_back(conv_skip, masks, grad_skip, global_sa, global_sb)
    grad_third_low = [tensor.astype(jnp.bfloat16) for tensor in grad_third]
    grad_skip_low = [tensor.astype(jnp.bfloat16) for tensor in grad_skip]
    grad_expand1 = reduce(
        jnp.add,
        [
            pointwise_weight_grad(hid_low, grad_low)
            for hid_low, grad_low in zip(hidden_two, grad_third_low)
        ],
    )
    grad_short = reduce(
        jnp.add,
        [
            pointwise_weight_grad(str_low, grad_low)
            for str_low, grad_low in zip(strided, grad_skip_low)
        ],
    )
    grad_hidden_two = [pointwise_input_grad(grad_low, expand1_low) for grad_low in grad_third_low]
    grad_second, grad_gain1, grad_bias1 = act_back(
        conv_second, sums_second, gain_segs[1], bias_segs[1], count_out, masks, grad_hidden_two
    )
    grad_second_low = [tensor.astype(jnp.bfloat16) for tensor in grad_second]
    grad_spatial = reduce(
        jnp.add,
        [
            conv_weight_grad(hid_low, grad_low, 2)
            for hid_low, grad_low in zip(hidden_one, grad_second_low)
        ],
    )
    grad_hidden_one = [
        conv_input_grad(grad_low, spatial_kernel, 2, hid_low.shape[1], hid_low.shape[2])
        for grad_low, hid_low in zip(grad_second_low, hidden_one)
    ]
    grad_first, grad_gain0, grad_bias0 = act_back(
        conv_first, sums_first, gain_segs[0], bias_segs[0], count_in, masks, grad_hidden_one
    )
    grad_first_low = [tensor.astype(jnp.bfloat16) for tensor in grad_first]
    grad_reduce1 = reduce(
        jnp.add,
        [
            pointwise_weight_grad(inp_low, grad_low)
            for inp_low, grad_low in zip(inputs, grad_first_low)
        ],
    )
    input_grads = []
    for grad_low, skip_low, live_mask in zip(grad_first_low, grad_skip_low, masks):
        through_skip = lax.pad(
            pointwise_input_grad(skip_low, short1_low),
            jnp.float32(0.0),
            ((0, 0, 0), (0, 1, 1), (0, 1, 1), (0, 0, 0)),
        )
        input_grads.append(
            (live_mask * (pointwise_input_grad(grad_low, reduce1_low) + through_skip)).astype(
                jnp.bfloat16
            )
        )
    grad_norm = jnp.stack(
        [
            jnp.concatenate(
                [grad_gain0, grad_gain1, grad_gain2, grad_gain3, grad_gain4, grad_gain5, grad_gain6]
            ),
            jnp.concatenate(
                [grad_bias0, grad_bias1, grad_bias2, grad_bias3, grad_bias4, grad_bias5, grad_bias6]
            ),
        ]
    )
    grad_spatial_rows = grad_spatial.reshape(9 * MID, MID)
    first_grads = (
        lax.psum_scatter(grad_reduce1, ("dp", "fsdp"), scatter_dimension=0, tiled=True),
        lax.psum_scatter(grad_spatial_rows, ("dp", "fsdp"), scatter_dimension=0, tiled=True),
        lax.psum_scatter(grad_expand1, ("dp", "fsdp"), scatter_dimension=0, tiled=True),
        lax.psum_scatter(grad_short, ("dp", "fsdp"), scatter_dimension=0, tiled=True),
        lax.psum_scatter(grad_norm, ("dp", "fsdp"), scatter_dimension=1, tiled=True),
    )
    every_grad = (
        first_grads[0],
        first_grads[1],
        first_grads[2],
        first_grads[3],
        second_grads[0],
        second_grads[1],
        second_grads[2],
        second_grads[3],
        second_grads[4],
        first_grads[4],
    )
    return (
        results[0].astype(jnp.bfloat16),
        results[1].astype(jnp.bfloat16),
        results[2].astype(jnp.bfloat16),
        input_grads[0],
        input_grads[1],
        input_grads[2],
        every_grad[0],
        every_grad[1],
        every_grad[2],
        every_grad[3],
        every_grad[4],
        every_grad[5],
        every_grad[6],
        every_grad[7],
        every_grad[8],
        every_grad[9],
        kernel_grad,
    )


def solution(mesh):
    return jax.shard_map(
        on_device,
        mesh=mesh,
        in_specs=(
            P(("dp", "fsdp"), None, None, None),
            P(("dp", "fsdp"), None, None, None),
            P(("dp", "fsdp"), None, None, None),
            P(("dp", "fsdp"), None),
            P(("dp", "fsdp"), None),
            P(("dp", "fsdp"), None),
            P(("dp", "fsdp"), None),
            P(("dp", "fsdp"), None),
            P(("dp", "fsdp"), None),
            P(("dp", "fsdp"), None),
            P(("dp", "fsdp"), None),
            P(None, ("dp", "fsdp")),
            P(None, ("dp", "fsdp")),
            P(("dp", "fsdp"), None),
            P(None, ("dp", "fsdp")),
            P(),
            P(("dp", "fsdp"), None, None, None),
            P(("dp", "fsdp"), None, None, None),
            P(("dp", "fsdp"), None, None, None),
        ),
        out_specs=(
            P(("dp", "fsdp"), None, None, None),
            P(("dp", "fsdp"), None, None, None),
            P(("dp", "fsdp"), None, None, None),
            P(("dp", "fsdp"), None, None, None),
            P(("dp", "fsdp"), None, None, None),
            P(("dp", "fsdp"), None, None, None),
            P(("dp", "fsdp"), None),
            P(("dp", "fsdp"), None),
            P(("dp", "fsdp"), None),
            P(("dp", "fsdp"), None),
            P(("dp", "fsdp"), None),
            P(("dp", "fsdp"), None),
            P(None, ("dp", "fsdp")),
            P(None, ("dp", "fsdp")),
            P(("dp", "fsdp"), None),
            P(None, ("dp", "fsdp")),
            P(),
        ),
        check_vma=False,
    )
```

profile of v0, /device:TPU:0, one launch (start us, length us, event | category | flops | bytes accessed | tf_op | source)
XLA Modules:
  0.0 2943.2 jit_solution(6554371059114663370)
XLA Ops:
  26.1 69.7 %all_gather.40 = bf16[2,8192]{1,0:T(2,128)(2,1)S(1)} all-gather(bf16[2,256]{1,0:T(2,128)(2,1)S(1)} %convert_element_type.475), channel_id=1, replica_groups=mesh['dp'=16,'fsdp'=2] {'dp','fsdp'}, dimensions={1}, use_global_device_ids=true | all-gather | bytes 33792 | tf_op jit(solution)/shard_map/all_gather | solution.py:282
  97.1 71.8 %all_gather.47 = bf16[27,16384]{1,0:T(8,128)(2,1)S(1)} all-gather(bf16[27,512]{1,0:T(8,128)(2,1)S(1)} %convert_element_type.494), channel_id=1, replica_groups=mesh['dp'=16,'fsdp'=2] {'dp','fsdp'}, dimensions={1}, use_global_device_ids=true | all-gather | bytes 912384 | tf_op jit(solution)/shard_map/all_gather | solution.py:354
  196.0 8.8 slice.1412
  204.9 71.1 %all_gather.45 = bf16[512,32]{1,0:T(8,128)(2,1)} all-gather(bf16[16,32]{1,0:T(8,128)(2,1)S(1)} %convert_element_type.491), channel_id=1, replica_groups=mesh['dp'=16,'fsdp'=2] {'dp','fsdp'}, dimensions={0}, use_global_device_ids=true | all-gather | bytes 33792 | tf_op jit(solution)/shard_map/all_gather | solution.py:352
  277.2 64.7 %all_gather.46 = bf16[32,512]{0,1:T(8,128)(2,1)S(1)} all-gather(bf16[32,16]{0,1:T(8,128)(2,1)S(1)} %convert_element_type.492), channel_id=1, replica_groups=mesh['dp'=16,'fsdp'=2] {'dp','fsdp'}, dimensions={1}, use_global_device_ids=true | all-gather | bytes 33792 | tf_op jit(solution)/shard_map/all_gather | solution.py:353
  352.0 37.7 %all-reduce.236 = (f32[512]{0:T(512)}, f32[]{:T(128)}, f32[512]{0:T(512)}) all-reduce(f32[512]{0:T(512)} %get-tuple-element.467, f32[]{:T(128)S(6)} %add.2144, f32[512]{0:T(512)} %get-tuple-element.468), channel_id=1, replica_groups=mesh['dp'=16,'fsdp'=2] {'dp','fsdp'}, use_global_device_ids=true, to_apply=%region_11.12 | all-reduce | flops 1025 | bytes 8200 | tf_op jit(solution)/shard_map/psum | solution.py:290
  394.6 11.7 slice.1388
  406.4 11.8 slice.1389
  418.2 11.8 slice.1390
  430.0 11.8 slice.1391
  441.8 11.8 slice.1392
  453.5 11.8 slice.1393
  533.0 8.6 slice.1397
  558.9 8.6 slice.1400
  576.1 8.6 slice.1402
  637.5 43.7 %all-reduce.235 = (f32[512]{0:T(512)}, f32[]{:T(128)}, f32[512]{0:T(512)}) all-reduce(f32[512]{0:T(512)} %add_add_fusion.45, f32[]{:T(128)S(6)} %add.2185, f32[512]{0:T(512)} %add_add_fusion.46), channel_id=1, replica_groups=mesh['dp'=16,'fsdp'=2] {'dp','fsdp'}, use_global_device_ids=true, to_apply=%region_20.21 | all-reduce | flops 1025 | bytes 8200 | tf_op jit(solution)/shard_map/psum | solution.py:117
  695.0 39.6 %all-reduce.234 = (f32[2048]{0:T(1024)}, f32[2048]{0:T(1024)}, f32[2048]{0:T(1024)}, f32[2048]{0:T(1024)}) all-reduce(f32[2048]{0:T(1024)} %add_add_fusion.25, f32[2048]{0:T(1024)} %add_add_fusion.26, f32[2048]{0:T(1024)} %add_add_fusion.27, f32[2048]{0:T(1024)} %add_add_fusion.28), channel_id=1, replica_groups=mesh['dp'=16,'fsdp'=2] {'dp','fsdp'}, use_global_device_ids=true, to_apply=%region_36.37 | all-reduce | flops 8192 | bytes 65536 | tf_op jit(solution)/shard_map/psum | solution.py:313
  753.1 42.6 %all-reduce.233 = (f32[512]{0:T(512)}, f32[512]{0:T(512)}) all-reduce(f32[512]{0:T(512)} %add_add_fusion.43, f32[512]{0:T(512)} %add_add_fusion.44), channel_id=1, replica_groups=mesh['dp'=16,'fsdp'=2] {'dp','fsdp'}, use_global_device_ids=true, to_apply=%region_44.45 | all-reduce | flops 1024 | bytes 8192 | tf_op jit(solution)/shard_map/psum | solution.py:117
  828.6 38.9 %all-reduce.232 = (f32[512]{0:T(512)}, f32[512]{0:T(512)}) all-reduce(f32[512]{0:T(512)} %add_add_fusion.41, f32[512]{0:T(512)S(1)} %add_add_fusion.42), channel_id=1, replica_groups=mesh['dp'=16,'fsdp'=2] {'dp','fsdp'}, use_global_device_ids=true, to_apply=%region_55.56 | all-reduce | flops 1024 | bytes 8192 | tf_op jit(solution)/shard_map/psum | solution.py:117
  879.9 42.3 %all-reduce.231 = (f32[2048]{0:T(1024)}, f32[2048]{0:T(1024)}) all-reduce(f32[2048]{0:T(1024)} %add_add_fusion.23, f32[2048]{0:T(1024)} %add_add_fusion.24), channel_id=1, replica_groups=mesh['dp'=16,'fsdp'=2] {'dp','fsdp'}, use_global_device_ids=true, to_apply=%region_63.64 | all-reduce | flops 4096 | bytes 32768 | tf_op jit(solution)/shard_map/psum | solution.py:117
  938.2 39.3 %all-reduce.230 = (f32[2048]{0:T(1024)}, f32[2048]{0:T(1024)}) all-reduce(f32[2048]{0:T(1024)} %get-tuple-element.350, f32[2048]{0:T(1024)} %get-tuple-element.349), channel_id=1, replica_groups=mesh['dp'=16,'fsdp'=2] {'dp','fsdp'}, use_global_device_ids=true, to_apply=%region_71.72 | all-reduce | flops 4096 | bytes 32768 | tf_op jit(solution)/shard_map/psum | solution.py:151
  992.7 42.8 %all-reduce.229 = (f32[512]{0:T(512)}, f32[512]{0:T(512)}) all-reduce(f32[512]{0:T(512)} %get-tuple-element.384, f32[512]{0:T(512)} %get-tuple-element.383), channel_id=1, replica_groups=mesh['dp'=16,'fsdp'=2] {'dp','fsdp'}, use_global_device_ids=true, to_apply=%region_79.80 | all-reduce | flops 1024 | bytes 8192 | tf_op jit(solution)/shard_map/psum | solution.py:151
  1080.5 38.7 %all-reduce.228 = (f32[512]{0:T(512)}, f32[512]{0:T(512)S(1)}) all-reduce(f32[512]{0:T(512)} %get-tuple-element.382, f32[512]{0:T(512)S(1)} %get-tuple-element.381), channel_id=1, replica_groups=mesh['dp'=16,'fsdp'=2] {'dp','fsdp'}, use_global_device_ids=true, to_apply=%region_90.91 | all-reduce | flops 1024 | bytes 8192 | tf_op jit(solution)/shard_map/psum | solution.py:467
  1137.6 42.0 %all-reduce.227 = (f32[2048]{0:T(1024)S(1)}, f32[2048]{0:T(1024)S(1)}) all-reduce(f32[2048]{0:T(1024)S(1)} %get-tuple-element.346, f32[2048]{0:T(1024)S(1)} %get-tuple-element.345), channel_id=1, replica_groups=mesh['dp'=16,'fsdp'=2] {'dp','fsdp'}, use_global_device_ids=true, to_apply=%region_98.99 | all-reduce | flops 4096 | bytes 32768 | tf_op jit(solution)/shard_map/psum | solution.py:523
  1191.9 38.7 %all-reduce.226 = (f32[512]{0:T(512)S(1)}, f32[512]{0:T(512)S(1)}) all-reduce(f32[512]{0:T(512)S(1)} %get-tuple-element.380, f32[512]{0:T(512)S(1)} %get-tuple-element.379), channel_id=1, replica_groups=mesh['dp'=16,'fsdp'=2] {'dp','fsdp'}, use_global_device_ids=true, to_apply=%region_106.107 | all-reduce | flops 1024 | bytes 8192 | tf_op jit(solution)/shard_map/psum | solution.py:151
  1234.1 10.0 pad.932
  1245.5 10.0 pad.933
  1256.9 9.8 pad.1174
  1268.1 9.8 pad.1175
  1279.4 9.9 pad.1177
  1290.8 9.9 pad.2320
  1302.1 9.9 pad.2321
  1313.5 9.9 pad.1178
  1326.0 8.6 pad.940
  1336.0 8.7 pad.941
  1346.1 8.7 pad.942
  1552.1 43.0 %all-reduce.225 = (f32[2048]{0:T(1024)}, f32[2048]{0:T(1024)}, f32[512]{0:T(512)S(1)}, f32[512]{0:T(512)S(1)}, f32[9,32]{1,0:T(8,128)}) all-reduce(f32[2048]{0:T(1024)S(1)} %get-tuple-element.348, f32[2048]{0:T(1024)S(1)} %get-tuple-element.347, f32[512]{0:T(512)S(1)} %get-tuple-element.378, ...), channel_id=1, replica_groups=mesh['dp'=16,'fsdp'=2] {'dp','fsdp'}, use_global_device_ids=true, to_apply=%region_122.123 | all-reduce | flops 5408 | bytes 43264 | tf_op jit(solution)/shard_map/psum | solution.py:523
  1708.3 10.9 pad.951
  1727.8 9.5 pad.950
  1750.6 33.7 %reduce-scatter.25.cloned.1.call-done = f32[32,16]{0,1:T(8,128)} async-done(((f32[32,512]{0,1:T(8,128)}), f32[32,16]{0,1:T(8,128)}) %reduce-scatter.25.cloned.1.call-update) | async-done | bytes 2064 | tf_op jit(solution)/shard_map/reduce_scatter | solution.py:487
  1784.3 132.3 %reduce-scatter.23.cloned.1.call-done = f32[16,32]{1,0:T(8,128)} async-done(((f32[512,32]{1,0:T(8,128)}), f32[16,32]{1,0:T(8,128)}) %reduce-scatter.23.cloned.1.call-update) | async-done | bytes 2064 | tf_op jit(solution)/shard_map/reduce_scatter | solution.py:486
  1916.6 136.2 %reduce-scatter.27.cloned.1.call-done = f32[27,512]{1,0:T(8,128)} async-done(((f32[27,16384]{1,0:T(8,128)}), f32[27,512]{1,0:T(8,128)}) %reduce-scatter.27.cloned.1.call-update) | async-done | bytes 55312 | tf_op jit(solution)/shard_map/reduce_scatter | solution.py:488
  2052.8 136.5 %reduce-scatter.13.cloned.1.call-done = f32[32,512]{1,0:T(8,128)} async-done(((f32[1024,512]{1,0:T(8,128)}), f32[32,512]{1,0:T(8,128)}) %reduce-scatter.13.cloned.1.call-update) | async-done | bytes 65552 | tf_op jit(solution)/shard_map/reduce_scatter | solution.py:595
  2189.2 140.3 %reduce-scatter.29.cloned.1.call-done = f32[16,2048]{1,0:T(8,128)} async-done(((f32[512,2048]{1,0:T(8,128)}), f32[16,2048]{1,0:T(8,128)}) %reduce-scatter.29.cloned.1.call-update) | async-done | bytes 131088 | tf_op jit(solution)/shard_map/reduce_scatter | solution.py:489
  2329.5 142.0 %reduce-scatter.21.cloned.1.call-done = f32[64,512]{1,0:T(8,128)} async-done(((f32[2048,512]{1,0:T(8,128)}), f32[64,512]{1,0:T(8,128)}) %reduce-scatter.21.cloned.1.call-update) | async-done | bytes 131088 | tf_op jit(solution)/shard_map/reduce_scatter | solution.py:485
  2471.5 141.3 %reduce-scatter.17.cloned.1.call-done = f32[16,2048]{1,0:T(8,128)} async-done(((f32[512,2048]{1,0:T(8,128)}), f32[16,2048]{1,0:T(8,128)}) %reduce-scatter.17.cloned.1.call-update) | async-done | bytes 131088 | tf_op jit(solution)/shard_map/reduce_scatter | solution.py:597
  2612.9 138.7 %reduce-scatter.15.cloned.1.call-done = f32[144,512]{1,0:T(8,128)} async-done(((f32[4608,512]{1,0:T(8,128)}), f32[144,512]{1,0:T(8,128)}) %reduce-scatter.15.cloned.1.call-update) | async-done | bytes 294928 | tf_op jit(solution)/shard_map/reduce_scatter | solution.py:596
  2751.6 184.9 %reduce-scatter.19.cloned.1.call-done = f32[32,2048]{1,0:T(8,128)} async-done(((f32[1024,2048]{1,0:T(8,128)}), f32[32,2048]{1,0:T(8,128)}) %reduce-scatter.19.cloned.1.call-update) | async-done | bytes 262160 | tf_op jit(solution)/shard_map/reduce_scatter | solution.py:598
  (1961 shorter events, 730.7 us)
Async XLA Ops:
  7.2 89.8 %copy-start.446 = (f32[27,512]{1,0:T(8,128)S(1)}, f32[27,512]{1,0:T(8,128)}, u32[]{:S(2)}) copy-start(f32[27,512]{1,0:T(8,128)} %param.31) | copy-start | bytes 165892
  7.2 337.2 %all-gather.7.cloned.1.call-start = ((), (), s32[]{:S(2)}) async-start(), calls=%async_computation.10 | async-start | bytes 1081344 | tf_op jit(solution)/shard_map/all_gather | solution.py:278
  8.8 601.8 %all-gather.13.cloned.1.call-start = ((), (), s32[]{:S(2)}) async-start(), calls=%async_computation.13 | async-start | bytes 4325376 | tf_op jit(solution)/shard_map/all_gather | solution.py:281
  10.5 607.5 %all-gather.9.cloned.1.call-start = ((), (), s32[]{:S(2)}) async-start(), calls=%async_computation.11 | async-start | bytes 4866048 | tf_op jit(solution)/shard_map/all_gather | solution.py:279
  12.2 670.9 %all-gather.11.cloned.1.call-start = ((), (), s32[]{:S(2)}) async-start(), calls=%async_computation.12 | async-start | bytes 2162688 | tf_op jit(solution)/shard_map/all_gather | solution.py:280
  13.8 730.7 %all-gather.15.cloned.1.call-start = ((), (), s32[]{:S(2)}) async-start(), calls=%async_computation.14 | async-start | bytes 2162688 | tf_op jit(solution)/shard_map/all_gather | solution.py:351
  15.5 854.0 %all-gather.17.cloned.1.call-start = ((), (), s32[]{:S(2)}) async-start(), calls=%async_computation.15 | async-start | bytes 2162688 | tf_op jit(solution)/shard_map/all_gather | solution.py:355
  16.2 1732.8 %reduce-scatter.31.cloned.1.call-start = ((), (), s32[]{:S(2)}) async-start(), calls=%async_computation.25 | async-start | bytes 4325376
  19.4 175.6 %copy-start.548 = (bf16[4]{0:T(256)(128)(2,1)}, bf16[4]{0:T(256)(128)(2,1)S(1)}, u32[]{:S(2)}) copy-start(bf16[4]{0:T(256)(128)(2,1)S(1)} %get-tuple-element.316) | copy-start | bytes 28
  19.4 1027.3 %copy-start.328 = (f32[4]{0:T(128)}, f32[4]{0:T(128)S(1)}, u32[]{:S(2)}) copy-start(f32[4]{0:T(128)S(1)} %get-tuple-element.317) | copy-start | bytes 52
  20.1 159.1 %copy-start.551 = (bf16[4]{0:T(256)(128)(2,1)}, bf16[4]{0:T(256)(128)(2,1)S(1)}, u32[]{:S(2)}) copy-start(bf16[4]{0:T(256)(128)(2,1)S(1)} %get-tuple-element.312) | copy-start | bytes 28
  20.1 1034.5 %copy-start.326 = (f32[4]{0:T(128)}, f32[4]{0:T(128)S(1)}, u32[]{:S(2)}) copy-start(f32[4]{0:T(128)S(1)} %get-tuple-element.313) | copy-start | bytes 52
  97.1 645.3 %copy-start.330 = (f32[1,2048]{1,0:T(1,128)}, f32[1,2048]{1,0:T(1,128)S(1)}, u32[]{:S(2)}) copy-start(f32[1,2048]{1,0:T(1,128)S(1)} %get-tuple-element.367) | copy-start | bytes 24580
  195.1 81.5 %copy-start.547 = (f32[9,32]{1,0:T(8,128)S(1)}, f32[9,32]{1,0:T(8,128)}, u32[]{:S(2)}) copy-start(f32[9,32]{1,0:T(8,128)} %param.34) | copy-start | bytes 3460
  195.1 82.1 %copy-start.525 = (f32[32,16]{0,1:T(8,128)S(1)}, f32[32,16]{0,1:T(8,128)}, u32[]{:S(2)}) copy-start(f32[32,16]{0,1:T(8,128)} %param.30) | copy-start | bytes 6148
  196.0 151.1 %copy-start.549 = (bf16[4]{0:T(256)(128)(2,1)S(1)}, bf16[4]{0:T(256)(128)(2,1)}, u32[]{:S(2)}) copy-start(bf16[4]{0:T(256)(128)(2,1)} %copy-done.548) | copy-start | bytes 28
  350.1 181.9 %copy-start.10 = (f32[4,14,14,512]{3,2,1,0:T(8,128)}, f32[4,14,14,512]{3,2,1,0:T(8,128)S(1)}, u32[]{:S(2)}) copy-start(f32[4,14,14,512]{3,2,1,0:T(8,128)S(1)} %get-tuple-element.434) | copy-start | bytes 4816900
  406.3 58.9 %copy-start.30 = (bf16[4,14,14,512]{3,2,1,0:T(8,128)(2,1)S(1)}, bf16[4,14,14,512]{3,2,1,0:T(8,128)(2,1)}, u32[]{:S(2)}) copy-start(bf16[4,14,14,512]{3,2,1,0:T(8,128)(2,1)} %pad.749) | copy-start | bytes 2408452
  406.3 81.1 %copy-start.75 = (f32[4,8,8,512]{3,2,1,0:T(8,128)S(1)}, f32[4,8,8,512]{3,2,1,0:T(8,128)}, u32[]{:S(2)}) copy-start(f32[4,8,8,512]{3,2,1,0:T(8,128)} %get-tuple-element.435) | copy-start | bytes 1572868
  406.3 81.1 %copy-start.388 = (f32[4]{0:T(128)S(1)}, f32[4]{0:T(128)}, u32[]{:S(2)}) copy-start(f32[4]{0:T(128)} %get-tuple-element.315) | copy-start | bytes 52
  406.4 81.1 %copy-start.399 = (f32[1,512]{1,0:T(1,128)S(1)}, f32[1,512]{1,0:T(1,128)}, u32[]{:S(2)}) copy-start(f32[1,512]{1,0:T(1,128)} %get-tuple-element.363) | copy-start | bytes 6148
  406.4 81.1 %copy-start.403 = (f32[512]{0:T(512)S(1)}, f32[512]{0:T(512)}, u32[]{:S(2)}) copy-start(f32[512]{0:T(512)} %copy-done.402) | copy-start | bytes 6148
  406.4 81.1 %copy-start.429 = (f32[1,512]{1,0:T(1,128)S(1)}, f32[1,512]{1,0:T(1,128)}, u32[]{:S(2)}) copy-start(f32[1,512]{1,0:T(1,128)} %get-tuple-element.364) | copy-start | bytes 6148
  406.4 81.1 %copy-start.432 = (f32[512]{0:T(512)S(1)}, f32[512]{0:T(512)}, u32[]{:S(2)}) copy-start(f32[512]{0:T(512)} %copy-done.431) | copy-start | bytes 6148
  541.6 69.0 %copy-start.192 = (bf16[4,6,6,1024]{3,2,1,0:T(8,128)(2,1)S(1)}, bf16[4,6,6,1024]{3,2,1,0:T(8,128)(2,1)}, u32[]{:S(2)}) copy-start(bf16[4,6,6,1024]{3,2,1,0:T(8,128)(2,1)} %slice.1411) | copy-start | bytes 884740
  614.3 515.1 %copy-start.14 = (f32[4,6,6,2048]{3,2,1,0:T(8,128)}, f32[4,6,6,2048]{3,2,1,0:T(8,128)S(1)}, u32[]{:S(2)}) copy-start(f32[4,6,6,2048]{3,2,1,0:T(8,128)S(1)} %fusion.8) | copy-start | bytes 3538948
  618.0 504.6 %copy-start.8 = (f32[4,7,7,2048]{3,2,1,0:T(8,128)}, f32[4,7,7,2048]{3,2,1,0:T(8,128)S(1)}, u32[]{:S(2)}) copy-start(f32[4,7,7,2048]{3,2,1,0:T(8,128)S(1)} %fusion.6) | copy-start | bytes 4816900
  750.0 47.8 %copy-start.376 = (f32[1,512]{1,0:T(1,128)S(1)}, f32[1,512]{1,0:T(1,128)}, u32[]{:S(2)}) copy-start(f32[1,512]{1,0:T(1,128)} %get-tuple-element.357) | copy-start | bytes 6148
  876.5 47.1 %copy-start.334 = (f32[1,2048]{1,0:T(1,128)S(1)}, f32[1,2048]{1,0:T(1,128)}, u32[]{:S(2)}) copy-start(f32[1,2048]{1,0:T(1,128)} %get-tuple-element.365) | copy-start | bytes 24580
  989.2 47.2 %copy-start.458 = (f32[1,512]{1,0:T(1,128)S(1)}, f32[1,512]{1,0:T(1,128)}, u32[]{:S(2)}) copy-start(f32[1,512]{1,0:T(1,128)} %get-tuple-element.359) | copy-start | bytes 6148
  989.2 47.2 %copy-start.465 = (f32[512]{0:T(512)S(1)}, f32[512]{0:T(512)}, u32[]{:S(2)}) copy-start(f32[512]{0:T(512)} %copy-done.463) | copy-start | bytes 6148
  1077.3 45.4 %copy-start.331 = (f32[1,2048]{1,0:T(1,128)S(1)}, f32[1,2048]{1,0:T(1,128)}, u32[]{:S(2)}) copy-start(f32[1,2048]{1,0:T(1,128)} %copy-done.330) | copy-start | bytes 24580
  1136.9 45.6 %copy-start.309 = (f32[4,4,4,2048]{3,2,1,0:T(4,128)}, f32[4,4,4,2048]{3,2,1,0:T(4,128)S(1)}, u32[]{:S(2)}) copy-start(f32[4,4,4,2048]{3,2,1,0:T(4,128)S(1)} %get-tuple-element.461) | copy-start | bytes 1572868
  1230.7 81.3 %copy-start.4 = (bf16[4,7,7,512]{3,2,1,0:T(8,128)(2,1)}, bf16[4,7,7,512]{3,2,1,0:T(8,128)(2,1)S(1)}, u32[]{:S(2)}) copy-start(bf16[4,7,7,512]{3,2,1,0:T(8,128)(2,1)S(1)} %add_convert_fusion.12) | copy-start | bytes 602116
  1324.5 80.3 %copy-start.6 = (bf16[4,6,6,512]{3,2,1,0:T(8,128)(2,1)}, bf16[4,6,6,512]{3,2,1,0:T(8,128)(2,1)S(1)}, u32[]{:S(2)}) copy-start(bf16[4,6,6,512]{3,2,1,0:T(8,128)(2,1)S(1)} %add_convert_fusion.14) | copy-start | bytes 442372
  1414.8 58.0 %copy-start.449 = (bf16[4,4,4,512]{3,2,1,0:T(4,128)(2,1)}, bf16[4,4,4,512]{3,2,1,0:T(4,128)(2,1)S(1)}, u32[]{:S(2)}) copy-start(bf16[4,4,4,512]{3,2,1,0:T(4,128)(2,1)S(1)} %add_convert_fusion.16) | copy-start | bytes 196612
  1507.2 277.2 %reduce-scatter.25.cloned.1.call-start = ((), (), s32[]{:S(2)}) async-start(), calls=%async_computation.22 | async-start | bytes 270336 | tf_op jit(solution)/shard_map/reduce_scatter | solution.py:487
  1543.8 51.9 %copy-start.398 = (f32[4]{0:T(128)S(1)}, f32[4]{0:T(128)}, u32[]{:S(2)}) copy-start(f32[4]{0:T(128)} %get-tuple-element.315) | copy-start | bytes 52
  1543.8 51.9 %copy-start.401 = (f32[1,512]{1,0:T(1,128)S(1)}, f32[1,512]{1,0:T(1,128)}, u32[]{:S(2)}) copy-start(f32[1,512]{1,0:T(1,128)} %get-tuple-element.363) | copy-start | bytes 6148
  1543.8 51.9 %copy-start.405 = (f32[512]{0:T(512)S(1)}, f32[512]{0:T(512)}, u32[]{:S(2)}) copy-start(f32[512]{0:T(512)} %copy-done.402) | copy-start | bytes 6148
  1601.2 315.4 %reduce-scatter.23.cloned.1.call-start = ((), (), s32[]{:S(2)}) async-start(), calls=%async_computation.21 | async-start | bytes 270336 | tf_op jit(solution)/shard_map/reduce_scatter | solution.py:486
  1604.4 448.4 %reduce-scatter.27.cloned.1.call-start = ((), (), s32[]{:S(2)}) async-start(), calls=%async_computation.23 | async-start | bytes 2162688 | tf_op jit(solution)/shard_map/reduce_scatter | solution.py:488
  1611.5 577.7 %reduce-scatter.13.cloned.1.call-start = ((), (), s32[]{:S(2)}) async-start(), calls=%async_computation.16 | async-start | bytes 2162688 | tf_op jit(solution)/shard_map/reduce_scatter | solution.py:595
  1621.4 708.1 %reduce-scatter.29.cloned.1.call-start = ((), (), s32[]{:S(2)}) async-start(), calls=%async_computation.24 | async-start | bytes 4325376 | tf_op jit(solution)/shard_map/reduce_scatter | solution.py:489
  1628.3 843.3 %reduce-scatter.21.cloned.1.call-start = ((), (), s32[]{:S(2)}) async-start(), calls=%async_computation.20 | async-start | bytes 4325376 | tf_op jit(solution)/shard_map/reduce_scatter | solution.py:485
  1634.7 978.2 %reduce-scatter.17.cloned.1.call-start = ((), (), s32[]{:S(2)}) async-start(), calls=%async_computation.18 | async-start | bytes 4325376 | tf_op jit(solution)/shard_map/reduce_scatter | solution.py:597
  1653.3 1098.3 %reduce-scatter.15.cloned.1.call-start = ((), (), s32[]{:S(2)}) async-start(), calls=%async_computation.17 | async-start | bytes 9732096 | tf_op jit(solution)/shard_map/reduce_scatter | solution.py:596
  1690.1 1246.4 %reduce-scatter.19.cloned.1.call-start = ((), (), s32[]{:S(2)}) async-start(), calls=%async_computation.19 | async-start | bytes 8650752 | tf_op jit(solution)/shard_map/reduce_scatter | solution.py:598
  (557 other events, 2378.8 us)
Sparse Core Ops, SparseCore 0:
  11.5 56.5 all-gather.6
  71.7 65.6 all-gather.12
  140.9 62.0 all-gather.8
  206.3 55.4 all-gather.10
  265.2 55.5 all-gather.14
  324.3 55.4 all-gather.16
  1507.3 143.3 reduce-scatter.30
  1653.6 130.7 reduce-scatter.24
  1787.3 129.3 reduce-scatter.22
  1919.3 133.4 reduce-scatter.26
  2055.7 133.4 reduce-scatter.12
  2191.9 137.5 reduce-scatter.28
  2332.4 139.1 reduce-scatter.20
  2474.2 138.5 reduce-scatter.16
  2619.2 132.3 reduce-scatter.14
  2754.4 182.0 reduce-scatter.18
where the time goes:
time: 2970 us; the launch traced here: 2940 us
  waiting for transfers between devices  1190 us (40%)
  blocking collectives  766 us (26%)
  local copies, waits for them, and re-layouts  537 us (18%)
  matrix products  290 us (10%)
  other arithmetic  133 us (4%)
    slice x27, local copies, waits for them, and re-layouts, tap_window(): padded[:, row_start:row_start + stride * (rows_out - 1) + 1:stride, col_s...  215 us
    reduce_scatter x1, waiting for transfers between devices, on_device(): lax.psum_scatter(grad_short, ('dp', 'fsdp'), scatter_dimension=0, tiled=T...  185 us
    psum x4, blocking collectives, global_sums(): return lax.psum((sum_first, sum_second), ('dp', 'fsdp'))  167 us
    reduce_scatter x1, waiting for transfers between devices, on_device(): lax.psum_scatter(grad_reduce2, ('dp', 'fsdp'), scatter_dimension=0, tiled...  142 us
    reduce_scatter x1, waiting for transfers between devices, on_device(): lax.psum_scatter(grad_expand1, ('dp', 'fsdp'), scatter_dimension=0, tiled...  141 us
    reduce_scatter x1, waiting for transfers between devices, on_device(): lax.psum_scatter(grad_expand2, ('dp', 'fsdp'), scatter_dimension=0, tiled...  140 us
    reduce_scatter x1, waiting for transfers between devices, on_device(): lax.psum_scatter(grad_spatial_rows, ('dp', 'fsdp'), scatter_dimension=0,...  139 us
    reduce_scatter x1, waiting for transfers between devices, on_device(): lax.psum_scatter(grad_reduce1, ('dp', 'fsdp'), scatter_dimension=0, tiled...  136 us
  transfers between devices with their start and end apart: 16, of which 9 were waited for; matrix products, arithmetic and copies ran while one was open for 18% of the time, Pallas kernels for 0%

commit v1 on v0

v1 whole, which is shorter than its diff:
```python
from functools import partial

import jax
import jax.numpy as jnp
from jax import lax
from jax.experimental import pallas as pl
from jax.experimental.pallas import tpu as pltpu
from jax.sharding import PartitionSpec as P
import numpy as np

MID = 512
C_OUT = 2048
FRAMES = 4
GROUP = 128
SHIFT = 16
SQUEEZE = 32
SIDES = (4, 6, 7)
AXES = ("dp", "fsdp")
EPS = 1e-05
HIGHEST = lax.Precision.HIGHEST
F32 = jnp.float32
BF16 = jnp.bfloat16

ROWS = (64, 192, 224)
CUTS = (0, 64, 256, 480)
R = 480


def row_tables():
    frame = np.zeros(R, np.int32)
    row = np.zeros(R, np.int32)
    col = np.zeros(R, np.int32)
    group = np.zeros(R, np.int32)
    at = 0
    for a in range(2):
        for i in range(4):
            for p in range(2):
                for j in range(4):
                    frame[at], row[at], col[at], group[at] = 2 * a + p, i, j, 0
                    at += 1
    for g in (1, 2):
        for f in range(4):
            for i in range(SIDES[g]):
                for j in range(8):
                    frame[at], row[at], col[at], group[at] = f, i, j, g
                    at += 1
    side = np.array(SIDES)[group]
    return group, frame, row, col, (col < side), side


GROUP_OF, FRAME_OF, ROW_OF, COL_OF, VALID, SIDE_OF = row_tables()
SLOT_OF = GROUP_OF * FRAMES + FRAME_OF


def window_table():
    table = np.zeros((12, 9, R), np.float32)
    for r in range(R):
        if not VALID[r]:
            continue
        for t in range(9):
            dy, dx = t // 3 - 1, t % 3 - 1
            i, j = ROW_OF[r] - dy, COL_OF[r] - dx
            if 0 <= i < SIDE_OF[r] and 0 <= j < SIDE_OF[r]:
                table[SLOT_OF[r], t, r] = 1.0
    return table.reshape(108, R)


WINDOWS = window_table()
SPREAD = ((SLOT_OF[:, None] == np.arange(12)[None]) & VALID[:, None]).astype(np.float32)
NPIX = np.repeat(np.array([s * s for s in SIDES], np.float32), FRAMES)


def split(v):
    c = v.shape[-1]
    return (
        v[0:64].reshape(2, 4, 8, c),
        v[64:256].reshape(4, 6, 8, c),
        v[256:480].reshape(4, 7, 8, c),
    )


def join(parts):
    return jnp.concatenate([p.reshape(-1, p.shape[-1]) for p in parts], axis=0)


def shift_rows(v, dy):
    if dy == 0:
        return v
    out = []
    for p in split(v):
        zero = jnp.zeros_like(p[:, :1])
        out.append(
            jnp.concatenate([p[:, 1:], zero] if dy > 0 else [zero, p[:, :-1]], axis=1)
        )
    return join(out)


def shift_cols(v, dx):
    if dx == 0:
        return v
    c = v.shape[-1]
    rolled = jnp.roll(v.reshape(R // 8, 8, c), -dx, axis=1).reshape(R, c)
    edge = COL_OF == (0 if dx < 0 else 3)
    keep = ~((GROUP_OF == 0) & edge)
    return jnp.where(keep[:, None], rolled, jnp.zeros_like(rolled))


def shift(v, dy, dx):
    return shift_rows(shift_cols(v, dx), dy)


def shift_frame(v, df):
    c = v.shape[-1]
    pc, pm, pf = split(v)
    half = jnp.roll(pc.reshape(8, 8, c), 4, axis=1).reshape(2, 4, 8, c)
    zero = jnp.zeros_like(half[:1])
    first = (np.arange(8) < 4)[None, None, :, None]
    if df < 0:
        other = jnp.concatenate([zero, half[:-1]], axis=0)
        oc = jnp.where(first, other, half)
    else:
        other = jnp.concatenate([half[1:], zero], axis=0)
        oc = jnp.where(first, half, other)
    out = [oc]
    for p in (pm, pf):
        zero = jnp.zeros_like(p[:1])
        out.append(jnp.concatenate([p[1:], zero] if df > 0 else [zero, p[:-1]], axis=0))
    return join(out)


def time_shift(v, back):
    a = shift_frame(v, 1 if back else -1)
    b = shift_frame(v, -1 if back else 1)
    return jnp.concatenate(
        [a[:, :SHIFT], b[:, SHIFT : 2 * SHIFT], v[:, 2 * SHIFT :]], axis=-1
    )


def dot(a, b):
    return jnp.dot(a, b, preferred_element_type=F32)


def dot_nt(a, b):
    return lax.dot_general(a, b, (((1,), (1,)), ((), ())), preferred_element_type=F32)


def dot_tn(a, b):
    return lax.dot_general(a, b, (((0,), (0,)), ((), ())), preferred_element_type=F32)


def sums_of(a):
    return jnp.stack([jnp.sum(a, axis=0), jnp.sum(a * a, axis=0)])


def allsum(vectors, n):
    flat = jnp.concatenate([v.reshape(-1) for v in vectors])
    size = flat.shape[0]
    padded = -(-size // 1024) * 1024
    flat = jnp.pad(flat, (0, padded - size)).reshape(padded // 128, 128)
    spread = jnp.broadcast_to(flat[None], (n,) + flat.shape)
    got = lax.all_to_all(spread, AXES, 0, 0, tiled=True)
    flat = jnp.sum(got, axis=0).reshape(-1)
    out = []
    at = 0
    for v in vectors:
        out.append(flat[at : at + v.size].reshape(v.shape))
        at += v.size
    return out


def norm_rows(sums, count, gb):
    mean = sums[0] / count
    var = sums[1] / count - mean * mean
    rstd = lax.rsqrt(var + EPS)
    return mean, rstd, gb[0], gb[1]


def normalize(a, st):
    mean, rstd, gain, bias = st
    xhat = (a - mean) * rstd
    return xhat, xhat * gain + bias


def silu(u):
    return u * jax.nn.sigmoid(u)


def silu_grad(u):
    s = jax.nn.sigmoid(u)
    return s * (1.0 + u * (1.0 - s))


def back_sums(g, xhat):
    return jnp.stack([jnp.sum(g * xhat, axis=0), jnp.sum(g, axis=0)])


def norm_back(g, xhat, mask, st, tot, count):
    mean, rstd, gain, bias = st
    return gain * rstd * (g - mask * (tot[1] + xhat * tot[0]) / count)


def to_rows(groups, phase):
    out = []
    for x, side in zip(groups, SIDES):
        c = x.shape[-1]
        if phase is not None:
            x = x.reshape(FRAMES, side, 2, side, 2, c)[:, :, phase // 2, :, phase % 2]
        if side == 4:
            x = x.reshape(2, 2, 4, 4, c).transpose(0, 2, 1, 3, 4).reshape(64, c)
        else:
            x = jnp.pad(x, ((0, 0), (0, 0), (0, 8 - side), (0, 0))).reshape(-1, c)
        out.append(x)
    return jnp.concatenate(out, axis=0)


def from_rows(v):
    c = v.shape[-1]
    pc, pm, pf = split(v)
    coarse = pc.reshape(2, 4, 2, 4, c).transpose(0, 2, 1, 3, 4).reshape(4, 4, 4, c)
    return [coarse, pm[:, :, :6], pf[:, :, :7]]


TAPS2 = []
for kh in range(3):
    for kw in range(3):
        pr, dy = (1, -1) if kh == 0 else ((0, 0) if kh == 1 else (1, 0))
        pc, dx = (1, -1) if kw == 0 else ((0, 0) if kw == 1 else (1, 0))
        TAPS2.append((pr * 2 + pc, dy, dx, kh * 3 + kw))


VMEM = pl.BlockSpec(memory_space=pltpu.VMEM)
SMEM = pl.BlockSpec(memory_space=pltpu.SMEM)


def call(kernel, outs, n_in, scratch=(), scalars=1, flops=0, moved=0):
    return pl.pallas_call(
        kernel,
        out_shape=outs,
        in_specs=[SMEM] * scalars + [VMEM] * n_in,
        out_specs=[VMEM] * len(outs),
        scratch_shapes=list(scratch),
        compiler_params=pltpu.CompilerParams(vmem_limit_bytes=56 * 1024 * 1024),
        cost_estimate=pl.CostEstimate(flops=flops, bytes_accessed=moved, transcendentals=0),
    )


def like(shape, dtype=F32):
    return jax.ShapeDtypeStruct(shape, dtype)


def kshift_cols(v, dx):
    if dx == 0:
        return v
    c = v.shape[-1]
    rolled = pltpu.roll(v.reshape(R // 8, 8, c), 1 if dx < 0 else 7, 1).reshape(R, c)
    top = rolled[:64]
    place = lax.broadcasted_iota(jnp.int32, (64, c), 0) & 3
    top = jnp.where(place == (0 if dx < 0 else 3), 0.0, top)
    return jnp.concatenate([top, rolled[64:]], axis=0)


def kshift_frame(v, df):
    c = v.shape[-1]
    pc, pm, pf = split(v)
    half = pltpu.roll(pc.reshape(8, 8, c), 4, 1).reshape(2, 4, 8, c)
    zero = jnp.zeros_like(half[:1])
    first = lax.broadcasted_iota(jnp.int32, (2, 4, 8, c), 2) < 4
    if df < 0:
        oc = jnp.where(first, jnp.concatenate([zero, half[:-1]], axis=0), half)
    else:
        oc = jnp.where(first, half, jnp.concatenate([half[1:], zero], axis=0))
    out = [oc]
    for p in (pm, pf):
        zero = jnp.zeros_like(p[:1])
        out.append(jnp.concatenate([p[1:], zero] if df > 0 else [zero, p[:-1]], axis=0))
    return join(out)


def ktime_shift(v, back):
    lane = lax.broadcasted_iota(jnp.int32, v.shape, 1)
    a = kshift_frame(v, 1 if back else -1)
    b = kshift_frame(v, -1 if back else 1)
    return jnp.where(lane < SHIFT, a, jnp.where(lane < 2 * SHIFT, b, v))


def kstats(sums, count, gb):
    mean = sums[0:1] / count
    var = sums[1:2] / count - mean * mean
    return mean, lax.rsqrt(var + EPS), gb[0:1], gb[1:2]


def ksums(a, b):
    return jnp.concatenate(
        [jnp.sum(a, axis=0, keepdims=True), jnp.sum(b, axis=0, keepdims=True)], axis=0
    )


def cols(st, c, w=128):
    return tuple(v[:, c * w : (c + 1) * w] for v in st)


def three(v):
    a = v.astype(BF16)
    rest = v - a.astype(F32)
    b = rest.astype(BF16)
    c = (rest - b.astype(F32)).astype(BF16)
    return a, b, c


def exact_dot(table, v):
    return sum(dot(table, part) for part in three(v))


def frame_sums(v):
    pc, pm, pf = split(v)
    first = lax.broadcasted_iota(jnp.int32, (2, 4, 8, v.shape[-1]), 2) < 4
    even = jnp.sum(jnp.where(first, pc, 0.0), axis=(1, 2))
    odd = jnp.sum(jnp.where(first, 0.0, pc), axis=(1, 2))
    pm = jnp.sum(pm, axis=(1, 2))
    pf = jnp.sum(pf, axis=(1, 2))
    rows = [even[0:1], odd[0:1], even[1:2], odd[1:2]]
    rows += [pm[f : f + 1] for f in range(4)] + [pf[f : f + 1] for f in range(4)]
    return jnp.concatenate(rows + [jnp.zeros((4, v.shape[-1]), F32)], axis=0)


def mix_forward(cnt, b1, s4, gb4, mask, wdown, wup, wmix, kern, scale, table, spread,
                z_ref, zl_ref, mixed_ref, im_ref, sig_ref, pooled_ref, wnext_ref, sums_ref):
    m = mask[...]
    st = kstats(s4[...], cnt[0], gb4[...])
    for c in range(4):
        sl = slice(c * 128, (c + 1) * 128)
        z = m * silu(normalize(b1[:, sl], cols(st, c))[1])
        z_ref[:, sl] = z
        zl_ref[:, sl] = z.astype(BF16)
    r = dot(zl_ref[...], wdown[...])
    ws = exact_dot(table[...], r)
    wnext_ref[...] = ws[:144]
    pooled = -ws[144:160]
    for t in range(9):
        pooled = pooled + kern[t : t + 1, :] * ws[t * 16 : (t + 1) * 16]
    pooled = scale[...] * pooled
    pooled_ref[...] = pooled
    sig = jax.nn.sigmoid(jnp.dot(pooled, wup[...], precision=HIGHEST))
    sig_ref[...] = sig
    gates = jnp.concatenate(three(0.5 + sig), axis=0)
    prev = None
    for c in range(4):
        sl = slice(c * 128, (c + 1) * 128)
        v = z_ref[:, sl] * dot(spread[...], gates[:, sl])
        if c > 0:
            low = ktime_shift(v + prev, False).astype(BF16).astype(F32)
            for dx in (-1, 0, 1):
                moved = kshift_cols(low, dx)
                for dy in (-1, 0, 1):
                    t = (dy + 1) * 3 + dx + 1
                    im_ref[c - 1, :, t * 128 : (t + 1) * 128] = shift_rows(moved, dy).astype(BF16)
            v = m * dot(im_ref[c - 1], wmix[c - 1])
        prev = v
        mixed_ref[:, sl] = v
        sums_ref[:, sl] = ksums(v, v * v)


def mix_backward(cnt, g5, t5, mixed, s5, gb5, mask, imt, wmix_t, z_ref, sig, pooled, wnext,
                 wup, kern, scale, table_t, spread, zl, wdown, b1, s4, gb4,
                 g4_ref, sums_ref, gkern_ref, gmix_ref, gdown_ref, gup_ref, gim, gzg):
    m = mask[...]
    count = cnt[0]
    st = kstats(s5[...], count, gb5[...])
    tot = t5[...]
    carried = None
    gsig = []
    for c in (3, 2, 1, 0):
        sl = slice(c * 128, (c + 1) * 128)
        stc = cols(st, c)
        x, _ = normalize(mixed[:, sl], stc)
        gm = norm_back(g5[:, sl], x, m, stc, (tot[0:1, sl], tot[1:2, sl]), count)
        if carried is not None:
            gm = gm + carried
        if c > 0:
            low = (m * gm).astype(BF16)
            gmix_ref[c - 1] = dot_tn(imt[c - 1], low).astype(BF16)
            low = low.astype(F32)
            for dx in (-1, 0, 1):
                moved = kshift_cols(low, -dx)
                for dy in (-1, 0, 1):
                    t = (dy + 1) * 3 + dx + 1
                    gim[:, t * 128 : (t + 1) * 128] = shift_rows(moved, -dy).astype(BF16)
            gm = ktime_shift(dot(gim[...], wmix_t[c - 1]), True)
            carried = gm
        gzg[:, sl] = gm
        gsig.insert(0, frame_sums(gm * z_ref[:, sl]))
    sg = sig[...]
    ge = jnp.concatenate(gsig, axis=1) * sg * (1.0 - sg)
    gup_ref[...] = lax.dot_general(
        pooled[...], ge, (((0,), (0,)), ((), ())), precision=HIGHEST, preferred_element_type=F32
    )
    q = scale[...] * lax.dot_general(
        ge, wup[...], (((1,), (1,)), ((), ())), precision=HIGHEST, preferred_element_type=F32
    )
    coef = []
    gk = []
    for t in range(9):
        gk.append(jnp.sum(q * wnext[t * 16 : (t + 1) * 16], axis=0, keepdims=True))
        coef.append(kern[t : t + 1, :] * q)
    gkern_ref[...] = jnp.concatenate(gk + [jnp.zeros((7, SQUEEZE), F32)], axis=0)
    coef = jnp.concatenate(coef + [-q], axis=0)
    gr = exact_dot(table_t[...], coef).astype(BF16)
    gdown_ref[...] = dot_tn(zl[...], gr)
    gates = jnp.concatenate(three(0.5 + sg), axis=0)
    st = kstats(s4[...], count, gb4[...])
    for c in range(4):
        sl = slice(c * 128, (c + 1) * 128)
        gz = gzg[:, sl] * dot(spread[...], gates[:, sl]) + dot_nt(gr, wdown[sl, :])
        x, u = normalize(b1[:, sl], cols(st, c))
        g = gz * m * silu_grad(u)
        g4_ref[:, sl] = g
        sums_ref[:, sl] = ksums(g * x, g)


def conv_forward(cnt, a1, s0, gb0, mask, valid, w, im_ref, a2_ref, sums_ref):
    m = mask[...]
    st = kstats(s0[...], 4.0 * cnt[0], gb0[...])
    for c in range(4):
        sl = slice(c * 128, (c + 1) * 128)
        stc = cols(st, c)
        for ph in range(4):
            h = m * silu(normalize(a1[ph, :, sl], stc)[1])
            h = h.astype(BF16).astype(F32)
            for dx in (0, -1):
                if dx and not ph & 1:
                    continue
                moved = kshift_cols(h, dx)
                for p, dy, dx2, t in TAPS2:
                    if p == ph and dx2 == dx:
                        at = t * MID + c * 128
                        im_ref[:, at : at + 128] = shift_rows(moved, dy).astype(BF16)
    a2 = dot(im_ref[...], w[...]) * valid[...]
    a2_ref[...] = a2
    sums_ref[...] = ksums(a2, a2 * a2)


def conv_backward(cnt, g1, t1, a2, s1, gb1, mask, w, a1, s0, gb0,
                  d1_ref, g0_ref, sums_ref, moved_ref):
    m = mask[...]
    count = cnt[0]
    st = kstats(s1[...], count, gb1[...])
    tot = t1[...]
    for c in range(4):
        sl = slice(c * 128, (c + 1) * 128)
        stc = cols(st, c)
        x, _ = normalize(a2[:, sl], stc)
        d = norm_back(g1[:, sl], x, m, stc, (tot[0:1, sl], tot[1:2, sl]), count).astype(BF16)
        d1_ref[:, sl] = d
        d = d.astype(F32)
        for dx in (0, 1):
            moved = kshift_cols(d, dx)
            for dy in (0, 1):
                moved_ref[dy * 2 + dx, :, sl] = shift_rows(moved, dy).astype(BF16)
    st = kstats(s0[...], 4.0 * count, gb0[...])
    sums = jnp.zeros((2, MID), F32)
    for ph in range(4):
        gh = None
        for p, dy, dx, t in TAPS2:
            if p == ph:
                part = dot_nt(moved_ref[-dy * 2 - dx], w[t * MID : (t + 1) * MID, :])
                gh = part if gh is None else gh + part
        halves = []
        for c in range(4):
            sl = slice(c * 128, (c + 1) * 128)
            x, u = normalize(a1[ph, :, sl], cols(st, c))
            g = gh[:, sl] * m * silu_grad(u)
            g0_ref[ph, :, sl] = g
            halves.append(ksums(g * x, g))
        sums = sums + jnp.concatenate(halves, axis=1)
    sums_ref[...] = sums


def window_tables():
    pixel = WINDOWS.reshape(12, 9, R)
    table = np.zeros((160, R), np.float32)
    for slot in range(12):
        if slot % 4 < 3:
            for t in range(9):
                table[t * 16 + slot] = pixel[slot + 1, t]
        table[144 + slot] = pixel[slot, 4]
    spread = np.zeros((R, 16), np.float32)
    spread[:, :12] = SPREAD
    return table, np.concatenate([spread] * 3, axis=1)


TABLE, SPREAD3 = window_tables()


def scatter_sum(grads, n, mesh_bits):
    sizes = [g.shape[1] for g in grads]
    x = jnp.concatenate([g.astype(BF16) for g in grads], axis=1)
    x = jnp.pad(x, ((0, 0), (0, -x.shape[1] % 1024)))
    x = x.reshape((2,) * (n.bit_length() - 1) + (-1, 128))
    me = lax.axis_index(AXES)
    bits = n.bit_length() - 1
    left = list(range(bits))
    for b in mesh_bits:
        axis = left.index(bits - 1 - b)
        mine = (me >> b) & 1
        keep = lax.dynamic_index_in_dim(x, mine, axis, keepdims=False)
        send = lax.dynamic_index_in_dim(x, 1 - mine, axis, keepdims=False)
        got = lax.ppermute(send, AXES, [(i, i ^ (1 << b)) for i in range(n)])
        total = keep.astype(F32) + got.astype(F32)
        left.pop(axis)
        x = total if b == mesh_bits[-1] else total.astype(BF16)
    flat = x.reshape(-1)
    out = []
    at = 0
    for s in sizes:
        out.append(flat[at : at + s])
        at += s
    return out


def body(n, fsdp, *args):
    (coarse, medium, fine, clip_counts, frame_counts, reduce_one, spatial_one, expand_one,
     shortcut_one, reduce_two, excite_down, excite_up, temporal_mix, expand_two, norm_params,
     motion_kernel, cot_c, cot_m, cot_f) = args
    bits = n.bit_length() - 1
    core = fsdp.bit_length() - 1
    order = [core] + [b for b in range(bits) if b != core]

    def gather(w):
        return lax.all_gather(w.astype(BF16), AXES, axis=0, tiled=True)

    def pack(ws):
        flat = jnp.concatenate([w.astype(BF16).reshape(-1) for w in ws])
        return jnp.pad(flat, (0, -flat.size % 1024)).reshape(-1, 128)

    def unpack(got, ws):
        flat = got.reshape(n, -1)
        out = []
        at = 0
        for w in ws:
            out.append(flat[:, at : at + w.size].reshape((n,) + w.shape))
            at += w.size
        return out

    early = (reduce_one, norm_params)
    packed = pack(early)
    got = lax.all_to_all(
        jnp.broadcast_to(packed[None], (n,) + packed.shape), AXES, 0, 0, tiled=True
    )
    w1, norms = unpack(got, early)
    w1 = w1.reshape(-1, MID)
    norms = norms.transpose(1, 0, 2).reshape(2, -1).astype(F32)
    wsp = gather(spatial_one)
    wsk = gather(shortcut_one)
    we1 = gather(expand_one)
    w2 = gather(reduce_two)
    narrow = (excite_down, excite_up, temporal_mix)
    wdown, wup, wmix = unpack(gather(pack(narrow)), narrow)
    wdown = wdown.reshape(MID, SQUEEZE)
    wup = wup.transpose(1, 0, 2).reshape(SQUEEZE, MID).astype(F32)
    wmix = wmix.transpose(1, 0, 2).reshape(3, 9 * GROUP, GROUP)
    we2 = gather(expand_two)
    edges = [0, 512, 1024, 3072, 5120, 5632, 6144, 8192]
    gb = [norms[:, edges[k] : edges[k + 1]] for k in range(7)]

    alive = (jnp.arange(4)[None, :] < frame_counts[0][:, None]) & (clip_counts[0][:, None] > 0)
    alive = alive.astype(F32)
    later = jnp.pad(alive[:, 1:], ((0, 0), (0, 1)))
    alive_slots = alive.reshape(12)
    later_slots = later.reshape(12)
    mask = (jnp.asarray(SPREAD) @ alive_slots)[:, None]
    per_group = jnp.sum(alive, axis=1)
    local_out = jnp.sum(per_group * jnp.array([16.0, 36.0, 49.0], F32))

    clips = [
        x * alive[g].astype(BF16)[:, None, None, None]
        for g, x in enumerate((coarse, medium, fine))
    ]
    xph = [to_rows(clips, ph) for ph in range(4)]
    cot = to_rows((cot_c, cot_m, cot_f), None).astype(F32)

    a1 = [dot(x, w1) for x in xph]
    s0 = sum(sums_of(a) for a in a1)
    ap = dot(xph[0], wsk)
    s3 = sums_of(ap)
    s0, count_out = allsum((s0, local_out.reshape(1)), n)
    count_out = count_out[0]
    count_in = 4.0 * count_out
    st0 = norm_rows(s0, count_in, gb[0])
    cnt = count_out.reshape(1)
    m128 = jnp.broadcast_to(mask, (R, 128))
    valid = jnp.asarray(np.broadcast_to(VALID[:, None], (R, MID)).astype(np.float32))
    a1 = jnp.stack(a1)
    im, a2, p1 = call(
        conv_forward,
        [like((R, 9 * MID), BF16), like((R, MID)), like((2, MID))],
        6,
    )(cnt, a1, s0, gb[0], m128, valid, wsp)
    s1, = allsum((p1,), n)
    st1 = norm_rows(s1, count_out, gb[1])
    h2 = (mask * silu(normalize(a2, st1)[1])).astype(BF16)
    a3 = dot(h2, we1)
    s2, s3 = allsum((sums_of(a3), s3), n)
    st2 = norm_rows(s2, count_out, gb[2])
    st3 = norm_rows(s3, count_out, gb[3])
    y1 = mask * silu(normalize(a3, st2)[1] + normalize(ap, st3)[1])
    y1_low = y1.astype(BF16)
    b1 = dot(y1_low, w2)
    s4, = allsum((sums_of(b1),), n)
    st4 = norm_rows(s4, count_out, gb[4])
    scale = later_slots / jnp.asarray(NPIX)
    scale = jnp.broadcast_to(jnp.pad(scale, (0, 4))[:, None], (16, SQUEEZE))
    table = jnp.asarray(TABLE, BF16)
    spread = jnp.asarray(SPREAD3, BF16)
    z, z_low, mixed, mix_im, sig, pooled, wnext, p5 = call(
        mix_forward,
        [like((R, MID)), like((R, MID), BF16), like((R, MID)), like((3, R, 9 * GROUP), BF16),
         like((16, MID)), like((16, SQUEEZE)), like((144, SQUEEZE)), like((2, MID))],
        11,
    )(cnt, b1, s4, gb[4], m128, wdown, wup, wmix, motion_kernel, scale, table, spread)
    s5, = allsum((p5,), n)
    st5 = norm_rows(s5, count_out, gb[5])
    w = (mask * silu(normalize(mixed, st5)[1])).astype(BF16)
    b3 = dot(w, we2)
    s6, = allsum((sums_of(b3),), n)
    st6 = norm_rows(s6, count_out, gb[6])
    x6, u6 = normalize(b3, st6)
    u6 = u6 + y1
    out = (mask * silu(u6)).astype(BF16)

    g6 = cot * mask * silu_grad(u6)
    t6, = allsum((back_sums(g6, x6),), n)
    d6 = norm_back(g6, x6, mask, st6, t6, count_out).astype(BF16)
    ge2 = dot_tn(w, d6)
    x5, u5 = normalize(mixed, st5)
    g5 = dot_nt(d6, we2) * mask * silu_grad(u5)
    t5, = allsum((back_sums(g5, x5),), n)
    wmix_t = wmix.reshape(3, 9, GROUP, GROUP).transpose(0, 1, 3, 2).reshape(3, 9 * GROUP, GROUP)
    g4, p4, gkernel, gmix, gdown, gup = call(
        mix_backward,
        [like((R, MID)), like((2, MID)), like((16, SQUEEZE)), like((3, 9 * GROUP, GROUP), BF16),
         like((MID, SQUEEZE)), like((SQUEEZE, MID))],
        22,
        [pltpu.VMEM((R, 9 * GROUP), BF16), pltpu.VMEM((R, MID), F32)],
    )(cnt, g5, t5, mixed, s5, gb[5], m128, mix_im, wmix_t, z, sig, pooled, wnext,
      wup, motion_kernel, scale, table.T, spread, z_low, wdown, b1, s4, gb[4])
    t4, gkernel = allsum((p4, gkernel), n)
    gkernel = gkernel[:9]
    x4, u4 = normalize(b1, st4)
    d4 = norm_back(g4, x4, mask, st4, t4, count_out).astype(BF16)
    gr2 = dot_tn(y1_low, d4)
    gy1 = g6 + dot_nt(d4, w2)
    x2, u2 = normalize(a3, st2)
    x3, u3 = normalize(ap, st3)
    gj = gy1 * mask * silu_grad(u2 + u3)
    tj, = allsum((jnp.stack([jnp.sum(gj * x2, 0), jnp.sum(gj * x3, 0), jnp.sum(gj, 0)]),), n)
    d2 = norm_back(gj, x2, mask, st2, tj[jnp.array([0, 2])], count_out).astype(BF16)
    d3 = norm_back(gj, x3, mask, st3, tj[1:], count_out).astype(BF16)
    ge1 = dot_tn(h2, d2)
    gsk = dot_tn(xph[0], d3)
    x1, u1 = normalize(a2, st1)
    g1 = dot_nt(d2, we1) * mask * silu_grad(u1)
    t1, = allsum((back_sums(g1, x1),), n)
    d1, g0, p0 = call(
        conv_backward,
        [like((R, MID), BF16), like((4, R, MID)), like((2, MID))],
        10,
        [pltpu.VMEM((4, R, MID), BF16)],
    )(cnt, g1, t1, a2, s1, gb[1], m128, wsp, a1, s0, gb[0])
    gsp = dot_tn(im, d1)
    t0, = allsum((p0,), n)
    d0 = [
        norm_back(g0[k], normalize(a1[k], st0)[0], mask, st0, t0, count_in).astype(BF16)
        for k in range(4)
    ]
    gr1 = sum(dot_tn(x, d) for x, d in zip(xph, d0))
    gx = [dot_nt(d, w1) for d in d0]
    gx[0] = gx[0] + dot_nt(d3, wsk)
    gx = [(mask * v).astype(BF16) for v in gx]
    phases = [from_rows(v) for v in gx]
    gin = []
    for g, side in enumerate(SIDES):
        st = jnp.stack([phases[k][g] for k in range(4)]).reshape(2, 2, 4, side, side, -1)
        gin.append(st.transpose(2, 3, 0, 4, 1, 5).reshape(4, 2 * side, 2 * side, -1))

    def shards(v):
        return v.reshape(n, -1)

    gmix = gmix.reshape(27, n, GROUP * GROUP // n).transpose(1, 0, 2)
    gup = gup.reshape(SQUEEZE, n, MID // n).transpose(1, 0, 2)
    second = scatter_sum(
        [shards(ge2), shards(gr2), shards(gmix), shards(gdown), shards(gup)], n, order
    )
    first = scatter_sum([shards(ge1), shards(gsk)], n, order)
    last = scatter_sum([shards(gsp), shards(gr1)], n, order)

    gain = jnp.concatenate([t0[0], t1[0], tj[0], tj[1], t4[0], t5[0], t6[0]])
    bias = jnp.concatenate([t0[1], t1[1], tj[2], tj[2], t4[1], t5[1], t6[1]])
    me = lax.axis_index(AXES)
    gnorm = lax.dynamic_slice_in_dim(jnp.stack([gain, bias]), me * (8192 // n), 8192 // n, 1)
    o = from_rows(out)
    return (
        o[0], o[1], o[2], gin[0], gin[1], gin[2],
        last[1].reshape(reduce_one.shape),
        last[0].reshape(spatial_one.shape),
        first[0].reshape(expand_one.shape),
        first[1].reshape(shortcut_one.shape),
        second[1].reshape(reduce_two.shape),
        second[3].reshape(excite_down.shape),
        second[4].reshape(excite_up.shape),
        second[2].reshape(temporal_mix.shape),
        second[0].reshape(expand_two.shape),
        gnorm,
        gkernel,
    )


def solution(mesh):
    n = mesh.shape["dp"] * mesh.shape["fsdp"]
    rows = P(AXES, None)
    cols = P(None, AXES)
    image = P(AXES, None, None, None)
    return jax.shard_map(
        partial(body, n, mesh.shape["fsdp"]),
        mesh=mesh,
        in_specs=(image, image, image, rows, rows, rows, rows, rows, rows, rows, rows, cols, cols,
                  rows, cols, P(), image, image, image),
        out_specs=(image, image, image, image, image, image, rows, rows, rows, rows, rows, rows,
                   cols, cols, rows, cols, P()),
        check_vma=False,
    )
```

time: 2970 us -> 774 us (0.26)
  waiting for transfers between devices: 1190 us -> 268 us
  blocking collectives: 766 us -> 86.5 us
  local copies, waits for them, and re-layouts: 537 us -> 132 us
  matrix products: 290 us -> 74.2 us
  starting transfers between devices: 1.45 us -> 67.8 us
  other arithmetic: 133 us -> 81.9 us
  Pallas kernels: 0 us -> 36.4 us
    reduce_scatter x9 -> x0, waiting for transfers between devices: 1190 us -> none  [the longest x1 185 us: on_device(): lax.psum_scatter(grad_short, ('dp', 'fsdp'), scatter_dimension=0, tiled=T...]
    psum x12 -> x0, blocking collectives: 489 us -> none  [the longest x4 167 us: global_sums(): return lax.psum((sum_first, sum_second), ('dp', 'fsdp'))]
    slice x108 -> x44, local copies, waits for them, and re-layouts: 345 us -> 4.18 us  [the longest x1 1.89 us: to_rows(): x = x.reshape(FRAMES, side, 2, side, 2, c)[:, :, phase // 2, :, phase % 2]]
    dot_general x387 -> x26, matrix products: 290 us -> 74.2 us  [the longest x8 28.6 us: dot(): return jnp.dot(a, b, preferred_element_type=F32)]
    all_gather x4 -> x1, blocking collectives: 277 us -> 86.5 us  [gather(): return lax.all_gather(w.astype(BF16), AXES, axis=0, tiled=True)]
    all_gather x6 -> x5, waiting for transfers between devices: 0.03 us -> 100 us  [gather(): return lax.all_gather(w.astype(BF16), AXES, axis=0, tiled=True)]
    ppermute x0 -> x15, waiting for transfers between devices: none -> 99.1 us  [scatter_sum(): got = lax.ppermute(send, AXES, [(i, i ^ 1 << b) for i in range(n)])]
    pad x18 -> x11, local copies, waits for them, and re-layouts: 87.2 us -> 8.26 us  [the longest x10 8.25 us: to_rows(): x = jnp.pad(x, ((0, 0), (0, 0), (0, 8 - side), (0, 0))).reshape(-1, c)]
  transfers between devices with their start and end apart: 16 -> 33, of which waited for: 9 -> 19; matrix products, arithmetic and copies ran while one was open for 18% -> 31% of each run, Pallas kernels for 0% -> 4%
where the time goes in v1:
time: 774 us; the launch traced here: 764 us
  waiting for transfers between devices  268 us (35%)
  local copies, waits for them, and re-layouts  132 us (17%)
  blocking collectives  86.5 us (11%)
  other arithmetic  81.9 us (11%)
  matrix products  74.2 us (10%)
  starting transfers between devices  67.8 us (9%)
  Pallas kernels  36.4 us (5%)
  between operations  17.5 us (2%)
    all_gather x5, waiting for transfers between devices, gather(): return lax.all_gather(w.astype(BF16), AXES, axis=0, tiled=True)  100 us
    ppermute x15, waiting for transfers between devices, scatter_sum(): got = lax.ppermute(send, AXES, [(i, i ^ 1 << b) for i in range(n)])  99.1 us
    all_gather x1, blocking collectives, gather(): return lax.all_gather(w.astype(BF16), AXES, axis=0, tiled=True)  86.5 us
    all_to_all x12, waiting for transfers between devices, allsum(): got = lax.all_to_all(spread, AXES, 0, 0, tiled=True)  50.9 us
    all_to_all x12, starting transfers between devices, allsum(): got = lax.all_to_all(spread, AXES, 0, 0, tiled=True)  41.8 us
    unnamed x296, local copies, waits for them, and re-layouts  31.8 us
    dot_general x8, matrix products, dot(): return jnp.dot(a, b, preferred_element_type=F32)  28.6 us
    dot_general x9, matrix products, dot_tn(): lax.dot_general(a, b, (((0,), (0,)), ((), ())), preferred_element_type=F32)  26.1 us
  transfers between devices with their start and end apart: 33, of which 19 were waited for; matrix products, arithmetic and copies ran while one was open for 31% of the time, Pallas kernels for 4%

profile of v1, /device:TPU:0, one launch (start us, length us, event | category | flops | bytes accessed | tf_op | source)
XLA Modules:
  0.0 764.1 jit_solution(17027398134619715063)
XLA Ops:
  15.1 7.3 all-to-all-start
  42.4 17.2 %all-to-all-done = bf16[32,136,128]{2,1,0:T(8,128)(2,1)S(1)} async-done(((bf16[32,136,128]{2,1,0:T(8,128)(2,1)}), bf16[32,136,128]{2,1,0:T(8,128)(2,1)S(1)}, u32[]{:S(2)}, u32[]{:S(2)}) %all-to-all-start) | async-done | bytes 1114144 | tf_op jit(solution)/shard_map/all_to_all | solution.py:546
  69.9 4.0 all-to-all-start.1
  73.9 4.2 pad_maximum_fusion.a1
  78.7 9.7 %all-to-all-done.1 = f32[32,16,128]{2,1,0:T(8,128)S(1)} async-done(((f32[32,16,128]{2,1,0:T(8,128)}), f32[32,16,128]{2,1,0:T(8,128)S(1)}, u32[]{:S(2)}, u32[]{:S(2)}) %all-to-all-start.1) | async-done | bytes 262176 | tf_op jit(solution)/shard_map/all_to_all | solution.py:161
  90.4 9.7 %shard_map.377 = (bf16[480,4608]{1,0:T(8,128)(2,1)}, f32[480,512]{1,0:T(8,128)}, f32[2,512]{1,0:T(2,128)}) custom-call(f32[1]{0:T(128)} %slice.538.cnt, f32[4,480,512]{2,1,0:T(8,128)} %pad_maximum_fusion.a1, f32[2,512]{1,0:T(2,128)} %reshape.806.s0, f32[2,512]{1,0:T(2,128)} %get-tuple-element.179.gb0, f32[480,128]{1,0:T(8,128)} %broadcast_in_dim.60.mask, ...), custom_call_target="tpu_custom_call" | custom-call | tf_op jit(solution)/shard_map/pallas_call | solution.py:593
  104.0 49.3 %all-gather.10.cloned.1.call-done = bf16[1024,2048]{1,0:T(8,128)(2,1)} async-done(((bf16[32,2048]{1,0:T(8,128)(2,1)}), bf16[1024,2048]{1,0:T(8,128)(2,1)}) %all-gather.10.cloned.1.call-update) | async-done | bytes 4194320 | tf_op jit(solution)/shard_map/all_gather | solution.py:529
  153.3 6.3 fusion.80
  160.9 51.1 %all-gather.8.cloned.1.call-done = bf16[512,2048]{1,0:T(8,128)(2,1)} async-done(((bf16[16,2048]{1,0:T(8,128)(2,1)}), bf16[512,2048]{1,0:T(8,128)(2,1)}) %all-gather.8.cloned.1.call-update) | async-done | bytes 2097168 | tf_op jit(solution)/shard_map/all_gather | solution.py:529
  212.0 4.9 fusion.79
  218.1 3.5 all-to-all-start.3
  222.6 86.5 %all_gather.22 = bf16[3840,128]{1,0:T(8,128)(2,1)S(1)} all-gather(bf16[120,128]{1,0:T(8,128)(2,1)S(1)} %fusion.39), channel_id=1, replica_groups=mesh['dp'=16,'fsdp'=2] {'dp','fsdp'}, dimensions={0}, use_global_device_ids=true | all-gather | bytes 1013760 | tf_op jit(solution)/shard_map/all_gather | solution.py:529
  311.0 5.7 multiply_multiply_fusion.2
  316.8 4.9 fusion.81
  330.7 4.5 all-to-all-done.4
  336.5 6.9 shard_map.378
  349.1 6.9 all-to-all-done.5
  357.2 5.3 fusion.78
  369.2 11.8 %all-to-all-done.6 = f32[32,32,128]{2,1,0:T(8,128)S(1)} async-done(((f32[32,32,128]{2,1,0:T(8,128)}), f32[32,32,128]{2,1,0:T(8,128)S(1)}, u32[]{:S(2)}, u32[]{:S(2)}) %all-to-all-start.6) | async-done | bytes 524320 | tf_op jit(solution)/shard_map/all_to_all | solution.py:161
  382.9 6.6 multiply_reduce_fusion.2
  390.4 3.8 all-to-all-start.7
  405.3 3.9 all-to-all-done.7
  409.3 5.4 multiply_convert_fusion.2
  418.0 3.6 all-to-all-start.8
  430.9 9.3 %shard_map.379 = (f32[480,512]{1,0:T(8,128)}, f32[2,512]{1,0:T(2,128)}, f32[16,32]{1,0:T(8,128)}, bf16[3,1152,128]{2,1,0:T(8,128)(2,1)}, f32[512,32]{1,0:T(8,128)}, /*index=5*/f32[32,512]{1,0:T(8,128)}) custom-call(f32[1]{0:T(128)} %slice.538.cnt, f32[480,512]{1,0:T(8,128)} %get-tuple-element.232.g5, f32[2,512]{1,0:T(2,128)} %reshape_reshape.49.t5, ...), custom_call_target="tpu_custom_call" | custom-call | tf_op jit(solution)/shard_map/pallas_call | solution.py:638
  450.1 6.4 all-to-all-done.9
  459.0 3.6 convolution_convert_fusion.2
  462.7 7.9 %multiply_reduce_fusion.1 = (f32[2048]{0:T(1024)S(1)}, f32[2048]{0:T(1024)S(1)}, f32[2048]{0:T(1024)S(1)}, f32[480,2048]{1,0:T(8,128)}) fusion(f32[480,2048]{1,0:T(8,128)} %get-tuple-element.229, f32[2048]{0:T(1024)S(1)} %get-tuple-element.190, f32[2048]{0:T(1024)S(1)} %copy-done.73, f32[2048]{0:T(1024)S(1)} %copy-done.69, f32[480,2048]{1,0:T(8,128)S(1)} %copy-done.2, ...), kind=kOutput, calls=%fused_computation.15 | convolution fusion | flops 1030219776 | bytes 18409344 | tf_op jit(solution)/shard_map/dot_general | solution.py:144
  471.5 3.3 all-to-all-start.10
  490.7 4.7 all-to-all-done.10
  497.5 7.3 multiply_convert_fusion
  510.8 3.7 all-to-all-start.11
  517.4 5.9 convolution_convert_fusion.1
  523.3 5.6 convert_element_type.447
  537.3 3.5 fusion.98
  541.5 10.6 %shard_map.380 = (bf16[480,512]{1,0:T(8,128)(2,1)}, f32[4,480,512]{2,1,0:T(8,128)}, f32[2,512]{1,0:T(2,128)}) custom-call(f32[1]{0:T(128)} %slice.538.cnt, f32[480,512]{1,0:T(8,128)} %get-tuple-element.234.g1, f32[2,512]{1,0:T(2,128)} %reshape_reshape.53.t1, f32[480,512]{1,0:T(8,128)} %get-tuple-element.37.a2, f32[2,512]{1,0:T(2,128)} %reshape_reshape.54.s1, ...), custom_call_target="tpu_custom_call" | custom-call | tf_op jit(solution)/shard_map/pallas_call | solution.py:663
  553.4 6.2 all-to-all-start.12
  559.6 7.2 convolution_convert_fusion
  566.8 6.1 convert_element_type.422
  573.0 4.5 fusion.18
  616.5 20.5 %collective-permute-done.11 = bf16[2,2,2,632,128]{4,3,2,1,0:T(8,128)(2,1)} collective-permute-done((bf16[2,2,2,632,128]{4,3,2,1,0:T(8,128)(2,1)}, bf16[2,2,2,632,128]{4,3,2,1,0:T(8,128)(2,1)}, u32[]{:S(2)}, u32[]{:S(2)}) %collective-permute-start.11) | collective-permute-done | bytes 1294368 | tf_op jit(solution)/shard_map/ppermute | solution.py:507
  651.3 3.6 collective-permute-done.12
  661.8 5.9 collective-permute-done.13
  670.3 16.9 %collective-permute-done.6 = bf16[2,2,2,768,128]{4,3,0,1,2:T(8,128)(2,1)S(1)} collective-permute-done((bf16[2,2,2,768,128]{4,3,0,1,2:T(8,128)(2,1)S(1)}, bf16[2,2,2,768,128]{4,3,0,1,2:T(8,128)(2,1)S(1)}, u32[]{:S(2)}, u32[]{:S(2)}) %collective-permute-start.6) | collective-permute-done | bytes 1572896 | tf_op jit(solution)/shard_map/ppermute | solution.py:507
  688.0 28.4 %collective-permute-done.1 = bf16[2,2,2,704,128]{4,3,0,1,2:T(8,128)(2,1)S(1)} collective-permute-done((bf16[2,2,2,704,128]{4,3,0,1,2:T(8,128)(2,1)S(1)}, bf16[2,2,2,704,128]{4,3,0,1,2:T(8,128)(2,1)S(1)}, u32[]{:S(2)}, u32[]{:S(2)}) %collective-permute-start.1) | collective-permute-done | bytes 1441824 | tf_op jit(solution)/shard_map/ppermute | solution.py:507
  724.2 10.2 %collective-permute-done.2 = bf16[2,2,704,128]{3,2,0,1:T(8,128)(2,1)S(1)} collective-permute-done((bf16[2,2,704,128]{3,2,0,1:T(8,128)(2,1)}, bf16[2,2,704,128]{3,2,0,1:T(8,128)(2,1)S(1)}, u32[]{:S(2)}, u32[]{:S(2)}) %collective-permute-start.2) | collective-permute-done | bytes 720928 | tf_op jit(solution)/shard_map/ppermute | solution.py:507
  739.8 7.9 %collective-permute-done.3 = bf16[2,704,128]{2,1,0:T(8,128)(2,1)S(1)} collective-permute-done((bf16[2,704,128]{2,1,0:T(8,128)(2,1)S(1)}, bf16[2,704,128]{2,1,0:T(8,128)(2,1)S(1)}, u32[]{:S(2)}, u32[]{:S(2)}) %collective-permute-start.3) | collective-permute-done | bytes 360480 | tf_op jit(solution)/shard_map/ppermute | solution.py:507
  749.9 5.8 collective-permute-done.4
  (628 shorter events, 229.1 us)
Async XLA Ops:
  7.2 15.9 %copy-start.121 = (s32[1,3]{1,0:T(1,128)S(1)}, s32[1,3]{1,0:T(1,128)}, u32[]{:S(2)}) copy-start(s32[1,3]{1,0:T(1,128)} %param.30) | copy-start | bytes 40
  7.2 16.1 %copy-start.20 = (bf16[4,14,14,1024]{3,0,2,1:T(4,128)(2,1)S(1)}, bf16[4,14,14,1024]{3,0,2,1:T(4,128)(2,1)}, u32[]{:S(2)}) copy-start(bf16[4,14,14,1024]{3,0,2,1:T(4,128)(2,1)} %param.28) | copy-start | bytes 4816900
  7.2 82.4 %all-gather.6.cloned.1.call-start = ((), (), s32[]{:S(2)}) async-start(), calls=%async_computation.13 | async-start | bytes 4866048 | tf_op jit(solution)/shard_map/all_gather | solution.py:529
  9.1 144.3 %all-gather.10.cloned.1.call-start = ((), (), s32[]{:S(2)}) async-start(), calls=%async_computation.15 | async-start | bytes 4325376 | tf_op jit(solution)/shard_map/all_gather | solution.py:529
  10.8 201.2 %all-gather.8.cloned.1.call-start = ((), (), s32[]{:S(2)}) async-start(), calls=%async_computation.14 | async-start | bytes 2162688 | tf_op jit(solution)/shard_map/all_gather | solution.py:529
  15.1 44.5 %all-to-all-start = ((bf16[32,136,128]{2,1,0:T(8,128)(2,1)}), bf16[32,136,128]{2,1,0:T(8,128)(2,1)S(1)}, u32[]{:S(2)}, u32[]{:S(2)}) async-start(bf16[32,136,128]{2,1,0:T(8,128)(2,1)} %broadcast_in_dim.57), calls=%async_computation | async-start | bytes 2228224 | tf_op jit(solution)/shard_map/all_to_all | solution.py:546
  22.4 294.4 %all-gather.12.cloned.1.call-start = ((), (), s32[]{:S(2)}) async-start(), calls=%async_computation.16 | async-start | bytes 2162688 | tf_op jit(solution)/shard_map/all_gather | solution.py:529
  40.4 26.4 %copy-start.18 = (bf16[4,7,8,1024]{3,2,1,0:T(8,128)(2,1)}, bf16[4,7,8,1024]{3,2,1,0:T(8,128)(2,1)S(1)}, u32[]{:S(2)}) copy-start(bf16[4,7,8,1024]{3,2,1,0:T(8,128)(2,1)S(1)} %pad.70.clone) | copy-start | bytes 1376260
  69.9 18.6 %all-to-all-start.1 = ((f32[32,16,128]{2,1,0:T(8,128)}), f32[32,16,128]{2,1,0:T(8,128)S(1)}, u32[]{:S(2)}, u32[]{:S(2)}) async-start(f32[32,16,128]{2,1,0:T(8,128)} %broadcast_in_dim.59), calls=%async_computation.1 | async-start | bytes 524288 | tf_op jit(solution)/shard_map/all_to_all | solution.py:161
  78.1 133.9 %copy-start.117 = (f32[1,512]{1,0:T(1,128)}, f32[1,512]{1,0:T(1,128)S(1)}, u32[]{:S(2)}) copy-start(f32[1,512]{1,0:T(1,128)S(1)} %get-tuple-element.184) | copy-start | bytes 6148
  78.1 133.9 %copy-start.119 = (f32[1,512]{1,0:T(1,128)}, f32[1,512]{1,0:T(1,128)S(1)}, u32[]{:S(2)}) copy-start(f32[1,512]{1,0:T(1,128)S(1)} %get-tuple-element.185) | copy-start | bytes 6148
  90.4 62.9 %copy-start.37 = (bf16[4,7,8,1024]{3,2,1,0:T(8,128)(2,1)S(1)}, bf16[4,7,8,1024]{3,2,1,0:T(8,128)(2,1)}, u32[]{:S(2)}) copy-start(bf16[4,7,8,1024]{3,2,1,0:T(8,128)(2,1)} %pad.63.clone) | copy-start | bytes 1376260
  90.4 62.9 %copy-start.46 = (bf16[4,6,8,1024]{3,2,1,0:T(8,128)(2,1)S(1)}, bf16[4,6,8,1024]{3,2,1,0:T(8,128)(2,1)}, u32[]{:S(2)}) copy-start(bf16[4,6,8,1024]{3,2,1,0:T(8,128)(2,1)} %pad.62.clone) | copy-start | bytes 1179652
  90.4 62.9 %copy-start.58 = (bf16[64,1024]{1,0:T(8,128)(2,1)S(1)}, bf16[64,1024]{1,0:T(8,128)(2,1)}, u32[]{:S(2)}) copy-start(bf16[64,1024]{1,0:T(8,128)(2,1)} %reshape.787) | copy-start | bytes 393220
  101.5 58.2 %all-to-all-start.2 = ((f32[32,8,128]{2,1,0:T(8,128)}), f32[32,8,128]{2,1,0:T(8,128)S(1)}, u32[]{:S(2)}, u32[]{:S(2)}) async-start(f32[32,8,128]{2,1,0:T(8,128)} %broadcast_in_dim.62), calls=%async_computation.2 | async-start | bytes 262144 | tf_op jit(solution)/shard_map/all_to_all | solution.py:161
  104.0 107.9 %copy-start.27 = (f32[480,512]{1,0:T(8,128)S(1)}, f32[480,512]{1,0:T(8,128)}, u32[]{:S(2)}) copy-start(f32[480,512]{1,0:T(8,128)} %get-tuple-element.37.a2) | copy-start | bytes 2949124
  160.3 56.6 %copy-start.109 = (f32[512]{0:T(512)}, f32[512]{0:T(512)S(1)}, u32[]{:S(2)}) copy-start(f32[512]{0:T(512)S(1)} %divide_bitcast_fusion.1) | copy-start | bytes 6148
  160.9 56.0 %copy-start.111 = (f32[512]{0:T(512)}, f32[512]{0:T(512)S(1)}, u32[]{:S(2)}) copy-start(f32[512]{0:T(512)S(1)} %fusion.63) | copy-start | bytes 6148
  218.1 91.6 %all-to-all-start.3 = ((f32[32,64,128]{2,1,0:T(8,128)}), f32[32,64,128]{2,1,0:T(8,128)S(1)}, u32[]{:S(2)}, u32[]{:S(2)}) async-start(f32[32,64,128]{2,1,0:T(8,128)} %broadcast_in_dim.63), calls=%async_computation.3 | async-start | bytes 2097152 | tf_op jit(solution)/shard_map/all_to_all | solution.py:161
  221.5 135.7 %all-gather.14.cloned.1.call-start = ((), (), s32[]{:S(2)}) async-start(), calls=%async_computation.17 | async-start | bytes 2162688 | tf_op jit(solution)/shard_map/all_gather | solution.py:529
  311.0 151.6 %copy-start.66 = (f32[2048]{0:T(1024)}, f32[2048]{0:T(1024)S(1)}, u32[]{:S(2)}) copy-start(f32[2048]{0:T(1024)S(1)} %get-tuple-element.190) | copy-start | bytes 24580
  322.4 12.9 %all-to-all-start.4 = ((f32[32,8,128]{2,1,0:T(8,128)}), f32[32,8,128]{2,1,0:T(8,128)S(1)}, u32[]{:S(2)}, u32[]{:S(2)}) async-start(f32[32,8,128]{2,1,0:T(8,128)} %broadcast_in_dim.65), calls=%async_computation.4 | async-start | bytes 262144 | tf_op jit(solution)/shard_map/all_to_all | solution.py:161
  344.8 11.2 %all-to-all-start.5 = ((f32[32,8,128]{2,1,0:T(8,128)}), f32[32,8,128]{2,1,0:T(8,128)S(1)}, u32[]{:S(2)}, u32[]{:S(2)}) async-start(f32[32,8,128]{2,1,0:T(8,128)} %broadcast_in_dim.68), calls=%async_computation.5 | async-start | bytes 262144 | tf_op jit(solution)/shard_map/all_to_all | solution.py:161
  363.5 17.6 %all-to-all-start.6 = ((f32[32,32,128]{2,1,0:T(8,128)}), f32[32,32,128]{2,1,0:T(8,128)S(1)}, u32[]{:S(2)}, u32[]{:S(2)}) async-start(f32[32,32,128]{2,1,0:T(8,128)} %broadcast_in_dim.70), calls=%async_computation.6 | async-start | bytes 1048576 | tf_op jit(solution)/shard_map/all_to_all | solution.py:161
  390.4 18.7 %all-to-all-start.7 = ((f32[32,32,128]{2,1,0:T(8,128)}), f32[32,32,128]{2,1,0:T(8,128)S(1)}, u32[]{:S(2)}, u32[]{:S(2)}) async-start(f32[32,32,128]{2,1,0:T(8,128)} %broadcast_in_dim.72), calls=%async_computation.7 | async-start | bytes 1048576 | tf_op jit(solution)/shard_map/all_to_all | solution.py:161
  418.0 12.3 %all-to-all-start.8 = ((f32[32,8,128]{2,1,0:T(8,128)}), f32[32,8,128]{2,1,0:T(8,128)S(1)}, u32[]{:S(2)}, u32[]{:S(2)}) async-start(f32[32,8,128]{2,1,0:T(8,128)} %broadcast_in_dim.74), calls=%async_computation.8 | async-start | bytes 262144 | tf_op jit(solution)/shard_map/all_to_all | solution.py:161
  442.5 13.9 %all-to-all-start.9 = ((f32[32,16,128]{2,1,0:T(8,128)}), f32[32,16,128]{2,1,0:T(8,128)S(1)}, u32[]{:S(2)}, u32[]{:S(2)}) async-start(f32[32,16,128]{2,1,0:T(8,128)} %broadcast_in_dim.76), calls=%async_computation.9 | async-start | bytes 524288 | tf_op jit(solution)/shard_map/all_to_all | solution.py:161
  471.5 23.9 %all-to-all-start.10 = ((f32[32,48,128]{2,1,0:T(8,128)}), f32[32,48,128]{2,1,0:T(8,128)}, u32[]{:S(2)}, u32[]{:S(2)}) async-start(f32[32,48,128]{2,1,0:T(8,128)} %broadcast_in_dim.78), calls=%async_computation.10 | async-start | bytes 1572864 | tf_op jit(solution)/shard_map/all_to_all | solution.py:161
  490.0 112.4 %collective-permute-start.10 = (bf16[2,2,2,2,632,128]{5,4,3,2,1,0:T(8,128)(2,1)}, bf16[2,2,2,2,632,128]{5,4,3,2,1,0:T(8,128)(2,1)}, u32[]{:S(2)}, u32[]{:S(2)}) collective-permute-start(bf16[2,2,2,2,632,128]{5,4,3,2,1,0:T(8,128)(2,1)} %dynamic-slice_bitcast_fusion), channel_id=1, source_target_pairs={{0,2},{1,3},{2,0},{3,1},{4,6},{5,7},{6,4},{7,5},{8,10},{9,11},{10,... | collective-permute-start | bytes 7766024 | tf_op jit(solution)/shard_map/ppermute | solution.py:507
  510.8 30.1 %all-to-all-start.11 = ((f32[32,8,128]{2,1,0:T(8,128)}), f32[32,8,128]{2,1,0:T(8,128)S(1)}, u32[]{:S(2)}, u32[]{:S(2)}) async-start(f32[32,8,128]{2,1,0:T(8,128)} %broadcast_in_dim.81), calls=%async_computation.11 | async-start | bytes 262144 | tf_op jit(solution)/shard_map/all_to_all | solution.py:161
  535.3 111.7 %collective-permute-start.5 = (bf16[2,2,2,2,768,128]{5,4,0,1,2,3:T(8,128)(2,1)}, bf16[2,2,2,2,768,128]{5,4,0,1,2,3:T(8,128)(2,1)}, u32[]{:S(2)}, u32[]{:S(2)}) collective-permute-start(bf16[2,2,2,2,768,128]{5,4,0,1,2,3:T(8,128)(2,1)} %bitcast.467), channel_id=1, source_target_pairs={{0,2},{1,3},{2,0},{3,1},{4,6},{5,7},{6,4},{7,5},{8,10},{9,11},{10,... | collective-permute-start | bytes 9437192 | tf_op jit(solution)/shard_map/ppermute | solution.py:507
  553.4 19.5 %all-to-all-start.12 = ((f32[32,8,128]{2,1,0:T(8,128)}), f32[32,8,128]{2,1,0:T(8,128)S(1)}, u32[]{:S(2)}, u32[]{:S(2)}) async-start(f32[32,8,128]{2,1,0:T(8,128)} %broadcast_in_dim.83), calls=%async_computation.12 | async-start | bytes 262144 | tf_op jit(solution)/shard_map/all_to_all | solution.py:161
  597.8 57.3 %collective-permute-start = (bf16[2,2,2,2,704,128]{5,4,0,1,2,3:T(8,128)(2,1)}, bf16[2,2,2,2,704,128]{5,4,0,1,2,3:T(8,128)(2,1)}, u32[]{:S(2)}, u32[]{:S(2)}) collective-permute-start(bf16[2,2,2,2,704,128]{5,4,0,1,2,3:T(8,128)(2,1)} %bitcast.468), channel_id=1, source_target_pairs={{0,2},{1,3},{2,0},{3,1},{4,6},{5,7},{6,4},{7,5},{8,10},{9,11},{10,... | collective-permute-start | bytes 8650760 | tf_op jit(solution)/shard_map/ppermute | solution.py:507
  606.0 31.0 %collective-permute-start.11 = (bf16[2,2,2,632,128]{4,3,2,1,0:T(8,128)(2,1)}, bf16[2,2,2,632,128]{4,3,2,1,0:T(8,128)(2,1)}, u32[]{:S(2)}, u32[]{:S(2)}) collective-permute-start(bf16[2,2,2,632,128]{4,3,2,1,0:T(8,128)(2,1)} %dynamic-slice_bitcast_fusion.3), channel_id=1, source_target_pairs={{0,1},{1,0},{2,3},{3,2},{4,5},{5,4},{6,7},{7,6},{8,9},{9,8},{10,11... | collective-permute-start | bytes 3883016 | tf_op jit(solution)/shard_map/ppermute | solution.py:507
  614.2 22.8 %copy-start.5 = (bf16[2,2,2,2,632,128]{5,4,3,2,1,0:T(8,128)(2,1)S(1)}, bf16[2,2,2,2,632,128]{5,4,3,2,1,0:T(8,128)(2,1)}, u32[]{:S(2)}) copy-start(bf16[2,2,2,2,632,128]{5,4,3,2,1,0:T(8,128)(2,1)} %copy-done.4) | copy-start | bytes 7766020
  616.3 24.2 %copy-start.34 = (bf16[2,4,2,4,1024]{4,3,1,2,0:T(4,128)(2,1)S(1)}, bf16[2,4,2,4,1024]{4,3,1,2,0:T(4,128)(2,1)}, u32[]{:S(2)}) copy-start(bf16[2,4,2,4,1024]{4,3,1,2,0:T(4,128)(2,1)} %copy.174) | copy-start | bytes 393220
  616.3 24.2 %copy-start.35 = (bf16[2,4,2,4,1024]{4,3,1,2,0:T(4,128)(2,1)S(1)}, bf16[2,4,2,4,1024]{4,3,1,2,0:T(4,128)(2,1)}, u32[]{:S(2)}) copy-start(bf16[2,4,2,4,1024]{4,3,1,2,0:T(4,128)(2,1)} %copy.175) | copy-start | bytes 393220
  638.7 16.2 %collective-permute-start.12 = (bf16[2,2,632,128]{3,2,1,0:T(8,128)(2,1)S(1)}, bf16[2,2,632,128]{3,2,1,0:T(8,128)(2,1)S(1)}, u32[]{:S(2)}, u32[]{:S(2)}) collective-permute-start(bf16[2,2,632,128]{3,2,1,0:T(8,128)(2,1)S(1)} %dynamic-slice_bitcast_fusion.6), channel_id=1, source_target_pairs={{0,4},{1,5},{2,6},{3,7},{4,0},{5,1},{6,2},{7,3},{8,12},{9,13},{10,... | collective-permute-start | bytes 1941512 | tf_op jit(solution)/shard_map/ppermute | solution.py:507
  649.8 37.4 %collective-permute-start.6 = (bf16[2,2,2,768,128]{4,3,0,1,2:T(8,128)(2,1)S(1)}, bf16[2,2,2,768,128]{4,3,0,1,2:T(8,128)(2,1)S(1)}, u32[]{:S(2)}, u32[]{:S(2)}) collective-permute-start(bf16[2,2,2,768,128]{4,3,0,1,2:T(8,128)(2,1)S(1)} %dynamic-slice_bitcast_fusion.1), channel_id=1, source_target_pairs={{0,1},{1,0},{2,3},{3,2},{4,5},{5,4},{6,7},{7,6},{8,9},{9,8},{10,11... | collective-permute-start | bytes 4718600 | tf_op jit(solution)/shard_map/ppermute | solution.py:507
  657.8 58.6 %collective-permute-start.1 = (bf16[2,2,2,704,128]{4,3,0,1,2:T(8,128)(2,1)S(1)}, bf16[2,2,2,704,128]{4,3,0,1,2:T(8,128)(2,1)S(1)}, u32[]{:S(2)}, u32[]{:S(2)}) collective-permute-start(bf16[2,2,2,704,128]{4,3,0,1,2:T(8,128)(2,1)S(1)} %dynamic-slice_bitcast_fusion.2), channel_id=1, source_target_pairs={{0,1},{1,0},{2,3},{3,2},{4,5},{5,4},{6,7},{7,6},{8,9},{9,8},{10,11... | collective-permute-start | bytes 4325384 | tf_op jit(solution)/shard_map/ppermute | solution.py:507
  659.6 8.1 %collective-permute-start.13 = (bf16[2,632,128]{2,1,0:T(8,128)(2,1)S(1)}, bf16[2,632,128]{2,1,0:T(8,128)(2,1)S(1)}, u32[]{:S(2)}, u32[]{:S(2)}) collective-permute-start(bf16[2,632,128]{2,1,0:T(8,128)(2,1)S(1)} %dynamic-slice_bitcast_fusion.9), channel_id=1, source_target_pairs={{0,8},{1,9},{2,10},{3,11},{4,12},{5,13},{6,14},{7,15},{8,0},{9,1},... | collective-permute-start | bytes 970760 | tf_op jit(solution)/shard_map/ppermute | solution.py:507
  667.8 20.2 %collective-permute-start.14 = (bf16[632,128]{1,0:T(8,128)(2,1)S(1)}, bf16[632,128]{1,0:T(8,128)(2,1)S(1)}, u32[]{:S(2)}, u32[]{:S(2)}) collective-permute-start(bf16[632,128]{1,0:T(8,128)(2,1)S(1)} %dynamic-slice_bitcast_fusion.12), channel_id=1, source_target_pairs={{0,16},{1,17},{2,18},{3,19},{4,20},{5,21},{6,22},{7,23},{8,24},{9,... | collective-permute-start | bytes 485384 | tf_op jit(solution)/shard_map/ppermute | solution.py:507
  687.6 30.4 %collective-permute-start.7 = (bf16[2,2,768,128]{3,2,0,1:T(8,128)(2,1)S(1)}, bf16[2,2,768,128]{3,2,0,1:T(8,128)(2,1)S(1)}, u32[]{:S(2)}, u32[]{:S(2)}) collective-permute-start(bf16[2,2,768,128]{3,2,0,1:T(8,128)(2,1)S(1)} %dynamic-slice_bitcast_fusion.4), channel_id=1, source_target_pairs={{0,4},{1,5},{2,6},{3,7},{4,0},{5,1},{6,2},{7,3},{8,12},{9,13},{10,... | collective-permute-start | bytes 2359304 | tf_op jit(solution)/shard_map/ppermute | solution.py:507
  717.7 16.7 %collective-permute-start.2 = (bf16[2,2,704,128]{3,2,0,1:T(8,128)(2,1)}, bf16[2,2,704,128]{3,2,0,1:T(8,128)(2,1)S(1)}, u32[]{:S(2)}, u32[]{:S(2)}) collective-permute-start(bf16[2,2,704,128]{3,2,0,1:T(8,128)(2,1)} %dynamic-slice_bitcast_fusion.5), channel_id=1, source_target_pairs={{0,4},{1,5},{2,6},{3,7},{4,0},{5,1},{6,2},{7,3},{8,12},{9,13},{10,... | collective-permute-start | bytes 2162696 | tf_op jit(solution)/shard_map/ppermute | solution.py:507
  719.0 17.1 %collective-permute-start.8 = (bf16[2,768,128]{2,1,0:T(8,128)(2,1)}, bf16[2,768,128]{2,1,0:T(8,128)(2,1)}, u32[]{:S(2)}, u32[]{:S(2)}) collective-permute-start(bf16[2,768,128]{2,1,0:T(8,128)(2,1)} %dynamic-slice_bitcast_fusion.7), channel_id=1, source_target_pairs={{0,8},{1,9},{2,10},{3,11},{4,12},{5,13},{6,14},{7,15},{8,0},{9,1},... | collective-permute-start | bytes 1179656 | tf_op jit(solution)/shard_map/ppermute | solution.py:507
  734.6 13.1 %collective-permute-start.3 = (bf16[2,704,128]{2,1,0:T(8,128)(2,1)S(1)}, bf16[2,704,128]{2,1,0:T(8,128)(2,1)S(1)}, u32[]{:S(2)}, u32[]{:S(2)}) collective-permute-start(bf16[2,704,128]{2,1,0:T(8,128)(2,1)S(1)} %dynamic-slice_bitcast_fusion.8), channel_id=1, source_target_pairs={{0,8},{1,9},{2,10},{3,11},{4,12},{5,13},{6,14},{7,15},{8,0},{9,1},... | collective-permute-start | bytes 1081352 | tf_op jit(solution)/shard_map/ppermute | solution.py:507
  737.3 11.1 %collective-permute-start.9 = (bf16[768,128]{1,0:T(8,128)(2,1)S(1)}, bf16[768,128]{1,0:T(8,128)(2,1)S(1)}, u32[]{:S(2)}, u32[]{:S(2)}) collective-permute-start(bf16[768,128]{1,0:T(8,128)(2,1)S(1)} %dynamic-slice_bitcast_fusion.10), channel_id=1, source_target_pairs={{0,16},{1,17},{2,18},{3,19},{4,20},{5,21},{6,22},{7,23},{8,24},{9,... | collective-permute-start | bytes 589832 | tf_op jit(solution)/shard_map/ppermute | solution.py:507
  747.8 7.9 %collective-permute-start.4 = (bf16[704,128]{1,0:T(8,128)(2,1)S(1)}, bf16[704,128]{1,0:T(8,128)(2,1)S(1)}, u32[]{:S(2)}, u32[]{:S(2)}) collective-permute-start(bf16[704,128]{1,0:T(8,128)(2,1)S(1)} %dynamic-slice_bitcast_fusion.11), channel_id=1, source_target_pairs={{0,16},{1,17},{2,18},{3,19},{4,20},{5,21},{6,22},{7,23},{8,24},{9,... | collective-permute-start | bytes 540680 | tf_op jit(solution)/shard_map/ppermute | solution.py:507
  (125 other events, 633.3 us)
Sparse Core Ops, SparseCore 0:
  11.6 77.7 all-gather.5
  92.4 60.9 all-gather.9
  156.9 55.0 all-gather.7
  215.4 61.4 all-gather.11
  280.3 55.9 all-gather.13

commit v2 on v1

--- a/solution.py
+++ b/solution.py
@@ -228,11 +228,12 @@
         TAPS2.append((pr * 2 + pc, dy, dx, kh * 3 + kw))
 
 
+FREE = pl.CostEstimate(flops=0, bytes_accessed=0, transcendentals=0)
 VMEM = pl.BlockSpec(memory_space=pltpu.VMEM)
 SMEM = pl.BlockSpec(memory_space=pltpu.SMEM)
 
 
-def call(kernel, outs, n_in, scratch=(), scalars=1, flops=0, moved=0):
+def call(kernel, outs, n_in, scratch=(), scalars=1):
     return pl.pallas_call(
         kernel,
         out_shape=outs,
@@ -240,7 +241,7 @@
         out_specs=[VMEM] * len(outs),
         scratch_shapes=list(scratch),
         compiler_params=pltpu.CompilerParams(vmem_limit_bytes=56 * 1024 * 1024),
-        cost_estimate=pl.CostEstimate(flops=flops, bytes_accessed=moved, transcendentals=0),
+        cost_estimate=FREE,
     )
 
 
@@ -439,24 +440,506 @@
     sums_ref[...] = ksums(a2, a2 * a2)
 
 
-def conv_backward(cnt, g1, t1, a2, s1, gb1, mask, w, a1, s0, gb0,
-                  d1_ref, g0_ref, sums_ref, moved_ref):
+def window_tables():
+    pixel = WINDOWS.reshape(12, 9, R)
+    table = np.zeros((160, R), np.float32)
+    for slot in range(12):
+        if slot % 4 < 3:
+            for t in range(9):
+                table[t * 16 + slot] = pixel[slot + 1, t]
+        table[144 + slot] = pixel[slot, 4]
+    spread = np.zeros((R, 16), np.float32)
+    spread[:, :12] = SPREAD
+    return table, np.concatenate([spread] * 3, axis=1)
+
+
+TABLE, SPREAD3 = window_tables()
+
+
+def phase_tables():
+    out = []
+    for side, pairs in zip(SIDES, (2, 1, 1)):
+        high = 2 * side
+        wide = 4 if side == 4 else 8
+        count = side * wide * pairs
+        t = np.zeros((4 * count, pairs * high * 16), np.float32)
+        for ph in range(4):
+            for p in range(pairs):
+                for i in range(side):
+                    for j in range(side):
+                        row = ph * count + (i * pairs + p) * wide + j
+                        at = (p * high + 2 * i + ph // 2) * 16 + 2 * j + ph % 2
+                        t[row, at] = 1.0
+        out.append(t)
+    return out
+
+
+PHASES = phase_tables()
+
+
+def split_phases(alive, xc, xm, xf, tc, tm, tf, out_ref, bc, bm, bf):
+    @pl.when(pl.program_id(0) == 0)
+    def _():
+        for b in (bc, bm, bf):
+            b[...] = jnp.zeros_like(b)
+
+    pieces = [[], [], [], []]
+    lanes = out_ref.shape[-1]
+    for g, (x, table, buf) in enumerate(((xc, tc, bc), (xm, tm, bm), (xf, tf, bf))):
+        pairs = buf.shape[0]
+        side = 2 * SIDES[g]
+        for f in range(0, FRAMES, pairs):
+            for p in range(pairs):
+                live = alive[g * FRAMES + f + p] > 0.0
+                buf[p, :, 0:side, :] = jnp.where(live, x[f + p], jnp.zeros_like(x[f + p]))
+            y = dot(table[...], buf[...].reshape(-1, lanes))
+            step = y.shape[0] // 4
+            for ph in range(4):
+                pieces[ph].append(y[ph * step : (ph + 1) * step])
+    for ph in range(4):
+        out_ref[ph] = jnp.concatenate(pieces[ph], axis=0).astype(BF16)
+
+
+def clip_blocks(lanes):
+    return [
+        pl.BlockSpec((FRAMES, 2 * s, 2 * s, lanes), lambda c: (0, 0, 0, c)) for s in SIDES
+    ]
+
+
+def image_blocks(lanes):
+    return [pl.BlockSpec((FRAMES, s, s, lanes), lambda c: (0, 0, 0, c)) for s in SIDES]
+
+
+def whole(v):
+    return pl.BlockSpec(v.shape, lambda c: (0,) * v.ndim)
+
+
+def column(rows, lanes):
+    return pl.BlockSpec((rows, lanes), lambda c: (0, c))
+
+
+LIMIT = pltpu.CompilerParams(vmem_limit_bytes=56 * 1024 * 1024)
+
+
+def run_split(alive, clips, tables):
+    lanes = 256
+    c_in = clips[0].shape[-1]
+    return pl.pallas_call(
+        split_phases,
+        grid=(c_in // lanes,),
+        out_shape=like((4, R, c_in), BF16),
+        in_specs=[SMEM] + clip_blocks(lanes) + [whole(t) for t in tables],
+        out_specs=pl.BlockSpec((4, R, lanes), lambda c: (0, 0, c)),
+        scratch_shapes=[
+            pltpu.VMEM((2 if s == 4 else 1, 2 * s, 16, lanes), BF16) for s in SIDES
+        ],
+        compiler_params=LIMIT,
+        cost_estimate=FREE,
+    )(alive, *clips, *tables)
+
+
+def input_grads(d0, d3, w1, wsk, mask, tc, tm, tf, oc, om, of):
+    lanes = oc.shape[-1]
     m = mask[...]
-    count = cnt[0]
-    st = kstats(s1[...], count, gb1[...])
-    tot = t1[...]
+    m = jnp.concatenate([m] * (lanes // 128), axis=1)
+    groups = []
+    for ph in range(4):
+        v = dot_nt(d0[ph], w1[...])
+        if ph == 0:
+            v = v + dot_nt(d3[...], wsk[...])
+        groups.append(m * v)
+    for g, (out, table) in enumerate(((oc, tc), (om, tm), (of, tf))):
+        pairs = 2 if g == 0 else 1
+        side = 2 * SIDES[g]
+        step = ROWS[g] // (FRAMES // pairs)
+        for f in range(0, FRAMES, pairs):
+            at = CUTS[g] + (f // pairs) * step
+            rows = jnp.concatenate([v[at : at + step] for v in groups], axis=0).astype(BF16)
+            y = dot(table[...], rows).reshape(pairs, side, 16, lanes)
+            for p in range(pairs):
+                out[f + p] = y[p, :, 0:side, :].astype(BF16)
+
+
+def run_input_grads(d0, d3, w1, wsk, mask, tables):
+    lanes = 256
+    c_in = w1.shape[0]
+    return pl.pallas_call(
+        input_grads,
+        grid=(c_in // lanes,),
+        out_shape=[like((FRAMES, 2 * s, 2 * s, c_in), BF16) for s in SIDES],
+        in_specs=[
+            whole(d0), whole(d3),
+            pl.BlockSpec((lanes, MID), lambda c: (c, 0)),
+            pl.BlockSpec((lanes, C_OUT), lambda c: (c, 0)),
+            whole(mask),
+        ] + [whole(t) for t in tables],
+        out_specs=clip_blocks(lanes),
+        compiler_params=LIMIT,
+        cost_estimate=FREE,
+    )(d0, d3, w1, wsk, mask, *tables)
+
+
+def first_grads(cnt, g0, t0, a1, s0, gb0, mask, xph, d0_ref, gr1_ref):
+    m = mask[...]
+    count = 4.0 * cnt[0]
+    st = kstats(s0[...], count, gb0[...])
+    tot = t0[...]
+    for ph in range(4):
+        for c in range(4):
+            sl = slice(c * 128, (c + 1) * 128)
+            stc = cols(st, c)
+            x, _ = normalize(a1[ph, :, sl], stc)
+            d = norm_back(g0[ph, :, sl], x, m, stc, (tot[0:1, sl], tot[1:2, sl]), count)
+            d0_ref[ph, :, sl] = d.astype(BF16)
+    c_in = xph.shape[-1]
+    gr1_ref[...] = dot_tn(
+        xph[...].reshape(4 * R, c_in), d0_ref[...].reshape(4 * R, MID)
+    ).astype(BF16)
+
+
+def last_norm(cnt, b3, y1, s6, gb6, mask, cc, cm, cf, oc, om, of, g6_ref, sums_ref, bc, bm, bf):
+    @pl.when(pl.program_id(0) == 0)
+    def _():
+        for b in (bc, bm, bf):
+            b[...] = jnp.zeros_like(b)
+
+    lanes = g6_ref.shape[-1]
+    for f in range(FRAMES):
+        p = f % 2
+        bc[f // 2, :, p * 4 : p * 4 + 4, :] = cc[f].astype(F32)
+    bm[:, :, 0:6, :] = cm[...].astype(F32)
+    bf[:, :, 0:7, :] = cf[...].astype(F32)
+    cot = join((bc[...], bm[...], bf[...]))
+    m = mask[...]
+    m = jnp.concatenate([m] * (lanes // 128), axis=1)
+    x, u = normalize(b3[...], kstats(s6[...], cnt[0], gb6[...]))
+    u = u + y1[...]
+    s = jax.nn.sigmoid(u)
+    pc, pm, pf = split(m * u * s)
+    for f in range(FRAMES):
+        p = f % 2
+        oc[f] = pc[f // 2, :, p * 4 : p * 4 + 4, :].astype(BF16)
+    om[...] = pm[:, :, 0:6, :].astype(BF16)
+    of[...] = pf[:, :, 0:7, :].astype(BF16)
+    g = cot * m * (s * (1.0 + u * (1.0 - s)))
+    g6_ref[...] = g
+    sums_ref[...] = ksums(g * x, g)
+
+
+def run_last_norm(cnt, b3, y1, s6, gb6, mask, cots):
+    lanes = 256
+    return pl.pallas_call(
+        last_norm,
+        grid=(C_OUT // lanes,),
+        out_shape=[like((FRAMES, s, s, C_OUT), BF16) for s in SIDES]
+        + [like((R, C_OUT)), like((2, C_OUT))],
+        in_specs=[SMEM, column(R, lanes), column(R, lanes), column(2, lanes), column(2, lanes),
+                  whole(mask)] + image_blocks(lanes),
+        out_specs=image_blocks(lanes) + [column(R, lanes), column(2, lanes)],
+        scratch_shapes=[
+            pltpu.VMEM((2 if s == 4 else 4, s, 8, lanes), F32) for s in SIDES
+        ],
+        compiler_params=LIMIT,
+        cost_estimate=FREE,
+    )(cnt, b3, y1, s6, gb6, mask, *cots)
+
+
+def joint_norm(cnt, a3, ap, s2, s3, gb2, gb3, mask, w2, y1_ref, yl_ref, b1_ref, sums_ref):
+    lanes = y1_ref.shape[-1]
+    m = mask[...]
+    m = jnp.concatenate([m] * (lanes // 128), axis=1)
+    _, u2 = normalize(a3[...], kstats(s2[...], cnt[0], gb2[...]))
+    _, u3 = normalize(ap[...], kstats(s3[...], cnt[0], gb3[...]))
+    y = m * silu(u2 + u3)
+    y1_ref[...] = y
+    low = y.astype(BF16)
+    yl_ref[...] = low
+    part = dot(low, w2[...])
+    step = pl.program_id(0)
+
+    @pl.when(step == 0)
+    def _():
+        b1_ref[...] = part
+
+    @pl.when(step > 0)
+    def _():
+        b1_ref[...] = b1_ref[...] + part
+
+    @pl.when(step == pl.num_programs(0) - 1)
+    def _():
+        b = b1_ref[...]
+        sums_ref[...] = ksums(b, b * b)
+
+
+def run_joint_norm(cnt, a3, ap, s2, s3, gb2, gb3, mask, w2):
+    lanes = 512
+    wide = column(R, lanes)
+    pair = column(2, lanes)
+    return pl.pallas_call(
+        joint_norm,
+        grid=(C_OUT // lanes,),
+        out_shape=[like((R, C_OUT)), like((R, C_OUT), BF16), like((R, MID)), like((2, MID))],
+        in_specs=[SMEM, wide, wide, pair, pair, pair, pair, whole(mask),
+                  pl.BlockSpec((lanes, MID), lambda c: (c, 0))],
+        out_specs=[wide, wide, pl.BlockSpec((R, MID), lambda c: (0, 0)),
+                   pl.BlockSpec((2, MID), lambda c: (0, 0))],
+        compiler_params=LIMIT,
+        cost_estimate=FREE,
+    )(cnt, a3, ap, s2, s3, gb2, gb3, mask, w2)
+
+
+def wide_grid(kernel, outs, out_specs, ins, in_specs, scratch=(), steps=4):
+    return pl.pallas_call(
+        kernel,
+        grid=(steps,),
+        out_shape=outs,
+        in_specs=in_specs,
+        out_specs=out_specs,
+        scratch_shapes=list(scratch),
+        compiler_params=LIMIT,
+        cost_estimate=FREE,
+    )(*ins)
+
+
+def fixed(shape):
+    return pl.BlockSpec(shape, lambda c: (0,) * len(shape))
+
+
+def row_block(rows, width):
+    return pl.BlockSpec((rows, width), lambda c: (c, 0))
+
+
+def first_step(fn):
+    pl.when(pl.program_id(0) == 0)(fn)
+
+
+def last_step(fn):
+    pl.when(pl.program_id(0) == pl.num_programs(0) - 1)(fn)
+
+
+def accumulate(ref, part):
+    first = pl.program_id(0) == 0
+
+    @pl.when(first)
+    def _():
+        ref[...] = part
+
+    @pl.when(jnp.logical_not(first))
+    def _():
+        ref[...] = ref[...] + part
+
+
+def tiled(m, lanes):
+    return jnp.concatenate([m] * (lanes // 128), axis=1)
+
+
+def enter(x, w, a1_ref, sums_ref):
+    a = dot(x[0], w[...])
+    a1_ref[0] = a
+    accumulate(sums_ref, ksums(a, a * a))
+
+
+def run_enter(xph, w1):
+    c_in = xph.shape[-1]
+    return wide_grid(
+        enter,
+        [like((4, R, MID)), like((2, MID))],
+        [pl.BlockSpec((1, R, MID), lambda c: (c, 0, 0)), fixed((2, MID))],
+        (xph, w1),
+        [pl.BlockSpec((1, R, c_in), lambda c: (c, 0, 0)), fixed((c_in, MID))],
+    )
+
+
+def expand_pair(cnt, a2, s1, gb1, mask, w, x, wsk, h_ref, a3_ref, ap_ref, s2_ref, s3_ref):
+    @first_step
+    def _():
+        m = tiled(mask[...], MID)
+        h = m * silu(normalize(a2[...], kstats(s1[...], cnt[0], gb1[...]))[1])
+        h_ref[...] = h.astype(BF16)
+
+    a = dot(h_ref[...], w[...])
+    a3_ref[...] = a
+    s2_ref[...] = ksums(a, a * a)
+    a = dot(x[0], wsk[...])
+    ap_ref[...] = a
+    s3_ref[...] = ksums(a, a * a)
+
+
+def run_expand_pair(cnt, a2, s1, gb1, mask, we1, xph, wsk):
+    c_in = xph.shape[-1]
+    wide, pair = column(R, MID), column(2, MID)
+    return wide_grid(
+        expand_pair,
+        [like((R, MID), BF16), like((R, C_OUT)), like((R, C_OUT)), like((2, C_OUT)), like((2, C_OUT))],
+        [fixed((R, MID)), wide, wide, pair, pair],
+        (cnt, a2, s1, gb1, mask, we1, xph, wsk),
+        [SMEM, fixed((R, MID)), fixed((2, MID)), fixed((2, MID)), fixed((R, 128)), column(MID, MID),
+         pl.BlockSpec((1, R, c_in), lambda c: (0, 0, 0)), column(c_in, MID)],
+    )
+
+
+def expand_last(cnt, mixed, s5, gb5, mask, w, h_ref, b3_ref, s6_ref):
+    @first_step
+    def _():
+        m = tiled(mask[...], MID)
+        h = m * silu(normalize(mixed[...], kstats(s5[...], cnt[0], gb5[...]))[1])
+        h_ref[...] = h.astype(BF16)
+
+    a = dot(h_ref[...], w[...])
+    b3_ref[...] = a
+    s6_ref[...] = ksums(a, a * a)
+
+
+def run_expand_last(cnt, mixed, s5, gb5, mask, we2):
+    wide, pair = column(R, MID), column(2, MID)
+    return wide_grid(
+        expand_last,
+        [like((R, MID), BF16), like((R, C_OUT)), like((2, C_OUT))],
+        [fixed((R, MID)), wide, pair],
+        (cnt, mixed, s5, gb5, mask, we2),
+        [SMEM, fixed((R, MID)), fixed((2, MID)), fixed((2, MID)), fixed((R, 128)), column(MID, MID)],
+    )
+
+
+def last_back(cnt, g6, b3, t6, s6, gb6, mask, w, we2, mixed, s5, gb5, ge2_ref, g5_ref, p5_ref):
+    m = tiled(mask[...], MID)
+    st = kstats(s6[...], cnt[0], gb6[...])
+    x, _ = normalize(b3[...], st)
+    tot = t6[...]
+    d = norm_back(g6[...], x, m, st, (tot[0:1], tot[1:2]), cnt[0]).astype(BF16)
+    ge2_ref[...] = dot_tn(w[...], d).astype(BF16)
+    accumulate(g5_ref, dot_nt(d, we2[...]))
+
+    @last_step
+    def _():
+        x5, u5 = normalize(mixed[...], kstats(s5[...], cnt[0], gb5[...]))
+        g = g5_ref[...] * m * silu_grad(u5)
+        g5_ref[...] = g
+        p5_ref[...] = ksums(g * x5, g)
+
+
+def run_last_back(cnt, g6, b3, t6, s6, gb6, mask, w, we2, mixed, s5, gb5):
+    wide, pair = column(R, MID), column(2, MID)
+    one, two = fixed((R, MID)), fixed((2, MID))
+    return wide_grid(
+        last_back,
+        [like((MID, C_OUT), BF16), like((R, MID)), like((2, MID))],
+        [column(MID, MID), one, two],
+        (cnt, g6, b3, t6, s6, gb6, mask, w, we2, mixed, s5, gb5),
+        [SMEM, wide, wide, pair, pair, pair, fixed((R, 128)), one, column(MID, MID), one, two, two],
+    )
+
+
+def joint_back(cnt, g4, t4, b1, s4, gb4, mask, yl, w2, g6, a3, ap, s2, s3, gb2, gb3,
+               gr2_ref, gj_ref, pj_ref, d4_ref):
+    m = tiled(mask[...], MID)
+
+    @first_step
+    def _():
+        st = kstats(s4[...], cnt[0], gb4[...])
+        x, _ = normalize(b1[...], st)
+        tot = t4[...]
+        d4_ref[...] = norm_back(g4[...], x, m, st, (tot[0:1], tot[1:2]), cnt[0]).astype(BF16)
+
+    d = d4_ref[...]
+    gr2_ref[...] = dot_tn(yl[...], d).astype(BF16)
+    gy = g6[...] + dot_nt(d, w2[...])
+    x2, u2 = normalize(a3[...], kstats(s2[...], cnt[0], gb2[...]))
+    x3, u3 = normalize(ap[...], kstats(s3[...], cnt[0], gb3[...]))
+    g = gy * m * silu_grad(u2 + u3)
+    gj_ref[...] = g
+    pj_ref[...] = jnp.concatenate(
+        [jnp.sum(v, axis=0, keepdims=True) for v in (g * x2, g * x3, g)], axis=0
+    )
+
+
+def run_joint_back(cnt, g4, t4, b1, s4, gb4, mask, yl, w2, g6, a3, ap, s2, s3, gb2, gb3):
+    wide, pair = column(R, MID), column(2, MID)
+    one, two = fixed((R, MID)), fixed((2, MID))
+    return wide_grid(
+        joint_back,
+        [like((C_OUT, MID), BF16), like((R, C_OUT)), like((3, C_OUT))],
+        [row_block(MID, MID), wide, column(3, MID)],
+        (cnt, g4, t4, b1, s4, gb4, mask, yl, w2, g6, a3, ap, s2, s3, gb2, gb3),
+        [SMEM, one, two, one, two, two, fixed((R, 128)), wide, row_block(MID, MID), wide, wide, wide,
+         pair, pair, pair, pair],
+        [pltpu.VMEM((R, MID), BF16)],
+    )
+
+
+def expand_back(cnt, gj, tj, a3, ap, s2, s3, gb2, gb3, mask, h2, xph, we1, a2, s1, gb1,
+                ge1_ref, gsk_ref, d3_ref, g1_ref, p1_ref):
+    m = tiled(mask[...], MID)
+    g = gj[...]
+    tot = tj[...]
+    st = kstats(s2[...], cnt[0], gb2[...])
+    x, _ = normalize(a3[...], st)
+    d = norm_back(g, x, m, st, (tot[0:1], tot[2:3]), cnt[0]).astype(BF16)
+    ge1_ref[...] = dot_tn(h2[...], d).astype(BF16)
+    accumulate(g1_ref, dot_nt(d, we1[...]))
+    st = kstats(s3[...], cnt[0], gb3[...])
+    x, _ = normalize(ap[...], st)
+    d = norm_back(g, x, m, st, (tot[1:2], tot[2:3]), cnt[0]).astype(BF16)
+    d3_ref[...] = d
+    gsk_ref[...] = dot_tn(xph[0], d).astype(BF16)
+
+    @last_step
+    def _():
+        x1, u1 = normalize(a2[...], kstats(s1[...], cnt[0], gb1[...]))
+        g = g1_ref[...] * m * silu_grad(u1)
+        g1_ref[...] = g
+        p1_ref[...] = ksums(g * x1, g)
+
+
+def run_expand_back(cnt, gj, tj, a3, ap, s2, s3, gb2, gb3, mask, h2, xph, we1, a2, s1, gb1):
+    wide, pair = column(R, MID), column(2, MID)
+    one, two = fixed((R, MID)), fixed((2, MID))
+    c_in = xph.shape[-1]
+    return wide_grid(
+        expand_back,
+        [like((MID, C_OUT), BF16), like((c_in, C_OUT), BF16), like((R, C_OUT), BF16), like((R, MID)),
+         like((2, MID))],
+        [column(MID, MID), column(c_in, MID), wide, one, two],
+        (cnt, gj, tj, a3, ap, s2, s3, gb2, gb3, mask, h2, xph, we1, a2, s1, gb1),
+        [SMEM, wide, column(3, MID), wide, wide, pair, pair, pair, pair, fixed((R, 128)), one,
+         pl.BlockSpec((1, R, c_in), lambda c: (0, 0, 0)), column(MID, MID), one, two, two],
+    )
+
+
+def spatial_grad(cnt, g1, t1, a2, s1, gb1, mask, im, d1_ref, gsp_ref):
+    @first_step
+    def _():
+        m = tiled(mask[...], MID)
+        st = kstats(s1[...], cnt[0], gb1[...])
+        x, _ = normalize(a2[...], st)
+        tot = t1[...]
+        d1_ref[...] = norm_back(g1[...], x, m, st, (tot[0:1], tot[1:2]), cnt[0]).astype(BF16)
+
+    gsp_ref[...] = dot_tn(im[...], d1_ref[...]).astype(BF16)
+
+
+def run_spatial_grad(cnt, g1, t1, a2, s1, gb1, mask, im):
+    one, two = fixed((R, MID)), fixed((2, MID))
+    return wide_grid(
+        spatial_grad,
+        [like((R, MID), BF16), like((9 * MID, MID), BF16)],
+        [one, row_block(MID, MID)],
+        (cnt, g1, t1, a2, s1, gb1, mask, im),
+        [SMEM, one, two, one, two, two, fixed((R, 128)), column(R, MID)],
+        steps=9,
+    )
+
+
+def conv_back(cnt, d1, mask, w, a1, s0, gb0, g0_ref, sums_ref, moved_ref):
+    m = mask[...]
     for c in range(4):
         sl = slice(c * 128, (c + 1) * 128)
-        stc = cols(st, c)
-        x, _ = normalize(a2[:, sl], stc)
-        d = norm_back(g1[:, sl], x, m, stc, (tot[0:1, sl], tot[1:2, sl]), count).astype(BF16)
-        d1_ref[:, sl] = d
-        d = d.astype(F32)
+        d = d1[:, sl].astype(F32)
         for dx in (0, 1):
             moved = kshift_cols(d, dx)
             for dy in (0, 1):
                 moved_ref[dy * 2 + dx, :, sl] = shift_rows(moved, dy).astype(BF16)
-    st = kstats(s0[...], 4.0 * count, gb0[...])
+    st = kstats(s0[...], 4.0 * cnt[0], gb0[...])
     sums = jnp.zeros((2, MID), F32)
     for ph in range(4):
         gh = None
@@ -475,92 +958,271 @@
     sums_ref[...] = sums
 
 
-def window_tables():
-    pixel = WINDOWS.reshape(12, 9, R)
-    table = np.zeros((160, R), np.float32)
-    for slot in range(12):
-        if slot % 4 < 3:
-            for t in range(9):
-                table[t * 16 + slot] = pixel[slot + 1, t]
-        table[144 + slot] = pixel[slot, 4]
-    spread = np.zeros((R, 16), np.float32)
-    spread[:, :12] = SPREAD
-    return table, np.concatenate([spread] * 3, axis=1)
-
-
-TABLE, SPREAD3 = window_tables()
-
-
-def scatter_sum(grads, n, mesh_bits):
-    sizes = [g.shape[1] for g in grads]
-    x = jnp.concatenate([g.astype(BF16) for g in grads], axis=1)
-    x = jnp.pad(x, ((0, 0), (0, -x.shape[1] % 1024)))
-    x = x.reshape((2,) * (n.bit_length() - 1) + (-1, 128))
-    me = lax.axis_index(AXES)
+def tie(*arrays):
+    return lax.optimization_barrier(arrays)
+
+
+def axes_bits(n, fsdp):
     bits = n.bit_length() - 1
-    left = list(range(bits))
-    for b in mesh_bits:
-        axis = left.index(bits - 1 - b)
-        mine = (me >> b) & 1
-        keep = lax.dynamic_index_in_dim(x, mine, axis, keepdims=False)
-        send = lax.dynamic_index_in_dim(x, 1 - mine, axis, keepdims=False)
-        got = lax.ppermute(send, AXES, [(i, i ^ (1 << b)) for i in range(n)])
-        total = keep.astype(F32) + got.astype(F32)
-        left.pop(axis)
-        x = total if b == mesh_bits[-1] else total.astype(BF16)
-    flat = x.reshape(-1)
+    core = fsdp.bit_length() - 1
+    return list(range(core)), core, core + 1, list(range(core + 2, bits))
+
+
+def swap(v, d, n):
+    return lax.ppermute(v, AXES, [(i, i ^ d) for i in range(n)])
+
+
+def allsum_wide(vectors, n, fsdp):
+    near, core, mid, far = axes_bits(n, fsdp)
+    flat = jnp.concatenate([v.reshape(-1) for v in vectors])
+    size = flat.shape[0]
+    flat = jnp.pad(flat, (0, -size % 1024)).reshape(-1, 128)
+    bits = near + [mid] + far
+    rounds = [[core]] + [bits[i : i + 2] for i in range(0, len(bits), 2)]
+    for r in rounds:
+        got = [
+            swap(flat, sum(1 << b for j, b in enumerate(r) if m >> j & 1), n)
+            for m in range(1, 1 << len(r))
+        ]
+        flat = sum(got, flat)
+    flat = flat.reshape(-1)
     out = []
     at = 0
-    for s in sizes:
-        out.append(flat[at : at + s])
-        at += s
+    for v in vectors:
+        out.append(flat[at : at + v.size].reshape(v.shape))
+        at += v.size
     return out
+
+
+def rows16(v):
+    return jnp.pad(v, ((0, 0),) * (v.ndim - 2) + ((0, -v.shape[-2] % 16), (0, 0)))
+
+
+def place_blocks(n, orders, core, heights, width):
+    part = width // len(orders)
+
+    def kernel(me_ref, *refs):
+        srcs = refs[: 2 * len(orders)]
+        outs = refs[2 * len(orders) : -1]
+        sem = refs[-1]
+        me = me_ref[0]
+        for rel in range(n):
+            for k, order in enumerate(orders):
+                at = sum((rel >> b & 1) << j for j, b in enumerate(order))
+                src = srcs[2 * k + (rel >> core & 1)]
+                row = 0
+                for i, (h, out) in enumerate(zip(heights, outs)):
+                    pltpu.make_async_copy(
+                        src.at[at, pl.ds(row, h)],
+                        out.at[me ^ rel, :, pl.ds(k * part, part)],
+                        sem.at[i],
+                    ).start()
+                    row += h
+        for i, out in enumerate(outs):
+            pltpu.make_async_copy(out, out, sem.at[i]).wait()
+
+    return pl.pallas_call(
+        kernel,
+        out_shape=[jax.ShapeDtypeStruct((n, h, width), BF16) for h in heights],
+        in_specs=[SMEM] + [pl.BlockSpec(memory_space=pl.ANY)] * (2 * len(orders)),
+        out_specs=[VMEM] * len(heights),
+        scratch_shapes=[pltpu.SemaphoreType.DMA((len(heights),))],
+        compiler_params=LIMIT,
+        cost_estimate=FREE,
+    )
+
+
+class Gather:
+    def __init__(self, shards, n, fsdp):
+        self.n = n
+        self.near, self.core, self.mid, self.far = axes_bits(n, fsdp)
+        self.shards = shards
+        padded = [rows16(v.astype(BF16)) for v in shards]
+        self.heights = [v.shape[0] for v in padded]
+        self.x = jnp.concatenate(padded, axis=0) if len(padded) > 1 else padded[0]
+
+    def first(self):
+        got = []
+        for m in range(1, 1 << len(self.far)):
+            got.append(swap(self.x, sum(1 << b for j, b in enumerate(self.far) if m >> j & 1), self.n))
+        self.hops = [self.x] + got
+
+    def second(self):
+        n = self.n
+        bits = self.near + [self.mid]
+        v = jnp.stack(self.hops)
+        got = [v]
+        for m in range(1, 1 << len(bits)):
+            got.append(swap(v, sum(1 << b for j, b in enumerate(bits) if m >> j & 1), n))
+        self.planes = [jnp.concatenate(got, axis=0)]
+        self.orders = [self.far + bits]
+
+    def split(self):
+        width = self.x.shape[1]
+        bits = self.near + [self.mid]
+        self.paths = [bits, bits[::-1]]
+        self.orders = [self.far + path for path in self.paths]
+        v = jnp.stack(self.hops)
+        self.planes = [v[..., : width // 2], v[..., width // 2 :]]
+
+    def hop(self, k):
+        self.got = [swap(v, 1 << p[k], self.n) for v, p in zip(self.planes, self.paths)]
+
+    def land(self):
+        self.planes = [jnp.concatenate([v, g], axis=0) for v, g in zip(self.planes, self.got)]
+
+    def third(self):
+        self.other = [swap(v, 1 << self.core, self.n) for v in self.planes]
+
+    def finish(self, me):
+        width = self.x.shape[1]
+        planes = [v for pair in zip(self.planes, self.other) for v in pair]
+        outs = place_blocks(self.n, self.orders, self.core, self.heights, width)(me, *planes)
+        return [
+            o.reshape(self.n * h, width)
+            if h == v.shape[0]
+            else o[:, : v.shape[0]].reshape(-1, width)
+            for o, h, v in zip(outs, self.heights, self.shards)
+        ]
+
+
+def order_blocks(n, orders, pieces, width, arrays):
+    heights = [arrays[i].shape[1] for i, _ in pieces]
+    total = sum(heights)
+    half = width // 2
+
+    def kernel(me_ref, *refs):
+        srcs = refs[: len(arrays)]
+        outs = refs[len(arrays) : len(arrays) + 2]
+        sem = refs[-1]
+        me = me_ref[0]
+        for rel in range(n):
+            for k, order in enumerate(orders):
+                at = 0
+                for b in order:
+                    at = at * 2 + (rel >> b & 1)
+                side = at * 2 // n
+                row = 0
+                for (i, col), h in zip(pieces, heights):
+                    pltpu.make_async_copy(
+                        srcs[i].at[me ^ rel, :, pl.ds(col + k * half, half)],
+                        outs[side].at[k, at % (n // 2), pl.ds(row, h)],
+                        sem.at[side],
+                    ).start()
+                    row += h
+        for k, out in enumerate(outs):
+            pltpu.make_async_copy(out, out, sem.at[k]).wait()
+
+    return pl.pallas_call(
+        kernel,
+        out_shape=[jax.ShapeDtypeStruct((2, n // 2, total, half), BF16)] * 2,
+        in_specs=[SMEM] + [pl.BlockSpec(memory_space=pl.ANY)] * len(arrays),
+        out_specs=[VMEM] * 2,
+        scratch_shapes=[pltpu.SemaphoreType.DMA((2,))],
+        compiler_params=LIMIT,
+        cost_estimate=FREE,
+    )
+
+
+def add_blocks(keep, got, joined):
+    m, rows, half = keep[0].shape[-3:]
+    k_in = len(keep)
+
+    def kernel(*refs):
+        ins, outs = refs[: 2 * k_in], refs[2 * k_in :]
+
+        def total(k, i):
+            if k_in == 1:
+                return ins[0][k, i].astype(F32) + ins[1][k, i].astype(F32)
+            return ins[k][i].astype(F32) + ins[2 + k][i].astype(F32)
+
+        if m == 1:
+            for k in range(2):
+                outs[0][:, k * half : (k + 1) * half] = total(k, 0)
+            return
+
+        @pl.loop(0, m // 2)
+        def _(i):
+            for k in range(2):
+                for side in range(2):
+                    v = total(k, i + side * (m // 2)).astype(BF16)
+                    if joined:
+                        outs[side][k, i] = v
+                    else:
+                        outs[2 * side + k][i] = v
+
+    if m == 1:
+        outs = [like((rows, 2 * half))]
+    elif joined:
+        outs = [like((2, m // 2, rows, half), BF16)] * 2
+    else:
+        outs = [like((m // 2, rows, half), BF16)] * 4
+    return call(kernel, outs, 2 * k_in, scalars=0)(*keep, *got)
+
+
+class Scatter:
+    def __init__(self, me, arrays, pieces, width, n, fsdp):
+        self.n = n
+        near, core, mid, self.far = axes_bits(n, fsdp)
+        bits = near + [mid]
+        self.paths = [bits, bits[::-1]]
+        self.heights = [arrays[i].shape[1] for i, _ in pieces]
+        orders = [[core] + path + self.far for path in self.paths]
+        send, keep = order_blocks(n, orders, pieces, width, arrays)(me, *arrays)[::-1]
+        self.send, self.keep = [send], [keep]
+        self.hops = [[core]] + list(zip(*self.paths)) + [[b] for b in self.far]
+        self.at = 0
+
+    def start(self):
+        self.got = [swap(v, 1 << b, self.n) for v, b in zip(self.send, self.hops[self.at])]
+        self.at += 1
+
+    def add(self):
+        after = self.hops[self.at : self.at + 1]
+        got = add_blocks(self.keep, self.got, bool(after) and len(after[0]) == 1)
+        if not after:
+            self.total = got[0]
+        else:
+            k = len(got) // 2
+            self.keep, self.send = got[:k], got[k:]
+
+    def end(self, x):
+        x, *self.got = tie(x, *self.got)
+        return x
+
+    def ready(self, x):
+        x, *self.send = tie(x, *self.send)
+        self.start()
+        return x
+
+    def rest(self):
+        self.add()
+        while self.at < len(self.hops):
+            self.start()
+            self.add()
+        out = []
+        at = 0
+        for h in self.heights:
+            out.append(self.total[at : at + h])
+            at += h
+        return out
 
 
 def body(n, fsdp, *args):
     (coarse, medium, fine, clip_counts, frame_counts, reduce_one, spatial_one, expand_one,
      shortcut_one, reduce_two, excite_down, excite_up, temporal_mix, expand_two, norm_params,
      motion_kernel, cot_c, cot_m, cot_f) = args
-    bits = n.bit_length() - 1
-    core = fsdp.bit_length() - 1
-    order = [core] + [b for b in range(bits) if b != core]
+    near, core, mid, far = axes_bits(n, fsdp)
 
     def gather(w):
         return lax.all_gather(w.astype(BF16), AXES, axis=0, tiled=True)
 
-    def pack(ws):
-        flat = jnp.concatenate([w.astype(BF16).reshape(-1) for w in ws])
-        return jnp.pad(flat, (0, -flat.size % 1024)).reshape(-1, 128)
-
-    def unpack(got, ws):
-        flat = got.reshape(n, -1)
-        out = []
-        at = 0
-        for w in ws:
-            out.append(flat[:, at : at + w.size].reshape((n,) + w.shape))
-            at += w.size
-        return out
-
-    early = (reduce_one, norm_params)
-    packed = pack(early)
-    got = lax.all_to_all(
-        jnp.broadcast_to(packed[None], (n,) + packed.shape), AXES, 0, 0, tiled=True
-    )
-    w1, norms = unpack(got, early)
-    w1 = w1.reshape(-1, MID)
-    norms = norms.transpose(1, 0, 2).reshape(2, -1).astype(F32)
-    wsp = gather(spatial_one)
-    wsk = gather(shortcut_one)
-    we1 = gather(expand_one)
-    w2 = gather(reduce_two)
-    narrow = (excite_down, excite_up, temporal_mix)
-    wdown, wup, wmix = unpack(gather(pack(narrow)), narrow)
-    wdown = wdown.reshape(MID, SQUEEZE)
-    wup = wup.transpose(1, 0, 2).reshape(SQUEEZE, MID).astype(F32)
-    wmix = wmix.transpose(1, 0, 2).reshape(3, 9 * GROUP, GROUP)
-    we2 = gather(expand_two)
-    edges = [0, 512, 1024, 3072, 5120, 5632, 6144, 8192]
-    gb = [norms[:, edges[k] : edges[k + 1]] for k in range(7)]
+    def flat(w):
+        v = w.reshape(-1)
+        return jnp.pad(v, (0, -v.size % MID)).reshape(-1, MID)
+
+    def flat_back(got, w):
+        return got.reshape(n, -1)[:, : w.size].reshape((n,) + w.shape)
 
     alive = (jnp.arange(4)[None, :] < frame_counts[0][:, None]) & (clip_counts[0][:, None] > 0)
     alive = alive.astype(F32)
@@ -571,46 +1233,88 @@
     per_group = jnp.sum(alive, axis=1)
     local_out = jnp.sum(per_group * jnp.array([16.0, 36.0, 49.0], F32))
 
-    clips = [
-        x * alive[g].astype(BF16)[:, None, None, None]
-        for g, x in enumerate((coarse, medium, fine))
-    ]
-    xph = [to_rows(clips, ph) for ph in range(4)]
-    cot = to_rows((cot_c, cot_m, cot_f), None).astype(F32)
-
-    a1 = [dot(x, w1) for x in xph]
-    s0 = sum(sums_of(a) for a in a1)
-    ap = dot(xph[0], wsk)
-    s3 = sums_of(ap)
-    s0, count_out = allsum((s0, local_out.reshape(1)), n)
-    count_out = count_out[0]
-    count_in = 4.0 * count_out
-    st0 = norm_rows(s0, count_in, gb[0])
-    cnt = count_out.reshape(1)
+    tables = [jnp.asarray(t, BF16) for t in PHASES]
+    tables_t = [jnp.asarray(t.T, BF16) for t in PHASES]
+    clips = [coarse, medium, fine]
+
     m128 = jnp.broadcast_to(mask, (R, 128))
     valid = jnp.asarray(np.broadcast_to(VALID[:, None], (R, MID)).astype(np.float32))
-    a1 = jnp.stack(a1)
+    scale = later_slots / jnp.asarray(NPIX)
+    scale = jnp.broadcast_to(jnp.pad(scale, (0, 4))[:, None], (16, SQUEEZE))
+    table = jnp.asarray(TABLE, BF16)
+    table_t = jnp.asarray(TABLE.T, BF16)
+    spread = jnp.asarray(SPREAD3, BF16)
+    me = lax.axis_index(AXES).astype(jnp.int32).reshape(1)
+    ga = Gather([reduce_one, flat(norm_params)], n, fsdp)
+    gb_ = Gather([spatial_one], n, fsdp)
+    gc_ = Gather([shortcut_one, expand_one], n, fsdp)
+    narrow = [reduce_two, flat(excite_down), flat(excite_up), flat(temporal_mix)]
+    rows = [v.shape[0] for v in narrow]
+    narrow = jnp.concatenate(narrow, axis=0)
+    got = gather(jnp.pad(narrow, ((0, -narrow.shape[0] % 16), (0, 0))))
+    we2 = gather(expand_two)
+    ga.first()
+    *ga.hops, gb_.x, clips[0], clips[1], clips[2] = tie(*ga.hops, gb_.x, *clips)
+    ga.second()
+    gb_.first()
+    xph = run_split(alive_slots, clips, tables)
+    ga.planes[0], xph = tie(ga.planes[0], xph)
+    ga.third()
+    w1, norms = ga.finish(me)
+    norms = flat_back(norms, norm_params).transpose(1, 0, 2).reshape(2, -1).astype(F32)
+    edges = [0, 512, 1024, 3072, 5120, 5632, 6144, 8192]
+    gb = [norms[:, edges[k] : edges[k + 1]] for k in range(7)]
+
+    w1, gc_.x, *gb_.hops = tie(w1, gc_.x, *gb_.hops)
+    gb_.split()
+    w1, *gb_.planes = tie(w1, *gb_.planes)
+    gb_.hop(0)
+    gc_.first()
+    a1, p0 = run_enter(xph, w1)
+    for k in range(1, len(gb_.paths[0])):
+        p0, *gb_.got = tie(p0, *gb_.got)
+        gb_.land()
+        p0, *gb_.planes = tie(p0, *gb_.planes)
+        gb_.hop(k)
+    s0, count_out = allsum((p0, local_out.reshape(1)), n)
+    cnt = count_out.reshape(1)
+    s0, *rest = tie(s0, *gb_.got, *gc_.hops)
+    gb_.got, gc_.hops = rest[:2], rest[2:]
+    gb_.land()
+    gb_.third()
+    gc_.split()
+    gc_.hop(0)
+    wsp, = gb_.finish(me)
     im, a2, p1 = call(
         conv_forward,
         [like((R, 9 * MID), BF16), like((R, MID)), like((2, MID))],
         6,
     )(cnt, a1, s0, gb[0], m128, valid, wsp)
+    for k in range(1, len(gc_.paths[0])):
+        p1, *gc_.got = tie(p1, *gc_.got)
+        gc_.land()
+        p1, *gc_.planes = tie(p1, *gc_.planes)
+        gc_.hop(k)
     s1, = allsum((p1,), n)
-    st1 = norm_rows(s1, count_out, gb[1])
-    h2 = (mask * silu(normalize(a2, st1)[1])).astype(BF16)
-    a3 = dot(h2, we1)
-    s2, s3 = allsum((sums_of(a3), s3), n)
-    st2 = norm_rows(s2, count_out, gb[2])
-    st3 = norm_rows(s3, count_out, gb[3])
-    y1 = mask * silu(normalize(a3, st2)[1] + normalize(ap, st3)[1])
-    y1_low = y1.astype(BF16)
-    b1 = dot(y1_low, w2)
-    s4, = allsum((sums_of(b1),), n)
-    st4 = norm_rows(s4, count_out, gb[4])
-    scale = later_slots / jnp.asarray(NPIX)
-    scale = jnp.broadcast_to(jnp.pad(scale, (0, 4))[:, None], (16, SQUEEZE))
-    table = jnp.asarray(TABLE, BF16)
-    spread = jnp.asarray(SPREAD3, BF16)
+    s1, *gc_.got = tie(s1, *gc_.got)
+    gc_.land()
+    gc_.third()
+    wsk, we1 = gc_.finish(me)
+    got = got.reshape(n, -1, MID)
+    w2 = got[:, : rows[0]].reshape(C_OUT, MID)
+    at = rows[0]
+    wdown = flat_back(got[:, at : at + rows[1]], excite_down).reshape(MID, SQUEEZE)
+    at += rows[1]
+    wup = flat_back(got[:, at : at + rows[2]], excite_up)
+    wup = wup.transpose(1, 0, 2).reshape(SQUEEZE, MID).astype(F32)
+    at += rows[2]
+    wmix = flat_back(got[:, at : at + rows[3]], temporal_mix)
+    wmix = wmix.transpose(1, 0, 2).reshape(3, 9 * GROUP, GROUP)
+    wmix_t = wmix.reshape(3, 9, GROUP, GROUP).transpose(0, 1, 3, 2).reshape(3, 9 * GROUP, GROUP)
+    h2, a3, ap, p2, p3 = run_expand_pair(cnt, a2, s1, gb[1], m128, we1, xph, wsk)
+    s2, s3 = allsum_wide((p2, p3), n, fsdp)
+    y1, y1_low, b1, p4 = run_joint_norm(cnt, a3, ap, s2, s3, gb[2], gb[3], m128, w2)
+    s4, = allsum((p4,), n)
     z, z_low, mixed, mix_im, sig, pooled, wnext, p5 = call(
         mix_forward,
         [like((R, MID)), like((R, MID), BF16), like((R, MID)), like((3, R, 9 * GROUP), BF16),
@@ -618,23 +1322,13 @@
         11,
     )(cnt, b1, s4, gb[4], m128, wdown, wup, wmix, motion_kernel, scale, table, spread)
     s5, = allsum((p5,), n)
-    st5 = norm_rows(s5, count_out, gb[5])
-    w = (mask * silu(normalize(mixed, st5)[1])).astype(BF16)
-    b3 = dot(w, we2)
-    s6, = allsum((sums_of(b3),), n)
-    st6 = norm_rows(s6, count_out, gb[6])
-    x6, u6 = normalize(b3, st6)
-    u6 = u6 + y1
-    out = (mask * silu(u6)).astype(BF16)
-
-    g6 = cot * mask * silu_grad(u6)
-    t6, = allsum((back_sums(g6, x6),), n)
-    d6 = norm_back(g6, x6, mask, st6, t6, count_out).astype(BF16)
-    ge2 = dot_tn(w, d6)
-    x5, u5 = normalize(mixed, st5)
-    g5 = dot_nt(d6, we2) * mask * silu_grad(u5)
-    t5, = allsum((back_sums(g5, x5),), n)
-    wmix_t = wmix.reshape(3, 9, GROUP, GROUP).transpose(0, 1, 3, 2).reshape(3, 9 * GROUP, GROUP)
+    w, b3, p6 = run_expand_last(cnt, mixed, s5, gb[5], m128, we2)
+    s6, = allsum((p6,), n)
+    o_c, o_m, o_f, g6, p6 = run_last_norm(cnt, b3, y1, s6, gb[6], m128, (cot_c, cot_m, cot_f))
+
+    t6, = allsum((p6,), n)
+    ge2, g5, p5 = run_last_back(cnt, g6, b3, t6, s6, gb[6], m128, w, we2, mixed, s5, gb[5])
+    t5, = allsum((p5,), n)
     g4, p4, gkernel, gmix, gdown, gup = call(
         mix_backward,
         [like((R, MID)), like((2, MID)), like((16, SQUEEZE)), like((3, 9 * GROUP, GROUP), BF16),
@@ -642,73 +1336,98 @@
         22,
         [pltpu.VMEM((R, 9 * GROUP), BF16), pltpu.VMEM((R, MID), F32)],
     )(cnt, g5, t5, mixed, s5, gb[5], m128, mix_im, wmix_t, z, sig, pooled, wnext,
-      wup, motion_kernel, scale, table.T, spread, z_low, wdown, b1, s4, gb[4])
+      wup, motion_kernel, scale, table_t, spread, z_low, wdown, b1, s4, gb[4])
     t4, gkernel = allsum((p4, gkernel), n)
     gkernel = gkernel[:9]
-    x4, u4 = normalize(b1, st4)
-    d4 = norm_back(g4, x4, mask, st4, t4, count_out).astype(BF16)
-    gr2 = dot_tn(y1_low, d4)
-    gy1 = g6 + dot_nt(d4, w2)
-    x2, u2 = normalize(a3, st2)
-    x3, u3 = normalize(ap, st3)
-    gj = gy1 * mask * silu_grad(u2 + u3)
-    tj, = allsum((jnp.stack([jnp.sum(gj * x2, 0), jnp.sum(gj * x3, 0), jnp.sum(gj, 0)]),), n)
-    d2 = norm_back(gj, x2, mask, st2, tj[jnp.array([0, 2])], count_out).astype(BF16)
-    d3 = norm_back(gj, x3, mask, st3, tj[1:], count_out).astype(BF16)
-    ge1 = dot_tn(h2, d2)
-    gsk = dot_tn(xph[0], d3)
-    x1, u1 = normalize(a2, st1)
-    g1 = dot_nt(d2, we1) * mask * silu_grad(u1)
-    t1, = allsum((back_sums(g1, x1),), n)
-    d1, g0, p0 = call(
-        conv_backward,
-        [like((R, MID), BF16), like((4, R, MID)), like((2, MID))],
-        10,
-        [pltpu.VMEM((4, R, MID), BF16)],
-    )(cnt, g1, t1, a2, s1, gb[1], m128, wsp, a1, s0, gb[0])
-    gsp = dot_tn(im, d1)
+    gr2, gj, pj = run_joint_back(cnt, g4, t4, b1, s4, gb[4], m128, y1_low, w2, g6, a3, ap, s2, s3,
+                                 gb[2], gb[3])
+
+    gmix = gmix.reshape(27, n, GROUP * GROUP // n).transpose(1, 0, 2).reshape(n, -1)
+    gup = gup.reshape(SQUEEZE, n, MID // n).transpose(1, 0, 2).reshape(n, -1)
+    thin = jnp.concatenate([gmix, gdown.reshape(n, -1).astype(BF16), gup.astype(BF16)], axis=1)
+    thin = jnp.pad(thin, ((0, 0), (0, -thin.shape[1] % (16 * MID)))).reshape(n, -1, MID)
+
+    def blocks(v):
+        return rows16(v.reshape(n, -1, v.shape[-1]))
+
+    starts = list(range(0, C_OUT, MID))
+    ra = Scatter(
+        me, [blocks(gr2), thin, blocks(ge2)], [(0, 0), (1, 0)] + [(2, c) for c in starts], MID,
+        n, fsdp,
+    )
+    pj = ra.ready(pj)
+    tj, = allsum_wide((pj,), n, fsdp)
+    tj = ra.end(tj)
+    ra.add()
+    tj = ra.ready(tj)
+    ge1, gsk, d3, g1, p1 = run_expand_back(cnt, gj, tj, a3, ap, s2, s3, gb[2], gb[3], m128, h2, xph,
+                                           we1, a2, s1, gb[1])
+    p1 = ra.end(p1)
+    t1, = allsum((p1,), n)
+    ra.add()
+    rb = Scatter(
+        me, [blocks(ge1), blocks(gsk)], [(i, c) for i in range(2) for c in starts], MID, n, fsdp
+    )
+    t1 = rb.ready(ra.ready(t1))
+    d1, gsp = run_spatial_grad(cnt, g1, t1, a2, s1, gb[1], m128, im)
+    d1 = rb.end(ra.end(d1))
+    rb.add()
+    ra.add()
+    d1 = ra.ready(rb.ready(d1))
+    gsp, d1 = tie(gsp, d1)
+    rc = Scatter(me, [blocks(gsp)], [(0, 0)], MID, n, fsdp)
+    d1 = rc.ready(d1)
+    g0, p0 = call(
+        conv_back, [like((4, R, MID)), like((2, MID))], 6, [pltpu.VMEM((4, R, MID), BF16)]
+    )(cnt, d1, m128, wsp, a1, s0, gb[0])
+    p0 = rc.end(rb.end(ra.end(p0)))
     t0, = allsum((p0,), n)
-    d0 = [
-        norm_back(g0[k], normalize(a1[k], st0)[0], mask, st0, t0, count_in).astype(BF16)
-        for k in range(4)
-    ]
-    gr1 = sum(dot_tn(x, d) for x, d in zip(xph, d0))
-    gx = [dot_nt(d, w1) for d in d0]
-    gx[0] = gx[0] + dot_nt(d3, wsk)
-    gx = [(mask * v).astype(BF16) for v in gx]
-    phases = [from_rows(v) for v in gx]
-    gin = []
-    for g, side in enumerate(SIDES):
-        st = jnp.stack([phases[k][g] for k in range(4)]).reshape(2, 2, 4, side, side, -1)
-        gin.append(st.transpose(2, 3, 0, 4, 1, 5).reshape(4, 2 * side, 2 * side, -1))
-
-    def shards(v):
-        return v.reshape(n, -1)
-
-    gmix = gmix.reshape(27, n, GROUP * GROUP // n).transpose(1, 0, 2)
-    gup = gup.reshape(SQUEEZE, n, MID // n).transpose(1, 0, 2)
-    second = scatter_sum(
-        [shards(ge2), shards(gr2), shards(gmix), shards(gdown), shards(gup)], n, order
-    )
-    first = scatter_sum([shards(ge1), shards(gsk)], n, order)
-    last = scatter_sum([shards(gsp), shards(gr1)], n, order)
+    rc.add()
+    rb.add()
+    ra.add()
+    t0 = ra.ready(rb.ready(rc.ready(t0)))
+    d0, gr1 = call(
+        first_grads,
+        [like((4, R, MID), BF16), like((xph.shape[-1], MID), BF16)],
+        7,
+    )(cnt, g0, t0, a1, s0, gb[0], m128, xph)
+    gr1 = blocks(gr1)
+    d0 = rc.end(rb.end(d0))
+    rc.add()
+    rb.add()
+    d0 = rb.ready(rc.ready(d0))
+    d0, gr1 = tie(d0, gr1)
+    got = lax.all_to_all(gr1, AXES, 0, 0, tiled=True)
+    gin = run_input_grads(d0, d3, w1, wsk, m128, tables_t)
+    gin = list(gin)
+    gin[0] = rc.end(rb.end(gin[0]))
+    gr1 = jnp.sum(got.astype(F32), axis=0)[: reduce_one.shape[0]]
+    second = ra.rest()
+    first = rb.rest()
+    gsp = rc.rest()[0][: spatial_one.shape[0]]
+
+    def wide_back(parts, like_):
+        return jnp.concatenate([p[: like_.shape[0]] for p in parts], axis=1)
+
+    thin = second[1].reshape(-1)
+    s1_ = temporal_mix.size
+    s2_ = s1_ + excite_down.size
+    s3_ = s2_ + excite_up.size
 
     gain = jnp.concatenate([t0[0], t1[0], tj[0], tj[1], t4[0], t5[0], t6[0]])
     bias = jnp.concatenate([t0[1], t1[1], tj[2], tj[2], t4[1], t5[1], t6[1]])
-    me = lax.axis_index(AXES)
-    gnorm = lax.dynamic_slice_in_dim(jnp.stack([gain, bias]), me * (8192 // n), 8192 // n, 1)
-    o = from_rows(out)
+    gnorm = lax.dynamic_slice_in_dim(jnp.stack([gain, bias]), me[0] * (8192 // n), 8192 // n, 1)
     return (
-        o[0], o[1], o[2], gin[0], gin[1], gin[2],
-        last[1].reshape(reduce_one.shape),
-        last[0].reshape(spatial_one.shape),
-        first[0].reshape(expand_one.shape),
-        first[1].reshape(shortcut_one.shape),
-        second[1].reshape(reduce_two.shape),
-        second[3].reshape(excite_down.shape),
-        second[4].reshape(excite_up.shape),
-        second[2].reshape(temporal_mix.shape),
-        second[0].reshape(expand_two.shape),
+        o_c, o_m, o_f, gin[0], gin[1], gin[2],
+        gr1,
+        gsp,
+        wide_back(first[:4], expand_one),
+        wide_back(first[4:], shortcut_one),
+        second[0][: reduce_two.shape[0]],
+        thin[s1_:s2_].reshape(excite_down.shape),
+        thin[s2_:s3_].reshape(excite_up.shape),
+        thin[:s1_].reshape(temporal_mix.shape),
+        wide_back(second[2:], expand_two),
         gnorm,
         gkernel,
     )

time: 774 us -> 617 us (0.80)
  Pallas kernels: 36.4 us -> 222 us
  waiting for transfers between devices: 268 us -> 123 us
  matrix products: 74.2 us -> 0.14 us
  other arithmetic: 81.9 us -> 20.8 us
  blocking collectives: 86.5 us -> 31.3 us
  local copies, waits for them, and re-layouts: 132 us -> 83.6 us
  starting transfers between devices: 67.8 us -> 110 us
    pallas_call x1 -> x34, Pallas kernels: 10.6 us -> 196 us  [the longest x7 69.2 us: wide_grid(): pl.pallas_call(kernel, grid=(steps,), out_shape=outs, in_specs=in_specs,...]
    all_gather x5 -> x2, waiting for transfers between devices: 100 us -> 0.01 us  [gather(): return lax.all_gather(w.astype(BF16), AXES, axis=0, tiled=True)]
    all_gather x1 -> x0, blocking collectives: 86.5 us -> none  [gather(): return lax.all_gather(w.astype(BF16), AXES, axis=0, tiled=True)]
    dot_general x25 -> x0, matrix products: 74 us -> none  [the longest x8 28.6 us: dot(): return jnp.dot(a, b, preferred_element_type=F32)]
    ppermute x15 -> x60, starting transfers between devices: 18.5 us -> 70.4 us  [swap(): return lax.ppermute(v, AXES, [(i, i ^ d) for i in range(n)])]
    all_to_all x0 -> x2, blocking collectives: none -> 31.3 us  [allsum(): got = lax.all_to_all(spread, AXES, 0, 0, tiled=True)]
    convert_element_type x22 -> x7, other arithmetic: 32.6 us -> 3.13 us  [the longest x4 1.97 us: __init__(): padded = [rows16(v.astype(BF16)) for v in shards]]
    ppermute x15 -> x60, waiting for transfers between devices: 99.1 us -> 74.9 us  [swap(): return lax.ppermute(v, AXES, [(i, i ^ d) for i in range(n)])]
  transfers between devices with their start and end apart: 33 -> 71, of which waited for: 19 -> 32; matrix products, arithmetic and copies ran while one was open for 31% -> 13% of each run, Pallas kernels for 4% -> 25%
where the time goes in v2:
time: 617 us; the launch traced here: 607 us
  Pallas kernels  222 us (36%)
  waiting for transfers between devices  123 us (20%)
  starting transfers between devices  110 us (18%)
  local copies, waits for them, and re-layouts  83.6 us (14%)
  blocking collectives  31.3 us (5%)
  other arithmetic  20.8 us (3%)
  between operations  15.5 us (3%)
    ppermute x60, waiting for transfers between devices, swap(): return lax.ppermute(v, AXES, [(i, i ^ d) for i in range(n)])  74.9 us
    ppermute x60, starting transfers between devices, swap(): return lax.ppermute(v, AXES, [(i, i ^ d) for i in range(n)])  70.4 us
    pallas_call x7, Pallas kernels, wide_grid(): pl.pallas_call(kernel, grid=(steps,), out_shape=outs, in_specs=in_specs,...  69.2 us
    all_to_all x8, waiting for transfers between devices, allsum(): got = lax.all_to_all(spread, AXES, 0, 0, tiled=True)  48.1 us
    pallas_call x15, Pallas kernels, add_blocks(): return call(kernel, outs, 2 * k_in, scalars=0)(*keep, *got)  41.5 us
    all_to_all x8, starting transfers between devices, allsum(): got = lax.all_to_all(spread, AXES, 0, 0, tiled=True)  36.5 us
    all_to_all x2, blocking collectives, allsum(): got = lax.all_to_all(spread, AXES, 0, 0, tiled=True)  31.3 us
    unnamed x152, local copies, waits for them, and re-layouts  28.3 us
  transfers between devices with their start and end apart: 71, of which 32 were waited for; matrix products, arithmetic and copies ran while one was open for 13% of the time, Pallas kernels for 25%

profile of v2, /device:TPU:0, one launch (start us, length us, event | category | flops | bytes accessed | tf_op | source)
XLA Modules:
  0.0 606.5 jit_solution(8702265705400267)
XLA Ops:
  28.7 5.9 shard_map.431.x.xph
  35.9 3.5 collective-permute-start.8
  44.8 5.8 collective-permute-done.8
  54.3 6.2 %shard_map.433 = (f32[4,480,512]{2,1,0:T(8,128)}, f32[2,512]{1,0:T(2,128)}) custom-call(bf16[4,480,1024]{2,1,0:T(8,128)(2,1)} %shard_map.431.x.xph, bf16[1024,512]{1,0:T(8,128)(2,1)} %bitcast.115), custom_call_target="tpu_custom_call" | custom-call | tf_op jit(solution)/shard_map/pallas_call | solution.py:692
  63.8 9.0 %all-to-all-start = ((f32[32,16,128]{2,1,0:T(8,128)}), f32[32,16,128]{2,1,0:T(8,128)}, u32[]{:S(2)}, u32[]{:S(2)}) async-start(f32[32,16,128]{2,1,0:T(8,128)} %broadcast_in_dim.84), calls=%async_computation | async-start | bytes 524288 | tf_op jit(solution)/shard_map/all_to_all | solution.py:161
  77.3 7.3 %all-to-all-done = f32[32,16,128]{2,1,0:T(8,128)} async-done(((f32[32,16,128]{2,1,0:T(8,128)}), f32[32,16,128]{2,1,0:T(8,128)}, u32[]{:S(2)}, u32[]{:S(2)}) %all-to-all-start) | async-done | bytes 262176 | tf_op jit(solution)/shard_map/all_to_all | solution.py:161
  86.2 5.8 collective-permute-done.14
  92.0 7.3 %collective-permute-done.15 = bf16[48,2048]{1,0:T(8,128)(2,1)} collective-permute-done((bf16[48,2048]{1,0:T(8,128)(2,1)}, bf16[48,2048]{1,0:T(8,128)(2,1)}, u32[]{:S(2)}, u32[]{:S(2)}) %collective-permute-start.15) | collective-permute-done | bytes 196640 | tf_op jit(solution)/shard_map/ppermute | solution.py:972
  110.9 4.5 shard_map.434
  116.2 9.6 %shard_map.435 = (bf16[480,4608]{1,0:T(8,128)(2,1)}, f32[480,512]{1,0:T(8,128)}, f32[2,512]{1,0:T(2,128)}) custom-call(f32[1]{0:T(128)} %slice.235.cnt, f32[4,480,512]{2,1,0:T(8,128)} %get-tuple-element.246.a1, f32[2,512]{1,0:T(2,128)} %reshape.269.s0, f32[2,512]{1,0:T(2,128)} %get-tuple-element.540.gb0, f32[480,128]{1,0:T(8,128)} %broadcast_in_dim.85.mask, ...), custom_call_target="tpu_custom_call" | custom-call | tf_op jit(solution)/shard_map/pallas_call | solution.py:1288
  129.7 6.5 %all-to-all-start.1 = ((f32[32,8,128]{2,1,0:T(8,128)}), f32[32,8,128]{2,1,0:T(8,128)S(1)}, u32[]{:S(2)}, u32[]{:S(2)}) async-start(f32[32,8,128]{2,1,0:T(8,128)} %broadcast_in_dim.87), calls=%async_computation.1 | async-start | bytes 262144 | tf_op jit(solution)/shard_map/all_to_all | solution.py:161
  138.9 10.8 %all-to-all-done.1 = f32[32,8,128]{2,1,0:T(8,128)S(1)} async-done(((f32[32,8,128]{2,1,0:T(8,128)}), f32[32,8,128]{2,1,0:T(8,128)S(1)}, u32[]{:S(2)}, u32[]{:S(2)}) %all-to-all-start.1) | async-done | bytes 131104 | tf_op jit(solution)/shard_map/all_to_all | solution.py:161
  157.4 5.6 shard_map.436
  163.1 9.2 %shard_map.437 = (bf16[480,512]{1,0:T(8,128)(2,1)}, f32[480,2048]{1,0:T(8,128)}, f32[480,2048]{1,0:T(8,128)}, f32[2,2048]{1,0:T(2,128)}, f32[2,2048]{1,0:T(2,128)}) custom-call(f32[1]{0:T(128)} %slice.235.cnt, f32[480,512]{1,0:T(8,128)} %get-tuple-element.254.a2, f32[2,512]{1,0:T(2,128)} %reshape_reshape.32.s1, f32[2,512]{1,0:T(2,128)} %get-tuple-element.539.gb1, ...), custom_call_target="tpu_custom_call" | custom-call | tf_op jit(solution)/shard_map/pallas_call | solution.py:692
  181.2 4.9 collective-permute-start.29
  196.8 9.3 %shard_map.438 = (f32[480,2048]{1,0:T(8,128)}, bf16[480,2048]{1,0:T(8,128)(2,1)}, f32[480,512]{1,0:T(8,128)}, f32[2,512]{1,0:T(2,128)}) custom-call(f32[1]{0:T(128)} %slice.235.cnt, f32[480,2048]{1,0:T(8,128)} %get-tuple-element.271.a3, f32[480,2048]{1,0:T(8,128)} %get-tuple-element.272.ap, f32[2,2048]{1,0:T(2,128)} %reshape.273.s2, f32[2,2048]{1,0:T(2,128)} %reshape.274.s3, ...), custom_call_target="tpu_custom_call" | custom-call | tf_op jit(solution)/shard_map/pallas_call | solution.py:678
  207.4 3.8 all-to-all-start.2
  221.2 7.0 %shard_map.439 = (f32[480,512]{1,0:T(8,128)}, bf16[480,512]{1,0:T(8,128)(2,1)}, f32[480,512]{1,0:T(8,128)}, bf16[3,480,1152]{2,1,0:T(8,128)(2,1)}, f32[16,512]{1...) custom-call(f32[1]{0:T(128)} %slice.235.cnt, f32[480,512]{1,0:T(8,128)} %get-tuple-element.275.b1, ...), custom_call_target="tpu_custom_call" | custom-call | tf_op jit(solution)/shard_map/pallas_call | solution.py:1318
  228.8 12.5 %all_to_all.55 = f32[32,8,128]{2,1,0:T(8,128)S(1)} all-to-all(f32[32,8,128]{2,1,0:T(8,128)S(1)} %broadcast_in_dim.92), channel_id=1, replica_groups=mesh['dp'=16,'fsdp'=2] {'dp','fsdp'}, dimensions={0} | all-to-all | bytes 262144 | tf_op jit(solution)/shard_map/all_to_all | solution.py:161
  242.0 6.4 %shard_map.440 = (bf16[480,512]{1,0:T(8,128)(2,1)}, f32[480,2048]{1,0:T(8,128)}, f32[2,2048]{1,0:T(2,128)}) custom-call(f32[1]{0:T(128)} %slice.235.cnt, f32[480,512]{1,0:T(8,128)} %get-tuple-element.277.mixed, f32[2,512]{1,0:T(2,128)} %reshape_reshape.34.s5, f32[2,512]{1,0:T(2,128)} %get-tuple-element.537.gb5, f32[480,128]{1,0:T(8,128)} %broadcast_in_dim.85.mask, ...), custom_call_target="tpu_custom_call" | custom-call | tf_op jit(solution)/shard_map/pallas_call | solution.py:692
  255.2 12.4 %all-to-all-done.4 = f32[32,32,128]{2,1,0:T(8,128)S(1)} async-done(((f32[32,32,128]{2,1,0:T(8,128)}), f32[32,32,128]{2,1,0:T(8,128)S(1)}, u32[]{:S(2)}, u32[]{:S(2)}) %all-to-all-start.4) | async-done | bytes 524320 | tf_op jit(solution)/shard_map/all_to_all | solution.py:161
  268.3 10.8 %shard_map.441 = (bf16[4,4,4,2048]{3,2,1,0:T(4,128)(2,1)}, bf16[4,6,6,2048]{3,2,1,0:T(8,128)(2,1)}, bf16[4,7,7,2048]{3,2,1,0:T(8,128)(2,1)}, f32[480,2048]{1,0:T(8,128)}, f32[2,2048]{1,0:T(2,128)}) custom-call(f32[1]{0:T(128)} %slice.235.cnt, f32[480,2048]{1,0:T(8,128)} %get-tuple-element.279.b3, f32[480,2048]{1,0:T(8,128)} %get-tuple-element.280.y1, ...), custom_call_target="tpu_custom_call" | custom-call | tf_op jit(solution)/shard_map/pallas_call | solution.py:631
  279.9 18.7 %all_to_all.56 = f32[32,32,128]{2,1,0:T(8,128)S(1)} all-to-all(f32[32,32,128]{2,1,0:T(8,128)S(1)} %broadcast_in_dim.96), channel_id=1, replica_groups=mesh['dp'=16,'fsdp'=2] {'dp','fsdp'}, dimensions={0} | all-to-all | bytes 1048576 | tf_op jit(solution)/shard_map/all_to_all | solution.py:161
  299.3 9.8 %shard_map.442 = (bf16[512,2048]{1,0:T(8,128)(2,1)}, f32[480,512]{1,0:T(8,128)}, f32[2,512]{1,0:T(2,128)}) custom-call(f32[1]{0:T(128)} %slice.235.cnt, f32[480,2048]{1,0:T(8,128)} %get-tuple-element.285.g6, f32[480,2048]{1,0:T(8,128)} %get-tuple-element.279.b3, f32[2,2048]{1,0:T(2,128)} %reshape_reshape.36.t6, f32[2,2048]{1,0:T(2,128)} %reshape_reshape.35.s6, ...), custom_call_target="tpu_custom_call" | custom-call | tf_op jit(solution)/shard_map/pallas_call | solution.py:692
  310.4 3.6 all-to-all-start.6
  316.2 6.5 %all-to-all-done.6 = f32[32,8,128]{2,1,0:T(8,128)S(1)} async-done(((f32[32,8,128]{2,1,0:T(8,128)}), f32[32,8,128]{2,1,0:T(8,128)S(1)}, u32[]{:S(2)}, u32[]{:S(2)}) %all-to-all-start.6) | async-done | bytes 131104 | tf_op jit(solution)/shard_map/all_to_all | solution.py:161
  323.3 9.4 %shard_map.443 = (f32[480,512]{1,0:T(8,128)}, f32[2,512]{1,0:T(2,128)}, f32[16,32]{1,0:T(8,128)}, bf16[3,1152,128]{2,1,0:T(8,128)(2,1)}, f32[512,32]{1,0:T(8,128)}, /*index=5*/f32[32,512]{1,0:T(8,128)}) custom-call(f32[1]{0:T(128)} %slice.235.cnt, f32[480,512]{1,0:T(8,128)} %get-tuple-element.288.g5, f32[2,512]{1,0:T(2,128)} %reshape_reshape.37.t5, ...), custom_call_target="tpu_custom_call" | custom-call | tf_op jit(solution)/shard_map/pallas_call | solution.py:1332
  340.0 9.3 %all-to-all-done.7 = f32[32,16,128]{2,1,0:T(8,128)S(1)} async-done(((f32[32,16,128]{2,1,0:T(8,128)}), f32[32,16,128]{2,1,0:T(8,128)S(1)}, u32[]{:S(2)}, u32[]{:S(2)}) %all-to-all-start.7) | async-done | bytes 262176 | tf_op jit(solution)/shard_map/all_to_all | solution.py:161
  350.0 12.2 %shard_map.444 = (bf16[2048,512]{1,0:T(8,128)(2,1)}, f32[480,2048]{1,0:T(8,128)}, f32[3,2048]{1,0:T(4,128)}) custom-call(f32[1]{0:T(128)} %slice.235.cnt, f32[480,512]{1,0:T(8,128)} %get-tuple-element.296.g4, f32[2,512]{1,0:T(2,128)} %reshape.284.t4, f32[480,512]{1,0:T(8,128)} %get-tuple-element.275.b1, f32[2,512]{1,0:T(2,128)} %reshape_reshape.33.s4, ...), custom_call_target="tpu_custom_call" | custom-call | tf_op jit(solution)/shard_map/pallas_call | solution.py:692
  362.2 5.2 shard_map.445
  368.1 4.1 collective-permute-done.32
  388.2 4.6 shard_map.446
  395.1 14.4 %shard_map.447 = (bf16[512,2048]{1,0:T(8,128)(2,1)}, bf16[1024,2048]{1,0:T(8,128)(2,1)}, bf16[480,2048]{1,0:T(8,128)(2,1)}, f32[480,512]{1,0:T(8,128)}, f32[2,512]{1,0:T(2,128)}) custom-call(f32[1]{0:T(128)} %slice.235.cnt, f32[480,2048]{1,0:T(8,128)} %get-tuple-element.300.gj, f32[3,2048]{1,0:T(4,128)} %reshape_reshape.39.tj, ...), custom_call_target="tpu_custom_call" | custom-call | tf_op jit(solution)/shard_map/pallas_call | solution.py:692
  411.0 3.7 all-to-all-start.8
  414.7 5.9 shard_map.449
  427.8 10.9 %shard_map.450 = (bf16[480,512]{1,0:T(8,128)(2,1)}, bf16[4608,512]{1,0:T(8,128)(2,1)}) custom-call(f32[1]{0:T(128)} %slice.235.cnt, f32[480,512]{1,0:T(8,128)} %get-tuple-element.317.g1, f32[2,512]{1,0:T(2,128)} %reshape_reshape.40.t1, f32[480,512]{1,0:T(8,128)} %get-tuple-element.254.a2, f32[2,512]{1,0:T(2,128)} %reshape_reshape.32.s1, ...), custom_call_target="tpu_custom_call" | custom-call | tf_op jit(solution)/shard_map/pallas_call | solution.py:692
  443.5 5.3 shard_map.451
  448.8 4.6 shard_map.453
  459.7 10.0 %shard_map.454 = (f32[4,480,512]{2,1,0:T(8,128)}, f32[2,512]{1,0:T(2,128)}) custom-call(f32[1]{0:T(128)} %slice.235.cnt, bf16[480,512]{1,0:T(8,128)(2,1)} %get-tuple-element.355.d1, f32[480,128]{1,0:T(8,128)} %broadcast_in_dim.85.mask, bf16[4608,512]{1,0:T(8,128)(2,1)} %bitcast.107, f32[4,480,512]{2,1,0:T(8,128)} %get-tuple-element.246.a1, ...), custom_call_target="tpu_custom_call" | custom-call | tf_op jit(solution)/shard_map/pallas_call | solution.py:1380
  469.7 4.1 collective-permute-done.46.refs_2_
  475.5 4.6 all-to-all-start.9
  485.4 4.4 shard_map.455
  492.7 9.3 %shard_map.458 = (bf16[4,480,512]{2,1,0:T(8,128)(2,1)}, bf16[1024,512]{1,0:T(8,128)(2,1)}) custom-call(f32[1]{0:T(128)} %slice.235.cnt, f32[4,480,512]{2,1,0:T(8,128)} %get-tuple-element.356.g0, f32[2,512]{1,0:T(2,128)} %copy-done.41, f32[4,480,512]{2,1,0:T(8,128)} %get-tuple-element.246.a1, f32[2,512]{1,0:T(2,128)} %reshape.269.s0, ...), custom_call_target="tpu_custom_call" | custom-call | tf_op jit(solution)/shard_map/pallas_call | solution.py:1389
  506.1 7.8 %collective-permute-done.49.refs_2_ = bf16[4,192,256]{2,1,0:T(8,128)(2,1)S(1)} collective-permute-done((bf16[4,192,256]{2,1,0:T(8,128)(2,1)S(1)}, bf16[4,192,256]{2,1,0:T(8,128)(2,1)S(1)}, u32[]{:S(2)}, u32[]{:S(2)}) %collective-permute-start.49) | collective-permute-done | bytes 393248 | tf_op jit(solution)/shard_map/ppermute | solution.py:972
  518.7 8.0 %collective-permute-done.51.refs_2_ = bf16[8,144,256]{2,1,0:T(8,128)(2,1)S(1)} collective-permute-done((bf16[8,144,256]{2,1,0:T(8,128)(2,1)S(1)}, bf16[8,144,256]{2,1,0:T(8,128)(2,1)S(1)}, u32[]{:S(2)}, u32[]{:S(2)}) %collective-permute-start.51) | collective-permute-done | bytes 589856 | tf_op jit(solution)/shard_map/ppermute | solution.py:972
  548.1 11.6 %shard_map.461 = (bf16[4,8,8,1024]{3,2,1,0:T(8,128)(2,1)}, bf16[4,12,12,1024]{3,2,1,0:T(8,128)(2,1)}, bf16[4,14,14,1024]{3,2,1,0:T(8,128)(2,1)}) custom-call(bf16[4,480,512]{2,1,0:T(8,128)(2,1)} %get-tuple-element.402.d0, bf16[480,2048]{1,0:T(8,128)(2,1)} %get-tuple-element.403.d3, bf16[1024,512]{1,0:T(8,128)(2,1)} %bitcast.116, ...), custom_call_target="tpu_custom_call" | custom-call | tf_op jit(solution)/shard_map/pallas_call | solution.py:566
  567.9 4.0 copy.151
  589.0 7.3 %collective-permute-done.57.refs_1_ = bf16[2,1,144,256]{3,2,1,0:T(8,128)(2,1)S(1)} collective-permute-done((bf16[2,1,144,256]{3,2,1,0:T(8,128)(2,1)}, bf16[2,1,144,256]{3,2,1,0:T(8,128)(2,1)S(1)}, u32[]{:S(2)}, u32[]{:S(2)}) %collective-permute-start.57) | collective-permute-done | bytes 147488 | tf_op jit(solution)/shard_map/ppermute | solution.py:972
  (435 shorter events, 227.4 us)
Async XLA Ops:
  7.2 186.4 %all-gather.3.cloned.1.call-start = ((), (), s32[]{:S(2)}) async-start(), calls=%async_computation.11 | async-start | bytes 3244032 | tf_op jit(solution)/shard_map/all_gather | solution.py:1218
  8.9 12.8 %collective-permute-start = (bf16[48,512]{1,0:T(8,128)(2,1)S(1)}, bf16[48,512]{1,0:T(8,128)(2,1)S(1)}, u32[]{:S(2)}, u32[]{:S(2)}) collective-permute-start(bf16[48,512]{1,0:T(8,128)(2,1)S(1)} %fusion.13), channel_id=1, source_target_pairs={{0,8},{1,9},{2,10},{3,11},{4,12},{5,13},{6,14},{7,15},{8,0},{9,1},... | collective-permute-start | bytes 147464 | tf_op jit(solution)/shard_map/ppermute | solution.py:972
  12.0 9.7 %collective-permute-start.1 = (bf16[48,512]{1,0:T(8,128)(2,1)S(1)}, bf16[48,512]{1,0:T(8,128)(2,1)S(1)}, u32[]{:S(2)}, u32[]{:S(2)}) collective-permute-start(bf16[48,512]{1,0:T(8,128)(2,1)S(1)} %fusion.13), channel_id=1, source_target_pairs={{0,16},{1,17},{2,18},{3,19},{4,20},{5,21},{6,22},{7,23},{8,24},{9,... | collective-permute-start | bytes 147464 | tf_op jit(solution)/shard_map/ppermute | solution.py:972
  21.8 12.8 %collective-permute-start.3 = (bf16[4,48,512]{2,1,0:T(8,128)(2,1)S(1)}, bf16[4,48,512]{2,1,0:T(8,128)(2,1)S(1)}, u32[]{:S(2)}, u32[]{:S(2)}) collective-permute-start(bf16[4,48,512]{2,1,0:T(8,128)(2,1)S(1)} %pad_maximum_fusion.7), channel_id=1, source_target_pairs={{0,1},{1,0},{2,3},{3,2},{4,5},{5,4},{6,7},{7,6},{8,9},{9,8},{10,11... | collective-permute-start | bytes 589832 | tf_op jit(solution)/shard_map/ppermute | solution.py:972
  23.5 11.1 %collective-permute-start.4 = (bf16[4,48,512]{2,1,0:T(8,128)(2,1)S(1)}, bf16[4,48,512]{2,1,0:T(8,128)(2,1)S(1)}, u32[]{:S(2)}, u32[]{:S(2)}) collective-permute-start(bf16[4,48,512]{2,1,0:T(8,128)(2,1)S(1)} %pad_maximum_fusion.7), channel_id=1, source_target_pairs={{0,4},{1,5},{2,6},{3,7},{4,0},{5,1},{6,2},{7,3},{8,12},{9,13},{10,... | collective-permute-start | bytes 589832 | tf_op jit(solution)/shard_map/ppermute | solution.py:972
  25.1 9.6 %collective-permute-start.5 = (bf16[4,48,512]{2,1,0:T(8,128)(2,1)S(1)}, bf16[4,48,512]{2,1,0:T(8,128)(2,1)S(1)}, u32[]{:S(2)}, u32[]{:S(2)}) collective-permute-start(bf16[4,48,512]{2,1,0:T(8,128)(2,1)S(1)} %pad_maximum_fusion.7), channel_id=1, source_target_pairs={{0,5},{1,4},{2,7},{3,6},{4,1},{5,0},{6,3},{7,2},{8,13},{9,12},{10,... | collective-permute-start | bytes 589832 | tf_op jit(solution)/shard_map/ppermute | solution.py:972
  34.9 9.9 %collective-permute-start.7 = (bf16[144,512]{1,0:T(8,128)(2,1)S(1)}, bf16[144,512]{1,0:T(8,128)(2,1)S(1)}, u32[]{:S(2)}, u32[]{:S(2)}) collective-permute-start(bf16[144,512]{1,0:T(8,128)(2,1)S(1)} %convert_element_type.95), channel_id=1, source_target_pairs={{0,8},{1,9},{2,10},{3,11},{4,12},{5,13},{6,14},{7,15},{8,0},{9,1},... | collective-permute-start | bytes 442376 | tf_op jit(solution)/shard_map/ppermute | solution.py:972
  35.9 14.7 %collective-permute-start.8 = (bf16[144,512]{1,0:T(8,128)(2,1)S(1)}, bf16[144,512]{1,0:T(8,128)(2,1)S(1)}, u32[]{:S(2)}, u32[]{:S(2)}) collective-permute-start(bf16[144,512]{1,0:T(8,128)(2,1)S(1)} %convert_element_type.95), channel_id=1, source_target_pairs={{0,16},{1,17},{2,18},{3,19},{4,20},{5,21},{6,22},{7,23},{8,24},{9,... | collective-permute-start | bytes 442376 | tf_op jit(solution)/shard_map/ppermute | solution.py:972
  39.3 11.2 %collective-permute-start.9 = (bf16[144,512]{1,0:T(8,128)(2,1)S(1)}, bf16[144,512]{1,0:T(8,128)(2,1)S(1)}, u32[]{:S(2)}, u32[]{:S(2)}) collective-permute-start(bf16[144,512]{1,0:T(8,128)(2,1)S(1)} %convert_element_type.95), channel_id=1, source_target_pairs={{0,24},{1,25},{2,26},{3,27},{4,28},{5,29},{6,30},{7,31},{8,16},{9,... | collective-permute-start | bytes 442376 | tf_op jit(solution)/shard_map/ppermute | solution.py:972
  50.7 9.9 %collective-permute-start.10 = (bf16[4,144,256]{2,1,0:T(8,128)(2,1)S(1)}, bf16[4,144,256]{2,1,0:T(8,128)(2,1)S(1)}, u32[]{:S(2)}, u32[]{:S(2)}) collective-permute-start(bf16[4,144,256]{2,1,0:T(8,128)(2,1)S(1)} %get-tuple-element.240), channel_id=1, source_target_pairs={{0,1},{1,0},{2,3},{3,2},{4,5},{5,4},{6,7},{7,6},{8,9},{9,8},{10,11... | collective-permute-start | bytes 884744 | tf_op jit(solution)/shard_map/ppermute | solution.py:972
  60.7 38.7 %collective-permute-start.12 = (bf16[8,144,256]{2,1,0:T(8,128)(2,1)S(1)}, bf16[8,144,256]{2,1,0:T(8,128)(2,1)}, u32[]{:S(2)}, u32[]{:S(2)}) collective-permute-start(bf16[8,144,256]{2,1,0:T(8,128)(2,1)S(1)} %get-tuple-element.247), channel_id=1, source_target_pairs={{0,4},{1,5},{2,6},{3,7},{4,0},{5,1},{6,2},{7,3},{8,12},{9,13},{10,... | collective-permute-start | bytes 1769480 | tf_op jit(solution)/shard_map/ppermute | solution.py:972
  61.8 37.5 %collective-permute-start.13 = (bf16[8,144,256]{2,1,0:T(8,128)(2,1)S(1)}, bf16[8,144,256]{2,1,0:T(8,128)(2,1)}, u32[]{:S(2)}, u32[]{:S(2)}) collective-permute-start(bf16[8,144,256]{2,1,0:T(8,128)(2,1)S(1)} %get-tuple-element.248), channel_id=1, source_target_pairs={{0,1},{1,0},{2,3},{3,2},{4,5},{5,4},{6,7},{7,6},{8,9},{9,8},{10,11... | collective-permute-start | bytes 1769480 | tf_op jit(solution)/shard_map/ppermute | solution.py:972
  63.8 20.9 %all-to-all-start = ((f32[32,16,128]{2,1,0:T(8,128)}), f32[32,16,128]{2,1,0:T(8,128)}, u32[]{:S(2)}, u32[]{:S(2)}) async-start(f32[32,16,128]{2,1,0:T(8,128)} %broadcast_in_dim.84), calls=%async_computation | async-start | bytes 524288 | tf_op jit(solution)/shard_map/all_to_all | solution.py:161
  72.8 19.2 %collective-permute-start.14 = (bf16[48,2048]{1,0:T(8,128)(2,1)}, bf16[48,2048]{1,0:T(8,128)(2,1)}, u32[]{:S(2)}, u32[]{:S(2)}) collective-permute-start(bf16[48,2048]{1,0:T(8,128)(2,1)} %pad_maximum_fusion.8), channel_id=1, source_target_pairs={{0,8},{1,9},{2,10},{3,11},{4,12},{5,13},{6,14},{7,15},{8,0},{9,1},... | collective-permute-start | bytes 589832 | tf_op jit(solution)/shard_map/ppermute | solution.py:972
  74.6 24.7 %collective-permute-start.15 = (bf16[48,2048]{1,0:T(8,128)(2,1)}, bf16[48,2048]{1,0:T(8,128)(2,1)}, u32[]{:S(2)}, u32[]{:S(2)}) collective-permute-start(bf16[48,2048]{1,0:T(8,128)(2,1)} %pad_maximum_fusion.8), channel_id=1, source_target_pairs={{0,16},{1,17},{2,18},{3,19},{4,20},{5,21},{6,22},{7,23},{8,24},{9,... | collective-permute-start | bytes 589832 | tf_op jit(solution)/shard_map/ppermute | solution.py:972
  77.0 22.3 %collective-permute-start.16 = (bf16[48,2048]{1,0:T(8,128)(2,1)}, bf16[48,2048]{1,0:T(8,128)(2,1)}, u32[]{:S(2)}, u32[]{:S(2)}) collective-permute-start(bf16[48,2048]{1,0:T(8,128)(2,1)} %pad_maximum_fusion.8), channel_id=1, source_target_pairs={{0,24},{1,25},{2,26},{3,27},{4,28},{5,29},{6,30},{7,31},{8,16},{9,... | collective-permute-start | bytes 589832 | tf_op jit(solution)/shard_map/ppermute | solution.py:972
  104.4 21.4 %collective-permute-start.19 = (bf16[4,48,1024]{2,1,0:T(8,128)(2,1)S(1)}, bf16[4,48,1024]{2,1,0:T(8,128)(2,1)S(1)}, u32[]{:S(2)}, u32[]{:S(2)}) collective-permute-start(bf16[4,48,1024]{2,1,0:T(8,128)(2,1)S(1)} %get-tuple-element.519), channel_id=1, source_target_pairs={{0,1},{1,0},{2,3},{3,2},{4,5},{5,4},{6,7},{7,6},{8,9},{9,8},{10,11... | collective-permute-start | bytes 1179656 | tf_op jit(solution)/shard_map/ppermute | solution.py:972
  106.1 19.7 %collective-permute-start.20 = (bf16[4,48,1024]{2,1,0:T(8,128)(2,1)S(1)}, bf16[4,48,1024]{2,1,0:T(8,128)(2,1)S(1)}, u32[]{:S(2)}, u32[]{:S(2)}) collective-permute-start(bf16[4,48,1024]{2,1,0:T(8,128)(2,1)S(1)} %get-tuple-element.518), channel_id=1, source_target_pairs={{0,4},{1,5},{2,6},{3,7},{4,0},{5,1},{6,2},{7,3},{8,12},{9,13},{10,... | collective-permute-start | bytes 1179656 | tf_op jit(solution)/shard_map/ppermute | solution.py:972
  127.7 22.6 %collective-permute-start.21 = (bf16[8,48,1024]{2,1,0:T(8,128)(2,1)}, bf16[8,48,1024]{2,1,0:T(8,128)(2,1)}, u32[]{:S(2)}, u32[]{:S(2)}) collective-permute-start(bf16[8,48,1024]{2,1,0:T(8,128)(2,1)} %pad_maximum_fusion.1), channel_id=1, source_target_pairs={{0,4},{1,5},{2,6},{3,7},{4,0},{5,1},{6,2},{7,3},{8,12},{9,13},{10,... | collective-permute-start | bytes 2359304 | tf_op jit(solution)/shard_map/ppermute | solution.py:972
  128.6 21.7 %collective-permute-start.22 = (bf16[8,48,1024]{2,1,0:T(8,128)(2,1)}, bf16[8,48,1024]{2,1,0:T(8,128)(2,1)}, u32[]{:S(2)}, u32[]{:S(2)}) collective-permute-start(bf16[8,48,1024]{2,1,0:T(8,128)(2,1)} %pad_maximum_fusion.2), channel_id=1, source_target_pairs={{0,1},{1,0},{2,3},{3,2},{4,5},{5,4},{6,7},{7,6},{8,9},{9,8},{10,11... | collective-permute-start | bytes 2359304 | tf_op jit(solution)/shard_map/ppermute | solution.py:972
  129.7 20.0 %all-to-all-start.1 = ((f32[32,8,128]{2,1,0:T(8,128)}), f32[32,8,128]{2,1,0:T(8,128)S(1)}, u32[]{:S(2)}, u32[]{:S(2)}) async-start(f32[32,8,128]{2,1,0:T(8,128)} %broadcast_in_dim.87), calls=%async_computation.1 | async-start | bytes 262144 | tf_op jit(solution)/shard_map/all_to_all | solution.py:161
  136.2 105.8 %all-gather.5.cloned.1.call-start = ((), (), s32[]{:S(2)}) async-start(), calls=%async_computation.12 | async-start | bytes 2162688 | tf_op jit(solution)/shard_map/all_gather | solution.py:1218
  207.4 12.4 %all-to-all-start.2 = ((f32[32,8,128]{2,1,0:T(8,128)}), f32[32,8,128]{2,1,0:T(8,128)S(1)}, u32[]{:S(2)}, u32[]{:S(2)}) async-start(f32[32,8,128]{2,1,0:T(8,128)} %broadcast_in_dim.89), calls=%async_computation.2 | async-start | bytes 262144 | tf_op jit(solution)/shard_map/all_to_all | solution.py:161
  250.0 17.6 %all-to-all-start.4 = ((f32[32,32,128]{2,1,0:T(8,128)}), f32[32,32,128]{2,1,0:T(8,128)S(1)}, u32[]{:S(2)}, u32[]{:S(2)}) async-start(f32[32,32,128]{2,1,0:T(8,128)} %broadcast_in_dim.94), calls=%async_computation.4 | async-start | bytes 1048576 | tf_op jit(solution)/shard_map/all_to_all | solution.py:161
  310.4 12.3 %all-to-all-start.6 = ((f32[32,8,128]{2,1,0:T(8,128)}), f32[32,8,128]{2,1,0:T(8,128)S(1)}, u32[]{:S(2)}, u32[]{:S(2)}) async-start(f32[32,8,128]{2,1,0:T(8,128)} %broadcast_in_dim.98), calls=%async_computation.6 | async-start | bytes 262144 | tf_op jit(solution)/shard_map/all_to_all | solution.py:161
  336.0 13.3 %all-to-all-start.7 = ((f32[32,16,128]{2,1,0:T(8,128)}), f32[32,16,128]{2,1,0:T(8,128)S(1)}, u32[]{:S(2)}, u32[]{:S(2)}) async-start(f32[32,16,128]{2,1,0:T(8,128)} %broadcast_in_dim.100), calls=%async_computation.7 | async-start | bytes 524288 | tf_op jit(solution)/shard_map/all_to_all | solution.py:161
  367.4 19.3 %collective-permute-start.39 = (bf16[2,16,160,256]{3,2,1,0:T(8,128)(2,1)}, bf16[2,16,160,256]{3,2,1,0:T(8,128)(2,1)S(1)}, u32[]{:S(2)}, u32[]{:S(2)}) collective-permute-start(bf16[2,16,160,256]{3,2,1,0:T(8,128)(2,1)} %get-tuple-element.309), channel_id=1, source_target_pairs={{0,2},{1,3},{2,0},{3,1},{4,6},{5,7},{6,4},{7,5},{8,10},{9,11},{10,... | collective-permute-start | bytes 7864328 | tf_op jit(solution)/shard_map/ppermute | solution.py:972
  392.9 16.6 %collective-permute-start.40 = (bf16[8,160,256]{2,1,0:T(8,128)(2,1)}, bf16[8,160,256]{2,1,0:T(8,128)(2,1)S(1)}, u32[]{:S(2)}, u32[]{:S(2)}) collective-permute-start(bf16[8,160,256]{2,1,0:T(8,128)(2,1)} %get-tuple-element.319), channel_id=1, source_target_pairs={{0,1},{1,0},{2,3},{3,2},{4,5},{5,4},{6,7},{7,6},{8,9},{9,8},{10,11... | collective-permute-start | bytes 1966088 | tf_op jit(solution)/shard_map/ppermute | solution.py:972
  394.0 15.6 %collective-permute-start.41 = (bf16[8,160,256]{2,1,0:T(8,128)(2,1)}, bf16[8,160,256]{2,1,0:T(8,128)(2,1)S(1)}, u32[]{:S(2)}, u32[]{:S(2)}) collective-permute-start(bf16[8,160,256]{2,1,0:T(8,128)(2,1)} %get-tuple-element.320), channel_id=1, source_target_pairs={{0,4},{1,5},{2,6},{3,7},{4,0},{5,1},{6,2},{7,3},{8,12},{9,13},{10,... | collective-permute-start | bytes 1966088 | tf_op jit(solution)/shard_map/ppermute | solution.py:972
  411.0 12.7 %all-to-all-start.8 = ((f32[32,8,128]{2,1,0:T(8,128)}), f32[32,8,128]{2,1,0:T(8,128)S(1)}, u32[]{:S(2)}, u32[]{:S(2)}) async-start(f32[32,8,128]{2,1,0:T(8,128)} %broadcast_in_dim.102), calls=%async_computation.8 | async-start | bytes 262144 | tf_op jit(solution)/shard_map/all_to_all | solution.py:161
  424.3 17.5 %collective-permute-start.44 = (bf16[2,16,192,256]{3,2,1,0:T(8,128)(2,1)}, bf16[2,16,192,256]{3,2,1,0:T(8,128)(2,1)S(1)}, u32[]{:S(2)}, u32[]{:S(2)}) collective-permute-start(bf16[2,16,192,256]{3,2,1,0:T(8,128)(2,1)} %get-tuple-element.339), channel_id=1, source_target_pairs={{0,2},{1,3},{2,0},{3,1},{4,6},{5,7},{6,4},{7,5},{8,10},{9,11},{10,... | collective-permute-start | bytes 9437192 | tf_op jit(solution)/shard_map/ppermute | solution.py:972
  424.7 14.1 %collective-permute-start.42 = (bf16[4,160,256]{2,1,0:T(8,128)(2,1)}, bf16[4,160,256]{2,1,0:T(8,128)(2,1)S(1)}, u32[]{:S(2)}, u32[]{:S(2)}) collective-permute-start(bf16[4,160,256]{2,1,0:T(8,128)(2,1)} %get-tuple-element.336), channel_id=1, source_target_pairs={{0,4},{1,5},{2,6},{3,7},{4,0},{5,1},{6,2},{7,3},{8,12},{9,13},{10,... | collective-permute-start | bytes 983048 | tf_op jit(solution)/shard_map/ppermute | solution.py:972
  426.4 12.4 %collective-permute-start.43 = (bf16[4,160,256]{2,1,0:T(8,128)(2,1)}, bf16[4,160,256]{2,1,0:T(8,128)(2,1)S(1)}, u32[]{:S(2)}, u32[]{:S(2)}) collective-permute-start(bf16[4,160,256]{2,1,0:T(8,128)(2,1)} %get-tuple-element.337), channel_id=1, source_target_pairs={{0,1},{1,0},{2,3},{3,2},{4,5},{5,4},{6,7},{7,6},{8,9},{9,8},{10,11... | collective-permute-start | bytes 983048 | tf_op jit(solution)/shard_map/ppermute | solution.py:972
  453.4 20.6 %collective-permute-start.48 = (bf16[2,16,144,256]{3,2,1,0:T(8,128)(2,1)}, bf16[2,16,144,256]{3,2,1,0:T(8,128)(2,1)S(1)}, u32[]{:S(2)}, u32[]{:S(2)}) collective-permute-start(bf16[2,16,144,256]{3,2,1,0:T(8,128)(2,1)} %get-tuple-element.363), channel_id=1, source_target_pairs={{0,2},{1,3},{2,0},{3,1},{4,6},{5,7},{6,4},{7,5},{8,10},{9,11},{10,... | collective-permute-start | bytes 7077896 | tf_op jit(solution)/shard_map/ppermute | solution.py:972
  453.5 20.3 %collective-permute-start.46 = (bf16[8,192,256]{2,1,0:T(8,128)(2,1)}, bf16[8,192,256]{2,1,0:T(8,128)(2,1)}, u32[]{:S(2)}, u32[]{:S(2)}) collective-permute-start(bf16[8,192,256]{2,1,0:T(8,128)(2,1)} %get-tuple-element.360), channel_id=1, source_target_pairs={{0,1},{1,0},{2,3},{3,2},{4,5},{5,4},{6,7},{7,6},{8,9},{9,8},{10,11... | collective-permute-start | bytes 2359304 | tf_op jit(solution)/shard_map/ppermute | solution.py:972
  454.1 19.9 %collective-permute-start.47 = (bf16[8,192,256]{2,1,0:T(8,128)(2,1)}, bf16[8,192,256]{2,1,0:T(8,128)(2,1)}, u32[]{:S(2)}, u32[]{:S(2)}) collective-permute-start(bf16[8,192,256]{2,1,0:T(8,128)(2,1)} %get-tuple-element.361), channel_id=1, source_target_pairs={{0,4},{1,5},{2,6},{3,7},{4,0},{5,1},{6,2},{7,3},{8,12},{9,13},{10,... | collective-permute-start | bytes 2359304 | tf_op jit(solution)/shard_map/ppermute | solution.py:972
  454.5 15.2 %collective-permute-start.45 = (bf16[2,2,160,256]{3,2,1,0:T(8,128)(2,1)}, bf16[2,2,160,256]{3,2,1,0:T(8,128)(2,1)}, u32[]{:S(2)}, u32[]{:S(2)}) collective-permute-start(bf16[2,2,160,256]{3,2,1,0:T(8,128)(2,1)} %get-tuple-element.358), channel_id=1, source_target_pairs={{0,8},{1,9},{2,10},{3,11},{4,12},{5,13},{6,14},{7,15},{8,0},{9,1},... | collective-permute-start | bytes 983048 | tf_op jit(solution)/shard_map/ppermute | solution.py:972
  475.5 14.3 %all-to-all-start.9 = ((f32[32,8,128]{2,1,0:T(8,128)}), f32[32,8,128]{2,1,0:T(8,128)S(1)}, u32[]{:S(2)}, u32[]{:S(2)}) async-start(f32[32,8,128]{2,1,0:T(8,128)} %broadcast_in_dim.104), calls=%async_computation.9 | async-start | bytes 262144 | tf_op jit(solution)/shard_map/all_to_all | solution.py:161
  489.9 46.7 %collective-permute-start.59 = (bf16[2,1,160,256]{3,2,1,0:T(8,128)(2,1)S(1)}, bf16[2,1,160,256]{3,2,1,0:T(8,128)(2,1)S(1)}, u32[]{:S(2)}, u32[]{:S(2)}) collective-permute-start(bf16[2,1,160,256]{3,2,1,0:T(8,128)(2,1)S(1)} %copy-done.57), channel_id=1, source_target_pairs={{0,16},{1,17},{2,18},{3,19},{4,20},{5,21},{6,22},{7,23},{8,24},{9,... | collective-permute-start | bytes 491528 | tf_op jit(solution)/shard_map/ppermute | solution.py:972
  502.0 12.0 %collective-permute-start.49 = (bf16[4,192,256]{2,1,0:T(8,128)(2,1)S(1)}, bf16[4,192,256]{2,1,0:T(8,128)(2,1)S(1)}, u32[]{:S(2)}, u32[]{:S(2)}) collective-permute-start(bf16[4,192,256]{2,1,0:T(8,128)(2,1)S(1)} %copy-done.54), channel_id=1, source_target_pairs={{0,4},{1,5},{2,6},{3,7},{4,0},{5,1},{6,2},{7,3},{8,12},{9,13},{10,... | collective-permute-start | bytes 1179656 | tf_op jit(solution)/shard_map/ppermute | solution.py:972
  503.5 12.0 %collective-permute-start.50 = (bf16[4,192,256]{2,1,0:T(8,128)(2,1)S(1)}, bf16[4,192,256]{2,1,0:T(8,128)(2,1)S(1)}, u32[]{:S(2)}, u32[]{:S(2)}) collective-permute-start(bf16[4,192,256]{2,1,0:T(8,128)(2,1)S(1)} %copy-done.53), channel_id=1, source_target_pairs={{0,1},{1,0},{2,3},{3,2},{4,5},{5,4},{6,7},{7,6},{8,9},{9,8},{10,11... | collective-permute-start | bytes 1179656 | tf_op jit(solution)/shard_map/ppermute | solution.py:972
  504.9 21.8 %collective-permute-start.51 = (bf16[8,144,256]{2,1,0:T(8,128)(2,1)S(1)}, bf16[8,144,256]{2,1,0:T(8,128)(2,1)S(1)}, u32[]{:S(2)}, u32[]{:S(2)}) collective-permute-start(bf16[8,144,256]{2,1,0:T(8,128)(2,1)S(1)} %copy-done.51), channel_id=1, source_target_pairs={{0,1},{1,0},{2,3},{3,2},{4,5},{5,4},{6,7},{7,6},{8,9},{9,8},{10,11... | collective-permute-start | bytes 1769480 | tf_op jit(solution)/shard_map/ppermute | solution.py:972
  505.5 21.2 %collective-permute-start.52 = (bf16[8,144,256]{2,1,0:T(8,128)(2,1)S(1)}, bf16[8,144,256]{2,1,0:T(8,128)(2,1)S(1)}, u32[]{:S(2)}, u32[]{:S(2)}) collective-permute-start(bf16[8,144,256]{2,1,0:T(8,128)(2,1)S(1)} %copy-done.50), channel_id=1, source_target_pairs={{0,4},{1,5},{2,6},{3,7},{4,0},{5,1},{6,2},{7,3},{8,12},{9,13},{10,... | collective-permute-start | bytes 1769480 | tf_op jit(solution)/shard_map/ppermute | solution.py:972
  530.7 68.0 %all-to-all-start.10 = ((bf16[32,32,512]{2,1,0:T(8,128)(2,1)}), bf16[32,32,512]{2,1,0:T(8,128)(2,1)S(1)}, u32[]{:S(2)}, u32[]{:S(2)}) async-start(bf16[32,32,512]{2,1,0:T(8,128)(2,1)} %bitcast.42), calls=%async_computation.10 | async-start | bytes 2097152 | tf_op jit(solution)/shard_map/all_to_all | solution.py:1400
  534.0 28.1 %collective-permute-start.53 = (bf16[2,2,192,256]{3,2,1,0:T(8,128)(2,1)S(1)}, bf16[2,2,192,256]{3,2,1,0:T(8,128)(2,1)S(1)}, u32[]{:S(2)}, u32[]{:S(2)}) collective-permute-start(bf16[2,2,192,256]{3,2,1,0:T(8,128)(2,1)S(1)} %copy-done.52), channel_id=1, source_target_pairs={{0,8},{1,9},{2,10},{3,11},{4,12},{5,13},{6,14},{7,15},{8,0},{9,1},... | collective-permute-start | bytes 1179656 | tf_op jit(solution)/shard_map/ppermute | solution.py:972
  542.8 31.0 %collective-permute-start.54 = (bf16[4,144,256]{2,1,0:T(8,128)(2,1)S(1)}, bf16[4,144,256]{2,1,0:T(8,128)(2,1)S(1)}, u32[]{:S(2)}, u32[]{:S(2)}) collective-permute-start(bf16[4,144,256]{2,1,0:T(8,128)(2,1)S(1)} %copy-done.56), channel_id=1, source_target_pairs={{0,4},{1,5},{2,6},{3,7},{4,0},{5,1},{6,2},{7,3},{8,12},{9,13},{10,... | collective-permute-start | bytes 884744 | tf_op jit(solution)/shard_map/ppermute | solution.py:972
  544.4 29.5 %collective-permute-start.55 = (bf16[4,144,256]{2,1,0:T(8,128)(2,1)S(1)}, bf16[4,144,256]{2,1,0:T(8,128)(2,1)S(1)}, u32[]{:S(2)}, u32[]{:S(2)}) collective-permute-start(bf16[4,144,256]{2,1,0:T(8,128)(2,1)S(1)} %copy-done.55), channel_id=1, source_target_pairs={{0,1},{1,0},{2,3},{3,2},{4,5},{5,4},{6,7},{7,6},{8,9},{9,8},{10,11... | collective-permute-start | bytes 884744 | tf_op jit(solution)/shard_map/ppermute | solution.py:972
  564.8 12.3 %collective-permute-start.58 = (bf16[2,1,192,256]{3,2,1,0:T(8,128)(2,1)}, bf16[2,1,192,256]{3,2,1,0:T(8,128)(2,1)S(1)}, u32[]{:S(2)}, u32[]{:S(2)}) collective-permute-start(bf16[2,1,192,256]{3,2,1,0:T(8,128)(2,1)} %get-tuple-element.424), channel_id=1, source_target_pairs={{0,16},{1,17},{2,18},{3,19},{4,20},{5,21},{6,22},{7,23},{8,24},{9,... | collective-permute-start | bytes 589832 | tf_op jit(solution)/shard_map/ppermute | solution.py:972
  (82 other events, 549.5 us)
Sparse Core Ops, SparseCore 0:
  18.8 74.1 all-gather.2
  154.4 57.1 all-gather.4

commit v3 on v2

v3 whole, which is shorter than its diff:
```python
from functools import partial

import jax
import jax.numpy as jnp
from jax import lax
from jax.experimental import pallas as pl
from jax.experimental.pallas import tpu as pltpu
from jax.sharding import PartitionSpec as P
import numpy as np

MID = 512
C_OUT = 2048
FRAMES = 4
GROUP = 128
SHIFT = 16
SQUEEZE = 32
SIDES = (4, 6, 7)
AXES = ("dp", "fsdp")
EPS = 1e-05
HIGHEST = lax.Precision.HIGHEST
F32 = jnp.float32
BF16 = jnp.bfloat16

ROWS = (64, 192, 224)
CUTS = (0, 64, 256, 480)
R = 480


def row_tables():
    frame = np.zeros(R, np.int32)
    row = np.zeros(R, np.int32)
    col = np.zeros(R, np.int32)
    group = np.zeros(R, np.int32)
    at = 0
    for a in range(2):
        for i in range(4):
            for p in range(2):
                for j in range(4):
                    frame[at], row[at], col[at], group[at] = 2 * a + p, i, j, 0
                    at += 1
    for g in (1, 2):
        for f in range(4):
            for i in range(SIDES[g]):
                for j in range(8):
                    frame[at], row[at], col[at], group[at] = f, i, j, g
                    at += 1
    side = np.array(SIDES)[group]
    return group, frame, row, col, (col < side), side


GROUP_OF, FRAME_OF, ROW_OF, COL_OF, VALID, SIDE_OF = row_tables()
SLOT_OF = GROUP_OF * FRAMES + FRAME_OF


def window_table():
    table = np.zeros((12, 9, R), np.float32)
    for r in range(R):
        if not VALID[r]:
            continue
        for t in range(9):
            dy, dx = t // 3 - 1, t % 3 - 1
            i, j = ROW_OF[r] - dy, COL_OF[r] - dx
            if 0 <= i < SIDE_OF[r] and 0 <= j < SIDE_OF[r]:
                table[SLOT_OF[r], t, r] = 1.0
    return table.reshape(108, R)


WINDOWS = window_table()
SPREAD = ((SLOT_OF[:, None] == np.arange(12)[None]) & VALID[:, None]).astype(np.float32)
NPIX = np.repeat(np.array([s * s for s in SIDES], np.float32), FRAMES)


def split(v):
    c = v.shape[-1]
    return (
        v[0:64].reshape(2, 4, 8, c),
        v[64:256].reshape(4, 6, 8, c),
        v[256:480].reshape(4, 7, 8, c),
    )


def join(parts):
    return jnp.concatenate([p.reshape(-1, p.shape[-1]) for p in parts], axis=0)


def shift_rows(v, dy):
    if dy == 0:
        return v
    out = []
    for p in split(v):
        zero = jnp.zeros_like(p[:, :1])
        out.append(
            jnp.concatenate([p[:, 1:], zero] if dy > 0 else [zero, p[:, :-1]], axis=1)
        )
    return join(out)


def dot(a, b):
    return jnp.dot(a, b, preferred_element_type=F32)


def dot_nt(a, b):
    return lax.dot_general(a, b, (((1,), (1,)), ((), ())), preferred_element_type=F32)


def dot_tn(a, b):
    return lax.dot_general(a, b, (((0,), (0,)), ((), ())), preferred_element_type=F32)


def normalize(a, st):
    mean, rstd, gain, bias = st
    xhat = (a - mean) * rstd
    return xhat, xhat * gain + bias


def silu(u):
    return u * jax.nn.sigmoid(u)


def silu_grad(u):
    s = jax.nn.sigmoid(u)
    return s * (1.0 + u * (1.0 - s))


def norm_back(g, xhat, mask, st, tot, count):
    mean, rstd, gain, bias = st
    return gain * rstd * (g - mask * (tot[1] + xhat * tot[0]) / count)


TAPS2 = []
for kh in range(3):
    for kw in range(3):
        pr, dy = (1, -1) if kh == 0 else ((0, 0) if kh == 1 else (1, 0))
        pc, dx = (1, -1) if kw == 0 else ((0, 0) if kw == 1 else (1, 0))
        TAPS2.append((pr * 2 + pc, dy, dx, kh * 3 + kw))


FREE = pl.CostEstimate(flops=0, bytes_accessed=0, transcendentals=0)
LONG = pl.CostEstimate(flops=20 * 10**9, bytes_accessed=60 * 10**6, transcendentals=0)
VMEM = pl.BlockSpec(memory_space=pltpu.VMEM)
SMEM = pl.BlockSpec(memory_space=pltpu.SMEM)


def call(kernel, outs, n_in, scratch=(), scalars=1):
    return pl.pallas_call(
        kernel,
        out_shape=outs,
        in_specs=[SMEM] * scalars + [VMEM] * n_in,
        out_specs=[VMEM] * len(outs),
        scratch_shapes=list(scratch),
        compiler_params=LIMIT,
        cost_estimate=FREE,
    )


def like(shape, dtype=F32):
    return jax.ShapeDtypeStruct(shape, dtype)


def kshift_cols(v, dx):
    if dx == 0:
        return v
    c = v.shape[-1]
    rolled = pltpu.roll(v.reshape(R // 8, 8, c), 1 if dx < 0 else 7, 1).reshape(R, c)
    top = rolled[:64]
    place = lax.broadcasted_iota(jnp.int32, (64, c), 0) & 3
    top = jnp.where(place == (0 if dx < 0 else 3), 0.0, top)
    return jnp.concatenate([top, rolled[64:]], axis=0)


def kshift_frame(v, df):
    c = v.shape[-1]
    pc, pm, pf = split(v)
    half = pltpu.roll(pc.reshape(8, 8, c), 4, 1).reshape(2, 4, 8, c)
    zero = jnp.zeros_like(half[:1])
    first = lax.broadcasted_iota(jnp.int32, (2, 4, 8, c), 2) < 4
    if df < 0:
        oc = jnp.where(first, jnp.concatenate([zero, half[:-1]], axis=0), half)
    else:
        oc = jnp.where(first, half, jnp.concatenate([half[1:], zero], axis=0))
    out = [oc]
    for p in (pm, pf):
        zero = jnp.zeros_like(p[:1])
        out.append(jnp.concatenate([p[1:], zero] if df > 0 else [zero, p[:-1]], axis=0))
    return join(out)


def ktime_shift(v, back):
    lane = lax.broadcasted_iota(jnp.int32, v.shape, 1)
    a = kshift_frame(v, 1 if back else -1)
    b = kshift_frame(v, -1 if back else 1)
    return jnp.where(lane < SHIFT, a, jnp.where(lane < 2 * SHIFT, b, v))


def cols(st, c, w=128):
    return tuple(v[:, c * w : (c + 1) * w] for v in st)


def three(v):
    a = v.astype(BF16)
    rest = v - a.astype(F32)
    b = rest.astype(BF16)
    c = (rest - b.astype(F32)).astype(BF16)
    return a, b, c


def exact_dot(table, v):
    return sum(dot(table, part) for part in three(v))


def frame_sums(v):
    pc, pm, pf = split(v)
    first = lax.broadcasted_iota(jnp.int32, (2, 4, 8, v.shape[-1]), 2) < 4
    even = jnp.sum(jnp.where(first, pc, 0.0), axis=(1, 2))
    odd = jnp.sum(jnp.where(first, 0.0, pc), axis=(1, 2))
    pm = jnp.sum(pm, axis=(1, 2))
    pf = jnp.sum(pf, axis=(1, 2))
    rows = [even[0:1], odd[0:1], even[1:2], odd[1:2]]
    rows += [pm[f : f + 1] for f in range(4)] + [pf[f : f + 1] for f in range(4)]
    return jnp.concatenate(rows + [jnp.zeros((4, v.shape[-1]), F32)], axis=0)


def window_tables():
    pixel = WINDOWS.reshape(12, 9, R)
    table = np.zeros((160, R), np.float32)
    for slot in range(12):
        if slot % 4 < 3:
            for t in range(9):
                table[t * 16 + slot] = pixel[slot + 1, t]
        table[144 + slot] = pixel[slot, 4]
    spread = np.zeros((R, 16), np.float32)
    spread[:, :12] = SPREAD
    return table, np.concatenate([spread] * 3, axis=1)


TABLE, SPREAD3 = window_tables()


def phase_tables():
    out = []
    for side, pairs in zip(SIDES, (2, 1, 1)):
        high = 2 * side
        wide = 4 if side == 4 else 8
        count = side * wide * pairs
        t = np.zeros((4 * count, pairs * high * 16), np.float32)
        for ph in range(4):
            for p in range(pairs):
                for i in range(side):
                    for j in range(side):
                        row = ph * count + (i * pairs + p) * wide + j
                        at = (p * high + 2 * i + ph // 2) * 16 + 2 * j + ph % 2
                        t[row, at] = 1.0
        out.append(t)
    return out


PHASES = phase_tables()


def split_phases(alive, xc, xm, xf, tc, tm, tf, out_ref, bc, bm, bf):
    @pl.when(pl.program_id(0) == 0)
    def _():
        for b in (bc, bm, bf):
            b[...] = jnp.zeros_like(b)

    pieces = [[], [], [], []]
    lanes = out_ref.shape[-1]
    for g, (x, table, buf) in enumerate(((xc, tc, bc), (xm, tm, bm), (xf, tf, bf))):
        pairs = buf.shape[0]
        side = 2 * SIDES[g]
        for f in range(0, FRAMES, pairs):
            for p in range(pairs):
                live = alive[g * FRAMES + f + p] > 0.0
                buf[p, :, 0:side, :] = jnp.where(live, x[f + p], jnp.zeros_like(x[f + p]))
            y = dot(table[...], buf[...].reshape(-1, lanes))
            step = y.shape[0] // 4
            for ph in range(4):
                pieces[ph].append(y[ph * step : (ph + 1) * step])
    for ph in range(4):
        out_ref[ph] = jnp.concatenate(pieces[ph], axis=0).astype(BF16)


def clip_blocks(lanes):
    return [
        pl.BlockSpec((FRAMES, 2 * s, 2 * s, lanes), lambda c: (0, 0, 0, c)) for s in SIDES
    ]


def whole(v):
    return pl.BlockSpec(v.shape, lambda c: (0,) * v.ndim)


LIMIT = pltpu.CompilerParams(vmem_limit_bytes=60 * 2**20)


def run_split(alive, clips, tables):
    lanes = 256
    c_in = clips[0].shape[-1]
    return pl.pallas_call(
        split_phases,
        grid=(c_in // lanes,),
        out_shape=like((4, R, c_in), BF16),
        in_specs=[SMEM] + clip_blocks(lanes) + [whole(t) for t in tables],
        out_specs=pl.BlockSpec((4, R, lanes), lambda c: (0, 0, c)),
        scratch_shapes=[
            pltpu.VMEM((2 if s == 4 else 1, 2 * s, 16, lanes), BF16) for s in SIDES
        ],
        compiler_params=LIMIT,
        cost_estimate=FREE,
    )(alive, *clips, *tables)


def tiled(m, lanes):
    return jnp.concatenate([m] * (lanes // 128), axis=1)


class Flow:
    def __init__(self, far, near, sem, parts, axis, out):
        self.far, self.v, self.sem = far, near, sem
        self.parts, self.axis, self.out = parts, axis, out

    def copy(self, c):
        size = self.v.shape[self.axis] // self.parts
        at = [slice(None)] * len(self.v.shape)
        at[self.axis] = pl.ds(c * size, size)
        a, b = self.far.at[tuple(at)], self.v.at[tuple(at)]
        return pltpu.make_async_copy(*((b, a) if self.out else (a, b)), self.sem.at[c])

    def get(self, c=0):
        self.copy(c).wait()

    def put(self, c=0):
        self.copy(c).start()


class Plain:
    def __init__(self, ref):
        self.v = ref

    def get(self, c=0):
        pass

    def put(self, c=0):
        pass


def plain_call(body, scalars, small, ins, outs, small_outs=(), scratch=(), only=()):
    n_s, n_m, n_i, n_o, n_p = len(scalars), len(small), len(ins), len(outs), len(small_outs)

    def kernel(*refs):
        at = 0

        def take(k):
            nonlocal at
            at += k
            return refs[at - k : at]

        s, m, fi, fo, so = take(n_s), take(n_m), take(n_i), take(n_o), take(n_p)
        body(s, m, [Plain(r) for r in fi], [Plain(r) for r in fo], so, take(len(scratch)))

    return pl.pallas_call(
        kernel,
        out_shape=[like(o[0], o[1]) for o in outs] + list(small_outs),
        in_specs=[SMEM] * n_s + [VMEM] * (n_m + n_i),
        out_specs=[VMEM] * (n_o + n_p),
        scratch_shapes=list(scratch),
        compiler_params=LIMIT,
        cost_estimate=FREE,
    )(*scalars, *small, *[v for v, _, _ in ins])


def flow_call(body, scalars, small, ins, outs, small_outs=(), scratch=(), only=(), cost=FREE):
    n_s, n_m, n_i, n_o, n_p = len(scalars), len(small), len(ins), len(outs), len(small_outs)

    def kernel(*refs):
        at = 0

        def take(k):
            nonlocal at
            at += k
            return refs[at - k : at]

        s, m, far_in, far_out, so = take(n_s), take(n_m), take(n_i), take(n_o), take(n_p)
        near_in, near_out, extra = take(n_i), take(n_o), take(len(scratch))
        sem_in, sem_out = take(n_i), take(n_o)
        fi = [
            Flow(f, v, q, p, a, False)
            for f, v, q, (_, p, a) in zip(far_in, near_in, sem_in, ins)
        ]
        fo = [
            Flow(f, v, q, p, a, True)
            for f, v, q, (_, _, p, a) in zip(far_out, near_out, sem_out, outs)
        ]
        for c in range(max([f.parts for f in fi])):
            for i, f in enumerate(fi):
                if c < f.parts and (c == 0 or i not in only):
                    f.put(c)
        body(s, m, fi, fo, so, extra)
        for f in fo:
            for c in range(f.parts):
                f.get(c)

    any_space = pl.BlockSpec(memory_space=pl.ANY)
    return pl.pallas_call(
        kernel,
        out_shape=[like(o[0], o[1]) for o in outs] + list(small_outs),
        in_specs=[SMEM] * n_s + [VMEM] * n_m + [any_space] * n_i,
        out_specs=[any_space] * n_o + [VMEM] * n_p,
        scratch_shapes=[pltpu.VMEM(v.shape, v.dtype) for v, _, _ in ins]
        + [pltpu.VMEM(o[0], o[1]) for o in outs]
        + list(scratch)
        + [pltpu.SemaphoreType.DMA((p,)) for _, p, _ in ins]
        + [pltpu.SemaphoreType.DMA((o[2],)) for o in outs],
        compiler_params=LIMIT,
        cost_estimate=cost,
    )(*scalars, *small, *[v for v, _, _ in ins])


def put_rows(ref, row, vec):
    for j in range(vec.shape[1] // 128):
        ref[row + j : row + j + 1, :] = vec[:, j * 128 : (j + 1) * 128]


def get_rows(t, row, width):
    return jnp.concatenate([t[row + j : row + j + 1, :] for j in range(width // 128)], axis=1)


def spread_rows(ref, rows):
    @pl.loop(0, ref.shape[0])
    def _(i):
        ref[i] = rows


def pack_sums(a, b):
    out = []
    for v in (a, b):
        v = jnp.sum(v, axis=0, keepdims=True)
        out += [v[:, j * 128 : (j + 1) * 128] for j in range(v.shape[1] // 128)]
    return jnp.concatenate(out, axis=0)


def stats_of(got, count, gb, row=0, second=4, width=MID, lane=0):
    mean = get_rows(got, row, width) / count
    var = get_rows(got, second, width) / count - mean * mean
    sl = slice(lane, lane + width)
    return mean, lax.rsqrt(var + EPS), gb[0:1, sl], gb[1:2, sl]


def total_of(ref):
    return jnp.sum(ref[...], axis=0) if len(ref.shape) == 3 else ref[...]


def wide_stats(got, count, gb, c, base=0):
    return stats_of(got, count, gb, base + 4 * c, base + 16 + 4 * c, MID, c * MID)


def enter(s, m, ins, outs, so, extra):
    (x, w), (a1,) = ins, outs
    w.get()
    total = jnp.zeros((8, 128), F32)
    for ph in range(4):
        x.get(ph)
        a = dot(x.v[ph], w.v[...])
        a1.v[ph] = a
        a1.put(ph)
        total = total + pack_sums(a, a * a)
    spread_rows(so[0], total)


def run_enter(n, xph, w1):
    return flow_call(
        enter, (), (), [(w1, 1, 0), (xph, 4, 0)][::-1], [((4, R, MID), F32, 4, 0)],
        [like((n, 8, 128))],
    )


def conv_forward(s, m, ins, outs, so, extra):
    (cnt,), (s0, gb0, mask), (a1, w), (im, a2) = s, m, ins, outs
    live = mask[...]
    st = stats_of(total_of(s0), 4.0 * cnt[0], gb0[...])
    acc = None
    for ph in range(4):
        a1.get(ph)
        taps = [q for q in TAPS2 if q[0] == ph]
        for c in range(4):
            sl = slice(c * 128, (c + 1) * 128)
            stc = cols(st, c)
            h = live * silu(normalize(a1.v[ph, :, sl], stc)[1])
            h = h.astype(BF16).astype(F32)
            for dx in (0, -1):
                if dx and not ph & 1:
                    continue
                moved = kshift_cols(h, dx)
                for _, dy, dx2, t in taps:
                    if dx2 == dx:
                        at = t * MID + c * 128
                        im.v[:, at : at + 128] = shift_rows(moved, dy).astype(BF16)
        for _, _, _, t in taps:
            im.put(t)
        if ph == 0:
            w.get()
        for _, _, _, t in taps:
            sl = slice(t * MID, (t + 1) * MID)
            part = dot(im.v[:, sl], w.v[sl, :])
            acc = part if acc is None else acc + part
    acc = acc * tiled(live, MID)
    a2.v[...] = acc
    a2.put()
    spread_rows(so[0], pack_sums(acc, acc * acc))


def run_conv_forward(n, cnt, s0, gb0, mask, a1, w):
    return flow_call(
        conv_forward, (cnt,), (s0, gb0, mask), [(a1, 4, 0), (w, 1, 0)],
        [((R, 9 * MID), BF16, 9, 1), ((R, MID), F32, 1, 0)], [like((n, 8, 128))],
    )


def joint_norm(s, m, ins, outs, so, extra):
    (cnt,), (s23, gb2, gb3, mask), (a3, ap, w2), (y1, yl, b1) = s, m, ins, outs
    live = tiled(mask[...], MID)
    got = s23[...]
    acc = None
    for c in range(4):
        sl = slice(c * MID, (c + 1) * MID)
        a3.get(c)
        ap.get(c)
        gbs = [b[:, sl] for b in (gb2, gb3)]
        _, u2 = normalize(a3.v[:, sl], stats_of(got[c], cnt[0], gbs[0]))
        _, u3 = normalize(ap.v[:, sl], stats_of(got[c], cnt[0], gbs[1], 8, 12))
        y = live * silu(u2 + u3)
        y1.v[:, sl] = y
        y1.put(c)
        low = y.astype(BF16)
        yl.v[:, sl] = low
        yl.put(c)
        w2.get(c)
        part = dot(low, w2.v[sl, :])
        acc = part if acc is None else acc + part
    b1.v[...] = acc
    b1.put()
    spread_rows(so[0], pack_sums(acc, acc * acc))


def run_joint_norm(n, cnt, s23, gb2, gb3, mask, a3, ap, w2):
    return flow_call(
        joint_norm, (cnt,), (s23, gb2, gb3, mask), [(a3, 4, 1), (ap, 4, 1), (w2, 4, 0)],
        [((R, C_OUT), F32, 4, 1), ((R, C_OUT), BF16, 4, 1), ((R, MID), F32, 1, 0)],
        [like((n, 8, 128))],
    )


def mix_forward(s, m, ins, outs, so, extra):
    (cnt,) = s
    s4, gb4, mask, wdown, wup, kern, scale, table, spread = m
    (b1, wmix), (z, zl, mixed, im) = ins, outs
    sig_ref, pooled_ref, wnext_ref, sums_ref = so
    live = mask[...]
    st = stats_of(total_of(s4), cnt[0], gb4[...])
    b1.get()
    for c in range(4):
        sl = slice(c * 128, (c + 1) * 128)
        v = live * silu(normalize(b1.v[:, sl], cols(st, c))[1])
        z.v[:, sl] = v
        zl.v[:, sl] = v.astype(BF16)
    z.put()
    zl.put()
    r = dot(zl.v[...], wdown[...])
    ws = exact_dot(table[...], r)
    wnext_ref[...] = ws[:144]
    pooled = -ws[144:160]
    for t in range(9):
        pooled = pooled + kern[t : t + 1, :] * ws[t * 16 : (t + 1) * 16]
    pooled = scale[...] * pooled
    pooled_ref[...] = pooled
    sig = jax.nn.sigmoid(jnp.dot(pooled, wup[...], precision=HIGHEST))
    sig_ref[...] = sig
    gates = jnp.concatenate(three(0.5 + sig), axis=0)
    prev = None
    sums = []
    for c in range(4):
        sl = slice(c * 128, (c + 1) * 128)
        v = z.v[:, sl] * dot(spread[...], gates[:, sl])
        if c > 0:
            low = ktime_shift(v + prev, False).astype(BF16).astype(F32)
            for dx in (-1, 0, 1):
                moved = kshift_cols(low, dx)
                for dy in (-1, 0, 1):
                    t = (dy + 1) * 3 + dx + 1
                    im.v[c - 1, :, t * 128 : (t + 1) * 128] = shift_rows(moved, dy).astype(BF16)
            im.put(c - 1)
            if c == 1:
                wmix.get()
            v = live * dot(im.v[c - 1], wmix.v[c - 1])
        prev = v
        mixed.v[:, sl] = v
        sums.append((jnp.sum(v, axis=0, keepdims=True), jnp.sum(v * v, axis=0, keepdims=True)))
    mixed.put()
    spread_rows(sums_ref, jnp.concatenate([q[0] for q in sums] + [q[1] for q in sums], axis=0))


def run_mix_forward(n, cnt, s4, gb4, mask, wdown, wup, kern, scale, table, spread, b1, wmix):
    return flow_call(
        mix_forward, (cnt,), (s4, gb4, mask, wdown, wup, kern, scale, table, spread),
        [(b1, 1, 0), (wmix, 1, 0)],
        [((R, MID), F32, 1, 0), ((R, MID), BF16, 1, 0), ((R, MID), F32, 1, 0),
         ((3, R, 9 * GROUP), BF16, 3, 0)],
        [like((16, MID)), like((16, SQUEEZE)), like((144, SQUEEZE)), like((n, 8, 128))],
    )


def expand_last(s, m, ins, outs, so, extra):
    (cnt,), (s5, gb5, mask), (mixed, we2), (w, b3), (rows,) = s, m, ins, outs, extra
    live = tiled(mask[...], MID)
    mixed.get()
    h = live * silu(normalize(mixed.v[...], stats_of(total_of(s5), cnt[0], gb5[...]))[1])
    w.v[...] = h.astype(BF16)
    w.put()
    for c in range(4):
        sl = slice(c * MID, (c + 1) * MID)
        we2.get(c)
        a = dot(w.v[...], we2.v[:, sl])
        b3.v[:, sl] = a
        b3.put(c)
        put_rows(rows, 4 * c, jnp.sum(a, axis=0, keepdims=True))
        put_rows(rows, 16 + 4 * c, jnp.sum(a * a, axis=0, keepdims=True))
    so[0][...] = rows[...]


def run_expand_last(cnt, s5, gb5, mask, mixed, we2):
    return plain_call(
        expand_last, (cnt,), (s5, gb5, mask), [(mixed, 1, 0), (we2, 4, 1)],
        [((R, MID), BF16, 1, 0), ((R, C_OUT), F32, 4, 1)], [like((32, 128))],
        [pltpu.VMEM((32, 128), F32)],
    )


def last_norm(s, m, ins, outs, so, extra):
    (cnt,), (s6, gb6, mask), (b3, y1, cc, cm, cf), (oc, om, of, g6) = s, m, ins, outs
    bc, bm, bf, rows = extra
    for b in (bc, bm, bf):
        b[...] = jnp.zeros_like(b)
    live = tiled(mask[...], MID)
    got = total_of(s6)
    for c in range(4):
        sl = slice(c * MID, (c + 1) * MID)
        for f in ins:
            f.get(c)
        for f in range(FRAMES):
            p = f % 2
            bc[f // 2, :, p * 4 : p * 4 + 4, :] = cc.v[f, :, :, sl].astype(F32)
        bm[:, :, 0:6, :] = cm.v[..., sl].astype(F32)
        bf[:, :, 0:7, :] = cf.v[..., sl].astype(F32)
        cot = join((bc[...], bm[...], bf[...]))
        x, u = normalize(b3.v[:, sl], wide_stats(got, cnt[0], gb6[...], c))
        u = u + y1.v[:, sl]
        sg = jax.nn.sigmoid(u)
        pc, pm, pf = split(live * u * sg)
        for f in range(FRAMES):
            p = f % 2
            oc.v[f, :, :, sl] = pc[f // 2, :, p * 4 : p * 4 + 4, :].astype(BF16)
        om.v[..., sl] = pm[:, :, 0:6, :].astype(BF16)
        of.v[..., sl] = pf[:, :, 0:7, :].astype(BF16)
        g = cot * live * (sg * (1.0 + u * (1.0 - sg)))
        g6.v[:, sl] = g
        for f in outs:
            f.put(c)
        put_rows(rows, 4 * c, jnp.sum(g * x, axis=0, keepdims=True))
        put_rows(rows, 16 + 4 * c, jnp.sum(g, axis=0, keepdims=True))
    so[0][...] = rows[...]


def run_last_norm(cnt, s6, gb6, mask, b3, y1, cots):
    return flow_call(
        last_norm, (cnt,), (s6, gb6, mask), [(b3, 4, 1), (y1, 4, 1)] + [(v, 4, 3) for v in cots],
        [((FRAMES, q, q, C_OUT), BF16, 4, 3) for q in SIDES] + [((R, C_OUT), F32, 4, 1)],
        [like((32, 128))],
        [pltpu.VMEM((2 if q == 4 else 4, q, 8, MID), F32) for q in SIDES]
        + [pltpu.VMEM((32, 128), F32)],
    )


def back_rows(tot, c=None):
    if c is None:
        return get_rows(tot, 0, MID), get_rows(tot, 4, MID)
    return get_rows(tot, 4 * c, MID), get_rows(tot, 16 + 4 * c, MID)


def last_back(s, m, ins, outs, so, extra):
    (cnt,), (t6, s6, gb6, mask, s5, gb5), (g6, b3, w, we2, mixed), (ge2, g5) = s, m, ins, outs
    live = tiled(mask[...], MID)
    tot, got = total_of(t6), total_of(s6)
    w.get()
    acc = None
    for c in range(4):
        sl = slice(c * MID, (c + 1) * MID)
        g6.get(c)
        b3.get(c)
        st = wide_stats(got, cnt[0], gb6[...], c)
        x, _ = normalize(b3.v[:, sl], st)
        d = norm_back(g6.v[:, sl], x, live, st, back_rows(tot, c), cnt[0]).astype(BF16)
        ge2.v[:, sl] = dot_tn(w.v[...], d).astype(BF16)
        ge2.put(c)
        we2.get(c)
        part = dot_nt(d, we2.v[:, sl])
        acc = part if acc is None else acc + part
    mixed.get()
    x, u = normalize(mixed.v[...], stats_of(total_of(s5), cnt[0], gb5[...]))
    g = acc * live * silu_grad(u)
    g5.v[...] = g
    g5.put()
    spread_rows(so[0], pack_sums(g * x, g))


def run_last_back(n, cnt, t6, s6, gb6, mask, s5, gb5, g6, b3, w, we2, mixed):
    return plain_call(
        last_back, (cnt,), (t6, s6, gb6, mask, s5, gb5),
        [(g6, 4, 1), (b3, 4, 1), (w, 1, 0), (we2, 4, 1), (mixed, 1, 0)],
        [((MID, C_OUT), BF16, 4, 1), ((R, MID), F32, 1, 0)], [like((n, 8, 128))],
    )


def mix_backward(s, m, ins, outs, so, extra):
    (cnt,) = s
    (t5, s5, gb5, mask, sig, pooled, wnext, wup, kern, scale, table_t, spread, wdown, s4, gb4) = m
    (g5, mixed, imt, wmix_t, z, zl, b1), (g4, gmix) = ins, outs
    gkern_ref, gdown_ref, gup_ref, sums_ref = so
    gim, gzg = extra
    live = mask[...]
    count = cnt[0]
    st = stats_of(total_of(s5), count, gb5[...])
    tot = back_rows(total_of(t5))
    g5.get()
    mixed.get()
    carried = None
    gsig = []
    for c in (3, 2, 1, 0):
        sl = slice(c * 128, (c + 1) * 128)
        stc = cols(st, c)
        x, _ = normalize(mixed.v[:, sl], stc)
        gm = norm_back(g5.v[:, sl], x, live, stc, cols(tot, c), count)
        if carried is not None:
            gm = gm + carried
        if c > 0:
            low = (live * gm).astype(BF16)
            imt.get(c - 1)
            gmix.v[c - 1] = dot_tn(imt.v[c - 1], low).astype(BF16)
            gmix.put(c - 1)
            low = low.astype(F32)
            for dx in (-1, 0, 1):
                moved = kshift_cols(low, -dx)
                for dy in (-1, 0, 1):
                    t = (dy + 1) * 3 + dx + 1
                    gim[:, t * 128 : (t + 1) * 128] = shift_rows(moved, -dy).astype(BF16)
            if c == 3:
                wmix_t.get()
                z.get()
            gm = ktime_shift(dot(gim[...], wmix_t.v[c - 1]), True)
            carried = gm
        gzg[:, sl] = gm
        gsig.insert(0, frame_sums(gm * z.v[:, sl]))
    sg = sig[...]
    ge = jnp.concatenate(gsig, axis=1) * sg * (1.0 - sg)
    gup_ref[...] = lax.dot_general(
        pooled[...], ge, (((0,), (0,)), ((), ())), precision=HIGHEST, preferred_element_type=F32
    )
    q = scale[...] * lax.dot_general(
        ge, wup[...], (((1,), (1,)), ((), ())), precision=HIGHEST, preferred_element_type=F32
    )
    coef = []
    gk = []
    for t in range(9):
        gk.append(jnp.sum(q * wnext[t * 16 : (t + 1) * 16], axis=0, keepdims=True))
        coef.append(kern[t : t + 1, :] * q)
    gk = jnp.concatenate(gk + [jnp.zeros((7, SQUEEZE), F32)], axis=0)
    gkern_ref[...] = jnp.concatenate([gk, jnp.zeros((16, 128 - SQUEEZE), F32)], axis=1)
    coef = jnp.concatenate(coef + [-q], axis=0)
    gr = exact_dot(table_t[...], coef).astype(BF16)
    zl.get()
    gdown_ref[...] = dot_tn(zl.v[...], gr)
    gates = jnp.concatenate(three(0.5 + sg), axis=0)
    st = stats_of(total_of(s4), count, gb4[...])
    b1.get()
    sums = []
    for c in range(4):
        sl = slice(c * 128, (c + 1) * 128)
        gz = gzg[:, sl] * dot(spread[...], gates[:, sl]) + dot_nt(gr, wdown[sl, :])
        x, u = normalize(b1.v[:, sl], cols(st, c))
        g = gz * live * silu_grad(u)
        g4.v[:, sl] = g
        sums.append((jnp.sum(g * x, axis=0, keepdims=True), jnp.sum(g, axis=0, keepdims=True)))
    g4.put()
    spread_rows(sums_ref, jnp.concatenate([v[0] for v in sums] + [v[1] for v in sums], axis=0))


def run_mix_backward(n, cnt, small, g5, mixed, im, wmix_t, z, zl, b1):
    return plain_call(
        mix_backward, (cnt,), small,
        [(g5, 1, 0), (mixed, 1, 0), (im, 3, 0), (wmix_t, 1, 0), (z, 1, 0), (zl, 1, 0), (b1, 1, 0)],
        [((R, MID), F32, 1, 0), ((3, 9 * GROUP, GROUP), BF16, 3, 0)],
        [like((16, 128)), like((MID, SQUEEZE)), like((SQUEEZE, MID)), like((n, 8, 128))],
        [pltpu.VMEM((R, 9 * GROUP), BF16), pltpu.VMEM((R, MID), F32)],
    )


def spatial_grad(s, m, ins, outs, so, extra):
    (cnt,), (t1, s1, gb1, mask), (g1, a2, im), (d1, gsp) = s, m, ins, outs
    live = tiled(mask[...], MID)
    st = stats_of(total_of(s1), cnt[0], gb1[...])
    g1.get()
    a2.get()
    x, _ = normalize(a2.v[...], st)
    d = norm_back(g1.v[...], x, live, st, back_rows(total_of(t1)), cnt[0]).astype(BF16)
    d1.v[...] = d
    d1.put()
    for t in range(9):
        sl = slice(t * MID, (t + 1) * MID)
        im.get(t)
        gsp.v[sl, :] = dot_tn(im.v[:, sl], d1.v[...]).astype(BF16)
        gsp.put(t)


def run_spatial_grad(cnt, small, g1, a2, im):
    return plain_call(
        spatial_grad, (cnt,), small, [(g1, 1, 0), (a2, 1, 0), (im, 9, 1)],
        [((R, MID), BF16, 1, 0), ((9 * MID, MID), BF16, 9, 0)],
    )


def conv_back(s, m, ins, outs, so, extra):
    (cnt,), (s0, gb0, mask), (d1, w, a1), (g0,), (moved_ref,) = s, m, ins, outs, extra
    live = mask[...]
    d1.get()
    for c in range(4):
        sl = slice(c * 128, (c + 1) * 128)
        d = d1.v[:, sl].astype(F32)
        for dx in (0, 1):
            moved = kshift_cols(d, dx)
            for dy in (0, 1):
                moved_ref[dy * 2 + dx, :, sl] = shift_rows(moved, dy).astype(BF16)
    st = stats_of(total_of(s0), 4.0 * cnt[0], gb0[...])
    w.get()
    total = jnp.zeros((8, 128), F32)
    for ph in range(4):
        gh = None
        for p, dy, dx, t in TAPS2:
            if p == ph:
                part = dot_nt(moved_ref[-dy * 2 - dx], w.v[t * MID : (t + 1) * MID, :])
                gh = part if gh is None else gh + part
        a1.get(ph)
        sums = []
        for c in range(4):
            sl = slice(c * 128, (c + 1) * 128)
            x, u = normalize(a1.v[ph, :, sl], cols(st, c))
            g = gh[:, sl] * live * silu_grad(u)
            g0.v[ph, :, sl] = g
            sums.append((jnp.sum(g * x, axis=0, keepdims=True), jnp.sum(g, axis=0, keepdims=True)))
        g0.put(ph)
        total = total + jnp.concatenate([v[0] for v in sums] + [v[1] for v in sums], axis=0)
    spread_rows(so[0], total)


def run_conv_back(n, cnt, small, d1, w, a1):
    return plain_call(
        conv_back, (cnt,), small, [(d1, 1, 0), (w, 1, 0), (a1, 4, 0)],
        [((4, R, MID), F32, 4, 0)], [like((n, 8, 128))], [pltpu.VMEM((4, R, MID), BF16)],
    )


def first_grads(s, m, ins, outs, so, extra):
    (cnt,), (t0, s0, gb0, mask), (g0, a1, x), (d0, gr1) = s, m, ins, outs
    live = mask[...]
    count = 4.0 * cnt[0]
    st = stats_of(total_of(s0), count, gb0[...])
    tot = back_rows(total_of(t0))
    acc = None
    for ph in range(4):
        g0.get(ph)
        a1.get(ph)
        for c in range(4):
            sl = slice(c * 128, (c + 1) * 128)
            stc = cols(st, c)
            xh, _ = normalize(a1.v[ph, :, sl], stc)
            d = norm_back(g0.v[ph, :, sl], xh, live, stc, cols(tot, c), count)
            d0.v[ph, :, sl] = d.astype(BF16)
        d0.put(ph)
        x.get(ph)
        part = dot_tn(x.v[ph], d0.v[ph])
        acc = part if acc is None else acc + part
    gr1.v[...] = acc.astype(BF16)
    gr1.put()


def run_first_grads(cnt, small, g0, a1, xph):
    return flow_call(
        first_grads, (cnt,), small, [(g0, 4, 0), (a1, 4, 0), (xph, 4, 0)],
        [((4, R, MID), BF16, 4, 0), ((xph.shape[-1], MID), BF16, 1, 0)], cost=LONG,
    )


def wide_grid(kernel, outs, out_specs, ins, in_specs, scratch=(), steps=4):
    return pl.pallas_call(
        kernel,
        grid=(steps,),
        out_shape=outs,
        in_specs=in_specs,
        out_specs=out_specs,
        scratch_shapes=list(scratch),
        compiler_params=LIMIT,
        cost_estimate=FREE,
    )(*ins)


def fixed(shape):
    return pl.BlockSpec(shape, lambda c: (0,) * len(shape))


def column(rows, lanes):
    return pl.BlockSpec((rows, lanes), lambda c: (0, c))


def row_block(rows, width):
    return pl.BlockSpec((rows, width), lambda c: (c, 0))


CHUNK = pl.BlockSpec((1, 16, 128), lambda c: (c, 0, 0))


def accumulate(ref, part):
    first = pl.program_id(0) == 0

    @pl.when(first)
    def _():
        ref[...] = part

    @pl.when(jnp.logical_not(first))
    def _():
        ref[...] = ref[...] + part


def expand_pair(cnt, a2, s1, gb1, mask, w, x, wsk, h_ref, a3_ref, ap_ref, s_ref):
    @pl.when(pl.program_id(0) == 0)
    def _():
        m = tiled(mask[...], MID)
        h = m * silu(normalize(a2[...], stats_of(total_of(s1), cnt[0], gb1[...]))[1])
        h_ref[...] = h.astype(BF16)

    a = dot(h_ref[...], w[...])
    a3_ref[...] = a
    b = dot(x[0], wsk[...])
    ap_ref[...] = b
    s_ref[0] = jnp.concatenate([pack_sums(a, a * a), pack_sums(b, b * b)], axis=0)


def run_expand_pair(cnt, s1, gb1, mask, a2, we1, xph, wsk):
    c_in = xph.shape[-1]
    wide = column(R, MID)
    return wide_grid(
        expand_pair,
        [like((R, MID), BF16), like((R, C_OUT)), like((R, C_OUT)), like((4, 16, 128))],
        [fixed((R, MID)), wide, wide, CHUNK],
        (cnt, a2, s1, gb1, mask, we1, xph, wsk),
        [SMEM, fixed((R, MID)), fixed(s1.shape), fixed((2, MID)), fixed((R, 128)),
         column(MID, MID), pl.BlockSpec((1, R, c_in), lambda c: (0, 0, 0)), column(c_in, MID)],
    )


def joint_back(cnt, t4, s4, gb4, s23, gb2, gb3, mask, gk, g4, b1, yl, w2, g6, a3, ap,
               gr2_ref, gj_ref, pj_ref, d4_ref):
    m = tiled(mask[...], MID)

    @pl.when(pl.program_id(0) == 0)
    def _():
        st = stats_of(total_of(s4), cnt[0], gb4[...])
        x, _ = normalize(b1[...], st)
        d4_ref[...] = norm_back(g4[...], x, m, st, back_rows(total_of(t4)), cnt[0]).astype(BF16)

    d = d4_ref[...]
    gr2_ref[...] = dot_tn(yl[...], d).astype(BF16)
    gy = g6[...] + dot_nt(d, w2[...])
    got = s23[0]
    x2, u2 = normalize(a3[...], stats_of(got, cnt[0], gb2[...]))
    x3, u3 = normalize(ap[...], stats_of(got, cnt[0], gb3[...], 8, 12))
    g = gy * m * silu_grad(u2 + u3)
    gj_ref[...] = g
    pj_ref[0] = jnp.concatenate(
        [pack_sums(g * x2, g * x3), pack_sums(g, g)[:4], gk[0]], axis=0
    )


def run_joint_back(cnt, small, g4, b1, yl, w2, g6, a3, ap):
    t4, s4, gb4, s23, gb2, gb3, mask, gk = small
    wide, pair = column(R, MID), column(2, MID)
    one = fixed((R, MID))
    return wide_grid(
        joint_back,
        [like((C_OUT, MID), BF16), like((R, C_OUT)), like((4, 16, 128))],
        [row_block(MID, MID), wide, CHUNK],
        (cnt, t4, s4, gb4, s23, gb2, gb3, mask, gk.reshape(4, 4, 128), g4, b1, yl, w2, g6, a3, ap),
        [SMEM, fixed(t4.shape), fixed(s4.shape), fixed((2, MID)), CHUNK, pair, pair,
         fixed((R, 128)), pl.BlockSpec((1, 4, 128), lambda c: (c, 0, 0)), one, one, wide,
         row_block(MID, MID), wide, wide, wide],
        [pltpu.VMEM((R, MID), BF16)],
    )


def expand_back(cnt, tj, s23, gb2, gb3, mask, s1, gb1, gj, a3, ap, h2, x0, we1, a2,
                ge1_ref, gsk_ref, d3_ref, g1_ref, p1_ref):
    m = tiled(mask[...], MID)
    g = gj[...]
    tot, got = tj[0], s23[0]
    sum2, sum3, sumg = (get_rows(tot, 4 * k, MID) for k in range(3))
    st = stats_of(got, cnt[0], gb2[...])
    x, _ = normalize(a3[...], st)
    d = norm_back(g, x, m, st, (sum2, sumg), cnt[0]).astype(BF16)
    ge1_ref[...] = dot_tn(h2[...], d).astype(BF16)
    accumulate(g1_ref, dot_nt(d, we1[...]))
    st = stats_of(got, cnt[0], gb3[...], 8, 12)
    x, _ = normalize(ap[...], st)
    d = norm_back(g, x, m, st, (sum3, sumg), cnt[0]).astype(BF16)
    d3_ref[...] = d
    gsk_ref[...] = dot_tn(x0[0], d).astype(BF16)

    @pl.when(pl.program_id(0) == pl.num_programs(0) - 1)
    def _():
        x1, u1 = normalize(a2[...], stats_of(total_of(s1), cnt[0], gb1[...]))
        v = g1_ref[...] * m * silu_grad(u1)
        g1_ref[...] = v
        spread_rows(p1_ref, pack_sums(v * x1, v))


def run_expand_back(n, cnt, small, gj, a3, ap, h2, xph, we1, a2):
    tj, s23, gb2, gb3, mask, s1, gb1 = small
    wide, pair = column(R, MID), column(2, MID)
    one = fixed((R, MID))
    c_in = xph.shape[-1]
    return wide_grid(
        expand_back,
        [like((MID, C_OUT), BF16), like((c_in, C_OUT), BF16), like((R, C_OUT), BF16),
         like((R, MID)), like((n, 8, 128))],
        [column(MID, MID), column(c_in, MID), wide, one, fixed((n, 8, 128))],
        (cnt, tj, s23, gb2, gb3, mask, s1, gb1, gj, a3, ap, h2, xph, we1, a2),
        [SMEM, CHUNK, CHUNK, pair, pair, fixed((R, 128)), fixed(s1.shape), fixed((2, MID)),
         wide, wide, wide, one, pl.BlockSpec((1, R, c_in), lambda c: (0, 0, 0)),
         column(MID, MID), one],
    )


def input_grads(mask, tc, tm, tf, d0, d3, w1, wsk, oc, om, of):
    lanes = oc.shape[-1]
    m = tiled(mask[...], lanes)
    groups = []
    for ph in range(4):
        v = dot_nt(d0[ph], w1[...])
        if ph == 0:
            v = v + dot_nt(d3[...], wsk[...])
        groups.append(m * v)
    for g, (out, table) in enumerate(((oc, tc), (om, tm), (of, tf))):
        pairs = 2 if g == 0 else 1
        side = 2 * SIDES[g]
        step = ROWS[g] // (FRAMES // pairs)
        for f in range(0, FRAMES, pairs):
            at = CUTS[g] + (f // pairs) * step
            rows = jnp.concatenate([v[at : at + step] for v in groups], axis=0).astype(BF16)
            y = dot(table[...], rows).reshape(pairs, side, 16, lanes)
            for p in range(pairs):
                out[f + p] = y[p, :, 0:side, :].astype(BF16)


def run_input_grads(mask, tables, d0, d3, w1, wsk):
    lanes = 256
    c_in = w1.shape[0]
    return wide_grid(
        input_grads,
        [like((FRAMES, 2 * q, 2 * q, c_in), BF16) for q in SIDES],
        clip_blocks(lanes),
        (mask, *tables, d0, d3, w1, wsk),
        [fixed((R, 128))] + [fixed(t.shape) for t in tables]
        + [fixed(d0.shape), fixed(d3.shape), row_block(lanes, MID), row_block(lanes, C_OUT)],
        steps=c_in // lanes,
    )


def tie(*arrays):
    return lax.optimization_barrier(arrays)


def axes_bits(n, fsdp):
    bits = n.bit_length() - 1
    core = fsdp.bit_length() - 1
    return list(range(core)), core, core + 1, list(range(core + 2, bits))


def swap(v, d, n):
    return lax.ppermute(v, AXES, [(i, i ^ d) for i in range(n)])


def exchange(spread):
    return lax.all_to_all(spread, AXES, 0, 0, tiled=True)


def exchange_wide(rows, n, fsdp):
    core = axes_bits(n, fsdp)[1]
    half = rows.shape[0] // 2
    mine = ((lax.axis_index(AXES) >> core) & 1) == 0
    low, high = rows[:half], rows[half:]
    part = jnp.where(mine, low, high) + swap(jnp.where(mine, high, low), 1 << core, n)
    groups = [[i for i in range(n) if (i >> core) & 1 == k] for k in range(2)]
    got = lax.all_to_all(
        jnp.broadcast_to(part[None], (n // 2,) + part.shape), AXES, 0, 0,
        axis_index_groups=groups, tiled=True,
    )
    part = jnp.sum(got, axis=0)
    other = swap(part, 1 << core, n)
    return jnp.where(
        mine, jnp.concatenate([part, other], axis=0), jnp.concatenate([other, part], axis=0)
    )


def allsum_wide(rows, n, fsdp, beside=()):
    near, core, mid, far = axes_bits(n, fsdp)
    bits = near + [mid] + far
    for r in [[core]] + [bits[i : i + 2] for i in range(0, len(bits), 2)]:
        got = [
            swap(rows, sum(1 << b for j, b in enumerate(r) if m >> j & 1), n)
            for m in range(1, 1 << len(r))
        ]
        rows = sum(got, rows)
        if r == [core]:
            rows, *beside = tie(rows, *beside)
    return (rows, *beside) if beside else rows


def rows16(v):
    return jnp.pad(v, ((0, 0),) * (v.ndim - 2) + ((0, -v.shape[-2] % 16), (0, 0)))


def place_blocks(n, orders, core, heights, width):
    part = width // len(orders)

    def kernel(me_ref, *refs):
        srcs = refs[: 2 * len(orders)]
        outs = refs[2 * len(orders) : -1]
        sem = refs[-1]
        me = me_ref[0]
        for rel in range(n):
            for k, order in enumerate(orders):
                at = sum((rel >> b & 1) << j for j, b in enumerate(order))
                src = srcs[2 * k + (rel >> core & 1)]
                row = 0
                for i, (h, out) in enumerate(zip(heights, outs)):
                    pltpu.make_async_copy(
                        src.at[at, pl.ds(row, h)],
                        out.at[me ^ rel, :, pl.ds(k * part, part)],
                        sem.at[i],
                    ).start()
                    row += h
        for i, out in enumerate(outs):
            pltpu.make_async_copy(out, out, sem.at[i]).wait()

    return pl.pallas_call(
        kernel,
        out_shape=[jax.ShapeDtypeStruct((n, h, width), BF16) for h in heights],
        in_specs=[SMEM] + [pl.BlockSpec(memory_space=pl.ANY)] * (2 * len(orders)),
        out_specs=[VMEM] * len(heights),
        scratch_shapes=[pltpu.SemaphoreType.DMA((len(heights),))],
        compiler_params=LIMIT,
        cost_estimate=FREE,
    )


class Gather:
    def __init__(self, shards, n, fsdp):
        self.n = n
        self.near, self.core, self.mid, self.far = axes_bits(n, fsdp)
        self.shards = shards
        padded = [rows16(v.astype(BF16)) for v in shards]
        self.heights = [v.shape[0] for v in padded]
        self.x = jnp.concatenate(padded, axis=0) if len(padded) > 1 else padded[0]

    def first(self):
        got = []
        for m in range(1, 1 << len(self.far)):
            got.append(swap(self.x, sum(1 << b for j, b in enumerate(self.far) if m >> j & 1), self.n))
        self.hops = [self.x] + got

    def second(self):
        n = self.n
        bits = self.near + [self.mid]
        v = jnp.stack(self.hops)
        got = [v]
        for m in range(1, 1 << len(bits)):
            got.append(swap(v, sum(1 << b for j, b in enumerate(bits) if m >> j & 1), n))
        self.planes = [jnp.concatenate(got, axis=0)]
        self.orders = [self.far + bits]

    def split(self):
        width = self.x.shape[1]
        bits = self.near + [self.mid]
        self.paths = [bits, bits[::-1]]
        self.orders = [self.far + path for path in self.paths]
        v = jnp.stack(self.hops)
        self.planes = [v[..., : width // 2], v[..., width // 2 :]]

    def hop(self, k):
        self.got = [swap(v, 1 << p[k], self.n) for v, p in zip(self.planes, self.paths)]

    def land(self):
        self.planes = [jnp.concatenate([v, g], axis=0) for v, g in zip(self.planes, self.got)]

    def third(self):
        self.other = [swap(v, 1 << self.core, self.n) for v in self.planes]

    def finish(self, me):
        width = self.x.shape[1]
        planes = [v for pair in zip(self.planes, self.other) for v in pair]
        outs = place_blocks(self.n, self.orders, self.core, self.heights, width)(me, *planes)
        return [
            o.reshape(self.n * h, width)
            if h == v.shape[0]
            else o[:, : v.shape[0]].reshape(-1, width)
            for o, h, v in zip(outs, self.heights, self.shards)
        ]


def order_blocks(n, orders, pieces, width, arrays):
    heights = [arrays[i].shape[1] for i, _ in pieces]
    total = sum(heights)
    half = width // 2

    def kernel(me_ref, *refs):
        srcs = refs[: len(arrays)]
        outs = refs[len(arrays) : len(arrays) + 2]
        sem = refs[-1]
        me = me_ref[0]
        for rel in range(n):
            for k, order in enumerate(orders):
                at = 0
                for b in order:
                    at = at * 2 + (rel >> b & 1)
                side = at * 2 // n
                row = 0
                for (i, col), h in zip(pieces, heights):
                    pltpu.make_async_copy(
                        srcs[i].at[me ^ rel, :, pl.ds(col + k * half, half)],
                        outs[side].at[k, at % (n // 2), pl.ds(row, h)],
                        sem.at[side],
                    ).start()
                    row += h
        for k, out in enumerate(outs):
            pltpu.make_async_copy(out, out, sem.at[k]).wait()

    return pl.pallas_call(
        kernel,
        out_shape=[jax.ShapeDtypeStruct((2, n // 2, total, half), BF16)] * 2,
        in_specs=[SMEM] + [pl.BlockSpec(memory_space=pl.ANY)] * len(arrays),
        out_specs=[VMEM] * 2,
        scratch_shapes=[pltpu.SemaphoreType.DMA((2,))],
        compiler_params=LIMIT,
        cost_estimate=FREE,
    )


def add_blocks(keep, got, joined):
    m, rows, half = keep[0].shape[-3:]
    k_in = len(keep)

    if m == 1:
        outs = [like((rows, 2 * half))]
    elif joined:
        outs = [like((2, m // 2, rows, half), BF16)] * 2
    else:
        outs = [like((m // 2, rows, half), BF16)] * 4
    given = [*keep, *got]

    def kernel(*refs):
        k = 2 * k_in
        far_in, far_out = refs[:k], refs[k : k + len(outs)]
        ins, near_out = refs[k + len(outs) : 2 * k + len(outs)], refs[2 * k + len(outs) : -1]
        sem = refs[-1]
        moves = [
            pltpu.make_async_copy(f, v, sem.at[i]) for i, (f, v) in enumerate(zip(far_in, ins))
        ]
        for c in moves:
            c.start()
        for c in moves:
            c.wait()

        def total(k, i):
            if k_in == 1:
                return ins[0][k, i].astype(F32) + ins[1][k, i].astype(F32)
            return ins[k][i].astype(F32) + ins[2 + k][i].astype(F32)

        if m == 1:
            for k in range(2):
                near_out[0][:, k * half : (k + 1) * half] = total(k, 0)
        else:

            @pl.loop(0, m // 2)
            def _(i):
                for k in range(2):
                    for side in range(2):
                        v = total(k, i + side * (m // 2)).astype(BF16)
                        if joined:
                            near_out[side][k, i] = v
                        else:
                            near_out[2 * side + k][i] = v

        moves = [
            pltpu.make_async_copy(v, f, sem.at[2 * k_in + i])
            for i, (f, v) in enumerate(zip(far_out, near_out))
        ]
        for c in moves:
            c.start()
        for c in moves:
            c.wait()

    any_space = pl.BlockSpec(memory_space=pl.ANY)
    need = 2 * sum(v.size * v.dtype.itemsize for v in given) + 4 * 2**20
    return pl.pallas_call(
        kernel,
        out_shape=outs,
        in_specs=[any_space] * len(given),
        out_specs=[any_space] * len(outs),
        scratch_shapes=[pltpu.VMEM(v.shape, v.dtype) for v in given + outs]
        + [pltpu.SemaphoreType.DMA((len(given) + len(outs),))],
        compiler_params=pltpu.CompilerParams(vmem_limit_bytes=min(need, 56 * 2**20)),
        cost_estimate=FREE,
    )(*given)


class Scatter:
    def __init__(self, me, arrays, pieces, width, n, fsdp):
        self.n = n
        near, core, mid, self.far = axes_bits(n, fsdp)
        bits = near + [mid]
        self.paths = [bits, bits[::-1]]
        self.heights = [arrays[i].shape[1] for i, _ in pieces]
        orders = [[core] + path + self.far for path in self.paths]
        send, keep = order_blocks(n, orders, pieces, width, arrays)(me, *arrays)[::-1]
        self.send, self.keep = [send], [keep]
        self.hops = [[core]] + list(zip(*self.paths)) + [[b] for b in self.far]
        self.at = 0

    def start(self):
        self.got = [swap(v, 1 << b, self.n) for v, b in zip(self.send, self.hops[self.at])]
        self.at += 1

    def add(self):
        after = self.hops[self.at : self.at + 1]
        got = add_blocks(self.keep, self.got, bool(after) and len(after[0]) == 1)
        if not after:
            self.total = got[0]
        else:
            k = len(got) // 2
            self.keep, self.send = got[:k], got[k:]

    def end(self, x):
        x, *self.got = tie(x, *self.got)
        return x

    def ready(self, x):
        x, *self.send = tie(x, *self.send)
        self.start()
        return x

    def rest(self):
        self.add()
        while self.at < len(self.hops):
            self.start()
            self.add()
        out = []
        at = 0
        for h in self.heights:
            out.append(self.total[at : at + h])
            at += h
        return out


def body(n, fsdp, *args):
    (coarse, medium, fine, clip_counts, frame_counts, reduce_one, spatial_one, expand_one,
     shortcut_one, reduce_two, excite_down, excite_up, temporal_mix, expand_two, norm_params,
     motion_kernel, cot_c, cot_m, cot_f) = args
    near, core, mid, far = axes_bits(n, fsdp)

    def gather(w):
        return lax.all_gather(w.astype(BF16), AXES, axis=0, tiled=True)

    def flat(w):
        v = w.reshape(-1)
        return jnp.pad(v, (0, -v.size % MID)).reshape(-1, MID)

    def flat_back(got, w):
        return got.reshape(n, -1)[:, : w.size].reshape((n,) + w.shape)

    alive = (jnp.arange(4)[None, :] < frame_counts[0][:, None]) & (clip_counts[0][:, None] > 0)
    alive = alive.astype(F32)
    later = jnp.pad(alive[:, 1:], ((0, 0), (0, 1)))
    alive_slots = alive.reshape(12)
    later_slots = later.reshape(12)
    mask = (jnp.asarray(SPREAD) @ alive_slots)[:, None]
    per_group = jnp.sum(alive, axis=1)
    tables = [jnp.asarray(t, BF16) for t in PHASES]
    tables_t = [jnp.asarray(t.T, BF16) for t in PHASES]
    clips = [coarse, medium, fine]

    m128 = jnp.broadcast_to(mask, (R, 128))
    scale = later_slots / jnp.asarray(NPIX)
    scale = jnp.broadcast_to(jnp.pad(scale, (0, 4))[:, None], (16, SQUEEZE))
    table = jnp.asarray(TABLE, BF16)
    table_t = jnp.asarray(TABLE.T, BF16)
    spread = jnp.asarray(SPREAD3, BF16)
    me = lax.axis_index(AXES).astype(jnp.int32).reshape(1)
    small = jnp.concatenate([flat(norm_params), jnp.pad(per_group, (0, MID - 3))[None]], axis=0)
    ga = Gather([reduce_one, small], n, fsdp)
    gb_ = Gather([spatial_one], n, fsdp)
    gc_ = Gather([shortcut_one, expand_one], n, fsdp)
    narrow = [reduce_two, flat(excite_down), flat(excite_up), flat(temporal_mix)]
    rows = [v.shape[0] for v in narrow]
    narrow = jnp.concatenate(narrow, axis=0)
    got = gather(jnp.pad(narrow, ((0, -narrow.shape[0] % 16), (0, 0))))
    we2 = gather(expand_two)
    ga.first()
    *ga.hops, gb_.x, clips[0], clips[1], clips[2] = tie(*ga.hops, gb_.x, *clips)
    ga.second()
    gb_.first()
    xph = run_split(alive_slots, clips, tables)
    ga.planes[0], xph = tie(ga.planes[0], xph)
    ga.third()
    w1, norms = ga.finish(me)
    norms = norms.reshape(n, -1, MID)
    counts = jnp.sum(norms[:, -1, :3].astype(F32), axis=0)
    cnt = jnp.sum(counts * np.array([q * q for q in SIDES], np.float32)).reshape(1)
    norms = flat_back(norms[:, :-1], norm_params).transpose(1, 0, 2).reshape(2, -1).astype(F32)
    edges = [0, 512, 1024, 3072, 5120, 5632, 6144, 8192]
    gb = [norms[:, edges[k] : edges[k + 1]] for k in range(7)]

    w1, gc_.x, *gb_.hops = tie(w1, gc_.x, *gb_.hops)
    gb_.split()
    w1, *gb_.planes = tie(w1, *gb_.planes)
    gb_.hop(0)
    gc_.first()
    a1, p0 = run_enter(n, xph, w1)
    for k in range(1, len(gb_.paths[0])):
        p0, *gb_.got = tie(p0, *gb_.got)
        gb_.land()
        p0, *gb_.planes = tie(p0, *gb_.planes)
        gb_.hop(k)
    s0 = exchange(p0)
    s0, *rest = tie(s0, *gb_.got, *gc_.hops)
    gb_.got, gc_.hops = rest[:2], rest[2:]
    gb_.land()
    gb_.third()
    gc_.split()
    gc_.hop(0)
    wsp, = gb_.finish(me)
    for k in range(1, len(gc_.paths[0])):
        wsp, *gc_.got = tie(wsp, *gc_.got)
        gc_.land()
        wsp, *gc_.planes = tie(wsp, *gc_.planes)
        gc_.hop(k)
    im, a2, p1 = run_conv_forward(n, cnt, s0, gb[0], m128, a1, wsp)
    s1 = exchange(p1)
    s1, *gc_.got = tie(s1, *gc_.got)
    gc_.land()
    gc_.third()
    wsk, we1 = gc_.finish(me)
    h2, a3, ap, p2 = run_expand_pair(cnt, s1, gb[1], m128, a2, we1, xph, wsk)
    s23, got = allsum_wide(p2, n, fsdp, (got,))
    got = got.reshape(n, -1, MID)
    w2 = got[:, : rows[0]].reshape(C_OUT, MID)
    at = rows[0]
    wdown = flat_back(got[:, at : at + rows[1]], excite_down).reshape(MID, SQUEEZE)
    at += rows[1]
    wup = flat_back(got[:, at : at + rows[2]], excite_up)
    wup = wup.transpose(1, 0, 2).reshape(SQUEEZE, MID).astype(F32)
    at += rows[2]
    wmix = flat_back(got[:, at : at + rows[3]], temporal_mix)
    wmix = wmix.transpose(1, 0, 2).reshape(3, 9 * GROUP, GROUP)
    wmix_t = wmix.reshape(3, 9, GROUP, GROUP).transpose(0, 1, 3, 2).reshape(3, 9 * GROUP, GROUP)
    y1, y1_low, b1, p4 = run_joint_norm(n, cnt, s23, gb[2], gb[3], m128, a3, ap, w2)
    s4 = exchange(p4)
    z, z_low, mixed, mix_im, sig, pooled, wnext, p5 = run_mix_forward(
        n, cnt, s4, gb[4], m128, wdown, wup, motion_kernel, scale, table, spread, b1, wmix
    )
    s5 = exchange(p5)
    w, b3, p6 = run_expand_last(cnt, s5, gb[5], m128, mixed, we2)
    s6 = exchange_wide(p6, n, fsdp)
    o_c, o_m, o_f, g6, p6 = run_last_norm(cnt, s6, gb[6], m128, b3, y1, (cot_c, cot_m, cot_f))

    t6 = exchange_wide(p6, n, fsdp)
    ge2, g5, p5 = run_last_back(n, cnt, t6, s6, gb[6], m128, s5, gb[5], g6, b3, w, we2, mixed)
    t5 = exchange(p5)
    g4, gmix, gkernel, gdown, gup, p4 = run_mix_backward(
        n, cnt,
        (t5, s5, gb[5], m128, sig, pooled, wnext, wup, motion_kernel, scale, table_t, spread,
         wdown, s4, gb[4]),
        g5, mixed, mix_im, wmix_t, z, z_low, b1,
    )
    t4 = exchange(p4)
    gr2, gj, pj = run_joint_back(
        cnt, (t4, s4, gb[4], s23, gb[2], gb[3], m128, gkernel), g4, b1, y1_low, w2, g6, a3, ap
    )

    gmix = gmix.reshape(27, n, GROUP * GROUP // n).transpose(1, 0, 2).reshape(n, -1)
    gup = gup.reshape(SQUEEZE, n, MID // n).transpose(1, 0, 2).reshape(n, -1)
    thin = jnp.concatenate([gmix, gdown.reshape(n, -1).astype(BF16), gup.astype(BF16)], axis=1)
    thin = jnp.pad(thin, ((0, 0), (0, -thin.shape[1] % (16 * MID)))).reshape(n, -1, MID)

    def blocks(v):
        return rows16(v.reshape(n, -1, v.shape[-1]))

    starts = list(range(0, C_OUT, MID))
    tj, gr2, ge2, thin = allsum_wide(pj, n, fsdp, (gr2, ge2, thin))
    ra = Scatter(
        me, [blocks(gr2), thin, blocks(ge2)], [(0, 0), (1, 0)] + [(2, c) for c in starts], MID,
        n, fsdp,
    )
    ra.start()
    ra.add()
    tj = ra.ready(tj)
    ge1, gsk, d3, g1, p1 = run_expand_back(
        n, cnt, (tj, s23, gb[2], gb[3], m128, s1, gb[1]), gj, a3, ap, h2, xph, we1, a2
    )
    p1 = ra.end(p1)
    p1, ge1, gsk = tie(p1, ge1, gsk)
    t1 = exchange(p1)
    ra.add()
    rb = Scatter(
        me, [blocks(ge1), blocks(gsk)], [(i, c) for i in range(2) for c in starts], MID, n, fsdp
    )
    t1 = rb.ready(ra.ready(t1))
    d1, gsp = run_spatial_grad(cnt, (t1, s1, gb[1], m128), g1, a2, im)
    d1 = rb.end(ra.end(d1))
    rb.add()
    d1 = rb.ready(d1)
    gsp, d1 = tie(gsp, d1)
    rc = Scatter(me, [blocks(gsp)], [(0, 0)], MID, n, fsdp)
    d1 = rc.ready(d1)
    ra.add()
    d1 = ra.ready(d1)
    g0, p0 = run_conv_back(n, cnt, (s0, gb[0], m128), d1, wsp, a1)
    p0 = rc.end(rb.end(ra.end(p0)))
    t0 = exchange(p0)
    rc.add()
    rb.add()
    ra.add()
    t0 = rb.ready(rc.ready(t0))
    d0, gr1 = run_first_grads(cnt, (t0, s0, gb[0], m128), g0, a1, xph)
    gr1 = blocks(gr1)
    gr1 = gr1.reshape(n // (2 * fsdp), 2, fsdp, -1, MID)
    side = (me[0] >> core) & 1
    kept = lax.dynamic_index_in_dim(gr1, side, 1, keepdims=False)
    sent = lax.dynamic_index_in_dim(gr1, 1 - side, 1, keepdims=False)
    gr1 = (kept.astype(F32) + swap(sent, 1 << core, n).astype(F32)).astype(BF16)
    groups = [[i for i in range(n) if (i >> core) & 1 == k] for k in range(2)]
    got = lax.all_to_all(
        gr1.reshape(n // 2, -1, MID), AXES, 0, 0, axis_index_groups=groups, tiled=True
    )
    gin = list(run_input_grads(m128, tables_t, d0, d3, w1, wsk))
    gin[0] = rc.end(rb.end(gin[0]))
    gin[0], got, *rest = tie(gin[0], got, *rb.got, *rc.got)
    rb.got, rc.got = rest[:2], rest[2:]
    rc.add()
    rb.add()
    gin[0] = ra.ready(rb.ready(rc.ready(gin[0])))
    *rc.got, t0, t1, t4, t5, t6, tj = tie(*rc.got, t0, t1, t4, t5, t6, tj)
    rc.add()
    rc.start()
    rb.add()
    rb.start()
    *rc.got, o_m, o_f, got = tie(*rc.got, o_m, o_f, got)
    gr1 = jnp.sum(got.astype(F32), axis=0)[: reduce_one.shape[0]]
    second = ra.rest()
    gsp = rc.rest()[0][: spatial_one.shape[0]]
    first = rb.rest()

    def wide_back(parts, like_):
        return jnp.concatenate([p[: like_.shape[0]] for p in parts], axis=1)

    thin = second[1].reshape(-1)
    s1_ = temporal_mix.size
    s2_ = s1_ + excite_down.size
    s3_ = s2_ + excite_up.size

    def split_rows(t, k):
        t = jnp.sum(t, axis=0) if t.ndim == 3 else t
        return t.reshape(k, -1)

    t0, t1, t4, t5 = (split_rows(t, 2) for t in (t0, t1, t4, t5))
    t6 = split_rows(t6, 2)
    gkernel = tj[:, 12:].reshape(16, 128)[:9, :SQUEEZE]
    tj = jnp.stack([tj[:, 4 * k : 4 * k + 4].reshape(-1) for k in range(3)])
    gain = jnp.concatenate([t0[0], t1[0], tj[0], tj[1], t4[0], t5[0], t6[0]])
    bias = jnp.concatenate([t0[1], t1[1], tj[2], tj[2], t4[1], t5[1], t6[1]])
    gnorm = lax.dynamic_slice_in_dim(jnp.stack([gain, bias]), me[0] * (8192 // n), 8192 // n, 1)
    return (
        o_c, o_m, o_f, gin[0], gin[1], gin[2],
        gr1,
        gsp,
        wide_back(first[:4], expand_one),
        wide_back(first[4:], shortcut_one),
        second[0][: reduce_two.shape[0]],
        thin[s1_:s2_].reshape(excite_down.shape),
        thin[s2_:s3_].reshape(excite_up.shape),
        thin[:s1_].reshape(temporal_mix.shape),
        wide_back(second[2:], expand_two),
        gnorm,
        gkernel,
    )


def solution(mesh):
    n = mesh.shape["dp"] * mesh.shape["fsdp"]
    rows = P(AXES, None)
    cols = P(None, AXES)
    image = P(AXES, None, None, None)
    return jax.shard_map(
        partial(body, n, mesh.shape["fsdp"]),
        mesh=mesh,
        in_specs=(image, image, image, rows, rows, rows, rows, rows, rows, rows, rows, cols, cols,
                  rows, cols, P(), image, image, image),
        out_specs=(image, image, image, image, image, image, rows, rows, rows, rows, rows, rows,
                   cols, cols, rows, cols, P()),
        check_vma=False,
    )
```

time: 617 us -> 571 us (0.925)
  local copies, waits for them, and re-layouts: 83.6 us -> 67.1 us
  Pallas kernels: 222 us -> 206 us
  waiting for transfers between devices: 123 us -> 108 us
  other arithmetic: 20.8 us -> 31.9 us
  blocking collectives: 31.3 us -> 21.9 us
    pallas_call x7 -> x4, Pallas kernels: 69.2 us -> 48.5 us  [wide_grid(): pl.pallas_call(kernel, grid=(steps,), out_shape=outs, in_specs=in_specs,...]
    all_to_all x9, waiting for transfers between devices: 48.1 us -> 36.6 us  [the longest x8 36.6 us: exchange(): return lax.all_to_all(spread, AXES, 0, 0, tiled=True)]
    broadcast_in_dim x18 -> x3, local copies, waits for them, and re-layouts: 10.8 us -> 0.03 us  [the longest x2 0.02 us: exchange_wide(): jnp.broadcast_to(part[None], (n // 2,) + part.shape)]
    all_to_all x2, blocking collectives: 31.3 us -> 21.9 us  [exchange_wide(): lax.all_to_all(jnp.broadcast_to(part[None], (n // 2,) + part.shape), AXES...]
    unnamed x152 -> x163, local copies, waits for them, and re-layouts: 28.3 us -> 36.5 us
    all_to_all x9, starting transfers between devices: 39.7 us -> 33.5 us  [the longest x8 26.4 us: exchange(): return lax.all_to_all(spread, AXES, 0, 0, tiled=True)]
    pallas_call x23 -> x26, Pallas kernels: 118 us -> 124 us  [the longest x6 53.7 us: flow_call(): pl.pallas_call(kernel, out_shape=[like(o[0], o[1]) for o in outs] + list(...]
    ppermute x60 -> x65, starting transfers between devices: 70.4 us -> 75 us  [swap(): return lax.ppermute(v, AXES, [(i, i ^ d) for i in range(n)])]
  transfers between devices with their start and end apart: 71 -> 76, of which waited for: 32 -> 35; matrix products, arithmetic and copies ran while one was open for 13% -> 12% of each run, Pallas kernels for 25% -> 23%
where the time goes in v3:
time: 571 us; the launch traced here: 561 us
  Pallas kernels  206 us (36%)
  starting transfers between devices  109 us (19%)
  waiting for transfers between devices  108 us (19%)
  local copies, waits for them, and re-layouts  67.1 us (12%)
  other arithmetic  31.9 us (6%)
  blocking collectives  21.9 us (4%)
  between operations  15.9 us (3%)
    ppermute x65, starting transfers between devices, swap(): return lax.ppermute(v, AXES, [(i, i ^ d) for i in range(n)])  75 us
    ppermute x65, waiting for transfers between devices, swap(): return lax.ppermute(v, AXES, [(i, i ^ d) for i in range(n)])  71.4 us
    pallas_call x6, Pallas kernels, flow_call(): pl.pallas_call(kernel, out_shape=[like(o[0], o[1]) for o in outs] + list(...  53.7 us
    pallas_call x4, Pallas kernels, wide_grid(): pl.pallas_call(kernel, grid=(steps,), out_shape=outs, in_specs=in_specs,...  48.5 us
    pallas_call x5, Pallas kernels, plain_call(): pl.pallas_call(kernel, out_shape=[like(o[0], o[1]) for o in outs] + list(...  45.5 us
    all_to_all x8, waiting for transfers between devices, exchange(): return lax.all_to_all(spread, AXES, 0, 0, tiled=True)  36.6 us
    unnamed x163, local copies, waits for them, and re-layouts  36.5 us
    all_to_all x8, starting transfers between devices, exchange(): return lax.all_to_all(spread, AXES, 0, 0, tiled=True)  26.4 us
  transfers between devices with their start and end apart: 76, of which 35 were waited for; matrix products, arithmetic and copies ran while one was open for 12% of the time, Pallas kernels for 23%

profile of v3, /device:TPU:0, one launch (start us, length us, event | category | flops | bytes accessed | tf_op | source)
XLA Modules:
  0.0 560.7 jit_solution(5285340212095183001)
XLA Ops:
  14.6 3.1 collective-permute-start
  33.2 5.8 %shard_map.422.refs_0_.x.x0.refs_7_ = bf16[4,480,1024]{2,1,0:T(8,128)(2,1)} custom-call(f32[12]{0:T(128)} %convert_element_type.96.alive, bf16[4,8,8,1024]{3,2,1,0:T(8,128)(2,1)} %xc, bf16[4,12,12,1024]{3,2,1,0:T(8,128)(2,1)} %copy.129.xm, bf16[4,14,14,1024]{3,2,1,0:T(8,128)(2,1)} %copy.130.xf, bf16[128,256]{1,0:T(8,128)(2,1)} %constant.58.clone.tc, ...), custom_call_target="tpu_custom_call" | custom-call | tf_op jit(solution)/shard_map/pallas_call | solution.py:299
  40.5 3.1 collective-permute-start.9
  49.9 6.5 %collective-permute-done.8 = bf16[144,512]{1,0:T(8,128)(2,1)S(1)} collective-permute-done((bf16[144,512]{1,0:T(8,128)(2,1)S(1)}, bf16[144,512]{1,0:T(8,128)(2,1)S(1)}, u32[]{:S(2)}, u32[]{:S(2)}) %collective-permute-start.8) | collective-permute-done | bytes 147488 | tf_op jit(solution)/shard_map/ppermute | solution.py:1095
  59.6 6.5 %shard_map.424 = (f32[4,480,512]{2,1,0:T(8,128)}, f32[32,8,128]{2,1,0:T(8,128)}) custom-call(bf16[4,480,1024]{2,1,0:T(8,128)(2,1)} %shard_map.422.refs_0_.x.x0.refs_7_, bf16[1024,512]{1,0:T(8,128)(2,1)} %bitcast.110), custom_call_target="tpu_custom_call" | custom-call | tf_op jit(solution)/shard_map/pallas_call | solution.py:404
  69.6 8.2 %collective-permute-start.14 = (bf16[48,2048]{1,0:T(8,128)(2,1)}, bf16[48,2048]{1,0:T(8,128)(2,1)}, u32[]{:S(2)}, u32[]{:S(2)}) collective-permute-start(bf16[48,2048]{1,0:T(8,128)(2,1)} %pad_maximum_fusion.8), channel_id=1, source_target_pairs={{0,8},{1,9},{2,10},{3,11},{4,12},{5,13},{6,14},{7,15},{8,0},{9,1},... | collective-permute-start | bytes 589832 | tf_op jit(solution)/shard_map/ppermute | solution.py:1095
  80.2 3.4 all-to-all-start
  83.7 4.2 collective-permute-done.14
  88.0 6.4 %collective-permute-done.15 = bf16[48,2048]{1,0:T(8,128)(2,1)} collective-permute-done((bf16[48,2048]{1,0:T(8,128)(2,1)}, bf16[48,2048]{1,0:T(8,128)(2,1)}, u32[]{:S(2)}, u32[]{:S(2)}) %collective-permute-start.15) | collective-permute-done | bytes 196640 | tf_op jit(solution)/shard_map/ppermute | solution.py:1095
  94.3 5.7 %all-to-all-done.refs_1_.refs_2_ = f32[32,8,128]{2,1,0:T(8,128)} async-done(((f32[32,8,128]{2,1,0:T(8,128)}), f32[32,8,128]{2,1,0:T(8,128)}, u32[]{:S(2)}, u32[]{:S(2)}) %all-to-all-start) | async-done | bytes 131104 | tf_op jit(solution)/shard_map/all_to_all | solution.py:1099
  108.7 4.6 shard_map.425
  126.6 10.4 %shard_map.426 = (bf16[480,4608]{1,0:T(8,128)(2,1)}, f32[480,512]{1,0:T(8,128)}, f32[32,8,128]{2,1,0:T(8,128)}) custom-call(f32[1]{0:T(128)} %bitcast.7.refs_0_.cnt, f32[32,8,128]{2,1,0:T(8,128)} %all-to-all-done.refs_1_.refs_2_, f32[2,512]{1,0:T(2,128)} %get-tuple-element.570.refs_2_.refs_3_, f32[480,128]{1,0:T(8,128)} %broadcast_in_dim.12.refs_3_.mask.refs_4_, ...), custom_call_target="tpu_custom_call" | custom-call | tf_op jit(solution)/shard_map/pallas_call | solution.py:404
  142.2 6.2 %all-to-all-done.1.s1.refs_2_ = f32[32,8,128]{2,1,0:T(8,128)S(1)} async-done(((f32[32,8,128]{2,1,0:T(8,128)}), f32[32,8,128]{2,1,0:T(8,128)S(1)}, u32[]{:S(2)}, u32[]{:S(2)}) %all-to-all-start.1) | async-done | bytes 131104 | tf_op jit(solution)/shard_map/all_to_all | solution.py:1099
  155.6 5.5 shard_map.427
  161.1 9.3 %shard_map.428 = (bf16[480,512]{1,0:T(8,128)(2,1)}, f32[480,2048]{1,0:T(8,128)}, f32[480,2048]{1,0:T(8,128)}, f32[4,16,128]{2,1,0:T(8,128)}) custom-call(f32[1]{0:T(128)} %bitcast.7.refs_0_.cnt, f32[480,512]{1,0:T(8,128)} %get-tuple-element.277.a2.refs_6_, f32[32,8,128]{2,1,0:T(8,128)} %copy-done.40, f32[2,512]{1,0:T(2,128)} %get-tuple-element.569.gb1.refs_3_, ...), custom_call_target="tpu_custom_call" | custom-call | tf_op jit(solution)/shard_map/pallas_call | solution.py:902
  184.7 3.1 slice.240
  188.4 9.4 %shard_map.429 = (f32[480,2048]{1,0:T(8,128)}, bf16[480,2048]{1,0:T(8,128)(2,1)}, f32[480,512]{1,0:T(8,128)}, f32[32,8,128]{2,1,0:T(8,128)}) custom-call(f32[1]{0:T(128)} %bitcast.7.refs_0_.cnt, f32[4,16,128]{2,1,0:T(8,128)} %add_add_fusion.2.refs_1_.s23, f32[2,2048]{1,0:T(2,128)} %get-tuple-element.566.refs_2_.gb2, ...), custom_call_target="tpu_custom_call" | custom-call | tf_op jit(solution)/shard_map/pallas_call | solution.py:404
  197.8 3.3 all-to-all-start.2
  206.3 3.4 all-to-all-done.2.refs_1_.refs_14_.s4
  210.4 8.1 %shard_map.430 = (f32[480,512]{1,0:T(8,128)}, bf16[480,512]{1,0:T(8,128)(2,1)}, f32[480,512]{1,0:T(8,128)}, bf16[3,480,1152]{2,1,0:T(8,128)(2,1)}, f32[16,512]{1...) custom-call(f32[1]{0:T(128)} %bitcast.7.refs_0_.cnt, f32[32,8,128]{2,1,0:T(8,128)} %copy-done.41, ...), custom_call_target="tpu_custom_call" | custom-call | tf_op jit(solution)/shard_map/pallas_call | solution.py:404
  221.2 8.6 %all-to-all-done.3.refs_1_.refs_5_.refs_2_ = f32[32,8,128]{2,1,0:T(8,128)S(1)} async-done(((f32[32,8,128]{2,1,0:T(8,128)}), f32[32,8,128]{2,1,0:T(8,128)S(1)}, u32[]{:S(2)}, u32[]{:S(2)}) %all-to-all-start.3) | async-done | bytes 131104 | tf_op jit(solution)/shard_map/all_to_all | solution.py:1099
  230.4 6.0 %shard_map.431 = (bf16[480,512]{1,0:T(8,128)(2,1)}, f32[480,2048]{1,0:T(8,128)}, f32[32,128]{1,0:T(8,128)}) custom-call(f32[1]{0:T(128)} %bitcast.7.refs_0_.cnt, f32[32,8,128]{2,1,0:T(8,128)} %copy-done.42, f32[2,512]{1,0:T(2,128)} %get-tuple-element.567.refs_2_.refs_6_.refs_3_, f32[480,128]{1,0:T(8,128)} %broadcast_in_dim.12.refs_3_.mask.refs_4_, ...), custom_call_target="tpu_custom_call" | custom-call | tf_op jit(solution)/shard_map/pallas_call | solution.py:361
  239.1 11.0 %all_to_all.55 = f32[16,16,128]{2,1,0:T(8,128)S(1)} all-to-all(f32[16,16,128]{2,1,0:T(8,128)S(1)} %broadcast_in_dim.14), channel_id=1, replica_groups={{0,1,4,5,8,9,12,13,16,17,20,21,24,25,28,29},{2,3,6,7,10,11,14,15,18,19,..., dimensions={0} | all-to-all | bytes 262144 | tf_op jit(solution)/shard_map/all_to_all | solution.py:1109
  253.5 10.5 %shard_map.432 = (bf16[4,4,4,2048]{3,2,1,0:T(4,128)(2,1)}, bf16[4,6,6,2048]{3,2,1,0:T(8,128)(2,1)}, bf16[4,7,7,2048]{3,2,1,0:T(8,128)(2,1)}, f32[480,2048]{1,0:T(8,128)}, f32[32,128]{1,0:T(8,128)}) custom-call(f32[1]{0:T(128)} %bitcast.7.refs_0_.cnt, f32[32,128]{1,0:T(8,128)} %maximum_select_fusion.refs_1_.refs_2_, ...), custom_call_target="tpu_custom_call" | custom-call | tf_op jit(solution)/shard_map/pallas_call | solution.py:404
  266.7 10.8 %all_to_all.56 = f32[16,16,128]{2,1,0:T(8,128)S(1)} all-to-all(f32[16,16,128]{2,1,0:T(8,128)S(1)} %broadcast_in_dim.15), channel_id=1, replica_groups={{0,1,4,5,8,9,12,13,16,17,20,21,24,25,28,29},{2,3,6,7,10,11,14,15,18,19,..., dimensions={0} | all-to-all | bytes 262144 | tf_op jit(solution)/shard_map/all_to_all | solution.py:1109
  279.4 9.8 %shard_map.433 = (bf16[512,2048]{1,0:T(8,128)(2,1)}, f32[480,512]{1,0:T(8,128)}, f32[32,8,128]{2,1,0:T(8,128)}) custom-call(f32[1]{0:T(128)} %bitcast.7.refs_0_.cnt, f32[32,128]{1,0:T(8,128)} %maximum_select_fusion.1.refs_1_, f32[32,128]{1,0:T(8,128)} %maximum_select_fusion.refs_1_.refs_2_, f32[2,2048]{1,0:T(2,128)} %get-tuple-element.564.refs_2_.refs_3_, ...), custom_call_target="tpu_custom_call" | custom-call | tf_op jit(solution)/shard_map/pallas_call | solution.py:361
  294.1 6.5 %all-to-all-done.6.refs_1_ = f32[32,8,128]{2,1,0:T(8,128)S(1)} async-done(((f32[32,8,128]{2,1,0:T(8,128)}), f32[32,8,128]{2,1,0:T(8,128)S(1)}, u32[]{:S(2)}, u32[]{:S(2)}) %all-to-all-start.6) | async-done | bytes 131104 | tf_op jit(solution)/shard_map/all_to_all | solution.py:1099
  301.3 10.3 %shard_map.434 = (f32[480,512]{1,0:T(8,128)}, bf16[3,1152,128]{2,1,0:T(8,128)(2,1)}, f32[16,128]{1,0:T(8,128)}, f32[512,32]{1,0:T(8,128)}, f32[32,512]{1,0:T(8,128)}, /*index=5*/f32[32,8,128]{2,1,0:T(8,128)}) custom-call(f32[1]{0:T(128)} %bitcast.7.refs_0_.cnt, f32[32,8,128]{2,1,0:T(8,128)} %copy-done.45, f32[32,8,128]{2,1,0:T(8,128)} %copy-done.42, ...), custom_call_target="tpu_custom_call" | custom-call | tf_op jit(solution)/shard_map/pallas_call | solution.py:361
  316.7 6.2 %all-to-all-done.7.t4 = f32[32,8,128]{2,1,0:T(8,128)S(1)} async-done(((f32[32,8,128]{2,1,0:T(8,128)}), f32[32,8,128]{2,1,0:T(8,128)S(1)}, u32[]{:S(2)}, u32[]{:S(2)}) %all-to-all-start.7) | async-done | bytes 131104 | tf_op jit(solution)/shard_map/all_to_all | solution.py:1099
  323.6 12.7 %shard_map.435 = (bf16[2048,512]{1,0:T(8,128)(2,1)}, f32[480,2048]{1,0:T(8,128)}, f32[4,16,128]{2,1,0:T(8,128)}) custom-call(f32[1]{0:T(128)} %bitcast.7.refs_0_.cnt, f32[32,8,128]{2,1,0:T(8,128)} %copy-done.47, f32[32,8,128]{2,1,0:T(8,128)} %copy-done.41, f32[2,512]{1,0:T(2,128)} %get-tuple-element.568.refs_2_.refs_15_.gb4, ...), custom_call_target="tpu_custom_call" | custom-call | tf_op jit(solution)/shard_map/pallas_call | solution.py:902
  337.8 5.2 shard_map.436
  363.9 14.7 %shard_map.438 = (bf16[512,2048]{1,0:T(8,128)(2,1)}, bf16[1024,2048]{1,0:T(8,128)(2,1)}, bf16[480,2048]{1,0:T(8,128)(2,1)}, f32[480,512]{1,0:T(8,128)}, f32[32,8,128]{2,1,0:T(8,128)}) custom-call(f32[1]{0:T(128)} %bitcast.7.refs_0_.cnt, f32[4,16,128]{2,1,0:T(8,128)} %add_add_fusion.tj, f32[4,16,128]{2,1,0:T(8,128)} %add_add_fusion.2.refs_1_.s23, ...), custom_call_target="tpu_custom_call" | custom-call | tf_op jit(solution)/shard_map/pallas_call | solution.py:902
  378.6 4.0 all-to-all-start.8
  382.6 6.0 %shard_map.440 = (bf16[2,16,192,256]{3,2,1,0:T(8,128)(2,1)}, bf16[2,16,192,256]{3,2,1,0:T(8,128)(2,1)}) custom-call(s32[1]{0:T(128)} %bitcast.me_ref, bf16[32,16,2048]{2,1,0:T(8,128)(2,1)} %bitcast.122, bf16[32,32,2048]{2,1,0:T(8,128)(2,1)} %bitcast.112), custom_call_target="tpu_custom_call" | custom-call | tf_op jit(solution)/shard_map/pallas_call | solution.py:1340
  396.4 9.0 %shard_map.441 = (bf16[480,512]{1,0:T(8,128)(2,1)}, bf16[4608,512]{1,0:T(8,128)(2,1)}) custom-call(f32[1]{0:T(128)} %bitcast.7.refs_0_.cnt, f32[32,8,128]{2,1,0:T(8,128)} %copy-done.49, f32[32,8,128]{2,1,0:T(8,128)} %copy-done.40, f32[2,512]{1,0:T(2,128)} %get-tuple-element.569.gb1.refs_3_, f32[480,128]{1,0:T(8,128)} %broadcast_in_dim.12.refs_3_.mask.refs_4_, ...), custom_call_target="tpu_custom_call" | custom-call | tf_op jit(solution)/shard_map/pallas_call | solution.py:361
  406.9 4.1 shard_map.442
  411.9 4.6 shard_map.443
  421.5 10.3 %shard_map.445 = (f32[4,480,512]{2,1,0:T(8,128)}, f32[32,8,128]{2,1,0:T(8,128)}) custom-call(f32[1]{0:T(128)} %bitcast.7.refs_0_.cnt, f32[32,8,128]{2,1,0:T(8,128)} %all-to-all-done.refs_1_.refs_2_, f32[2,512]{1,0:T(2,128)} %get-tuple-element.570.refs_2_.refs_3_, f32[480,128]{1,0:T(8,128)} %broadcast_in_dim.12.refs_3_.mask.refs_4_, ...), custom_call_target="tpu_custom_call" | custom-call | tf_op jit(solution)/shard_map/pallas_call | solution.py:361
  432.5 4.4 collective-permute-done.50.refs_2_
  437.2 4.8 all-to-all-start.9
  448.8 3.5 shard_map.446
  453.1 8.8 %shard_map.448 = (bf16[4,480,512]{2,1,0:T(8,128)(2,1)}, bf16[1024,512]{1,0:T(8,128)(2,1)}) custom-call(f32[1]{0:T(128)} %bitcast.7.refs_0_.cnt, f32[32,8,128]{2,1,0:T(8,128)} %all-to-all-done.9.refs_1_, f32[32,8,128]{2,1,0:T(8,128)} %all-to-all-done.refs_1_.refs_2_, f32[2,512]{1,0:T(2,128)} %get-tuple-element.570.refs_2_.refs_3_, ...), custom_call_target="tpu_custom_call" | custom-call | flops 20000000000 | bytes 60000000 | tf_op jit(solution)/shard_map/pallas_call | solution.py:404
  467.1 7.1 %all-to-all-start.10 = ((bf16[16,32,512]{2,1,0:T(8,128)(2,1)}), bf16[16,32,512]{2,1,0:T(8,128)(2,1)}, u32[]{:S(2)}, u32[]{:S(2)}) async-start(bf16[16,32,512]{2,1,0:T(8,128)(2,1)} %bitcast.43), calls=%async_computation.10 | async-start | bytes 1048576 | tf_op jit(solution)/shard_map/all_to_all | solution.py:1557
  479.6 11.8 %shard_map.449 = (bf16[4,8,8,1024]{3,2,1,0:T(8,128)(2,1)}, bf16[4,12,12,1024]{3,2,1,0:T(8,128)(2,1)}, bf16[4,14,14,1024]{3,2,1,0:T(8,128)(2,1)}) custom-call(f32[480,128]{1,0:T(8,128)} %broadcast_in_dim.12.refs_3_.mask.refs_4_, bf16[256,128]{1,0:T(8,128)(2,1)} %constant.61.clone.tc, bf16[192,192]{1,0:T(8,128)(2,1)} %constant.62.clone.tm, ...), custom_call_target="tpu_custom_call" | custom-call | tf_op jit(solution)/shard_map/pallas_call | solution.py:902
  491.4 12.6 %collective-permute-done.53.refs_2_ = bf16[4,192,256]{2,1,0:T(8,128)(2,1)S(1)} collective-permute-done((bf16[4,192,256]{2,1,0:T(8,128)(2,1)}, bf16[4,192,256]{2,1,0:T(8,128)(2,1)S(1)}, u32[]{:S(2)}, u32[]{:S(2)}) %collective-permute-start.53) | collective-permute-done | bytes 393248 | tf_op jit(solution)/shard_map/ppermute | solution.py:1095
  510.9 4.0 copy.150
  514.9 3.5 copy.149
  534.5 8.9 %collective-permute-done.63.refs_1_ = bf16[2,1,192,256]{3,2,1,0:T(8,128)(2,1)S(1)} collective-permute-done((bf16[2,1,192,256]{3,2,1,0:T(8,128)(2,1)S(1)}, bf16[2,1,192,256]{3,2,1,0:T(8,128)(2,1)S(1)}, u32[]{:S(2)}, u32[]{:S(2)}) %collective-permute-start.63) | collective-permute-done | bytes 196640 | tf_op jit(solution)/shard_map/ppermute | solution.py:1095
  (420 shorter events, 208.7 us)
Async XLA Ops:
  7.2 165.5 %all-gather.3.cloned.1.call-start = ((), (), s32[]{:S(2)}) async-start(), calls=%async_computation.11 | async-start | bytes 3244032 | tf_op jit(solution)/shard_map/all_gather | solution.py:1387
  26.2 12.7 %collective-permute-start.3 = (bf16[4,48,512]{2,1,0:T(8,128)(2,1)S(1)}, bf16[4,48,512]{2,1,0:T(8,128)(2,1)S(1)}, u32[]{:S(2)}, u32[]{:S(2)}) collective-permute-start(bf16[4,48,512]{2,1,0:T(8,128)(2,1)S(1)} %pad_maximum_fusion.7), channel_id=1, source_target_pairs={{0,1},{1,0},{2,3},{3,2},{4,5},{5,4},{6,7},{7,6},{8,9},{9,8},{10,11... | collective-permute-start | bytes 589832 | tf_op jit(solution)/shard_map/ppermute | solution.py:1095
  27.8 11.2 %collective-permute-start.4 = (bf16[4,48,512]{2,1,0:T(8,128)(2,1)S(1)}, bf16[4,48,512]{2,1,0:T(8,128)(2,1)S(1)}, u32[]{:S(2)}, u32[]{:S(2)}) collective-permute-start(bf16[4,48,512]{2,1,0:T(8,128)(2,1)S(1)} %pad_maximum_fusion.7), channel_id=1, source_target_pairs={{0,4},{1,5},{2,6},{3,7},{4,0},{5,1},{6,2},{7,3},{8,12},{9,13},{10,... | collective-permute-start | bytes 589832 | tf_op jit(solution)/shard_map/ppermute | solution.py:1095
  29.3 9.7 %collective-permute-start.5 = (bf16[4,48,512]{2,1,0:T(8,128)(2,1)S(1)}, bf16[4,48,512]{2,1,0:T(8,128)(2,1)S(1)}, u32[]{:S(2)}, u32[]{:S(2)}) collective-permute-start(bf16[4,48,512]{2,1,0:T(8,128)(2,1)S(1)} %pad_maximum_fusion.7), channel_id=1, source_target_pairs={{0,5},{1,4},{2,7},{3,6},{4,1},{5,0},{6,3},{7,2},{8,13},{9,12},{10,... | collective-permute-start | bytes 589832 | tf_op jit(solution)/shard_map/ppermute | solution.py:1095
  39.2 10.6 %collective-permute-start.7 = (bf16[144,512]{1,0:T(8,128)(2,1)S(1)}, bf16[144,512]{1,0:T(8,128)(2,1)S(1)}, u32[]{:S(2)}, u32[]{:S(2)}) collective-permute-start(bf16[144,512]{1,0:T(8,128)(2,1)S(1)} %convert_element_type.95), channel_id=1, source_target_pairs={{0,8},{1,9},{2,10},{3,11},{4,12},{5,13},{6,14},{7,15},{8,0},{9,1},... | collective-permute-start | bytes 442376 | tf_op jit(solution)/shard_map/ppermute | solution.py:1095
  39.3 17.1 %collective-permute-start.8 = (bf16[144,512]{1,0:T(8,128)(2,1)S(1)}, bf16[144,512]{1,0:T(8,128)(2,1)S(1)}, u32[]{:S(2)}, u32[]{:S(2)}) collective-permute-start(bf16[144,512]{1,0:T(8,128)(2,1)S(1)} %convert_element_type.95), channel_id=1, source_target_pairs={{0,16},{1,17},{2,18},{3,19},{4,20},{5,21},{6,22},{7,23},{8,24},{9,... | collective-permute-start | bytes 442376 | tf_op jit(solution)/shard_map/ppermute | solution.py:1095
  40.5 15.8 %collective-permute-start.9 = (bf16[144,512]{1,0:T(8,128)(2,1)S(1)}, bf16[144,512]{1,0:T(8,128)(2,1)S(1)}, u32[]{:S(2)}, u32[]{:S(2)}) collective-permute-start(bf16[144,512]{1,0:T(8,128)(2,1)S(1)} %convert_element_type.95), channel_id=1, source_target_pairs={{0,24},{1,25},{2,26},{3,27},{4,28},{5,29},{6,30},{7,31},{8,16},{9,... | collective-permute-start | bytes 442376 | tf_op jit(solution)/shard_map/ppermute | solution.py:1095
  56.5 9.6 %collective-permute-start.10 = (bf16[4,144,256]{2,1,0:T(8,128)(2,1)S(1)}, bf16[4,144,256]{2,1,0:T(8,128)(2,1)S(1)}, u32[]{:S(2)}, u32[]{:S(2)}) collective-permute-start(bf16[4,144,256]{2,1,0:T(8,128)(2,1)S(1)} %get-tuple-element.256), channel_id=1, source_target_pairs={{0,1},{1,0},{2,3},{3,2},{4,5},{5,4},{6,7},{7,6},{8,9},{9,8},{10,11... | collective-permute-start | bytes 884744 | tf_op jit(solution)/shard_map/ppermute | solution.py:1095
  58.1 8.9 %collective-permute-start.11 = (bf16[4,144,256]{2,1,0:T(8,128)(2,1)S(1)}, bf16[4,144,256]{2,1,0:T(8,128)(2,1)S(1)}, u32[]{:S(2)}, u32[]{:S(2)}) collective-permute-start(bf16[4,144,256]{2,1,0:T(8,128)(2,1)S(1)} %get-tuple-element.257), channel_id=1, source_target_pairs={{0,4},{1,5},{2,6},{3,7},{4,0},{5,1},{6,2},{7,3},{8,12},{9,13},{10,... | collective-permute-start | bytes 884744 | tf_op jit(solution)/shard_map/ppermute | solution.py:1095
  67.0 33.0 %collective-permute-start.12 = (bf16[8,144,256]{2,1,0:T(8,128)(2,1)S(1)}, bf16[8,144,256]{2,1,0:T(8,128)(2,1)}, u32[]{:S(2)}, u32[]{:S(2)}) collective-permute-start(bf16[8,144,256]{2,1,0:T(8,128)(2,1)S(1)} %get-tuple-element.262), channel_id=1, source_target_pairs={{0,4},{1,5},{2,6},{3,7},{4,0},{5,1},{6,2},{7,3},{8,12},{9,13},{10,... | collective-permute-start | bytes 1769480 | tf_op jit(solution)/shard_map/ppermute | solution.py:1095
  69.6 30.5 %collective-permute-start.13 = (bf16[8,144,256]{2,1,0:T(8,128)(2,1)S(1)}, bf16[8,144,256]{2,1,0:T(8,128)(2,1)}, u32[]{:S(2)}, u32[]{:S(2)}) collective-permute-start(bf16[8,144,256]{2,1,0:T(8,128)(2,1)S(1)} %get-tuple-element.263), channel_id=1, source_target_pairs={{0,1},{1,0},{2,3},{3,2},{4,5},{5,4},{6,7},{7,6},{8,9},{9,8},{10,11... | collective-permute-start | bytes 1769480 | tf_op jit(solution)/shard_map/ppermute | solution.py:1095
  69.6 18.4 %collective-permute-start.14 = (bf16[48,2048]{1,0:T(8,128)(2,1)}, bf16[48,2048]{1,0:T(8,128)(2,1)}, u32[]{:S(2)}, u32[]{:S(2)}) collective-permute-start(bf16[48,2048]{1,0:T(8,128)(2,1)} %pad_maximum_fusion.8), channel_id=1, source_target_pairs={{0,8},{1,9},{2,10},{3,11},{4,12},{5,13},{6,14},{7,15},{8,0},{9,1},... | collective-permute-start | bytes 589832 | tf_op jit(solution)/shard_map/ppermute | solution.py:1095
  77.8 16.5 %collective-permute-start.15 = (bf16[48,2048]{1,0:T(8,128)(2,1)}, bf16[48,2048]{1,0:T(8,128)(2,1)}, u32[]{:S(2)}, u32[]{:S(2)}) collective-permute-start(bf16[48,2048]{1,0:T(8,128)(2,1)} %pad_maximum_fusion.8), channel_id=1, source_target_pairs={{0,16},{1,17},{2,18},{3,19},{4,20},{5,21},{6,22},{7,23},{8,24},{9,... | collective-permute-start | bytes 589832 | tf_op jit(solution)/shard_map/ppermute | solution.py:1095
  77.8 16.5 %collective-permute-start.16 = (bf16[48,2048]{1,0:T(8,128)(2,1)}, bf16[48,2048]{1,0:T(8,128)(2,1)}, u32[]{:S(2)}, u32[]{:S(2)}) collective-permute-start(bf16[48,2048]{1,0:T(8,128)(2,1)} %pad_maximum_fusion.8), channel_id=1, source_target_pairs={{0,24},{1,25},{2,26},{3,27},{4,28},{5,29},{6,30},{7,31},{8,16},{9,... | collective-permute-start | bytes 589832 | tf_op jit(solution)/shard_map/ppermute | solution.py:1095
  80.2 19.9 %all-to-all-start = ((f32[32,8,128]{2,1,0:T(8,128)}), f32[32,8,128]{2,1,0:T(8,128)}, u32[]{:S(2)}, u32[]{:S(2)}) async-start(f32[32,8,128]{2,1,0:T(8,128)} %get-tuple-element.261), calls=%async_computation | async-start | bytes 262144 | tf_op jit(solution)/shard_map/all_to_all | solution.py:1099
  83.6 137.6 %all-gather.5.cloned.1.call-start = ((), (), s32[]{:S(2)}) async-start(), calls=%async_computation.12 | async-start | bytes 2162688 | tf_op jit(solution)/shard_map/all_gather | solution.py:1387
  104.6 11.2 %collective-permute-start.19 = (bf16[4,48,1024]{2,1,0:T(8,128)(2,1)S(1)}, bf16[4,48,1024]{2,1,0:T(8,128)(2,1)S(1)}, u32[]{:S(2)}, u32[]{:S(2)}) collective-permute-start(bf16[4,48,1024]{2,1,0:T(8,128)(2,1)S(1)} %get-tuple-element.549), channel_id=1, source_target_pairs={{0,1},{1,0},{2,3},{3,2},{4,5},{5,4},{6,7},{7,6},{8,9},{9,8},{10,11... | collective-permute-start | bytes 1179656 | tf_op jit(solution)/shard_map/ppermute | solution.py:1095
  105.5 11.2 %collective-permute-start.20 = (bf16[4,48,1024]{2,1,0:T(8,128)(2,1)S(1)}, bf16[4,48,1024]{2,1,0:T(8,128)(2,1)}, u32[]{:S(2)}, u32[]{:S(2)}) collective-permute-start(bf16[4,48,1024]{2,1,0:T(8,128)(2,1)S(1)} %get-tuple-element.548), channel_id=1, source_target_pairs={{0,4},{1,5},{2,6},{3,7},{4,0},{5,1},{6,2},{7,3},{8,12},{9,13},{10,... | collective-permute-start | bytes 1179656 | tf_op jit(solution)/shard_map/ppermute | solution.py:1095
  119.6 28.8 %collective-permute-start.21 = (bf16[8,48,1024]{2,1,0:T(8,128)(2,1)}, bf16[8,48,1024]{2,1,0:T(8,128)(2,1)}, u32[]{:S(2)}, u32[]{:S(2)}) collective-permute-start(bf16[8,48,1024]{2,1,0:T(8,128)(2,1)} %pad_maximum_fusion.1), channel_id=1, source_target_pairs={{0,4},{1,5},{2,6},{3,7},{4,0},{5,1},{6,2},{7,3},{8,12},{9,13},{10,... | collective-permute-start | bytes 2359304 | tf_op jit(solution)/shard_map/ppermute | solution.py:1095
  121.2 27.2 %collective-permute-start.22 = (bf16[8,48,1024]{2,1,0:T(8,128)(2,1)}, bf16[8,48,1024]{2,1,0:T(8,128)(2,1)}, u32[]{:S(2)}, u32[]{:S(2)}) collective-permute-start(bf16[8,48,1024]{2,1,0:T(8,128)(2,1)} %pad_maximum_fusion.2), channel_id=1, source_target_pairs={{0,1},{1,0},{2,3},{3,2},{4,5},{5,4},{6,7},{7,6},{8,9},{9,8},{10,11... | collective-permute-start | bytes 2359304 | tf_op jit(solution)/shard_map/ppermute | solution.py:1095
  136.9 11.4 %all-to-all-start.1 = ((f32[32,8,128]{2,1,0:T(8,128)}), f32[32,8,128]{2,1,0:T(8,128)S(1)}, u32[]{:S(2)}, u32[]{:S(2)}) async-start(f32[32,8,128]{2,1,0:T(8,128)} %get-tuple-element.278), calls=%async_computation.1 | async-start | bytes 262144 | tf_op jit(solution)/shard_map/all_to_all | solution.py:1099
  178.5 9.3 %collective-permute-start.29 = (f32[4,16,128]{2,1,0:T(8,128)S(1)}, f32[4,16,128]{2,1,0:T(8,128)S(1)}, u32[]{:S(2)}, u32[]{:S(2)}) collective-permute-start(f32[4,16,128]{2,1,0:T(8,128)S(1)} %add_add_fusion.3), channel_id=1, source_target_pairs={{0,8},{1,9},{2,10},{3,11},{4,12},{5,13},{6,14},{7,15},{8,0},{9,1},... | collective-permute-start | bytes 98312 | tf_op jit(solution)/shard_map/ppermute | solution.py:1095
  179.6 8.2 %collective-permute-start.30 = (f32[4,16,128]{2,1,0:T(8,128)S(1)}, f32[4,16,128]{2,1,0:T(8,128)S(1)}, u32[]{:S(2)}, u32[]{:S(2)}) collective-permute-start(f32[4,16,128]{2,1,0:T(8,128)S(1)} %add_add_fusion.3), channel_id=1, source_target_pairs={{0,16},{1,17},{2,18},{3,19},{4,20},{5,21},{6,22},{7,23},{8,24},{9,... | collective-permute-start | bytes 98312 | tf_op jit(solution)/shard_map/ppermute | solution.py:1095
  197.8 11.9 %all-to-all-start.2 = ((f32[32,8,128]{2,1,0:T(8,128)}), f32[32,8,128]{2,1,0:T(8,128)S(1)}, u32[]{:S(2)}, u32[]{:S(2)}) async-start(f32[32,8,128]{2,1,0:T(8,128)} %get-tuple-element.291), calls=%async_computation.2 | async-start | bytes 262144 | tf_op jit(solution)/shard_map/all_to_all | solution.py:1099
  218.5 11.2 %all-to-all-start.3 = ((f32[32,8,128]{2,1,0:T(8,128)}), f32[32,8,128]{2,1,0:T(8,128)S(1)}, u32[]{:S(2)}, u32[]{:S(2)}) async-start(f32[32,8,128]{2,1,0:T(8,128)} %get-tuple-element.293), calls=%async_computation.3 | async-start | bytes 262144 | tf_op jit(solution)/shard_map/all_to_all | solution.py:1099
  289.2 11.4 %all-to-all-start.6 = ((f32[32,8,128]{2,1,0:T(8,128)}), f32[32,8,128]{2,1,0:T(8,128)S(1)}, u32[]{:S(2)}, u32[]{:S(2)}) async-start(f32[32,8,128]{2,1,0:T(8,128)} %get-tuple-element.302), calls=%async_computation.6 | async-start | bytes 262144 | tf_op jit(solution)/shard_map/all_to_all | solution.py:1099
  311.6 11.4 %all-to-all-start.7 = ((f32[32,8,128]{2,1,0:T(8,128)}), f32[32,8,128]{2,1,0:T(8,128)S(1)}, u32[]{:S(2)}, u32[]{:S(2)}) async-start(f32[32,8,128]{2,1,0:T(8,128)} %get-tuple-element.310), calls=%async_computation.7 | async-start | bytes 262144 | tf_op jit(solution)/shard_map/all_to_all | solution.py:1099
  343.0 14.6 %collective-permute-start.43 = (bf16[2,16,160,256]{3,2,1,0:T(8,128)(2,1)}, bf16[2,16,160,256]{3,2,1,0:T(8,128)(2,1)S(1)}, u32[]{:S(2)}, u32[]{:S(2)}) collective-permute-start(bf16[2,16,160,256]{3,2,1,0:T(8,128)(2,1)} %get-tuple-element.325), channel_id=1, source_target_pairs={{0,2},{1,3},{2,0},{3,1},{4,6},{5,7},{6,4},{7,5},{8,10},{9,11},{10,... | collective-permute-start | bytes 7864328 | tf_op jit(solution)/shard_map/ppermute | solution.py:1095
  361.6 17.0 %collective-permute-start.44 = (bf16[8,160,256]{2,1,0:T(8,128)(2,1)}, bf16[8,160,256]{2,1,0:T(8,128)(2,1)S(1)}, u32[]{:S(2)}, u32[]{:S(2)}) collective-permute-start(bf16[8,160,256]{2,1,0:T(8,128)(2,1)} %get-tuple-element.332), channel_id=1, source_target_pairs={{0,1},{1,0},{2,3},{3,2},{4,5},{5,4},{6,7},{7,6},{8,9},{9,8},{10,11... | collective-permute-start | bytes 1966088 | tf_op jit(solution)/shard_map/ppermute | solution.py:1095
  362.7 15.9 %collective-permute-start.45 = (bf16[8,160,256]{2,1,0:T(8,128)(2,1)S(1)}, bf16[8,160,256]{2,1,0:T(8,128)(2,1)S(1)}, u32[]{:S(2)}, u32[]{:S(2)}) collective-permute-start(bf16[8,160,256]{2,1,0:T(8,128)(2,1)S(1)} %get-tuple-element.333), channel_id=1, source_target_pairs={{0,4},{1,5},{2,6},{3,7},{4,0},{5,1},{6,2},{7,3},{8,12},{9,13},{10,... | collective-permute-start | bytes 1966088 | tf_op jit(solution)/shard_map/ppermute | solution.py:1095
  378.6 13.6 %all-to-all-start.8 = ((f32[32,8,128]{2,1,0:T(8,128)}), f32[32,8,128]{2,1,0:T(8,128)S(1)}, u32[]{:S(2)}, u32[]{:S(2)}) async-start(f32[32,8,128]{2,1,0:T(8,128)} %get-tuple-element.337), calls=%async_computation.8 | async-start | bytes 262144 | tf_op jit(solution)/shard_map/all_to_all | solution.py:1099
  392.9 14.0 %collective-permute-start.48 = (bf16[2,16,192,256]{3,2,1,0:T(8,128)(2,1)}, bf16[2,16,192,256]{3,2,1,0:T(8,128)(2,1)}, u32[]{:S(2)}, u32[]{:S(2)}) collective-permute-start(bf16[2,16,192,256]{3,2,1,0:T(8,128)(2,1)} %get-tuple-element.356), channel_id=1, source_target_pairs={{0,2},{1,3},{2,0},{3,1},{4,6},{5,7},{6,4},{7,5},{8,10},{9,11},{10,... | collective-permute-start | bytes 9437192 | tf_op jit(solution)/shard_map/ppermute | solution.py:1095
  393.2 12.2 %collective-permute-start.46 = (bf16[4,160,256]{2,1,0:T(8,128)(2,1)}, bf16[4,160,256]{2,1,0:T(8,128)(2,1)S(1)}, u32[]{:S(2)}, u32[]{:S(2)}) collective-permute-start(bf16[4,160,256]{2,1,0:T(8,128)(2,1)} %get-tuple-element.353), channel_id=1, source_target_pairs={{0,4},{1,5},{2,6},{3,7},{4,0},{5,1},{6,2},{7,3},{8,12},{9,13},{10,... | collective-permute-start | bytes 983048 | tf_op jit(solution)/shard_map/ppermute | solution.py:1095
  394.9 11.2 %collective-permute-start.47 = (bf16[4,160,256]{2,1,0:T(8,128)(2,1)S(1)}, bf16[4,160,256]{2,1,0:T(8,128)(2,1)S(1)}, u32[]{:S(2)}, u32[]{:S(2)}) collective-permute-start(bf16[4,160,256]{2,1,0:T(8,128)(2,1)S(1)} %get-tuple-element.354), channel_id=1, source_target_pairs={{0,1},{1,0},{2,3},{3,2},{4,5},{5,4},{6,7},{7,6},{8,9},{9,8},{10,11... | collective-permute-start | bytes 983048 | tf_op jit(solution)/shard_map/ppermute | solution.py:1095
  416.6 20.6 %collective-permute-start.52 = (bf16[2,16,144,256]{3,2,1,0:T(8,128)(2,1)}, bf16[2,16,144,256]{3,2,1,0:T(8,128)(2,1)}, u32[]{:S(2)}, u32[]{:S(2)}) collective-permute-start(bf16[2,16,144,256]{3,2,1,0:T(8,128)(2,1)} %get-tuple-element.380), channel_id=1, source_target_pairs={{0,2},{1,3},{2,0},{3,1},{4,6},{5,7},{6,4},{7,5},{8,10},{9,11},{10,... | collective-permute-start | bytes 7077896 | tf_op jit(solution)/shard_map/ppermute | solution.py:1095
  416.7 20.3 %collective-permute-start.50 = (bf16[8,192,256]{2,1,0:T(8,128)(2,1)}, bf16[8,192,256]{2,1,0:T(8,128)(2,1)}, u32[]{:S(2)}, u32[]{:S(2)}) collective-permute-start(bf16[8,192,256]{2,1,0:T(8,128)(2,1)} %get-tuple-element.377), channel_id=1, source_target_pairs={{0,1},{1,0},{2,3},{3,2},{4,5},{5,4},{6,7},{7,6},{8,9},{9,8},{10,11... | collective-permute-start | bytes 2359304 | tf_op jit(solution)/shard_map/ppermute | solution.py:1095
  417.3 19.9 %collective-permute-start.51 = (bf16[8,192,256]{2,1,0:T(8,128)(2,1)}, bf16[8,192,256]{2,1,0:T(8,128)(2,1)}, u32[]{:S(2)}, u32[]{:S(2)}) collective-permute-start(bf16[8,192,256]{2,1,0:T(8,128)(2,1)} %get-tuple-element.378), channel_id=1, source_target_pairs={{0,4},{1,5},{2,6},{3,7},{4,0},{5,1},{6,2},{7,3},{8,12},{9,13},{10,... | collective-permute-start | bytes 2359304 | tf_op jit(solution)/shard_map/ppermute | solution.py:1095
  420.1 11.8 %collective-permute-start.49 = (bf16[2,2,160,256]{3,2,1,0:T(8,128)(2,1)}, bf16[2,2,160,256]{3,2,1,0:T(8,128)(2,1)S(1)}, u32[]{:S(2)}, u32[]{:S(2)}) collective-permute-start(bf16[2,2,160,256]{3,2,1,0:T(8,128)(2,1)} %get-tuple-element.375), channel_id=1, source_target_pairs={{0,8},{1,9},{2,10},{3,11},{4,12},{5,13},{6,14},{7,15},{8,0},{9,1},... | collective-permute-start | bytes 983048 | tf_op jit(solution)/shard_map/ppermute | solution.py:1095
  437.2 15.9 %all-to-all-start.9 = ((f32[32,8,128]{2,1,0:T(8,128)}), f32[32,8,128]{2,1,0:T(8,128)}, u32[]{:S(2)}, u32[]{:S(2)}) async-start(f32[32,8,128]{2,1,0:T(8,128)} %get-tuple-element.384), calls=%async_computation.9 | async-start | bytes 262144 | tf_op jit(solution)/shard_map/all_to_all | solution.py:1099
  467.1 37.6 %all-to-all-start.10 = ((bf16[16,32,512]{2,1,0:T(8,128)(2,1)}), bf16[16,32,512]{2,1,0:T(8,128)(2,1)}, u32[]{:S(2)}, u32[]{:S(2)}) async-start(bf16[16,32,512]{2,1,0:T(8,128)(2,1)} %bitcast.43), calls=%async_computation.10 | async-start | bytes 1048576 | tf_op jit(solution)/shard_map/all_to_all | solution.py:1557
  474.2 30.5 %collective-permute-start.55 = (bf16[8,144,256]{2,1,0:T(8,128)(2,1)}, bf16[8,144,256]{2,1,0:T(8,128)(2,1)S(1)}, u32[]{:S(2)}, u32[]{:S(2)}) collective-permute-start(bf16[8,144,256]{2,1,0:T(8,128)(2,1)} %get-tuple-element.402), channel_id=1, source_target_pairs={{0,1},{1,0},{2,3},{3,2},{4,5},{5,4},{6,7},{7,6},{8,9},{9,8},{10,11... | collective-permute-start | bytes 1769480 | tf_op jit(solution)/shard_map/ppermute | solution.py:1095
  476.3 28.4 %collective-permute-start.56 = (bf16[8,144,256]{2,1,0:T(8,128)(2,1)}, bf16[8,144,256]{2,1,0:T(8,128)(2,1)S(1)}, u32[]{:S(2)}, u32[]{:S(2)}) collective-permute-start(bf16[8,144,256]{2,1,0:T(8,128)(2,1)} %copy-done.29), channel_id=1, source_target_pairs={{0,4},{1,5},{2,6},{3,7},{4,0},{5,1},{6,2},{7,3},{8,12},{9,13},{10,... | collective-permute-start | bytes 1769480 | tf_op jit(solution)/shard_map/ppermute | solution.py:1095
  477.8 26.2 %collective-permute-start.53 = (bf16[4,192,256]{2,1,0:T(8,128)(2,1)}, bf16[4,192,256]{2,1,0:T(8,128)(2,1)S(1)}, u32[]{:S(2)}, u32[]{:S(2)}) collective-permute-start(bf16[4,192,256]{2,1,0:T(8,128)(2,1)} %copy-done.31), channel_id=1, source_target_pairs={{0,4},{1,5},{2,6},{3,7},{4,0},{5,1},{6,2},{7,3},{8,12},{9,13},{10,... | collective-permute-start | bytes 1179656 | tf_op jit(solution)/shard_map/ppermute | solution.py:1095
  478.3 25.6 %collective-permute-start.54 = (bf16[4,192,256]{2,1,0:T(8,128)(2,1)}, bf16[4,192,256]{2,1,0:T(8,128)(2,1)S(1)}, u32[]{:S(2)}, u32[]{:S(2)}) collective-permute-start(bf16[4,192,256]{2,1,0:T(8,128)(2,1)} %copy-done.30), channel_id=1, source_target_pairs={{0,1},{1,0},{2,3},{3,2},{4,5},{5,4},{6,7},{7,6},{8,9},{9,8},{10,11... | collective-permute-start | bytes 1179656 | tf_op jit(solution)/shard_map/ppermute | solution.py:1095
  508.7 13.0 %collective-permute-start.64 = (bf16[2,1,160,256]{3,2,1,0:T(8,128)(2,1)}, bf16[2,1,160,256]{3,2,1,0:T(8,128)(2,1)S(1)}, u32[]{:S(2)}, u32[]{:S(2)}) collective-permute-start(bf16[2,1,160,256]{3,2,1,0:T(8,128)(2,1)} %get-tuple-element.450), channel_id=1, source_target_pairs={{0,16},{1,17},{2,18},{3,19},{4,20},{5,21},{6,22},{7,23},{8,24},{9,... | collective-permute-start | bytes 491528 | tf_op jit(solution)/shard_map/ppermute | solution.py:1095
  520.5 11.9 %collective-permute-start.62 = (bf16[2,2,192,256]{3,2,1,0:T(8,128)(2,1)S(1)}, bf16[2,2,192,256]{3,2,1,0:T(8,128)(2,1)S(1)}, u32[]{:S(2)}, u32[]{:S(2)}) collective-permute-start(bf16[2,2,192,256]{3,2,1,0:T(8,128)(2,1)S(1)} %get-tuple-element.446), channel_id=1, source_target_pairs={{0,8},{1,9},{2,10},{3,11},{4,12},{5,13},{6,14},{7,15},{8,0},{9,1},... | collective-permute-start | bytes 1179656 | tf_op jit(solution)/shard_map/ppermute | solution.py:1095
  530.2 14.0 %collective-permute-start.60 = (bf16[2,2,144,256]{3,2,1,0:T(8,128)(2,1)S(1)}, bf16[2,2,144,256]{3,2,1,0:T(8,128)(2,1)S(1)}, u32[]{:S(2)}, u32[]{:S(2)}) collective-permute-start(bf16[2,2,144,256]{3,2,1,0:T(8,128)(2,1)S(1)} %get-tuple-element.421), channel_id=1, source_target_pairs={{0,8},{1,9},{2,10},{3,11},{4,12},{5,13},{6,14},{7,15},{8,0},{9,1},... | collective-permute-start | bytes 884744 | tf_op jit(solution)/shard_map/ppermute | solution.py:1095
  533.5 9.9 %collective-permute-start.63 = (bf16[2,1,192,256]{3,2,1,0:T(8,128)(2,1)S(1)}, bf16[2,1,192,256]{3,2,1,0:T(8,128)(2,1)S(1)}, u32[]{:S(2)}, u32[]{:S(2)}) collective-permute-start(bf16[2,1,192,256]{3,2,1,0:T(8,128)(2,1)S(1)} %get-tuple-element.448), channel_id=1, source_target_pairs={{0,16},{1,17},{2,18},{3,19},{4,20},{5,21},{6,22},{7,23},{8,24},{9,... | collective-permute-start | bytes 589832 | tf_op jit(solution)/shard_map/ppermute | solution.py:1095
  (95 other events, 565.0 us)
Sparse Core Ops, SparseCore 0:
  11.6 75.4 all-gather.2
  107.6 54.9 all-gather.4

commit v4 on v3

--- a/solution.py
+++ b/solution.py
@@ -804,42 +804,36 @@
 
 
 def spatial_grad(s, m, ins, outs, so, extra):
-    (cnt,), (t1, s1, gb1, mask), (g1, a2, im), (d1, gsp) = s, m, ins, outs
-    live = tiled(mask[...], MID)
-    st = stats_of(total_of(s1), cnt[0], gb1[...])
-    g1.get()
-    a2.get()
-    x, _ = normalize(a2.v[...], st)
-    d = norm_back(g1.v[...], x, live, st, back_rows(total_of(t1)), cnt[0]).astype(BF16)
-    d1.v[...] = d
-    d1.put()
+    (d1, im), (gsp,) = ins, outs
     for t in range(9):
         sl = slice(t * MID, (t + 1) * MID)
-        im.get(t)
         gsp.v[sl, :] = dot_tn(im.v[:, sl], d1.v[...]).astype(BF16)
-        gsp.put(t)
-
-
-def run_spatial_grad(cnt, small, g1, a2, im):
+
+
+def run_spatial_grad(d1, im):
     return plain_call(
-        spatial_grad, (cnt,), small, [(g1, 1, 0), (a2, 1, 0), (im, 9, 1)],
-        [((R, MID), BF16, 1, 0), ((9 * MID, MID), BF16, 9, 0)],
-    )
+        spatial_grad, (), (), [(d1, 1, 0), (im, 9, 1)], [((9 * MID, MID), BF16, 9, 0)],
+    )[0]
 
 
 def conv_back(s, m, ins, outs, so, extra):
-    (cnt,), (s0, gb0, mask), (d1, w, a1), (g0,), (moved_ref,) = s, m, ins, outs, extra
+    (cnt,), (t1, s1, gb1, s0, gb0, mask), (moved_ref,) = s, m, extra
+    (g1, a2, w, a1), (d1, g0) = ins, outs
     live = mask[...]
-    d1.get()
+    st = stats_of(total_of(s1), cnt[0], gb1[...])
+    tot = back_rows(total_of(t1))
     for c in range(4):
         sl = slice(c * 128, (c + 1) * 128)
-        d = d1.v[:, sl].astype(F32)
+        stc = cols(st, c)
+        x, _ = normalize(a2.v[:, sl], stc)
+        d = norm_back(g1.v[:, sl], x, live, stc, cols(tot, c), cnt[0]).astype(BF16)
+        d1.v[:, sl] = d
+        d = d.astype(F32)
         for dx in (0, 1):
             moved = kshift_cols(d, dx)
             for dy in (0, 1):
                 moved_ref[dy * 2 + dx, :, sl] = shift_rows(moved, dy).astype(BF16)
     st = stats_of(total_of(s0), 4.0 * cnt[0], gb0[...])
-    w.get()
     total = jnp.zeros((8, 128), F32)
     for ph in range(4):
         gh = None
@@ -847,7 +841,6 @@
             if p == ph:
                 part = dot_nt(moved_ref[-dy * 2 - dx], w.v[t * MID : (t + 1) * MID, :])
                 gh = part if gh is None else gh + part
-        a1.get(ph)
         sums = []
         for c in range(4):
             sl = slice(c * 128, (c + 1) * 128)
@@ -855,15 +848,15 @@
             g = gh[:, sl] * live * silu_grad(u)
             g0.v[ph, :, sl] = g
             sums.append((jnp.sum(g * x, axis=0, keepdims=True), jnp.sum(g, axis=0, keepdims=True)))
-        g0.put(ph)
         total = total + jnp.concatenate([v[0] for v in sums] + [v[1] for v in sums], axis=0)
     spread_rows(so[0], total)
 
 
-def run_conv_back(n, cnt, small, d1, w, a1):
+def run_conv_back(n, cnt, small, g1, a2, w, a1):
     return plain_call(
-        conv_back, (cnt,), small, [(d1, 1, 0), (w, 1, 0), (a1, 4, 0)],
-        [((4, R, MID), F32, 4, 0)], [like((n, 8, 128))], [pltpu.VMEM((4, R, MID), BF16)],
+        conv_back, (cnt,), small, [(g1, 1, 0), (a2, 1, 0), (w, 1, 0), (a1, 4, 0)],
+        [((R, MID), BF16, 1, 0), ((4, R, MID), F32, 4, 0)], [like((n, 8, 128))],
+        [pltpu.VMEM((4, R, MID), BF16)],
     )
 
 
@@ -1329,6 +1322,22 @@
     )(*given)
 
 
+def norm_rows(t0, t1, tj, t4, t5, t6, out):
+    for half in range(2):
+        row = 64 * half
+        short = slice(4 * half, 4 * half + 4)
+        out[row : row + 4, :] = total_of(t0)[short]
+        out[row + 4 : row + 8, :] = total_of(t1)[short]
+        for k in range(2):
+            at = 8 if half else 4 * k
+            for c in range(4):
+                base = row + 8 + 16 * k + 4 * c
+                out[base : base + 4, :] = tj[c, at : at + 4, :]
+        out[row + 40 : row + 44, :] = total_of(t4)[short]
+        out[row + 44 : row + 48, :] = total_of(t5)[short]
+        out[row + 48 : row + 64, :] = t6[16 * half : 16 * half + 16, :]
+
+
 class Scatter:
     def __init__(self, me, arrays, pieces, width, n, fsdp):
         self.n = n
@@ -1415,17 +1424,22 @@
     ga = Gather([reduce_one, small], n, fsdp)
     gb_ = Gather([spatial_one], n, fsdp)
     gc_ = Gather([shortcut_one, expand_one], n, fsdp)
-    narrow = [reduce_two, flat(excite_down), flat(excite_up), flat(temporal_mix)]
+    tall = ga.x.shape[0]
+    both = Gather([jnp.concatenate([ga.x, gb_.x], axis=0)], n, fsdp)
+    both.first()
+    xph = run_split(alive_slots, clips, tables)
+    *both.hops, xph = tie(*both.hops, xph)
+    xph, *late = tie(xph, reduce_two, excite_down, excite_up, temporal_mix, expand_two)
+    narrow = [late[0], flat(late[1]), flat(late[2]), flat(late[3])]
     rows = [v.shape[0] for v in narrow]
     narrow = jnp.concatenate(narrow, axis=0)
     got = gather(jnp.pad(narrow, ((0, -narrow.shape[0] % 16), (0, 0))))
-    we2 = gather(expand_two)
-    ga.first()
-    *ga.hops, gb_.x, clips[0], clips[1], clips[2] = tie(*ga.hops, gb_.x, *clips)
+    we2 = gather(late[4])
+    ga.hops = [v[:tall] for v in both.hops]
+    gb_.hops = [v[tall:] for v in both.hops]
     ga.second()
-    gb_.first()
-    xph = run_split(alive_slots, clips, tables)
-    ga.planes[0], xph = tie(ga.planes[0], xph)
+    gb_.split()
+    gb_.hop(0)
     ga.third()
     w1, norms = ga.finish(me)
     norms = norms.reshape(n, -1, MID)
@@ -1435,17 +1449,14 @@
     edges = [0, 512, 1024, 3072, 5120, 5632, 6144, 8192]
     gb = [norms[:, edges[k] : edges[k + 1]] for k in range(7)]
 
-    w1, gc_.x, *gb_.hops = tie(w1, gc_.x, *gb_.hops)
-    gb_.split()
-    w1, *gb_.planes = tie(w1, *gb_.planes)
-    gb_.hop(0)
+    for k in range(1, len(gb_.paths[0])):
+        w1, *gb_.got = tie(w1, *gb_.got)
+        gb_.land()
+        w1, *gb_.planes = tie(w1, *gb_.planes)
+        gb_.hop(k)
+    w1, gc_.x = tie(w1, gc_.x)
     gc_.first()
     a1, p0 = run_enter(n, xph, w1)
-    for k in range(1, len(gb_.paths[0])):
-        p0, *gb_.got = tie(p0, *gb_.got)
-        gb_.land()
-        p0, *gb_.planes = tie(p0, *gb_.planes)
-        gb_.hop(k)
     s0 = exchange(p0)
     s0, *rest = tie(s0, *gb_.got, *gc_.hops)
     gb_.got, gc_.hops = rest[:2], rest[2:]
@@ -1530,23 +1541,20 @@
         me, [blocks(ge1), blocks(gsk)], [(i, c) for i in range(2) for c in starts], MID, n, fsdp
     )
     t1 = rb.ready(ra.ready(t1))
-    d1, gsp = run_spatial_grad(cnt, (t1, s1, gb[1], m128), g1, a2, im)
-    d1 = rb.end(ra.end(d1))
+    d1, g0, p0 = run_conv_back(
+        n, cnt, (t1, s1, gb[1], s0, gb[0], m128), g1, a2, wsp, a1
+    )
+    p0 = rb.end(ra.end(p0))
+    p0, d1 = tie(p0, d1)
+    t0 = exchange(p0)
+    gsp = run_spatial_grad(d1, im)
+    rc = Scatter(me, [blocks(gsp)], [(0, 0)], MID, n, fsdp)
     rb.add()
-    d1 = rb.ready(d1)
-    gsp, d1 = tie(gsp, d1)
-    rc = Scatter(me, [blocks(gsp)], [(0, 0)], MID, n, fsdp)
-    d1 = rc.ready(d1)
-    ra.add()
-    d1 = ra.ready(d1)
-    g0, p0 = run_conv_back(n, cnt, (s0, gb[0], m128), d1, wsp, a1)
-    p0 = rc.end(rb.end(ra.end(p0)))
-    t0 = exchange(p0)
-    rc.add()
-    rb.add()
-    ra.add()
     t0 = rb.ready(rc.ready(t0))
     d0, gr1 = run_first_grads(cnt, (t0, s0, gb[0], m128), g0, a1, xph)
+    d0 = rc.end(d0)
+    rc.add()
+    d0 = rc.ready(d0)
     gr1 = blocks(gr1)
     gr1 = gr1.reshape(n // (2 * fsdp), 2, fsdp, -1, MID)
     side = (me[0] >> core) & 1
@@ -1559,17 +1567,21 @@
     )
     gin = list(run_input_grads(m128, tables_t, d0, d3, w1, wsk))
     gin[0] = rc.end(rb.end(gin[0]))
-    gin[0], got, *rest = tie(gin[0], got, *rb.got, *rc.got)
-    rb.got, rc.got = rest[:2], rest[2:]
     rc.add()
     rb.add()
+    ra.add()
     gin[0] = ra.ready(rb.ready(rc.ready(gin[0])))
-    *rc.got, t0, t1, t4, t5, t6, tj = tie(*rc.got, t0, t1, t4, t5, t6, tj)
+    *rc.got, rb.got[0], ra.got[0] = tie(*rc.got, rb.got[0], ra.got[0])
     rc.add()
     rc.start()
     rb.add()
     rb.start()
-    *rc.got, o_m, o_f, got = tie(*rc.got, o_m, o_f, got)
+    ra.add()
+    ra.start()
+    *rc.got, t0, t1, t4, t5, t6, tj, o_m, o_f = tie(*rc.got, t0, t1, t4, t5, t6, tj, o_m, o_f)
+    rc.add()
+    rc.start()
+    *rc.got, got = tie(*rc.got, got)
     gr1 = jnp.sum(got.astype(F32), axis=0)[: reduce_one.shape[0]]
     second = ra.rest()
     gsp = rc.rest()[0][: spatial_one.shape[0]]
@@ -1583,17 +1595,9 @@
     s2_ = s1_ + excite_down.size
     s3_ = s2_ + excite_up.size
 
-    def split_rows(t, k):
-        t = jnp.sum(t, axis=0) if t.ndim == 3 else t
-        return t.reshape(k, -1)
-
-    t0, t1, t4, t5 = (split_rows(t, 2) for t in (t0, t1, t4, t5))
-    t6 = split_rows(t6, 2)
     gkernel = tj[:, 12:].reshape(16, 128)[:9, :SQUEEZE]
-    tj = jnp.stack([tj[:, 4 * k : 4 * k + 4].reshape(-1) for k in range(3)])
-    gain = jnp.concatenate([t0[0], t1[0], tj[0], tj[1], t4[0], t5[0], t6[0]])
-    bias = jnp.concatenate([t0[1], t1[1], tj[2], tj[2], t4[1], t5[1], t6[1]])
-    gnorm = lax.dynamic_slice_in_dim(jnp.stack([gain, bias]), me[0] * (8192 // n), 8192 // n, 1)
+    gnorm = call(norm_rows, [like((128, 128))], 6, scalars=0)(t0, t1, tj, t4, t5, t6)[0]
+    gnorm = lax.dynamic_slice_in_dim(gnorm.reshape(2, 8192), me[0] * (8192 // n), 8192 // n, 1)
     return (
         o_c, o_m, o_f, gin[0], gin[1], gin[2],
         gr1,

time: 571 us -> 541 us (0.947)
  waiting for transfers between devices: 108 us -> 93.3 us
  starting transfers between devices: 109 us -> 98.8 us
    ppermute x65 -> x62, waiting for transfers between devices: 71.4 us -> 58.4 us  [swap(): return lax.ppermute(v, AXES, [(i, i ^ d) for i in range(n)])]
    ppermute x65 -> x62, starting transfers between devices: 75 us -> 67.3 us  [swap(): return lax.ppermute(v, AXES, [(i, i ^ d) for i in range(n)])]
    unnamed x163 -> x139, local copies, waits for them, and re-layouts: 36.5 us -> 39.1 us
  transfers between devices with their start and end apart: 76 -> 73, of which waited for: 35 -> 34; matrix products, arithmetic and copies ran while one was open for 12% -> 13% of each run, Pallas kernels for 23% -> 28%
where the time goes in v4:
time: 541 us; the launch traced here: 531 us
  Pallas kernels  204 us (38%)
  starting transfers between devices  98.8 us (18%)
  waiting for transfers between devices  93.3 us (17%)
  local copies, waits for them, and re-layouts  67.9 us (13%)
  other arithmetic  27.9 us (5%)
  blocking collectives  21.9 us (4%)
  between operations  15.8 us (3%)
    ppermute x62, starting transfers between devices, swap(): return lax.ppermute(v, AXES, [(i, i ^ d) for i in range(n)])  67.3 us
    ppermute x62, waiting for transfers between devices, swap(): return lax.ppermute(v, AXES, [(i, i ^ d) for i in range(n)])  58.4 us
    pallas_call x6, Pallas kernels, flow_call(): pl.pallas_call(kernel, out_shape=[like(o[0], o[1]) for o in outs] + list(...  53.4 us
    pallas_call x4, Pallas kernels, wide_grid(): pl.pallas_call(kernel, grid=(steps,), out_shape=outs, in_specs=in_specs,...  48.3 us
    pallas_call x5, Pallas kernels, plain_call(): pl.pallas_call(kernel, out_shape=[like(o[0], o[1]) for o in outs] + list(...  44.4 us
    unnamed x139, local copies, waits for them, and re-layouts  39.1 us
    all_to_all x8, waiting for transfers between devices, exchange(): return lax.all_to_all(spread, AXES, 0, 0, tiled=True)  34.9 us
    all_to_all x8, starting transfers between devices, exchange(): return lax.all_to_all(spread, AXES, 0, 0, tiled=True)  26.4 us
  transfers between devices with their start and end apart: 73, of which 34 were waited for; matrix products, arithmetic and copies ran while one was open for 13% of the time, Pallas kernels for 28%

profile of v4, /device:TPU:0, one launch (start us, length us, event | category | flops | bytes accessed | tf_op | source)
XLA Modules:
  0.0 531.0 jit_solution(15176945257401065328)
XLA Ops:
  11.4 3.1 collective-permute-start
  17.7 3.2 copy.130.xf
  22.4 5.8 %shard_map.422.refs_0_.x.x0.refs_7_ = bf16[4,480,1024]{2,1,0:T(8,128)(2,1)} custom-call(f32[12]{0:T(128)} %convert_element_type.96.alive, bf16[4,8,8,1024]{3,2,1,0:T(8,128)(2,1)} %xc.1, bf16[4,12,12,1024]{3,2,1,0:T(8,128)(2,1)} %copy.129.xm, bf16[4,14,14,1024]{3,2,1,0:T(8,128)(2,1)} %copy.130.xf, bf16[128,256]{1,0:T(8,128)(2,1)} %constant.58.clone.tc, ...), custom_call_target="tpu_custom_call" | custom-call | tf_op jit(solution)/shard_map/pallas_call | solution.py:299
  28.3 3.4 collective-permute-done.1
  36.4 3.1 collective-permute-done.3
  39.5 3.2 collective-permute-done.4
  48.5 4.6 collective-permute-done.7
  57.5 5.2 collective-permute-start.11
  65.2 6.5 %shard_map.424 = (f32[4,480,512]{2,1,0:T(8,128)}, f32[32,8,128]{2,1,0:T(8,128)}) custom-call(bf16[4,480,1024]{2,1,0:T(8,128)(2,1)} %shard_map.422.refs_0_.x.x0.refs_7_, bf16[1024,512]{1,0:T(8,128)(2,1)} %bitcast.97), custom_call_target="tpu_custom_call" | custom-call | tf_op jit(solution)/shard_map/pallas_call | solution.py:404
  71.8 3.3 all-to-all-start
  75.2 8.9 %collective-permute-done.12 = bf16[48,2048]{1,0:T(8,128)(2,1)} collective-permute-done((bf16[48,2048]{1,0:T(8,128)(2,1)}, bf16[48,2048]{1,0:T(8,128)(2,1)}, u32[]{:S(2)}, u32[]{:S(2)}) %collective-permute-start.12) | collective-permute-done | bytes 196640 | tf_op jit(solution)/shard_map/ppermute | solution.py:1088
  84.2 3.9 all-to-all-done.refs_1_.refs_4_.refs_2_
  97.9 4.6 shard_map.425
  114.0 10.3 %shard_map.426 = (bf16[480,4608]{1,0:T(8,128)(2,1)}, f32[480,512]{1,0:T(8,128)}, f32[32,8,128]{2,1,0:T(8,128)}) custom-call(f32[1]{0:T(128)} %bitcast.7.refs_0_.cnt, f32[32,8,128]{2,1,0:T(8,128)} %all-to-all-done.refs_1_.refs_4_.refs_2_, f32[2,512]{1,0:T(2,128)} %get-tuple-element.532.refs_2_.refs_5_.refs_3_, ...), custom_call_target="tpu_custom_call" | custom-call | tf_op jit(solution)/shard_map/pallas_call | solution.py:404
  124.3 3.7 all-to-all-start.1
  130.4 6.2 %all-to-all-done.1.s1.refs_2_ = f32[32,8,128]{2,1,0:T(8,128)S(1)} async-done(((f32[32,8,128]{2,1,0:T(8,128)}), f32[32,8,128]{2,1,0:T(8,128)S(1)}, u32[]{:S(2)}, u32[]{:S(2)}) %all-to-all-start.1) | async-done | bytes 131104 | tf_op jit(solution)/shard_map/all_to_all | solution.py:1092
  143.7 5.5 %shard_map.427 = (bf16[32,32,2048]{2,1,0:T(8,128)(2,1)}, bf16[32,16,2048]{2,1,0:T(8,128)(2,1)}) custom-call(s32[1]{0:T(128)} %bitcast.me_ref, bf16[16,48,1024]{2,1,0:T(8,128)(2,1)} %copy-done.28, bf16[16,48,1024]{2,1,0:T(8,128)(2,1)} %collective-permute-done.20.refs_1_, bf16[16,48,1024]{2,1,0:T(8,128)(2,1)} %copy-done.29, bf16[16,48,1024]{2,1,0:T(8,128)(2,1)} %copy-done.36), custom_call_target="tpu_custom_call" | custom-call | tf_op jit(solution)/shard_map/pallas_call | solution.py:1210
  149.3 9.3 %shard_map.428 = (bf16[480,512]{1,0:T(8,128)(2,1)}, f32[480,2048]{1,0:T(8,128)}, f32[480,2048]{1,0:T(8,128)}, f32[4,16,128]{2,1,0:T(8,128)}) custom-call(f32[1]{0:T(128)} %bitcast.7.refs_0_.cnt, f32[480,512]{1,0:T(8,128)} %get-tuple-element.247.a2.refs_8_, f32[32,8,128]{2,1,0:T(8,128)} %copy-done.32, f32[2,512]{1,0:T(2,128)} %get-tuple-element.531.gb1.refs_3_, ...), custom_call_target="tpu_custom_call" | custom-call | tf_op jit(solution)/shard_map/pallas_call | solution.py:895
  172.8 3.1 slice.210
  176.5 9.4 %shard_map.429 = (f32[480,2048]{1,0:T(8,128)}, bf16[480,2048]{1,0:T(8,128)(2,1)}, f32[480,512]{1,0:T(8,128)}, f32[32,8,128]{2,1,0:T(8,128)}) custom-call(f32[1]{0:T(128)} %bitcast.7.refs_0_.cnt, f32[4,16,128]{2,1,0:T(8,128)} %add_add_fusion.2.refs_1_.s23, f32[2,2048]{1,0:T(2,128)} %get-tuple-element.528.refs_2_.gb2, ...), custom_call_target="tpu_custom_call" | custom-call | tf_op jit(solution)/shard_map/pallas_call | solution.py:404
  185.9 3.5 all-to-all-start.2
  194.6 3.5 all-to-all-done.2.refs_1_.refs_14_.s4
  198.7 8.0 %shard_map.430 = (f32[480,512]{1,0:T(8,128)}, bf16[480,512]{1,0:T(8,128)(2,1)}, f32[480,512]{1,0:T(8,128)}, bf16[3,480,1152]{2,1,0:T(8,128)(2,1)}, f32[16,512]{1...) custom-call(f32[1]{0:T(128)} %bitcast.7.refs_0_.cnt, f32[32,8,128]{2,1,0:T(8,128)} %copy-done.33, ...), custom_call_target="tpu_custom_call" | custom-call | tf_op jit(solution)/shard_map/pallas_call | solution.py:404
  209.4 8.6 %all-to-all-done.3.refs_1_.refs_5_.refs_2_ = f32[32,8,128]{2,1,0:T(8,128)S(1)} async-done(((f32[32,8,128]{2,1,0:T(8,128)}), f32[32,8,128]{2,1,0:T(8,128)S(1)}, u32[]{:S(2)}, u32[]{:S(2)}) %all-to-all-start.3) | async-done | bytes 131104 | tf_op jit(solution)/shard_map/all_to_all | solution.py:1092
  218.6 6.0 %shard_map.431 = (bf16[480,512]{1,0:T(8,128)(2,1)}, f32[480,2048]{1,0:T(8,128)}, f32[32,128]{1,0:T(8,128)}) custom-call(f32[1]{0:T(128)} %bitcast.7.refs_0_.cnt, f32[32,8,128]{2,1,0:T(8,128)} %copy-done.34, f32[2,512]{1,0:T(2,128)} %get-tuple-element.529.refs_2_.refs_6_.refs_3_, f32[480,128]{1,0:T(8,128)} %broadcast_in_dim.12.refs_3_.mask.refs_4_.refs_6_, ...), custom_call_target="tpu_custom_call" | custom-call | tf_op jit(solution)/shard_map/pallas_call | solution.py:361
  227.2 11.0 %all_to_all.55 = f32[16,16,128]{2,1,0:T(8,128)S(1)} all-to-all(f32[16,16,128]{2,1,0:T(8,128)S(1)} %broadcast_in_dim.14), channel_id=1, replica_groups={{0,1,4,5,8,9,12,13,16,17,20,21,24,25,28,29},{2,3,6,7,10,11,14,15,18,19,..., dimensions={0} | all-to-all | bytes 262144 | tf_op jit(solution)/shard_map/all_to_all | solution.py:1102
  241.5 10.4 %shard_map.432 = (bf16[4,4,4,2048]{3,2,1,0:T(4,128)(2,1)}, bf16[4,6,6,2048]{3,2,1,0:T(8,128)(2,1)}, bf16[4,7,7,2048]{3,2,1,0:T(8,128)(2,1)}, f32[480,2048]{1,0:T(8,128)}, f32[32,128]{1,0:T(8,128)}) custom-call(f32[1]{0:T(128)} %bitcast.7.refs_0_.cnt, f32[32,128]{1,0:T(8,128)} %maximum_select_fusion.refs_1_.refs_2_, ...), custom_call_target="tpu_custom_call" | custom-call | tf_op jit(solution)/shard_map/pallas_call | solution.py:404
  254.7 10.8 %all_to_all.56 = f32[16,16,128]{2,1,0:T(8,128)S(1)} all-to-all(f32[16,16,128]{2,1,0:T(8,128)S(1)} %broadcast_in_dim.15), channel_id=1, replica_groups={{0,1,4,5,8,9,12,13,16,17,20,21,24,25,28,29},{2,3,6,7,10,11,14,15,18,19,..., dimensions={0} | all-to-all | bytes 262144 | tf_op jit(solution)/shard_map/all_to_all | solution.py:1102
  267.4 9.8 %shard_map.433 = (bf16[512,2048]{1,0:T(8,128)(2,1)}, f32[480,512]{1,0:T(8,128)}, f32[32,8,128]{2,1,0:T(8,128)}) custom-call(f32[1]{0:T(128)} %bitcast.7.refs_0_.cnt, f32[32,128]{1,0:T(8,128)} %maximum_select_fusion.1.refs_1_.t6, f32[32,128]{1,0:T(8,128)} %maximum_select_fusion.refs_1_.refs_2_, f32[2,2048]{1,0:T(2,128)} %get-tuple-element.526.refs_2_.refs_3_, ...), custom_call_target="tpu_custom_call" | custom-call | tf_op jit(solution)/shard_map/pallas_call | solution.py:361
  282.1 6.5 %all-to-all-done.6.refs_1_.t5 = f32[32,8,128]{2,1,0:T(8,128)S(1)} async-done(((f32[32,8,128]{2,1,0:T(8,128)}), f32[32,8,128]{2,1,0:T(8,128)S(1)}, u32[]{:S(2)}, u32[]{:S(2)}) %all-to-all-start.6) | async-done | bytes 131104 | tf_op jit(solution)/shard_map/all_to_all | solution.py:1092
  289.2 10.3 %shard_map.434 = (f32[480,512]{1,0:T(8,128)}, bf16[3,1152,128]{2,1,0:T(8,128)(2,1)}, f32[16,128]{1,0:T(8,128)}, f32[512,32]{1,0:T(8,128)}, f32[32,512]{1,0:T(8,128)}, /*index=5*/f32[32,8,128]{2,1,0:T(8,128)}) custom-call(f32[1]{0:T(128)} %bitcast.7.refs_0_.cnt, f32[32,8,128]{2,1,0:T(8,128)} %copy-done.37, f32[32,8,128]{2,1,0:T(8,128)} %copy-done.34, ...), custom_call_target="tpu_custom_call" | custom-call | tf_op jit(solution)/shard_map/pallas_call | solution.py:361
  304.6 6.2 %all-to-all-done.7.t4 = f32[32,8,128]{2,1,0:T(8,128)S(1)} async-done(((f32[32,8,128]{2,1,0:T(8,128)}), f32[32,8,128]{2,1,0:T(8,128)S(1)}, u32[]{:S(2)}, u32[]{:S(2)}) %all-to-all-start.7) | async-done | bytes 131104 | tf_op jit(solution)/shard_map/all_to_all | solution.py:1092
  311.5 12.6 %shard_map.435 = (bf16[2048,512]{1,0:T(8,128)(2,1)}, f32[480,2048]{1,0:T(8,128)}, f32[4,16,128]{2,1,0:T(8,128)}) custom-call(f32[1]{0:T(128)} %bitcast.7.refs_0_.cnt, f32[32,8,128]{2,1,0:T(8,128)} %copy-done.38, f32[32,8,128]{2,1,0:T(8,128)} %copy-done.33, f32[2,512]{1,0:T(2,128)} %get-tuple-element.530.refs_2_.refs_15_.gb4, ...), custom_call_target="tpu_custom_call" | custom-call | tf_op jit(solution)/shard_map/pallas_call | solution.py:895
  325.7 5.2 shard_map.436
  351.7 14.6 %shard_map.438 = (bf16[512,2048]{1,0:T(8,128)(2,1)}, bf16[1024,2048]{1,0:T(8,128)(2,1)}, bf16[480,2048]{1,0:T(8,128)(2,1)}, f32[480,512]{1,0:T(8,128)}, f32[32,8,128]{2,1,0:T(8,128)}) custom-call(f32[1]{0:T(128)} %bitcast.7.refs_0_.cnt, f32[4,16,128]{2,1,0:T(8,128)} %add_add_fusion.tj, f32[4,16,128]{2,1,0:T(8,128)} %add_add_fusion.2.refs_1_.s23, ...), custom_call_target="tpu_custom_call" | custom-call | tf_op jit(solution)/shard_map/pallas_call | solution.py:895
  366.4 4.0 all-to-all-start.8
  370.4 5.9 %shard_map.440 = (bf16[2,16,192,256]{3,2,1,0:T(8,128)(2,1)}, bf16[2,16,192,256]{3,2,1,0:T(8,128)(2,1)}) custom-call(s32[1]{0:T(128)} %bitcast.me_ref, bf16[32,16,2048]{2,1,0:T(8,128)(2,1)} %bitcast.109, bf16[32,32,2048]{2,1,0:T(8,128)(2,1)} %bitcast.99), custom_call_target="tpu_custom_call" | custom-call | tf_op jit(solution)/shard_map/pallas_call | solution.py:1349
  384.1 11.2 %shard_map.441 = (bf16[480,512]{1,0:T(8,128)(2,1)}, f32[4,480,512]{2,1,0:T(8,128)}, f32[32,8,128]{2,1,0:T(8,128)}) custom-call(f32[1]{0:T(128)} %bitcast.7.refs_0_.cnt, f32[32,8,128]{2,1,0:T(8,128)} %copy-done.39, f32[32,8,128]{2,1,0:T(8,128)} %copy-done.32, f32[2,512]{1,0:T(2,128)} %get-tuple-element.531.gb1.refs_3_, ...), custom_call_target="tpu_custom_call" | custom-call | tf_op jit(solution)/shard_map/pallas_call | solution.py:361
  398.5 3.7 all-to-all-start.9
  402.2 7.3 %shard_map.442 = bf16[4608,512]{1,0:T(8,128)(2,1)} custom-call(bf16[480,512]{1,0:T(8,128)(2,1)} %get-tuple-element.332.refs_0_, bf16[480,4608]{1,0:T(8,128)(2,1)} %get-tuple-element.333.refs_1_), custom_call_target="tpu_custom_call" | custom-call | tf_op jit(solution)/shard_map/pallas_call | solution.py:361
  409.5 4.8 shard_map.443
  423.9 8.8 %shard_map.445 = (bf16[4,480,512]{2,1,0:T(8,128)(2,1)}, bf16[1024,512]{1,0:T(8,128)(2,1)}) custom-call(f32[1]{0:T(128)} %bitcast.7.refs_0_.cnt, f32[32,8,128]{2,1,0:T(8,128)} %copy-done.47, f32[32,8,128]{2,1,0:T(8,128)} %all-to-all-done.refs_1_.refs_4_.refs_2_, f32[2,512]{1,0:T(2,128)} %get-tuple-element.532.refs_2_.refs_5_.refs_3_, ...), custom_call_target="tpu_custom_call" | custom-call | flops 20000000000 | bytes 60000000 | tf_op jit(solution)/shard_map/pallas_call | solution.py:404
  432.8 3.8 shard_map.446
  439.2 11.8 %shard_map.447 = (bf16[4,8,8,1024]{3,2,1,0:T(8,128)(2,1)}, bf16[4,12,12,1024]{3,2,1,0:T(8,128)(2,1)}, bf16[4,14,14,1024]{3,2,1,0:T(8,128)(2,1)}) custom-call(f32[480,128]{1,0:T(8,128)} %broadcast_in_dim.12.refs_3_.mask.refs_4_.refs_6_, bf16[256,128]{1,0:T(8,128)(2,1)} %constant.61.clone.tc, bf16[192,192]{1,0:T(8,128)(2,1)} %constant.62.clone.tm, ...), custom_call_target="tpu_custom_call" | custom-call | tf_op jit(solution)/shard_map/pallas_call | solution.py:895
  467.1 5.1 all-to-all-start.10
  472.2 4.6 collective-permute-done.51.refs_2_
  479.5 4.1 copy.150
  493.8 6.6 %collective-permute-done.55.refs_1_ = bf16[2,2,144,256]{3,2,1,0:T(8,128)(2,1)S(1)} collective-permute-done((bf16[2,2,144,256]{3,2,1,0:T(8,128)(2,1)S(1)}, bf16[2,2,144,256]{3,2,1,0:T(8,128)(2,1)S(1)}, u32[]{:S(2)}, u32[]{:S(2)}) %collective-permute-start.55) | collective-permute-done | bytes 294944 | tf_op jit(solution)/shard_map/ppermute | solution.py:1088
  (388 shorter events, 200.0 us)
Async XLA Ops:
  7.2 153.6 %all-gather.3.cloned.1.call-start = ((), (), s32[]{:S(2)}) async-start(), calls=%async_computation.11 | async-start | bytes 3244032 | tf_op jit(solution)/shard_map/all_gather | solution.py:1396
  11.4 16.8 %collective-permute-start = (bf16[192,512]{1,0:T(8,128)(2,1)S(1)}, bf16[192,512]{1,0:T(8,128)(2,1)S(1)}, u32[]{:S(2)}, u32[]{:S(2)}) collective-permute-start(bf16[192,512]{1,0:T(8,128)(2,1)S(1)} %pad_maximum_fusion.7), channel_id=1, source_target_pairs={{0,8},{1,9},{2,10},{3,11},{4,12},{5,13},{6,14},{7,15},{8,0},{9,1},... | collective-permute-start | bytes 589832 | tf_op jit(solution)/shard_map/ppermute | solution.py:1088
  14.5 17.2 %collective-permute-start.1 = (bf16[192,512]{1,0:T(8,128)(2,1)S(1)}, bf16[192,512]{1,0:T(8,128)(2,1)S(1)}, u32[]{:S(2)}, u32[]{:S(2)}) collective-permute-start(bf16[192,512]{1,0:T(8,128)(2,1)S(1)} %pad_maximum_fusion.7), channel_id=1, source_target_pairs={{0,16},{1,17},{2,18},{3,19},{4,20},{5,21},{6,22},{7,23},{8,24},{9,... | collective-permute-start | bytes 589832 | tf_op jit(solution)/shard_map/ppermute | solution.py:1088
  17.1 14.6 %collective-permute-start.2 = (bf16[192,512]{1,0:T(8,128)(2,1)S(1)}, bf16[192,512]{1,0:T(8,128)(2,1)S(1)}, u32[]{:S(2)}, u32[]{:S(2)}) collective-permute-start(bf16[192,512]{1,0:T(8,128)(2,1)S(1)} %pad_maximum_fusion.7), channel_id=1, source_target_pairs={{0,24},{1,25},{2,26},{3,27},{4,28},{5,29},{6,30},{7,31},{8,16},{9,... | collective-permute-start | bytes 589832 | tf_op jit(solution)/shard_map/ppermute | solution.py:1088
  43.0 10.1 %collective-permute-start.7 = (bf16[4,144,256]{2,1,0:T(8,128)(2,1)S(1)}, bf16[4,144,256]{2,1,0:T(8,128)(2,1)S(1)}, u32[]{:S(2)}, u32[]{:S(2)}) collective-permute-start(bf16[4,144,256]{2,1,0:T(8,128)(2,1)S(1)} %get-tuple-element.513), channel_id=1, source_target_pairs={{0,1},{1,0},{2,3},{3,2},{4,5},{5,4},{6,7},{7,6},{8,9},{9,8},{10,11... | collective-permute-start | bytes 884744 | tf_op jit(solution)/shard_map/ppermute | solution.py:1088
  44.0 9.4 %collective-permute-start.8 = (bf16[4,144,256]{2,1,0:T(8,128)(2,1)S(1)}, bf16[4,144,256]{2,1,0:T(8,128)(2,1)S(1)}, u32[]{:S(2)}, u32[]{:S(2)}) collective-permute-start(bf16[4,144,256]{2,1,0:T(8,128)(2,1)S(1)} %get-tuple-element.512), channel_id=1, source_target_pairs={{0,4},{1,5},{2,6},{3,7},{4,0},{5,1},{6,2},{7,3},{8,12},{9,13},{10,... | collective-permute-start | bytes 884744 | tf_op jit(solution)/shard_map/ppermute | solution.py:1088
  53.5 34.6 %collective-permute-start.10 = (bf16[8,144,256]{2,1,0:T(8,128)(2,1)S(1)}, bf16[8,144,256]{2,1,0:T(8,128)(2,1)}, u32[]{:S(2)}, u32[]{:S(2)}) collective-permute-start(bf16[8,144,256]{2,1,0:T(8,128)(2,1)S(1)} %pad_maximum_fusion.5), channel_id=1, source_target_pairs={{0,1},{1,0},{2,3},{3,2},{4,5},{5,4},{6,7},{7,6},{8,9},{9,8},{10,11... | collective-permute-start | bytes 1769480 | tf_op jit(solution)/shard_map/ppermute | solution.py:1088
  55.0 33.2 %collective-permute-start.9 = (bf16[8,144,256]{2,1,0:T(8,128)(2,1)S(1)}, bf16[8,144,256]{2,1,0:T(8,128)(2,1)}, u32[]{:S(2)}, u32[]{:S(2)}) collective-permute-start(bf16[8,144,256]{2,1,0:T(8,128)(2,1)S(1)} %pad_maximum_fusion.4), channel_id=1, source_target_pairs={{0,4},{1,5},{2,6},{3,7},{4,0},{5,1},{6,2},{7,3},{8,12},{9,13},{10,... | collective-permute-start | bytes 1769480 | tf_op jit(solution)/shard_map/ppermute | solution.py:1088
  57.5 17.7 %collective-permute-start.11 = (bf16[48,2048]{1,0:T(8,128)(2,1)}, bf16[48,2048]{1,0:T(8,128)(2,1)}, u32[]{:S(2)}, u32[]{:S(2)}) collective-permute-start(bf16[48,2048]{1,0:T(8,128)(2,1)} %pad_maximum_fusion.9), channel_id=1, source_target_pairs={{0,8},{1,9},{2,10},{3,11},{4,12},{5,13},{6,14},{7,15},{8,0},{9,1},... | collective-permute-start | bytes 589832 | tf_op jit(solution)/shard_map/ppermute | solution.py:1088
  62.6 21.5 %collective-permute-start.12 = (bf16[48,2048]{1,0:T(8,128)(2,1)}, bf16[48,2048]{1,0:T(8,128)(2,1)}, u32[]{:S(2)}, u32[]{:S(2)}) collective-permute-start(bf16[48,2048]{1,0:T(8,128)(2,1)} %pad_maximum_fusion.9), channel_id=1, source_target_pairs={{0,16},{1,17},{2,18},{3,19},{4,20},{5,21},{6,22},{7,23},{8,24},{9,... | collective-permute-start | bytes 589832 | tf_op jit(solution)/shard_map/ppermute | solution.py:1088
  63.7 20.4 %collective-permute-start.13 = (bf16[48,2048]{1,0:T(8,128)(2,1)}, bf16[48,2048]{1,0:T(8,128)(2,1)}, u32[]{:S(2)}, u32[]{:S(2)}) collective-permute-start(bf16[48,2048]{1,0:T(8,128)(2,1)} %pad_maximum_fusion.9), channel_id=1, source_target_pairs={{0,24},{1,25},{2,26},{3,27},{4,28},{5,29},{6,30},{7,31},{8,16},{9,... | collective-permute-start | bytes 589832 | tf_op jit(solution)/shard_map/ppermute | solution.py:1088
  71.8 16.4 %all-to-all-start = ((f32[32,8,128]{2,1,0:T(8,128)}), f32[32,8,128]{2,1,0:T(8,128)}, u32[]{:S(2)}, u32[]{:S(2)}) async-start(f32[32,8,128]{2,1,0:T(8,128)} %get-tuple-element.231), calls=%async_computation | async-start | bytes 262144 | tf_op jit(solution)/shard_map/all_to_all | solution.py:1092
  75.1 134.3 %all-gather.5.cloned.1.call-start = ((), (), s32[]{:S(2)}) async-start(), calls=%async_computation.12 | async-start | bytes 2162688 | tf_op jit(solution)/shard_map/all_gather | solution.py:1396
  89.2 8.7 %collective-permute-start.15 = (bf16[16,144,256]{2,1,0:T(8,128)(2,1)S(1)}, bf16[16,144,256]{2,1,0:T(8,128)(2,1)}, u32[]{:S(2)}, u32[]{:S(2)}) collective-permute-start(bf16[16,144,256]{2,1,0:T(8,128)(2,1)S(1)} %constant_dynamic-update-slice_fusion.9.refs_2_), channel_id=1, source_target_pairs={{0,2},{1,3},{2,0},{3,1},{4,6},{5,7},{6,4},{7,5},{8,10},{9,11},{10,... | collective-permute-start | bytes 3538952 | tf_op jit(solution)/shard_map/ppermute | solution.py:1088
  92.6 11.4 %collective-permute-start.16 = (bf16[4,48,1024]{2,1,0:T(8,128)(2,1)S(1)}, bf16[4,48,1024]{2,1,0:T(8,128)(2,1)S(1)}, u32[]{:S(2)}, u32[]{:S(2)}) collective-permute-start(bf16[4,48,1024]{2,1,0:T(8,128)(2,1)S(1)} %get-tuple-element.511), channel_id=1, source_target_pairs={{0,1},{1,0},{2,3},{3,2},{4,5},{5,4},{6,7},{7,6},{8,9},{9,8},{10,11... | collective-permute-start | bytes 1179656 | tf_op jit(solution)/shard_map/ppermute | solution.py:1088
  94.0 11.0 %collective-permute-start.17 = (bf16[4,48,1024]{2,1,0:T(8,128)(2,1)S(1)}, bf16[4,48,1024]{2,1,0:T(8,128)(2,1)}, u32[]{:S(2)}, u32[]{:S(2)}) collective-permute-start(bf16[4,48,1024]{2,1,0:T(8,128)(2,1)S(1)} %get-tuple-element.510), channel_id=1, source_target_pairs={{0,4},{1,5},{2,6},{3,7},{4,0},{5,1},{6,2},{7,3},{8,12},{9,13},{10,... | collective-permute-start | bytes 1179656 | tf_op jit(solution)/shard_map/ppermute | solution.py:1088
  107.8 28.8 %collective-permute-start.18 = (bf16[8,48,1024]{2,1,0:T(8,128)(2,1)}, bf16[8,48,1024]{2,1,0:T(8,128)(2,1)}, u32[]{:S(2)}, u32[]{:S(2)}) collective-permute-start(bf16[8,48,1024]{2,1,0:T(8,128)(2,1)} %pad_maximum_fusion.1), channel_id=1, source_target_pairs={{0,4},{1,5},{2,6},{3,7},{4,0},{5,1},{6,2},{7,3},{8,12},{9,13},{10,... | collective-permute-start | bytes 2359304 | tf_op jit(solution)/shard_map/ppermute | solution.py:1088
  109.1 27.5 %collective-permute-start.19 = (bf16[8,48,1024]{2,1,0:T(8,128)(2,1)}, bf16[8,48,1024]{2,1,0:T(8,128)(2,1)}, u32[]{:S(2)}, u32[]{:S(2)}) collective-permute-start(bf16[8,48,1024]{2,1,0:T(8,128)(2,1)} %pad_maximum_fusion.2), channel_id=1, source_target_pairs={{0,1},{1,0},{2,3},{3,2},{4,5},{5,4},{6,7},{7,6},{8,9},{9,8},{10,11... | collective-permute-start | bytes 2359304 | tf_op jit(solution)/shard_map/ppermute | solution.py:1088
  124.3 12.3 %all-to-all-start.1 = ((f32[32,8,128]{2,1,0:T(8,128)}), f32[32,8,128]{2,1,0:T(8,128)S(1)}, u32[]{:S(2)}, u32[]{:S(2)}) async-start(f32[32,8,128]{2,1,0:T(8,128)} %get-tuple-element.248), calls=%async_computation.1 | async-start | bytes 262144 | tf_op jit(solution)/shard_map/all_to_all | solution.py:1092
  166.6 9.3 %collective-permute-start.26 = (f32[4,16,128]{2,1,0:T(8,128)S(1)}, f32[4,16,128]{2,1,0:T(8,128)S(1)}, u32[]{:S(2)}, u32[]{:S(2)}) collective-permute-start(f32[4,16,128]{2,1,0:T(8,128)S(1)} %add_add_fusion.3), channel_id=1, source_target_pairs={{0,8},{1,9},{2,10},{3,11},{4,12},{5,13},{6,14},{7,15},{8,0},{9,1},... | collective-permute-start | bytes 98312 | tf_op jit(solution)/shard_map/ppermute | solution.py:1088
  185.9 12.2 %all-to-all-start.2 = ((f32[32,8,128]{2,1,0:T(8,128)}), f32[32,8,128]{2,1,0:T(8,128)S(1)}, u32[]{:S(2)}, u32[]{:S(2)}) async-start(f32[32,8,128]{2,1,0:T(8,128)} %get-tuple-element.265), calls=%async_computation.2 | async-start | bytes 262144 | tf_op jit(solution)/shard_map/all_to_all | solution.py:1092
  206.7 11.2 %all-to-all-start.3 = ((f32[32,8,128]{2,1,0:T(8,128)}), f32[32,8,128]{2,1,0:T(8,128)S(1)}, u32[]{:S(2)}, u32[]{:S(2)}) async-start(f32[32,8,128]{2,1,0:T(8,128)} %get-tuple-element.267), calls=%async_computation.3 | async-start | bytes 262144 | tf_op jit(solution)/shard_map/all_to_all | solution.py:1092
  277.2 11.4 %all-to-all-start.6 = ((f32[32,8,128]{2,1,0:T(8,128)}), f32[32,8,128]{2,1,0:T(8,128)S(1)}, u32[]{:S(2)}, u32[]{:S(2)}) async-start(f32[32,8,128]{2,1,0:T(8,128)} %get-tuple-element.277), calls=%async_computation.6 | async-start | bytes 262144 | tf_op jit(solution)/shard_map/all_to_all | solution.py:1092
  299.5 11.4 %all-to-all-start.7 = ((f32[32,8,128]{2,1,0:T(8,128)}), f32[32,8,128]{2,1,0:T(8,128)S(1)}, u32[]{:S(2)}, u32[]{:S(2)}) async-start(f32[32,8,128]{2,1,0:T(8,128)} %get-tuple-element.285), calls=%async_computation.7 | async-start | bytes 262144 | tf_op jit(solution)/shard_map/all_to_all | solution.py:1092
  330.9 14.6 %collective-permute-start.40 = (bf16[2,16,160,256]{3,2,1,0:T(8,128)(2,1)}, bf16[2,16,160,256]{3,2,1,0:T(8,128)(2,1)S(1)}, u32[]{:S(2)}, u32[]{:S(2)}) collective-permute-start(bf16[2,16,160,256]{3,2,1,0:T(8,128)(2,1)} %get-tuple-element.300), channel_id=1, source_target_pairs={{0,2},{1,3},{2,0},{3,1},{4,6},{5,7},{6,4},{7,5},{8,10},{9,11},{10,... | collective-permute-start | bytes 7864328 | tf_op jit(solution)/shard_map/ppermute | solution.py:1088
  349.5 16.9 %collective-permute-start.41 = (bf16[8,160,256]{2,1,0:T(8,128)(2,1)}, bf16[8,160,256]{2,1,0:T(8,128)(2,1)S(1)}, u32[]{:S(2)}, u32[]{:S(2)}) collective-permute-start(bf16[8,160,256]{2,1,0:T(8,128)(2,1)} %get-tuple-element.307), channel_id=1, source_target_pairs={{0,1},{1,0},{2,3},{3,2},{4,5},{5,4},{6,7},{7,6},{8,9},{9,8},{10,11... | collective-permute-start | bytes 1966088 | tf_op jit(solution)/shard_map/ppermute | solution.py:1088
  350.6 15.8 %collective-permute-start.42 = (bf16[8,160,256]{2,1,0:T(8,128)(2,1)S(1)}, bf16[8,160,256]{2,1,0:T(8,128)(2,1)S(1)}, u32[]{:S(2)}, u32[]{:S(2)}) collective-permute-start(bf16[8,160,256]{2,1,0:T(8,128)(2,1)S(1)} %get-tuple-element.308), channel_id=1, source_target_pairs={{0,4},{1,5},{2,6},{3,7},{4,0},{5,1},{6,2},{7,3},{8,12},{9,13},{10,... | collective-permute-start | bytes 1966088 | tf_op jit(solution)/shard_map/ppermute | solution.py:1088
  366.4 13.6 %all-to-all-start.8 = ((f32[32,8,128]{2,1,0:T(8,128)}), f32[32,8,128]{2,1,0:T(8,128)S(1)}, u32[]{:S(2)}, u32[]{:S(2)}) async-start(f32[32,8,128]{2,1,0:T(8,128)} %get-tuple-element.312), calls=%async_computation.8 | async-start | bytes 262144 | tf_op jit(solution)/shard_map/all_to_all | solution.py:1092
  380.6 16.2 %collective-permute-start.45 = (bf16[2,16,192,256]{3,2,1,0:T(8,128)(2,1)}, bf16[2,16,192,256]{3,2,1,0:T(8,128)(2,1)S(1)}, u32[]{:S(2)}, u32[]{:S(2)}) collective-permute-start(bf16[2,16,192,256]{3,2,1,0:T(8,128)(2,1)} %get-tuple-element.329), channel_id=1, source_target_pairs={{0,2},{1,3},{2,0},{3,1},{4,6},{5,7},{6,4},{7,5},{8,10},{9,11},{10,... | collective-permute-start | bytes 9437192 | tf_op jit(solution)/shard_map/ppermute | solution.py:1088
  381.0 14.3 %collective-permute-start.43 = (bf16[4,160,256]{2,1,0:T(8,128)(2,1)}, bf16[4,160,256]{2,1,0:T(8,128)(2,1)S(1)}, u32[]{:S(2)}, u32[]{:S(2)}) collective-permute-start(bf16[4,160,256]{2,1,0:T(8,128)(2,1)} %get-tuple-element.326), channel_id=1, source_target_pairs={{0,4},{1,5},{2,6},{3,7},{4,0},{5,1},{6,2},{7,3},{8,12},{9,13},{10,... | collective-permute-start | bytes 983048 | tf_op jit(solution)/shard_map/ppermute | solution.py:1088
  382.7 13.4 %collective-permute-start.44 = (bf16[4,160,256]{2,1,0:T(8,128)(2,1)S(1)}, bf16[4,160,256]{2,1,0:T(8,128)(2,1)S(1)}, u32[]{:S(2)}, u32[]{:S(2)}) collective-permute-start(bf16[4,160,256]{2,1,0:T(8,128)(2,1)S(1)} %get-tuple-element.327), channel_id=1, source_target_pairs={{0,1},{1,0},{2,3},{3,2},{4,5},{5,4},{6,7},{7,6},{8,9},{9,8},{10,11... | collective-permute-start | bytes 983048 | tf_op jit(solution)/shard_map/ppermute | solution.py:1088
  398.5 15.8 %all-to-all-start.9 = ((f32[32,8,128]{2,1,0:T(8,128)}), f32[32,8,128]{2,1,0:T(8,128)S(1)}, u32[]{:S(2)}, u32[]{:S(2)}) async-start(f32[32,8,128]{2,1,0:T(8,128)} %get-tuple-element.335), calls=%async_computation.9 | async-start | bytes 262144 | tf_op jit(solution)/shard_map/all_to_all | solution.py:1092
  414.3 18.5 %collective-permute-start.46 = (bf16[2,16,144,256]{3,2,1,0:T(8,128)(2,1)}, bf16[2,16,144,256]{3,2,1,0:T(8,128)(2,1)}, u32[]{:S(2)}, u32[]{:S(2)}) collective-permute-start(bf16[2,16,144,256]{3,2,1,0:T(8,128)(2,1)} %get-tuple-element.345), channel_id=1, source_target_pairs={{0,2},{1,3},{2,0},{3,1},{4,6},{5,7},{6,4},{7,5},{8,10},{9,11},{10,... | collective-permute-start | bytes 7077896 | tf_op jit(solution)/shard_map/ppermute | solution.py:1088
  420.8 30.2 %collective-permute-start.47 = (bf16[8,192,256]{2,1,0:T(8,128)(2,1)}, bf16[8,192,256]{2,1,0:T(8,128)(2,1)S(1)}, u32[]{:S(2)}, u32[]{:S(2)}) collective-permute-start(bf16[8,192,256]{2,1,0:T(8,128)(2,1)} %get-tuple-element.355), channel_id=1, source_target_pairs={{0,1},{1,0},{2,3},{3,2},{4,5},{5,4},{6,7},{7,6},{8,9},{9,8},{10,11... | collective-permute-start | bytes 2359304 | tf_op jit(solution)/shard_map/ppermute | solution.py:1088
  422.5 28.6 %collective-permute-start.48 = (bf16[8,192,256]{2,1,0:T(8,128)(2,1)}, bf16[8,192,256]{2,1,0:T(8,128)(2,1)S(1)}, u32[]{:S(2)}, u32[]{:S(2)}) collective-permute-start(bf16[8,192,256]{2,1,0:T(8,128)(2,1)} %get-tuple-element.356), channel_id=1, source_target_pairs={{0,4},{1,5},{2,6},{3,7},{4,0},{5,1},{6,2},{7,3},{8,12},{9,13},{10,... | collective-permute-start | bytes 2359304 | tf_op jit(solution)/shard_map/ppermute | solution.py:1088
  437.5 16.0 %collective-permute-start.49 = (bf16[8,144,256]{2,1,0:T(8,128)(2,1)}, bf16[8,144,256]{2,1,0:T(8,128)(2,1)}, u32[]{:S(2)}, u32[]{:S(2)}) collective-permute-start(bf16[8,144,256]{2,1,0:T(8,128)(2,1)} %get-tuple-element.358), channel_id=1, source_target_pairs={{0,1},{1,0},{2,3},{3,2},{4,5},{5,4},{6,7},{7,6},{8,9},{9,8},{10,11... | collective-permute-start | bytes 1769480 | tf_op jit(solution)/shard_map/ppermute | solution.py:1088
  438.0 16.9 %collective-permute-start.50 = (bf16[8,144,256]{2,1,0:T(8,128)(2,1)}, bf16[8,144,256]{2,1,0:T(8,128)(2,1)}, u32[]{:S(2)}, u32[]{:S(2)}) collective-permute-start(bf16[8,144,256]{2,1,0:T(8,128)(2,1)} %get-tuple-element.359), channel_id=1, source_target_pairs={{0,4},{1,5},{2,6},{3,7},{4,0},{5,1},{6,2},{7,3},{8,12},{9,13},{10,... | collective-permute-start | bytes 1769480 | tf_op jit(solution)/shard_map/ppermute | solution.py:1088
  439.2 24.2 %collective-permute-start.57 = (bf16[8,2,32,512]{3,2,1,0:T(8,128)(2,1)}, bf16[8,2,32,512]{3,2,1,0:T(8,128)(2,1)}, u32[]{:S(2)}, u32[]{:S(2)}) collective-permute-start(bf16[8,2,32,512]{3,2,1,0:T(8,128)(2,1)} %dynamic-slice_bitcast_fusion), channel_id=1, source_target_pairs={{0,2},{1,3},{2,0},{3,1},{4,6},{5,7},{6,4},{7,5},{8,10},{9,11},{10,... | collective-permute-start | bytes 1572872 | tf_op jit(solution)/shard_map/ppermute | solution.py:1088
  458.5 18.3 %collective-permute-start.53 = (bf16[4,192,256]{2,1,0:T(8,128)(2,1)}, bf16[4,192,256]{2,1,0:T(8,128)(2,1)S(1)}, u32[]{:S(2)}, u32[]{:S(2)}) collective-permute-start(bf16[4,192,256]{2,1,0:T(8,128)(2,1)} %get-tuple-element.376), channel_id=1, source_target_pairs={{0,4},{1,5},{2,6},{3,7},{4,0},{5,1},{6,2},{7,3},{8,12},{9,13},{10,... | collective-permute-start | bytes 1179656 | tf_op jit(solution)/shard_map/ppermute | solution.py:1088
  460.8 16.0 %collective-permute-start.54 = (bf16[2,2,160,256]{3,2,1,0:T(8,128)(2,1)S(1)}, bf16[2,2,160,256]{3,2,1,0:T(8,128)(2,1)S(1)}, u32[]{:S(2)}, u32[]{:S(2)}) collective-permute-start(bf16[2,2,160,256]{3,2,1,0:T(8,128)(2,1)S(1)} %get-tuple-element.383), channel_id=1, source_target_pairs={{0,8},{1,9},{2,10},{3,11},{4,12},{5,13},{6,14},{7,15},{8,0},{9,1},... | collective-permute-start | bytes 983048 | tf_op jit(solution)/shard_map/ppermute | solution.py:1088
  462.3 14.5 %collective-permute-start.51 = (bf16[4,144,256]{2,1,0:T(8,128)(2,1)}, bf16[4,144,256]{2,1,0:T(8,128)(2,1)S(1)}, u32[]{:S(2)}, u32[]{:S(2)}) collective-permute-start(bf16[4,144,256]{2,1,0:T(8,128)(2,1)} %copy-done.27), channel_id=1, source_target_pairs={{0,4},{1,5},{2,6},{3,7},{4,0},{5,1},{6,2},{7,3},{8,12},{9,13},{10,... | collective-permute-start | bytes 884744 | tf_op jit(solution)/shard_map/ppermute | solution.py:1088
  462.9 13.9 %collective-permute-start.52 = (bf16[4,144,256]{2,1,0:T(8,128)(2,1)}, bf16[4,144,256]{2,1,0:T(8,128)(2,1)S(1)}, u32[]{:S(2)}, u32[]{:S(2)}) collective-permute-start(bf16[4,144,256]{2,1,0:T(8,128)(2,1)} %copy-done.26), channel_id=1, source_target_pairs={{0,1},{1,0},{2,3},{3,2},{4,5},{5,4},{6,7},{7,6},{8,9},{9,8},{10,11... | collective-permute-start | bytes 884744 | tf_op jit(solution)/shard_map/ppermute | solution.py:1088
  463.5 25.2 %collective-permute-start.58 = (bf16[4,192,256]{2,1,0:T(8,128)(2,1)}, bf16[4,192,256]{2,1,0:T(8,128)(2,1)S(1)}, u32[]{:S(2)}, u32[]{:S(2)}) collective-permute-start(bf16[4,192,256]{2,1,0:T(8,128)(2,1)} %copy-done.25), channel_id=1, source_target_pairs={{0,1},{1,0},{2,3},{3,2},{4,5},{5,4},{6,7},{7,6},{8,9},{9,8},{10,11... | collective-permute-start | bytes 1179656 | tf_op jit(solution)/shard_map/ppermute | solution.py:1088
  467.1 49.3 %all-to-all-start.10 = ((bf16[16,32,512]{2,1,0:T(8,128)(2,1)}), bf16[16,32,512]{2,1,0:T(8,128)(2,1)}, u32[]{:S(2)}, u32[]{:S(2)}) async-start(bf16[16,32,512]{2,1,0:T(8,128)(2,1)} %bitcast.112), calls=%async_computation.10 | async-start | bytes 1048576 | tf_op jit(solution)/shard_map/all_to_all | solution.py:1565
  477.6 14.9 %collective-permute-start.61 = (bf16[2,1,160,256]{3,2,1,0:T(8,128)(2,1)S(1)}, bf16[2,1,160,256]{3,2,1,0:T(8,128)(2,1)S(1)}, u32[]{:S(2)}, u32[]{:S(2)}) collective-permute-start(bf16[2,1,160,256]{3,2,1,0:T(8,128)(2,1)S(1)} %get-tuple-element.412), channel_id=1, source_target_pairs={{0,16},{1,17},{2,18},{3,19},{4,20},{5,21},{6,22},{7,23},{8,24},{9,... | collective-permute-start | bytes 491528 | tf_op jit(solution)/shard_map/ppermute | solution.py:1088
  486.1 14.3 %collective-permute-start.55 = (bf16[2,2,144,256]{3,2,1,0:T(8,128)(2,1)S(1)}, bf16[2,2,144,256]{3,2,1,0:T(8,128)(2,1)S(1)}, u32[]{:S(2)}, u32[]{:S(2)}) collective-permute-start(bf16[2,2,144,256]{3,2,1,0:T(8,128)(2,1)S(1)} %get-tuple-element.386), channel_id=1, source_target_pairs={{0,8},{1,9},{2,10},{3,11},{4,12},{5,13},{6,14},{7,15},{8,0},{9,1},... | collective-permute-start | bytes 884744 | tf_op jit(solution)/shard_map/ppermute | solution.py:1088
  490.0 21.8 %collective-permute-start.59 = (bf16[2,2,192,256]{3,2,1,0:T(8,128)(2,1)S(1)}, bf16[2,2,192,256]{3,2,1,0:T(8,128)(2,1)S(1)}, u32[]{:S(2)}, u32[]{:S(2)}) collective-permute-start(bf16[2,2,192,256]{3,2,1,0:T(8,128)(2,1)S(1)} %get-tuple-element.406), channel_id=1, source_target_pairs={{0,8},{1,9},{2,10},{3,11},{4,12},{5,13},{6,14},{7,15},{8,0},{9,1},... | collective-permute-start | bytes 1179656 | tf_op jit(solution)/shard_map/ppermute | solution.py:1088
  501.0 15.4 %collective-permute-start.56 = (bf16[2,1,144,256]{3,2,1,0:T(8,128)(2,1)S(1)}, bf16[2,1,144,256]{3,2,1,0:T(8,128)(2,1)S(1)}, u32[]{:S(2)}, u32[]{:S(2)}) collective-permute-start(bf16[2,1,144,256]{3,2,1,0:T(8,128)(2,1)S(1)} %get-tuple-element.396), channel_id=1, source_target_pairs={{0,16},{1,17},{2,18},{3,19},{4,20},{5,21},{6,22},{7,23},{8,24},{9,... | collective-permute-start | bytes 442376 | tf_op jit(solution)/shard_map/ppermute | solution.py:1088
  (83 other events, 435.3 us)
Sparse Core Ops, SparseCore 0:
  32.8 70.5 all-gather.2
  107.0 55.6 all-gather.4

commit v5 on v4

--- a/solution.py
+++ b/solution.py
@@ -1457,14 +1457,17 @@
     w1, gc_.x = tie(w1, gc_.x)
     gc_.first()
     a1, p0 = run_enter(n, xph, w1)
-    s0 = exchange(p0)
-    s0, *rest = tie(s0, *gb_.got, *gc_.hops)
+    p0, *rest = tie(p0, *gb_.got, *gc_.hops)
     gb_.got, gc_.hops = rest[:2], rest[2:]
     gb_.land()
+    gc_.split()
+    p0, *rest = tie(p0, *gb_.planes, *gc_.planes)
+    gb_.planes, gc_.planes = rest[:2], rest[2:]
     gb_.third()
-    gc_.split()
     gc_.hop(0)
+    s0 = exchange(p0)
     wsp, = gb_.finish(me)
+    s0, wsp, cnt, gb[0], *gc_.got = tie(s0, wsp, cnt, gb[0], *gc_.got)
     for k in range(1, len(gc_.paths[0])):
         wsp, *gc_.got = tie(wsp, *gc_.got)
         gc_.land()

time: 541 us -> 537 us (level)
    unnamed x139 -> x151, local copies, waits for them, and re-layouts: 39.1 us -> 40.7 us
  transfers between devices with their start and end apart: 73 -> 73, of which waited for: 34 -> 32; matrix products, arithmetic and copies ran while one was open for 13% -> 12% of each run, Pallas kernels for 28% -> 28%
where the time goes in v5:
time: 537 us; the launch traced here: 528 us
  Pallas kernels  204 us (38%)
  starting transfers between devices  100 us (19%)
  waiting for transfers between devices  92.4 us (17%)
  local copies, waits for them, and re-layouts  67.3 us (13%)
  other arithmetic  26.3 us (5%)
  blocking collectives  21.9 us (4%)
  between operations  15.8 us (3%)
    ppermute x62, starting transfers between devices, swap(): return lax.ppermute(v, AXES, [(i, i ^ d) for i in range(n)])  65.6 us
    ppermute x62, waiting for transfers between devices, swap(): return lax.ppermute(v, AXES, [(i, i ^ d) for i in range(n)])  57.5 us
    pallas_call x6, Pallas kernels, flow_call(): pl.pallas_call(kernel, out_shape=[like(o[0], o[1]) for o in outs] + list(...  53 us
    pallas_call x4, Pallas kernels, wide_grid(): pl.pallas_call(kernel, grid=(steps,), out_shape=outs, in_specs=in_specs,...  48.3 us
    pallas_call x5, Pallas kernels, plain_call(): pl.pallas_call(kernel, out_shape=[like(o[0], o[1]) for o in outs] + list(...  44.1 us
    unnamed x151, local copies, waits for them, and re-layouts  40.7 us
    all_to_all x8, waiting for transfers between devices, exchange(): return lax.all_to_all(spread, AXES, 0, 0, tiled=True)  34.9 us
    all_to_all x8, starting transfers between devices, exchange(): return lax.all_to_all(spread, AXES, 0, 0, tiled=True)  29.4 us
  transfers between devices with their start and end apart: 73, of which 32 were waited for; matrix products, arithmetic and copies ran while one was open for 12% of the time, Pallas kernels for 28%

profile of v5, /device:TPU:0, one launch (start us, length us, event | category | flops | bytes accessed | tf_op | source)
XLA Modules:
  0.0 527.6 jit_solution(5355950964825135791)
XLA Ops:
  11.4 3.1 collective-permute-start
  17.7 3.2 copy.130.xf
  22.4 5.8 %shard_map.422.refs_0_.x.x0.refs_7_ = bf16[4,480,1024]{2,1,0:T(8,128)(2,1)} custom-call(f32[12]{0:T(128)} %convert_element_type.96.alive, bf16[4,8,8,1024]{3,2,1,0:T(8,128)(2,1)} %xc.1, bf16[4,12,12,1024]{3,2,1,0:T(8,128)(2,1)} %copy.129.xm, bf16[4,14,14,1024]{3,2,1,0:T(8,128)(2,1)} %copy.130.xf, bf16[128,256]{1,0:T(8,128)(2,1)} %constant.58.clone.tc, ...), custom_call_target="tpu_custom_call" | custom-call | tf_op jit(solution)/shard_map/pallas_call | solution.py:299
  28.3 3.4 collective-permute-done.1
  36.4 3.1 collective-permute-done.3
  39.5 3.2 collective-permute-done.4
  48.5 4.6 collective-permute-done.7
  56.8 5.2 collective-permute-start.11
  64.6 6.5 %shard_map.424 = (f32[4,480,512]{2,1,0:T(8,128)}, f32[32,8,128]{2,1,0:T(8,128)}) custom-call(bf16[4,480,1024]{2,1,0:T(8,128)(2,1)} %shard_map.422.refs_0_.x.x0.refs_7_, bf16[1024,512]{1,0:T(8,128)(2,1)} %bitcast.97), custom_call_target="tpu_custom_call" | custom-call | tf_op jit(solution)/shard_map/pallas_call | solution.py:404
  72.8 9.1 %collective-permute-done.12 = bf16[48,2048]{1,0:T(8,128)(2,1)S(1)} collective-permute-done((bf16[48,2048]{1,0:T(8,128)(2,1)S(1)}, bf16[48,2048]{1,0:T(8,128)(2,1)S(1)}, u32[]{:S(2)}, u32[]{:S(2)}) %collective-permute-start.12) | collective-permute-done | bytes 196640 | tf_op jit(solution)/shard_map/ppermute | solution.py:1088
  88.4 5.0 all-to-all-start
  94.7 4.6 shard_map.425
  99.3 3.7 all-to-all-done.refs_1_.refs_4_.refs_2_
  110.0 10.2 %shard_map.426 = (bf16[480,4608]{1,0:T(8,128)(2,1)}, f32[480,512]{1,0:T(8,128)}, f32[32,8,128]{2,1,0:T(8,128)}) custom-call(f32[1]{0:T(128)} %bitcast.17.refs_0_.cnt, f32[32,8,128]{2,1,0:T(8,128)} %copy-done.37, f32[2,512]{1,0:T(2,128)} %get-tuple-element.260.refs_2_.refs_5_.refs_3_, f32[480,128]{1,0:T(8,128)} %broadcast_in_dim.12.refs_3_.mask.refs_4_.refs_6_, ...), custom_call_target="tpu_custom_call" | custom-call | tf_op jit(solution)/shard_map/pallas_call | solution.py:404
  120.2 5.3 %all-to-all-start.1 = ((f32[32,8,128]{2,1,0:T(8,128)}), f32[32,8,128]{2,1,0:T(8,128)S(1)}, u32[]{:S(2)}, u32[]{:S(2)}) async-start(f32[32,8,128]{2,1,0:T(8,128)} %get-tuple-element.270), calls=%async_computation.1 | async-start | bytes 262144 | tf_op jit(solution)/shard_map/all_to_all | solution.py:1092
  128.0 6.3 %all-to-all-done.1.s1.refs_2_ = f32[32,8,128]{2,1,0:T(8,128)S(1)} async-done(((f32[32,8,128]{2,1,0:T(8,128)}), f32[32,8,128]{2,1,0:T(8,128)S(1)}, u32[]{:S(2)}, u32[]{:S(2)}) %all-to-all-start.1) | async-done | bytes 131104 | tf_op jit(solution)/shard_map/all_to_all | solution.py:1092
  141.4 5.5 %shard_map.427 = (bf16[32,32,2048]{2,1,0:T(8,128)(2,1)}, bf16[32,16,2048]{2,1,0:T(8,128)(2,1)}) custom-call(s32[1]{0:T(128)} %bitcast.2.me_ref, bf16[16,48,1024]{2,1,0:T(8,128)(2,1)} %copy-done.30, bf16[16,48,1024]{2,1,0:T(8,128)(2,1)} %collective-permute-done.20.refs_1_, bf16[16,48,1024]{2,1,0:T(8,128)(2,1)} %copy-done.31, bf16[16,48,1024]{2,1,0:T(8,128)(2,1)} %copy-done.36), custom_call_target="tpu_custom_call" | custom-call | tf_op jit(solution)/shard_map/pallas_call | solution.py:1210
  146.9 9.3 %shard_map.428 = (bf16[480,512]{1,0:T(8,128)(2,1)}, f32[480,2048]{1,0:T(8,128)}, f32[480,2048]{1,0:T(8,128)}, f32[4,16,128]{2,1,0:T(8,128)}) custom-call(f32[1]{0:T(128)} %bitcast.17.refs_0_.cnt, f32[480,512]{1,0:T(8,128)} %get-tuple-element.269.a2.refs_8_, f32[32,8,128]{2,1,0:T(8,128)} %copy-done.32, f32[2,512]{1,0:T(2,128)} %get-tuple-element.553.gb1.refs_3_, ...), custom_call_target="tpu_custom_call" | custom-call | tf_op jit(solution)/shard_map/pallas_call | solution.py:895
  170.3 3.1 slice.210
  174.0 9.3 %shard_map.429 = (f32[480,2048]{1,0:T(8,128)}, bf16[480,2048]{1,0:T(8,128)(2,1)}, f32[480,512]{1,0:T(8,128)}, f32[32,8,128]{2,1,0:T(8,128)}) custom-call(f32[1]{0:T(128)} %bitcast.17.refs_0_.cnt, f32[4,16,128]{2,1,0:T(8,128)} %add_add_fusion.2.refs_1_.s23, f32[2,2048]{1,0:T(2,128)} %get-tuple-element.550.refs_2_.gb2, ...), custom_call_target="tpu_custom_call" | custom-call | tf_op jit(solution)/shard_map/pallas_call | solution.py:404
  183.3 3.3 all-to-all-start.2
  191.8 3.5 all-to-all-done.2.refs_1_.refs_14_.s4
  195.9 7.9 %shard_map.430 = (f32[480,512]{1,0:T(8,128)}, bf16[480,512]{1,0:T(8,128)(2,1)}, f32[480,512]{1,0:T(8,128)}, bf16[3,480,1152]{2,1,0:T(8,128)(2,1)}, f32[16,512]{1...) custom-call(f32[1]{0:T(128)} %bitcast.17.refs_0_.cnt, f32[32,8,128]{2,1,0:T(8,128)} %copy-done.33, ...), custom_call_target="tpu_custom_call" | custom-call | tf_op jit(solution)/shard_map/pallas_call | solution.py:404
  206.5 8.6 %all-to-all-done.3.refs_1_.refs_5_.refs_2_ = f32[32,8,128]{2,1,0:T(8,128)S(1)} async-done(((f32[32,8,128]{2,1,0:T(8,128)}), f32[32,8,128]{2,1,0:T(8,128)S(1)}, u32[]{:S(2)}, u32[]{:S(2)}) %all-to-all-start.3) | async-done | bytes 131104 | tf_op jit(solution)/shard_map/all_to_all | solution.py:1092
  215.7 5.9 %shard_map.431 = (bf16[480,512]{1,0:T(8,128)(2,1)}, f32[480,2048]{1,0:T(8,128)}, f32[32,128]{1,0:T(8,128)}) custom-call(f32[1]{0:T(128)} %bitcast.17.refs_0_.cnt, f32[32,8,128]{2,1,0:T(8,128)} %copy-done.34, f32[2,512]{1,0:T(2,128)} %get-tuple-element.551.refs_2_.refs_6_.refs_3_, f32[480,128]{1,0:T(8,128)} %broadcast_in_dim.12.refs_3_.mask.refs_4_.refs_6_, ...), custom_call_target="tpu_custom_call" | custom-call | tf_op jit(solution)/shard_map/pallas_call | solution.py:361
  224.2 11.0 %all_to_all.55 = f32[16,16,128]{2,1,0:T(8,128)S(1)} all-to-all(f32[16,16,128]{2,1,0:T(8,128)S(1)} %broadcast_in_dim.14), channel_id=1, replica_groups={{0,1,4,5,8,9,12,13,16,17,20,21,24,25,28,29},{2,3,6,7,10,11,14,15,18,19,..., dimensions={0} | all-to-all | bytes 262144 | tf_op jit(solution)/shard_map/all_to_all | solution.py:1102
  238.6 10.3 %shard_map.432 = (bf16[4,4,4,2048]{3,2,1,0:T(4,128)(2,1)}, bf16[4,6,6,2048]{3,2,1,0:T(8,128)(2,1)}, bf16[4,7,7,2048]{3,2,1,0:T(8,128)(2,1)}, f32[480,2048]{1,0:T(8,128)}, f32[32,128]{1,0:T(8,128)}) custom-call(f32[1]{0:T(128)} %bitcast.17.refs_0_.cnt, f32[32,128]{1,0:T(8,128)} %maximum_select_fusion.refs_1_.refs_2_, ...), custom_call_target="tpu_custom_call" | custom-call | tf_op jit(solution)/shard_map/pallas_call | solution.py:404
  251.7 10.8 %all_to_all.56 = f32[16,16,128]{2,1,0:T(8,128)S(1)} all-to-all(f32[16,16,128]{2,1,0:T(8,128)S(1)} %broadcast_in_dim.15), channel_id=1, replica_groups={{0,1,4,5,8,9,12,13,16,17,20,21,24,25,28,29},{2,3,6,7,10,11,14,15,18,19,..., dimensions={0} | all-to-all | bytes 262144 | tf_op jit(solution)/shard_map/all_to_all | solution.py:1102
  264.4 9.7 %shard_map.433 = (bf16[512,2048]{1,0:T(8,128)(2,1)}, f32[480,512]{1,0:T(8,128)}, f32[32,8,128]{2,1,0:T(8,128)}) custom-call(f32[1]{0:T(128)} %bitcast.17.refs_0_.cnt, f32[32,128]{1,0:T(8,128)} %maximum_select_fusion.1.refs_1_.t6, f32[32,128]{1,0:T(8,128)} %maximum_select_fusion.refs_1_.refs_2_, f32[2,2048]{1,0:T(2,128)} %get-tuple-element.548.refs_2_.refs_3_, ...), custom_call_target="tpu_custom_call" | custom-call | tf_op jit(solution)/shard_map/pallas_call | solution.py:361
  278.9 6.5 %all-to-all-done.6.refs_1_.t5 = f32[32,8,128]{2,1,0:T(8,128)S(1)} async-done(((f32[32,8,128]{2,1,0:T(8,128)}), f32[32,8,128]{2,1,0:T(8,128)S(1)}, u32[]{:S(2)}, u32[]{:S(2)}) %all-to-all-start.6) | async-done | bytes 131104 | tf_op jit(solution)/shard_map/all_to_all | solution.py:1092
  286.1 10.2 %shard_map.434 = (f32[480,512]{1,0:T(8,128)}, bf16[3,1152,128]{2,1,0:T(8,128)(2,1)}, f32[16,128]{1,0:T(8,128)}, f32[512,32]{1,0:T(8,128)}, f32[32,512]{1,0:T(8,128)}, /*index=5*/f32[32,8,128]{2,1,0:T(8,128)}) custom-call(f32[1]{0:T(128)} %bitcast.17.refs_0_.cnt, f32[32,8,128]{2,1,0:T(8,128)} %copy-done.38, f32[32,8,128]{2,1,0:T(8,128)} %copy-done.34, ...), custom_call_target="tpu_custom_call" | custom-call | tf_op jit(solution)/shard_map/pallas_call | solution.py:361
  301.4 6.2 %all-to-all-done.7.t4 = f32[32,8,128]{2,1,0:T(8,128)S(1)} async-done(((f32[32,8,128]{2,1,0:T(8,128)}), f32[32,8,128]{2,1,0:T(8,128)S(1)}, u32[]{:S(2)}, u32[]{:S(2)}) %all-to-all-start.7) | async-done | bytes 131104 | tf_op jit(solution)/shard_map/all_to_all | solution.py:1092
  308.3 12.6 %shard_map.435 = (bf16[2048,512]{1,0:T(8,128)(2,1)}, f32[480,2048]{1,0:T(8,128)}, f32[4,16,128]{2,1,0:T(8,128)}) custom-call(f32[1]{0:T(128)} %bitcast.17.refs_0_.cnt, f32[32,8,128]{2,1,0:T(8,128)} %copy-done.39, f32[32,8,128]{2,1,0:T(8,128)} %copy-done.33, f32[2,512]{1,0:T(2,128)} %get-tuple-element.552.refs_2_.refs_15_.gb4, ...), custom_call_target="tpu_custom_call" | custom-call | tf_op jit(solution)/shard_map/pallas_call | solution.py:895
  322.4 5.2 shard_map.436
  348.5 14.7 %shard_map.438 = (bf16[512,2048]{1,0:T(8,128)(2,1)}, bf16[1024,2048]{1,0:T(8,128)(2,1)}, bf16[480,2048]{1,0:T(8,128)(2,1)}, f32[480,512]{1,0:T(8,128)}, f32[32,8,128]{2,1,0:T(8,128)}) custom-call(f32[1]{0:T(128)} %bitcast.17.refs_0_.cnt, f32[4,16,128]{2,1,0:T(8,128)} %add_add_fusion.tj, f32[4,16,128]{2,1,0:T(8,128)} %add_add_fusion.2.refs_1_.s23, ...), custom_call_target="tpu_custom_call" | custom-call | tf_op jit(solution)/shard_map/pallas_call | solution.py:895
  363.2 4.0 all-to-all-start.8
  367.2 5.9 %shard_map.440 = (bf16[2,16,192,256]{3,2,1,0:T(8,128)(2,1)}, bf16[2,16,192,256]{3,2,1,0:T(8,128)(2,1)}) custom-call(s32[1]{0:T(128)} %bitcast.2.me_ref, bf16[32,16,2048]{2,1,0:T(8,128)(2,1)} %bitcast.109, bf16[32,32,2048]{2,1,0:T(8,128)(2,1)} %bitcast.99), custom_call_target="tpu_custom_call" | custom-call | tf_op jit(solution)/shard_map/pallas_call | solution.py:1349
  381.0 11.1 %shard_map.441 = (bf16[480,512]{1,0:T(8,128)(2,1)}, f32[4,480,512]{2,1,0:T(8,128)}, f32[32,8,128]{2,1,0:T(8,128)}) custom-call(f32[1]{0:T(128)} %bitcast.17.refs_0_.cnt, f32[32,8,128]{2,1,0:T(8,128)} %copy-done.40, f32[32,8,128]{2,1,0:T(8,128)} %copy-done.32, f32[2,512]{1,0:T(2,128)} %get-tuple-element.553.gb1.refs_3_, f32[32,8,128]{2,1,0:T(8,128)} %copy-done.37, ...), custom_call_target="tpu_custom_call" | custom-call | tf_op jit(solution)/shard_map/pallas_call | solution.py:361
  395.2 3.7 all-to-all-start.9
  399.0 7.2 %shard_map.442 = bf16[4608,512]{1,0:T(8,128)(2,1)} custom-call(bf16[480,512]{1,0:T(8,128)(2,1)} %get-tuple-element.354.refs_0_, bf16[480,4608]{1,0:T(8,128)(2,1)} %get-tuple-element.355.refs_1_), custom_call_target="tpu_custom_call" | custom-call | tf_op jit(solution)/shard_map/pallas_call | solution.py:361
  406.2 4.8 shard_map.443
  420.7 8.7 %shard_map.445 = (bf16[4,480,512]{2,1,0:T(8,128)(2,1)}, bf16[1024,512]{1,0:T(8,128)(2,1)}) custom-call(f32[1]{0:T(128)} %bitcast.17.refs_0_.cnt, f32[32,8,128]{2,1,0:T(8,128)} %copy-done.48, f32[32,8,128]{2,1,0:T(8,128)} %copy-done.37, f32[2,512]{1,0:T(2,128)} %get-tuple-element.260.refs_2_.refs_5_.refs_3_, ...), custom_call_target="tpu_custom_call" | custom-call | flops 20000000000 | bytes 60000000 | tf_op jit(solution)/shard_map/pallas_call | solution.py:404
  429.5 3.8 shard_map.446
  435.9 11.8 %shard_map.447 = (bf16[4,8,8,1024]{3,2,1,0:T(8,128)(2,1)}, bf16[4,12,12,1024]{3,2,1,0:T(8,128)(2,1)}, bf16[4,14,14,1024]{3,2,1,0:T(8,128)(2,1)}) custom-call(f32[480,128]{1,0:T(8,128)} %broadcast_in_dim.12.refs_3_.mask.refs_4_.refs_6_, bf16[256,128]{1,0:T(8,128)(2,1)} %constant.61.clone.tc, bf16[192,192]{1,0:T(8,128)(2,1)} %constant.62.clone.tm, ...), custom_call_target="tpu_custom_call" | custom-call | tf_op jit(solution)/shard_map/pallas_call | solution.py:895
  463.8 5.1 all-to-all-start.10
  468.9 4.6 collective-permute-done.51.refs_2_
  476.3 4.1 copy.150
  490.4 6.6 %collective-permute-done.55.refs_1_ = bf16[2,2,144,256]{3,2,1,0:T(8,128)(2,1)S(1)} collective-permute-done((bf16[2,2,144,256]{3,2,1,0:T(8,128)(2,1)S(1)}, bf16[2,2,144,256]{3,2,1,0:T(8,128)(2,1)S(1)}, u32[]{:S(2)}, u32[]{:S(2)}) %collective-permute-start.55) | collective-permute-done | bytes 294944 | tf_op jit(solution)/shard_map/ppermute | solution.py:1088
  (400 shorter events, 194.2 us)
Async XLA Ops:
  7.2 151.2 %all-gather.3.cloned.1.call-start = ((), (), s32[]{:S(2)}) async-start(), calls=%async_computation.11 | async-start | bytes 3244032 | tf_op jit(solution)/shard_map/all_gather | solution.py:1396
  11.4 16.8 %collective-permute-start = (bf16[192,512]{1,0:T(8,128)(2,1)S(1)}, bf16[192,512]{1,0:T(8,128)(2,1)S(1)}, u32[]{:S(2)}, u32[]{:S(2)}) collective-permute-start(bf16[192,512]{1,0:T(8,128)(2,1)S(1)} %pad_maximum_fusion.9), channel_id=1, source_target_pairs={{0,8},{1,9},{2,10},{3,11},{4,12},{5,13},{6,14},{7,15},{8,0},{9,1},... | collective-permute-start | bytes 589832 | tf_op jit(solution)/shard_map/ppermute | solution.py:1088
  14.5 17.2 %collective-permute-start.1 = (bf16[192,512]{1,0:T(8,128)(2,1)S(1)}, bf16[192,512]{1,0:T(8,128)(2,1)S(1)}, u32[]{:S(2)}, u32[]{:S(2)}) collective-permute-start(bf16[192,512]{1,0:T(8,128)(2,1)S(1)} %pad_maximum_fusion.9), channel_id=1, source_target_pairs={{0,16},{1,17},{2,18},{3,19},{4,20},{5,21},{6,22},{7,23},{8,24},{9,... | collective-permute-start | bytes 589832 | tf_op jit(solution)/shard_map/ppermute | solution.py:1088
  17.1 14.6 %collective-permute-start.2 = (bf16[192,512]{1,0:T(8,128)(2,1)S(1)}, bf16[192,512]{1,0:T(8,128)(2,1)S(1)}, u32[]{:S(2)}, u32[]{:S(2)}) collective-permute-start(bf16[192,512]{1,0:T(8,128)(2,1)S(1)} %pad_maximum_fusion.9), channel_id=1, source_target_pairs={{0,24},{1,25},{2,26},{3,27},{4,28},{5,29},{6,30},{7,31},{8,16},{9,... | collective-permute-start | bytes 589832 | tf_op jit(solution)/shard_map/ppermute | solution.py:1088
  43.0 10.1 %collective-permute-start.7 = (bf16[4,144,256]{2,1,0:T(8,128)(2,1)S(1)}, bf16[4,144,256]{2,1,0:T(8,128)(2,1)S(1)}, u32[]{:S(2)}, u32[]{:S(2)}) collective-permute-start(bf16[4,144,256]{2,1,0:T(8,128)(2,1)S(1)} %get-tuple-element.535), channel_id=1, source_target_pairs={{0,1},{1,0},{2,3},{3,2},{4,5},{5,4},{6,7},{7,6},{8,9},{9,8},{10,11... | collective-permute-start | bytes 884744 | tf_op jit(solution)/shard_map/ppermute | solution.py:1088
  44.0 9.4 %collective-permute-start.8 = (bf16[4,144,256]{2,1,0:T(8,128)(2,1)S(1)}, bf16[4,144,256]{2,1,0:T(8,128)(2,1)S(1)}, u32[]{:S(2)}, u32[]{:S(2)}) collective-permute-start(bf16[4,144,256]{2,1,0:T(8,128)(2,1)S(1)} %get-tuple-element.534), channel_id=1, source_target_pairs={{0,4},{1,5},{2,6},{3,7},{4,0},{5,1},{6,2},{7,3},{8,12},{9,13},{10,... | collective-permute-start | bytes 884744 | tf_op jit(solution)/shard_map/ppermute | solution.py:1088
  53.5 28.4 %collective-permute-start.10 = (bf16[8,144,256]{2,1,0:T(8,128)(2,1)S(1)}, bf16[8,144,256]{2,1,0:T(8,128)(2,1)S(1)}, u32[]{:S(2)}, u32[]{:S(2)}) collective-permute-start(bf16[8,144,256]{2,1,0:T(8,128)(2,1)S(1)} %pad_maximum_fusion.7), channel_id=1, source_target_pairs={{0,1},{1,0},{2,3},{3,2},{4,5},{5,4},{6,7},{7,6},{8,9},{9,8},{10,11... | collective-permute-start | bytes 1769480 | tf_op jit(solution)/shard_map/ppermute | solution.py:1088
  55.0 27.0 %collective-permute-start.9 = (bf16[8,144,256]{2,1,0:T(8,128)(2,1)S(1)}, bf16[8,144,256]{2,1,0:T(8,128)(2,1)S(1)}, u32[]{:S(2)}, u32[]{:S(2)}) collective-permute-start(bf16[8,144,256]{2,1,0:T(8,128)(2,1)S(1)} %pad_maximum_fusion.6), channel_id=1, source_target_pairs={{0,4},{1,5},{2,6},{3,7},{4,0},{5,1},{6,2},{7,3},{8,12},{9,13},{10,... | collective-permute-start | bytes 1769480 | tf_op jit(solution)/shard_map/ppermute | solution.py:1088
  56.8 16.0 %collective-permute-start.11 = (bf16[48,2048]{1,0:T(8,128)(2,1)S(1)}, bf16[48,2048]{1,0:T(8,128)(2,1)S(1)}, u32[]{:S(2)}, u32[]{:S(2)}) collective-permute-start(bf16[48,2048]{1,0:T(8,128)(2,1)S(1)} %pad_maximum_fusion.11), channel_id=1, source_target_pairs={{0,8},{1,9},{2,10},{3,11},{4,12},{5,13},{6,14},{7,15},{8,0},{9,1},... | collective-permute-start | bytes 589832 | tf_op jit(solution)/shard_map/ppermute | solution.py:1088
  62.0 19.9 %collective-permute-start.12 = (bf16[48,2048]{1,0:T(8,128)(2,1)S(1)}, bf16[48,2048]{1,0:T(8,128)(2,1)S(1)}, u32[]{:S(2)}, u32[]{:S(2)}) collective-permute-start(bf16[48,2048]{1,0:T(8,128)(2,1)S(1)} %pad_maximum_fusion.11), channel_id=1, source_target_pairs={{0,16},{1,17},{2,18},{3,19},{4,20},{5,21},{6,22},{7,23},{8,24},{9,... | collective-permute-start | bytes 589832 | tf_op jit(solution)/shard_map/ppermute | solution.py:1088
  63.2 18.7 %collective-permute-start.13 = (bf16[48,2048]{1,0:T(8,128)(2,1)S(1)}, bf16[48,2048]{1,0:T(8,128)(2,1)S(1)}, u32[]{:S(2)}, u32[]{:S(2)}) collective-permute-start(bf16[48,2048]{1,0:T(8,128)(2,1)S(1)} %pad_maximum_fusion.11), channel_id=1, source_target_pairs={{0,24},{1,25},{2,26},{3,27},{4,28},{5,29},{6,30},{7,31},{8,16},{9,... | collective-permute-start | bytes 589832 | tf_op jit(solution)/shard_map/ppermute | solution.py:1088
  84.0 10.7 %collective-permute-start.14 = (bf16[16,144,256]{2,1,0:T(8,128)(2,1)S(1)}, bf16[16,144,256]{2,1,0:T(8,128)(2,1)}, u32[]{:S(2)}, u32[]{:S(2)}) collective-permute-start(bf16[16,144,256]{2,1,0:T(8,128)(2,1)S(1)} %pad_maximum_fusion.refs_0_), channel_id=1, source_target_pairs={{0,2},{1,3},{2,0},{3,1},{4,6},{5,7},{6,4},{7,5},{8,10},{9,11},{10,... | collective-permute-start | bytes 3538952 | tf_op jit(solution)/shard_map/ppermute | solution.py:1088
  84.1 10.6 %collective-permute-start.15 = (bf16[16,144,256]{2,1,0:T(8,128)(2,1)S(1)}, bf16[16,144,256]{2,1,0:T(8,128)(2,1)}, u32[]{:S(2)}, u32[]{:S(2)}) collective-permute-start(bf16[16,144,256]{2,1,0:T(8,128)(2,1)S(1)} %pad_maximum_fusion.1.refs_2_), channel_id=1, source_target_pairs={{0,2},{1,3},{2,0},{3,1},{4,6},{5,7},{6,4},{7,5},{8,10},{9,11},{10,... | collective-permute-start | bytes 3538952 | tf_op jit(solution)/shard_map/ppermute | solution.py:1088
  85.7 17.4 %collective-permute-start.16 = (bf16[4,48,1024]{2,1,0:T(8,128)(2,1)S(1)}, bf16[4,48,1024]{2,1,0:T(8,128)(2,1)}, u32[]{:S(2)}, u32[]{:S(2)}) collective-permute-start(bf16[4,48,1024]{2,1,0:T(8,128)(2,1)S(1)} %get-tuple-element.256), channel_id=1, source_target_pairs={{0,1},{1,0},{2,3},{3,2},{4,5},{5,4},{6,7},{7,6},{8,9},{9,8},{10,11... | collective-permute-start | bytes 1179656 | tf_op jit(solution)/shard_map/ppermute | solution.py:1088
  86.4 16.7 %collective-permute-start.17 = (bf16[4,48,1024]{2,1,0:T(8,128)(2,1)S(1)}, bf16[4,48,1024]{2,1,0:T(8,128)(2,1)}, u32[]{:S(2)}, u32[]{:S(2)}) collective-permute-start(bf16[4,48,1024]{2,1,0:T(8,128)(2,1)S(1)} %get-tuple-element.257), channel_id=1, source_target_pairs={{0,4},{1,5},{2,6},{3,7},{4,0},{5,1},{6,2},{7,3},{8,12},{9,13},{10,... | collective-permute-start | bytes 1179656 | tf_op jit(solution)/shard_map/ppermute | solution.py:1088
  88.4 14.7 %all-to-all-start = ((f32[32,8,128]{2,1,0:T(8,128)}), f32[32,8,128]{2,1,0:T(8,128)S(1)}, u32[]{:S(2)}, u32[]{:S(2)}) async-start(f32[32,8,128]{2,1,0:T(8,128)} %get-tuple-element.252), calls=%async_computation | async-start | bytes 262144 | tf_op jit(solution)/shard_map/all_to_all | solution.py:1092
  93.4 113.1 %all-gather.5.cloned.1.call-start = ((), (), s32[]{:S(2)}) async-start(), calls=%async_computation.12 | async-start | bytes 2162688 | tf_op jit(solution)/shard_map/all_gather | solution.py:1396
  107.0 27.2 %collective-permute-start.18 = (bf16[8,48,1024]{2,1,0:T(8,128)(2,1)}, bf16[8,48,1024]{2,1,0:T(8,128)(2,1)}, u32[]{:S(2)}, u32[]{:S(2)}) collective-permute-start(bf16[8,48,1024]{2,1,0:T(8,128)(2,1)} %pad_maximum_fusion.3), channel_id=1, source_target_pairs={{0,4},{1,5},{2,6},{3,7},{4,0},{5,1},{6,2},{7,3},{8,12},{9,13},{10,... | collective-permute-start | bytes 2359304 | tf_op jit(solution)/shard_map/ppermute | solution.py:1088
  107.7 26.6 %collective-permute-start.19 = (bf16[8,48,1024]{2,1,0:T(8,128)(2,1)}, bf16[8,48,1024]{2,1,0:T(8,128)(2,1)}, u32[]{:S(2)}, u32[]{:S(2)}) collective-permute-start(bf16[8,48,1024]{2,1,0:T(8,128)(2,1)} %pad_maximum_fusion.4), channel_id=1, source_target_pairs={{0,1},{1,0},{2,3},{3,2},{4,5},{5,4},{6,7},{7,6},{8,9},{9,8},{10,11... | collective-permute-start | bytes 2359304 | tf_op jit(solution)/shard_map/ppermute | solution.py:1088
  120.2 14.0 %all-to-all-start.1 = ((f32[32,8,128]{2,1,0:T(8,128)}), f32[32,8,128]{2,1,0:T(8,128)S(1)}, u32[]{:S(2)}, u32[]{:S(2)}) async-start(f32[32,8,128]{2,1,0:T(8,128)} %get-tuple-element.270), calls=%async_computation.1 | async-start | bytes 262144 | tf_op jit(solution)/shard_map/all_to_all | solution.py:1092
  183.3 11.9 %all-to-all-start.2 = ((f32[32,8,128]{2,1,0:T(8,128)}), f32[32,8,128]{2,1,0:T(8,128)S(1)}, u32[]{:S(2)}, u32[]{:S(2)}) async-start(f32[32,8,128]{2,1,0:T(8,128)} %get-tuple-element.287), calls=%async_computation.2 | async-start | bytes 262144 | tf_op jit(solution)/shard_map/all_to_all | solution.py:1092
  203.8 11.2 %all-to-all-start.3 = ((f32[32,8,128]{2,1,0:T(8,128)}), f32[32,8,128]{2,1,0:T(8,128)S(1)}, u32[]{:S(2)}, u32[]{:S(2)}) async-start(f32[32,8,128]{2,1,0:T(8,128)} %get-tuple-element.289), calls=%async_computation.3 | async-start | bytes 262144 | tf_op jit(solution)/shard_map/all_to_all | solution.py:1092
  274.1 11.4 %all-to-all-start.6 = ((f32[32,8,128]{2,1,0:T(8,128)}), f32[32,8,128]{2,1,0:T(8,128)S(1)}, u32[]{:S(2)}, u32[]{:S(2)}) async-start(f32[32,8,128]{2,1,0:T(8,128)} %get-tuple-element.299), calls=%async_computation.6 | async-start | bytes 262144 | tf_op jit(solution)/shard_map/all_to_all | solution.py:1092
  296.3 11.4 %all-to-all-start.7 = ((f32[32,8,128]{2,1,0:T(8,128)}), f32[32,8,128]{2,1,0:T(8,128)S(1)}, u32[]{:S(2)}, u32[]{:S(2)}) async-start(f32[32,8,128]{2,1,0:T(8,128)} %get-tuple-element.307), calls=%async_computation.7 | async-start | bytes 262144 | tf_op jit(solution)/shard_map/all_to_all | solution.py:1092
  327.6 14.6 %collective-permute-start.40 = (bf16[2,16,160,256]{3,2,1,0:T(8,128)(2,1)}, bf16[2,16,160,256]{3,2,1,0:T(8,128)(2,1)S(1)}, u32[]{:S(2)}, u32[]{:S(2)}) collective-permute-start(bf16[2,16,160,256]{3,2,1,0:T(8,128)(2,1)} %get-tuple-element.322), channel_id=1, source_target_pairs={{0,2},{1,3},{2,0},{3,1},{4,6},{5,7},{6,4},{7,5},{8,10},{9,11},{10,... | collective-permute-start | bytes 7864328 | tf_op jit(solution)/shard_map/ppermute | solution.py:1088
  346.2 16.9 %collective-permute-start.41 = (bf16[8,160,256]{2,1,0:T(8,128)(2,1)}, bf16[8,160,256]{2,1,0:T(8,128)(2,1)S(1)}, u32[]{:S(2)}, u32[]{:S(2)}) collective-permute-start(bf16[8,160,256]{2,1,0:T(8,128)(2,1)} %get-tuple-element.329), channel_id=1, source_target_pairs={{0,1},{1,0},{2,3},{3,2},{4,5},{5,4},{6,7},{7,6},{8,9},{9,8},{10,11... | collective-permute-start | bytes 1966088 | tf_op jit(solution)/shard_map/ppermute | solution.py:1088
  347.3 15.8 %collective-permute-start.42 = (bf16[8,160,256]{2,1,0:T(8,128)(2,1)S(1)}, bf16[8,160,256]{2,1,0:T(8,128)(2,1)S(1)}, u32[]{:S(2)}, u32[]{:S(2)}) collective-permute-start(bf16[8,160,256]{2,1,0:T(8,128)(2,1)S(1)} %get-tuple-element.330), channel_id=1, source_target_pairs={{0,4},{1,5},{2,6},{3,7},{4,0},{5,1},{6,2},{7,3},{8,12},{9,13},{10,... | collective-permute-start | bytes 1966088 | tf_op jit(solution)/shard_map/ppermute | solution.py:1088
  363.2 13.6 %all-to-all-start.8 = ((f32[32,8,128]{2,1,0:T(8,128)}), f32[32,8,128]{2,1,0:T(8,128)S(1)}, u32[]{:S(2)}, u32[]{:S(2)}) async-start(f32[32,8,128]{2,1,0:T(8,128)} %get-tuple-element.334), calls=%async_computation.8 | async-start | bytes 262144 | tf_op jit(solution)/shard_map/all_to_all | solution.py:1092
  377.5 16.1 %collective-permute-start.45 = (bf16[2,16,192,256]{3,2,1,0:T(8,128)(2,1)}, bf16[2,16,192,256]{3,2,1,0:T(8,128)(2,1)S(1)}, u32[]{:S(2)}, u32[]{:S(2)}) collective-permute-start(bf16[2,16,192,256]{3,2,1,0:T(8,128)(2,1)} %get-tuple-element.351), channel_id=1, source_target_pairs={{0,2},{1,3},{2,0},{3,1},{4,6},{5,7},{6,4},{7,5},{8,10},{9,11},{10,... | collective-permute-start | bytes 9437192 | tf_op jit(solution)/shard_map/ppermute | solution.py:1088
  377.8 14.3 %collective-permute-start.43 = (bf16[4,160,256]{2,1,0:T(8,128)(2,1)}, bf16[4,160,256]{2,1,0:T(8,128)(2,1)S(1)}, u32[]{:S(2)}, u32[]{:S(2)}) collective-permute-start(bf16[4,160,256]{2,1,0:T(8,128)(2,1)} %get-tuple-element.348), channel_id=1, source_target_pairs={{0,4},{1,5},{2,6},{3,7},{4,0},{5,1},{6,2},{7,3},{8,12},{9,13},{10,... | collective-permute-start | bytes 983048 | tf_op jit(solution)/shard_map/ppermute | solution.py:1088
  379.5 13.3 %collective-permute-start.44 = (bf16[4,160,256]{2,1,0:T(8,128)(2,1)S(1)}, bf16[4,160,256]{2,1,0:T(8,128)(2,1)S(1)}, u32[]{:S(2)}, u32[]{:S(2)}) collective-permute-start(bf16[4,160,256]{2,1,0:T(8,128)(2,1)S(1)} %get-tuple-element.349), channel_id=1, source_target_pairs={{0,1},{1,0},{2,3},{3,2},{4,5},{5,4},{6,7},{7,6},{8,9},{9,8},{10,11... | collective-permute-start | bytes 983048 | tf_op jit(solution)/shard_map/ppermute | solution.py:1088
  395.2 15.8 %all-to-all-start.9 = ((f32[32,8,128]{2,1,0:T(8,128)}), f32[32,8,128]{2,1,0:T(8,128)S(1)}, u32[]{:S(2)}, u32[]{:S(2)}) async-start(f32[32,8,128]{2,1,0:T(8,128)} %get-tuple-element.357), calls=%async_computation.9 | async-start | bytes 262144 | tf_op jit(solution)/shard_map/all_to_all | solution.py:1092
  411.0 18.4 %collective-permute-start.46 = (bf16[2,16,144,256]{3,2,1,0:T(8,128)(2,1)}, bf16[2,16,144,256]{3,2,1,0:T(8,128)(2,1)}, u32[]{:S(2)}, u32[]{:S(2)}) collective-permute-start(bf16[2,16,144,256]{3,2,1,0:T(8,128)(2,1)} %get-tuple-element.367), channel_id=1, source_target_pairs={{0,2},{1,3},{2,0},{3,1},{4,6},{5,7},{6,4},{7,5},{8,10},{9,11},{10,... | collective-permute-start | bytes 7077896 | tf_op jit(solution)/shard_map/ppermute | solution.py:1088
  417.5 30.2 %collective-permute-start.47 = (bf16[8,192,256]{2,1,0:T(8,128)(2,1)}, bf16[8,192,256]{2,1,0:T(8,128)(2,1)S(1)}, u32[]{:S(2)}, u32[]{:S(2)}) collective-permute-start(bf16[8,192,256]{2,1,0:T(8,128)(2,1)} %get-tuple-element.377), channel_id=1, source_target_pairs={{0,1},{1,0},{2,3},{3,2},{4,5},{5,4},{6,7},{7,6},{8,9},{9,8},{10,11... | collective-permute-start | bytes 2359304 | tf_op jit(solution)/shard_map/ppermute | solution.py:1088
  419.2 28.5 %collective-permute-start.48 = (bf16[8,192,256]{2,1,0:T(8,128)(2,1)}, bf16[8,192,256]{2,1,0:T(8,128)(2,1)S(1)}, u32[]{:S(2)}, u32[]{:S(2)}) collective-permute-start(bf16[8,192,256]{2,1,0:T(8,128)(2,1)} %get-tuple-element.378), channel_id=1, source_target_pairs={{0,4},{1,5},{2,6},{3,7},{4,0},{5,1},{6,2},{7,3},{8,12},{9,13},{10,... | collective-permute-start | bytes 2359304 | tf_op jit(solution)/shard_map/ppermute | solution.py:1088
  434.1 16.1 %collective-permute-start.49 = (bf16[8,144,256]{2,1,0:T(8,128)(2,1)}, bf16[8,144,256]{2,1,0:T(8,128)(2,1)}, u32[]{:S(2)}, u32[]{:S(2)}) collective-permute-start(bf16[8,144,256]{2,1,0:T(8,128)(2,1)} %get-tuple-element.380), channel_id=1, source_target_pairs={{0,1},{1,0},{2,3},{3,2},{4,5},{5,4},{6,7},{7,6},{8,9},{9,8},{10,11... | collective-permute-start | bytes 1769480 | tf_op jit(solution)/shard_map/ppermute | solution.py:1088
  434.7 17.0 %collective-permute-start.50 = (bf16[8,144,256]{2,1,0:T(8,128)(2,1)}, bf16[8,144,256]{2,1,0:T(8,128)(2,1)}, u32[]{:S(2)}, u32[]{:S(2)}) collective-permute-start(bf16[8,144,256]{2,1,0:T(8,128)(2,1)} %get-tuple-element.381), channel_id=1, source_target_pairs={{0,4},{1,5},{2,6},{3,7},{4,0},{5,1},{6,2},{7,3},{8,12},{9,13},{10,... | collective-permute-start | bytes 1769480 | tf_op jit(solution)/shard_map/ppermute | solution.py:1088
  435.9 24.3 %collective-permute-start.57 = (bf16[8,2,32,512]{3,2,1,0:T(8,128)(2,1)}, bf16[8,2,32,512]{3,2,1,0:T(8,128)(2,1)}, u32[]{:S(2)}, u32[]{:S(2)}) collective-permute-start(bf16[8,2,32,512]{3,2,1,0:T(8,128)(2,1)} %dynamic-slice_bitcast_fusion), channel_id=1, source_target_pairs={{0,2},{1,3},{2,0},{3,1},{4,6},{5,7},{6,4},{7,5},{8,10},{9,11},{10,... | collective-permute-start | bytes 1572872 | tf_op jit(solution)/shard_map/ppermute | solution.py:1088
  455.2 18.3 %collective-permute-start.53 = (bf16[4,192,256]{2,1,0:T(8,128)(2,1)}, bf16[4,192,256]{2,1,0:T(8,128)(2,1)S(1)}, u32[]{:S(2)}, u32[]{:S(2)}) collective-permute-start(bf16[4,192,256]{2,1,0:T(8,128)(2,1)} %get-tuple-element.398), channel_id=1, source_target_pairs={{0,4},{1,5},{2,6},{3,7},{4,0},{5,1},{6,2},{7,3},{8,12},{9,13},{10,... | collective-permute-start | bytes 1179656 | tf_op jit(solution)/shard_map/ppermute | solution.py:1088
  457.5 16.0 %collective-permute-start.54 = (bf16[2,2,160,256]{3,2,1,0:T(8,128)(2,1)S(1)}, bf16[2,2,160,256]{3,2,1,0:T(8,128)(2,1)S(1)}, u32[]{:S(2)}, u32[]{:S(2)}) collective-permute-start(bf16[2,2,160,256]{3,2,1,0:T(8,128)(2,1)S(1)} %get-tuple-element.405), channel_id=1, source_target_pairs={{0,8},{1,9},{2,10},{3,11},{4,12},{5,13},{6,14},{7,15},{8,0},{9,1},... | collective-permute-start | bytes 983048 | tf_op jit(solution)/shard_map/ppermute | solution.py:1088
  459.1 14.4 %collective-permute-start.51 = (bf16[4,144,256]{2,1,0:T(8,128)(2,1)}, bf16[4,144,256]{2,1,0:T(8,128)(2,1)S(1)}, u32[]{:S(2)}, u32[]{:S(2)}) collective-permute-start(bf16[4,144,256]{2,1,0:T(8,128)(2,1)} %copy-done.27), channel_id=1, source_target_pairs={{0,4},{1,5},{2,6},{3,7},{4,0},{5,1},{6,2},{7,3},{8,12},{9,13},{10,... | collective-permute-start | bytes 884744 | tf_op jit(solution)/shard_map/ppermute | solution.py:1088
  459.6 13.9 %collective-permute-start.52 = (bf16[4,144,256]{2,1,0:T(8,128)(2,1)}, bf16[4,144,256]{2,1,0:T(8,128)(2,1)S(1)}, u32[]{:S(2)}, u32[]{:S(2)}) collective-permute-start(bf16[4,144,256]{2,1,0:T(8,128)(2,1)} %copy-done.26), channel_id=1, source_target_pairs={{0,1},{1,0},{2,3},{3,2},{4,5},{5,4},{6,7},{7,6},{8,9},{9,8},{10,11... | collective-permute-start | bytes 884744 | tf_op jit(solution)/shard_map/ppermute | solution.py:1088
  460.2 25.2 %collective-permute-start.58 = (bf16[4,192,256]{2,1,0:T(8,128)(2,1)}, bf16[4,192,256]{2,1,0:T(8,128)(2,1)S(1)}, u32[]{:S(2)}, u32[]{:S(2)}) collective-permute-start(bf16[4,192,256]{2,1,0:T(8,128)(2,1)} %copy-done.25), channel_id=1, source_target_pairs={{0,1},{1,0},{2,3},{3,2},{4,5},{5,4},{6,7},{7,6},{8,9},{9,8},{10,11... | collective-permute-start | bytes 1179656 | tf_op jit(solution)/shard_map/ppermute | solution.py:1088
  463.8 49.3 %all-to-all-start.10 = ((bf16[16,32,512]{2,1,0:T(8,128)(2,1)}), bf16[16,32,512]{2,1,0:T(8,128)(2,1)}, u32[]{:S(2)}, u32[]{:S(2)}) async-start(bf16[16,32,512]{2,1,0:T(8,128)(2,1)} %bitcast.112), calls=%async_computation.10 | async-start | bytes 1048576 | tf_op jit(solution)/shard_map/all_to_all | solution.py:1568
  474.3 14.9 %collective-permute-start.61 = (bf16[2,1,160,256]{3,2,1,0:T(8,128)(2,1)S(1)}, bf16[2,1,160,256]{3,2,1,0:T(8,128)(2,1)S(1)}, u32[]{:S(2)}, u32[]{:S(2)}) collective-permute-start(bf16[2,1,160,256]{3,2,1,0:T(8,128)(2,1)S(1)} %get-tuple-element.434), channel_id=1, source_target_pairs={{0,16},{1,17},{2,18},{3,19},{4,20},{5,21},{6,22},{7,23},{8,24},{9,... | collective-permute-start | bytes 491528 | tf_op jit(solution)/shard_map/ppermute | solution.py:1088
  482.9 14.2 %collective-permute-start.55 = (bf16[2,2,144,256]{3,2,1,0:T(8,128)(2,1)S(1)}, bf16[2,2,144,256]{3,2,1,0:T(8,128)(2,1)S(1)}, u32[]{:S(2)}, u32[]{:S(2)}) collective-permute-start(bf16[2,2,144,256]{3,2,1,0:T(8,128)(2,1)S(1)} %get-tuple-element.408), channel_id=1, source_target_pairs={{0,8},{1,9},{2,10},{3,11},{4,12},{5,13},{6,14},{7,15},{8,0},{9,1},... | collective-permute-start | bytes 884744 | tf_op jit(solution)/shard_map/ppermute | solution.py:1088
  486.8 21.8 %collective-permute-start.59 = (bf16[2,2,192,256]{3,2,1,0:T(8,128)(2,1)S(1)}, bf16[2,2,192,256]{3,2,1,0:T(8,128)(2,1)S(1)}, u32[]{:S(2)}, u32[]{:S(2)}) collective-permute-start(bf16[2,2,192,256]{3,2,1,0:T(8,128)(2,1)S(1)} %get-tuple-element.428), channel_id=1, source_target_pairs={{0,8},{1,9},{2,10},{3,11},{4,12},{5,13},{6,14},{7,15},{8,0},{9,1},... | collective-permute-start | bytes 1179656 | tf_op jit(solution)/shard_map/ppermute | solution.py:1088
  497.7 15.4 %collective-permute-start.56 = (bf16[2,1,144,256]{3,2,1,0:T(8,128)(2,1)S(1)}, bf16[2,1,144,256]{3,2,1,0:T(8,128)(2,1)S(1)}, u32[]{:S(2)}, u32[]{:S(2)}) collective-permute-start(bf16[2,1,144,256]{3,2,1,0:T(8,128)(2,1)S(1)} %get-tuple-element.418), channel_id=1, source_target_pairs={{0,16},{1,17},{2,18},{3,19},{4,20},{5,21},{6,22},{7,23},{8,24},{9,... | collective-permute-start | bytes 442376 | tf_op jit(solution)/shard_map/ppermute | solution.py:1088
  (90 other events, 471.4 us)
Sparse Core Ops, SparseCore 0:
  32.8 72.5 all-gather.2
  109.3 57.4 all-gather.4
